TPU v7x, 32 devices: a whole 2x2x4 slice. The times are simulated.
32 devices in a mesh: dp: 4 (over y, x), fsdp: 8 (over z, core).
Axes of the slice: x: 2, y: 2, z: 4, core: 2. Of those that a mesh axis runs over, the one named last changes fastest.
Arguments:
- tokens: bfloat16 [32768, 1024], P(('dp', 'fsdp')), may hold values from -6 to 6
- lengths: int32 [64], P(('dp', 'fsdp')), may hold values from 64 to 512, as said below
- w_qkv: bfloat16 [1024, 3072], P(('dp', 'fsdp')), may hold values from -0.1875 to 0.1875
- w_out: bfloat16 [1024, 1024], P(('dp', 'fsdp')), may hold values from -1.5 to 1.5
- w_in: bfloat16 [1024, 4096], P(('dp', 'fsdp')), may hold values from -0.1875 to 0.1875
- w_down: bfloat16 [4096, 1024], P(('dp', 'fsdp')), may hold values from -0.09375 to 0.09375
- gain_one: float32 [1024], replicated, may hold values from 0.5 to 1.5
- gain_two: float32 [1024], replicated, may hold values from 0.5 to 1.5
- bias_q: float32 [1024], replicated, may hold values from -3 to 3
- bias_v: float32 [1024], replicated, may hold values from -3 to 3
- bias_out: float32 [1024], replicated, may hold values from -3 to 3
- beta_one: float32 [1024], replicated, may hold values from -3 to 3
- bias_in: float32 [4096], replicated, may hold values from -3 to 3
- bias_down: float32 [1024], replicated, may hold values from -3 to 3
- beta_two: float32 [1024], replicated, may hold values from -3 to 3
- cotangent: bfloat16 [32768, 1024], P(('dp', 'fsdp')), may hold values from -6 to 6
Outputs:
- output: bfloat16 [32768, 1024], P(('dp', 'fsdp'))
- input_grad: bfloat16 [32768, 1024], P(('dp', 'fsdp'))
- grad_bias_q: float32 [1024], P(('dp', 'fsdp'))
- grad_bias_v: float32 [1024], P(('dp', 'fsdp'))
- grad_bias_out: float32 [1024], P(('dp', 'fsdp'))
- grad_beta_one: float32 [1024], P(('dp', 'fsdp'))
- grad_bias_in: float32 [4096], P(('dp', 'fsdp'))
- grad_bias_down: float32 [1024], P(('dp', 'fsdp'))
- grad_beta_two: float32 [1024], P(('dp', 'fsdp'))
Inputs may be any that keep to these rules, and one draw needn't show every extreme that they name: `lengths`: one sequence, drawn from the seed, has exactly 512 live tokens.
All inputs are finite; a program needn't handle non-finite values.
Results may differ from a plain program's by a relative error of at most 0.013.
Values may be sent and summed in bfloat16 or wider, within the bound.
No kernel may reach another device: no remote copies, remote signals or barrier semaphores. Data moves between devices by JAX's collectives and lax.ppermute only.
A program may use at most 192 MiB of HBM per device.

v0:
```python
import math

import jax
import jax.numpy as jnp
from jax import lax
from jax.sharding import PartitionSpec as P

HD = 64
L = 512
SEQ_DEV = 1
MB = 2


LN_EPS = 1e-12


def norm_rows(hidden, gain_vec, shift_vec):
    row_mean = jnp.mean(hidden, axis=-1, keepdims=True)
    centered = hidden - row_mean
    row_var = jnp.mean(centered * centered, axis=-1, keepdims=True)
    return centered * lax.rsqrt(row_var + LN_EPS) * gain_vec + shift_vec


def gather_attention(w_qkv, w_out):
    return (
        lax.all_gather(w_qkv, ("dp", "fsdp"), axis=0, tiled=True),
        lax.all_gather(w_out, ("dp", "fsdp"), axis=0, tiled=True),
    )


def gather_feed(w_in, w_down):
    return (
        lax.all_gather(w_in, ("dp", "fsdp"), axis=0, tiled=True),
        lax.all_gather(w_down, ("dp", "fsdp"), axis=0, tiled=True),
    )


def masked_scores(queries, key_vals, live_keys, score_scale):
    scores = (
        jnp.einsum("bqhe,bkhe->bhqk", queries, key_vals, preferred_element_type=jnp.float32)
        * score_scale
    )
    return jnp.where(live_keys[:, None, None, :], scores, -1e30)


def on_device(
    tokens,
    lengths,
    w_qkv,
    w_out,
    w_in,
    w_down,
    gain_one,
    gain_two,
    bias_q,
    bias_v,
    bias_out,
    beta_one,
    bias_in,
    bias_down,
    beta_two,
    cotangent,
):
    model_width = w_out.shape[1]
    head_count = model_width // HD
    score_scale = 1.0 / math.sqrt(HD)
    row_block = SEQ_DEV * L
    sums = tuple(
        (
            jnp.zeros_like(vector)
            for vector in (bias_q, bias_v, bias_out, beta_one, bias_in, bias_down, beta_two)
        )
    )
    shares = None
    outputs = []
    in_grads = []
    for micro_index in range(MB):
        attn_pair = gather_attention(w_qkv, w_out)
        feed_pair = gather_feed(w_in, w_down)
        full_qkv, full_out = attn_pair
        full_in, full_down = feed_pair
        block_rows = tokens[micro_index * row_block : (micro_index + 1) * row_block]
        seq_lengths = lengths[micro_index * SEQ_DEV : (micro_index + 1) * SEQ_DEV]
        live_keys = jnp.arange(L)[None, :] < seq_lengths[:, None]
        row_mask = live_keys.reshape(row_block).astype(jnp.float32)
        projected = jnp.dot(block_rows, full_qkv, preferred_element_type=jnp.float32)
        queries = (
            (projected[:, :model_width] + bias_q)
            .astype(jnp.bfloat16)
            .reshape(SEQ_DEV, L, head_count, HD)
        )
        key_vals = (
            projected[:, model_width : 2 * model_width]
            .astype(jnp.bfloat16)
            .reshape(SEQ_DEV, L, head_count, HD)
        )
        values = (
            (projected[:, 2 * model_width :] + bias_v)
            .astype(jnp.bfloat16)
            .reshape(SEQ_DEV, L, head_count, HD)
        )
        scores = masked_scores(queries, key_vals, live_keys, score_scale)
        peak = jnp.max(scores, axis=-1, keepdims=True)
        powers = jnp.exp(scores - peak)
        denominator = jnp.sum(powers, axis=-1, keepdims=True)
        log_total = peak + jnp.log(denominator)
        attn_probs = (powers / denominator).astype(jnp.bfloat16)
        context = jnp.einsum(
            "bhqk,bkhe->bqhe", attn_probs, values, preferred_element_type=jnp.float32
        )
        context = context.reshape(row_block, model_width).astype(jnp.bfloat16)
        attended = jnp.dot(context, full_out, preferred_element_type=jnp.float32) + bias_out
        joined = block_rows.astype(jnp.float32) + attended
        normed_one, first_pull = jax.vjp(
            lambda joined_in, shift_in: norm_rows(joined_in, gain_one, shift_in), joined, beta_one
        )
        hidden_pre = (
            jnp.dot(normed_one.astype(jnp.bfloat16), full_in, preferred_element_type=jnp.float32)
            + bias_in
        )
        active, gelu_pull = jax.vjp(
            lambda pre_in: jax.nn.gelu(pre_in, approximate=False), hidden_pre
        )
        branch_out = (
            jnp.dot(active.astype(jnp.bfloat16), full_down, preferred_element_type=jnp.float32)
            + bias_down
        )
        result, second_pull = jax.vjp(
            lambda summed_in, shift_in: norm_rows(summed_in, gain_two, shift_in),
            normed_one + branch_out,
            beta_two,
        )
        outputs.append(result.astype(jnp.bfloat16))
        back_in, back_down = (
            lax.all_gather(w_in, ("dp", "fsdp"), axis=0, tiled=True),
            lax.all_gather(w_down, ("dp", "fsdp"), axis=0, tiled=True),
        )
        back_qkv, back_out = (
            lax.all_gather(w_qkv, ("dp", "fsdp"), axis=0, tiled=True),
            lax.all_gather(w_out, ("dp", "fsdp"), axis=0, tiled=True),
        )
        grad_out = (
            cotangent[micro_index * row_block : (micro_index + 1) * row_block].astype(jnp.float32)
            * row_mask[:, None]
        )
        d_second, d_beta_two = second_pull(grad_out)
        d_branch = d_second.astype(jnp.bfloat16)
        d_bias_down = jnp.sum(d_branch.astype(jnp.float32), axis=0)
        d_active = jnp.einsum("rd,fd->rf", d_branch, back_down, preferred_element_type=jnp.float32)
        (d_hidden,) = gelu_pull(d_active)
        d_hidden = d_hidden.astype(jnp.bfloat16)
        d_bias_in = jnp.sum(d_hidden.astype(jnp.float32), axis=0)
        d_normed = d_second + jnp.einsum(
            "rf,df->rd", d_hidden, back_in, preferred_element_type=jnp.float32
        )
        d_joined, d_beta_one = first_pull(d_normed)
        d_attended = d_joined.astype(jnp.bfloat16)
        d_bias_out = jnp.sum(d_attended.astype(jnp.float32), axis=0)
        d_context = jnp.einsum(
            "rd,ed->re", d_attended, back_out, preferred_element_type=jnp.float32
        )
        d_context = d_context.astype(jnp.bfloat16).reshape(SEQ_DEV, L, head_count, HD)
        again = masked_scores(queries, key_vals, live_keys, score_scale)
        probs_full = jnp.exp(again - log_total)
        d_probs = jnp.einsum(
            "bqhe,bkhe->bhqk", d_context, values, preferred_element_type=jnp.float32
        )
        row_dot = jnp.sum(d_probs * probs_full, axis=-1, keepdims=True)
        d_scores = (probs_full * (d_probs - row_dot)).astype(jnp.bfloat16)
        d_queries = (
            jnp.einsum("bhqk,bkhe->bqhe", d_scores, key_vals, preferred_element_type=jnp.float32)
            * score_scale
        ).astype(jnp.bfloat16)
        d_keys = (
            jnp.einsum("bhqk,bqhe->bkhe", d_scores, queries, preferred_element_type=jnp.float32)
            * score_scale
        ).astype(jnp.bfloat16)
        d_values = jnp.einsum(
            "bhqk,bqhe->bkhe",
            probs_full.astype(jnp.bfloat16),
            d_context,
            preferred_element_type=jnp.float32,
        ).astype(jnp.bfloat16)
        d_queries = d_queries.reshape(row_block, model_width)
        d_keys = d_keys.reshape(row_block, model_width)
        d_values = d_values.reshape(row_block, model_width)
        d_bias_q = jnp.sum(d_queries.astype(jnp.float32), axis=0)
        d_bias_v = jnp.sum(d_values.astype(jnp.float32), axis=0)
        d_projected = jnp.concatenate([d_queries, d_keys, d_values], axis=1)
        d_rows = d_joined + jnp.einsum(
            "re,de->rd", d_projected, back_qkv, preferred_element_type=jnp.float32
        )
        in_grads.append(d_rows.astype(jnp.bfloat16))
        block_sums = (
            d_bias_q,
            d_bias_v,
            d_bias_out,
            d_beta_one,
            d_bias_in,
            d_bias_down,
            d_beta_two,
        )
        sums = tuple((left + right for left, right in zip(sums, block_sums)))
    shares = lax.psum_scatter(sums, ("dp", "fsdp"), scatter_dimension=0, tiled=True)
    output = jnp.concatenate(outputs, axis=0)
    input_grad = jnp.concatenate(in_grads, axis=0)
    return (
        output,
        input_grad,
        shares[0],
        shares[1],
        shares[2],
        shares[3],
        shares[4],
        shares[5],
        shares[6],
    )


def solution(mesh):
    in_specs = (
        P(("dp", "fsdp"), None),
        P(("dp", "fsdp")),
        P(("dp", "fsdp"), None),
        P(("dp", "fsdp"), None),
        P(("dp", "fsdp"), None),
        P(("dp", "fsdp"), None),
        P(),
        P(),
        P(),
        P(),
        P(),
        P(),
        P(),
        P(),
        P(),
        P(("dp", "fsdp"), None),
    )
    out_specs = (
        P(("dp", "fsdp"), None),
        P(("dp", "fsdp"), None),
        P(("dp", "fsdp")),
        P(("dp", "fsdp")),
        P(("dp", "fsdp")),
        P(("dp", "fsdp")),
        P(("dp", "fsdp")),
        P(("dp", "fsdp")),
        P(("dp", "fsdp")),
    )
    return jax.shard_map(
        on_device, mesh=mesh, in_specs=in_specs, out_specs=out_specs, check_vma=False
    )
```

profile of v0, /device:TPU:0, one launch (start us, length us, event | category | flops | bytes accessed | tf_op | source)
XLA Modules:
  0.0 550.5 jit_solution(205615601787338553)
XLA Ops:
  10.0 1.3 fusion.98
  15.1 68.1 %all-gather.5.cloned.1.call-done = bf16[1024,3072]{1,0:T(8,128)(2,1)} async-done(((bf16[32,3072]{1,0:T(8,128)(2,1)}), bf16[1024,3072]{1,0:T(8,128)(2,1)}) %all-gather.5.cloned.1.call-update) | async-done | bytes 6291472 | tf_op jit(solution)/shard_map/all_gather | solution.py:26
  83.2 5.8 %fusion.76 = f32[512,3072]{1,0:T(8,128)S(1)} fusion(bf16[1024,3072]{1,0:T(8,128)(2,1)} %all-gather.5.cloned.1.call-done, bf16[1024,1024]{1,0:T(8,128)(2,1)} %param.16), kind=kOutput, calls=%fused_computation.152 | convolution fusion | flops 3221225472 | bytes 13631488 | tf_op jit(solution)/shard_map/dot_general | solution.py:86
  89.0 2.6 copy-done.22
  92.4 6.2 %fusion.78 = f32[512,3072]{1,0:T(8,128)S(1)} fusion(bf16[1024,3072]{1,0:T(8,128)(2,1)} %all-gather.5.cloned.1.call-done, bf16[1024,1024]{1,0:T(8,128)(2,1)} %param.16), kind=kOutput, calls=%fused_computation.154 | convolution fusion | flops 3221225472 | bytes 13631488 | tf_op jit(solution)/shard_map/dot_general | solution.py:86
  98.6 2.6 copy-done.23
  102.0 6.4 %fusion.42 = (bf16[512,1024]{1,0:T(8,128)(2,1)}, bf16[512,1024]{1,0:T(8,128)(2,1)}, bf16[512,1024]{1,0:T(8,128)(2,1)S(1)}, bf16[512,1024]{1,0:T(8,128)(2,1)}) fusion(f32[512,3072]{1,0:T(8,128)} %copy-done.22, f32[1024]{0:T(1024)S(1)} %copy-done.54, f32[1024]{0:T(1024)S(1)} %copy-done.55, f32[512,3072]{1,0:T(8,128)} %copy-done.23), kind=kLoop, calls=%fused_computation.82 | loop fusion | flops 4194304 | bytes 12591104 | tf_op jit(solution)/shard_map/convert_element_type | solution.py:89
  108.3 2.3 copy.70
  110.6 2.3 copy.69
  112.9 1.3 copy.65
  114.2 1.5 copy.66
  115.7 7.6 %fusion.99 = (f32[16,512]{1,0:T(8,128)S(1)}, f32[16,512,512]{1,2,0:T(8,128)}) fusion(bf16[512,16,64]{0,2,1:T(8,128)(2,1)S(1)} %bitcast.108, bf16[512,16,64]{0,2,1:T(8,128)(2,1)S(1)} %bitcast.100, pred[512]{0:T(512)(128)(4,1)S(1)} %iota_compare_fusion.1), kind=kOutput, calls=%fused_computation.195 | convolution fusion | flops 549445632 | bytes 18907648 | tf_op jit(solution)/shard_map/bqhe,bkhe->bhqk/dot_general | solution.py:40
  123.3 8.6 %fusion = f32[16,512]{1,0:T(8,128)S(1)} fusion(f32[16,512,512]{1,2,0:T(8,128)} %get-tuple-element.58, f32[16,512]{1,0:T(8,128)S(1)} %get-tuple-element.57), kind=kLoop, calls=%fused_computation.12 | loop fusion | flops 8380416 | bytes 16842752 | tf_op jit(solution)/shard_map/reduce_sum | solution.py:105
  132.5 8.7 %fusion.57 = bf16[16,64,512]{2,1,0:T(8,128)(2,1)} fusion(bf16[512,16,64]{0,2,1:T(8,128)(2,1)S(1)} %bitcast.113, f32[16,512,512]{1,2,0:T(8,128)} %get-tuple-element.58, f32[16,512]{1,0:T(8,128)S(1)} %fusion, f32[16,512]{1,0:T(8,128)S(1)} %get-tuple-element.57), kind=kOutput, calls=%fused_computation.137 | convolution fusion | flops 549978112 | bytes 18939904 | tf_op jit(solution)/shard_map/bhqk,bkhe->bqhe/dot_general | solution.py:108
  141.3 3.6 fusion.100
  145.9 7.8 %fusion.101 = (f32[16,512]{1,0:T(8,128)S(1)}, f32[16,512,512]{1,2,0:T(8,128)}) fusion(bf16[512,16,64]{0,2,1:T(8,128)(2,1)S(1)} %bitcast.106, bf16[512,16,64]{0,2,1:T(8,128)(2,1)S(1)} %bitcast.98, pred[512]{0:T(512)(128)(4,1)S(1)} %iota_compare_fusion), kind=kOutput, calls=%fused_computation.197 | convolution fusion | flops 549445632 | bytes 18907648 | tf_op jit(solution)/shard_map/bqhe,bkhe->bhqk/dot_general | solution.py:40
  153.7 8.4 %fusion.1 = f32[16,512]{1,0:T(8,128)S(1)} fusion(f32[16,512,512]{1,2,0:T(8,128)} %get-tuple-element.62, f32[16,512]{1,0:T(8,128)S(1)} %get-tuple-element.61), kind=kLoop, calls=%fused_computation.13 | loop fusion | flops 8380416 | bytes 16842752 | tf_op jit(solution)/shard_map/reduce_sum | solution.py:105
  162.8 7.7 %fusion.56 = bf16[16,64,512]{2,1,0:T(8,128)(2,1)S(1)} fusion(bf16[512,16,64]{0,2,1:T(8,128)(2,1)S(1)} %bitcast.111, f32[16,512,512]{1,2,0:T(8,128)} %get-tuple-element.62, f32[16,512]{1,0:T(8,128)S(1)} %fusion.1, f32[16,512]{1,0:T(8,128)S(1)} %get-tuple-element.61), kind=kOutput, calls=%fused_computation.136 | convolution fusion | flops 549978112 | bytes 18939904 | tf_op jit(solution)/shard_map/bhqk,bkhe->bqhe/dot_general | solution.py:108
  170.5 1.4 fusion.102
  173.6 46.9 %all-gather.9.cloned.1.call-done = bf16[1024,4096]{1,0:T(8,128)(2,1)} async-done(((bf16[32,4096]{1,0:T(8,128)(2,1)}), bf16[1024,4096]{1,0:T(8,128)(2,1)}) %all-gather.9.cloned.1.call-update) | async-done | bytes 8388624 | tf_op jit(solution)/shard_map/all_gather | solution.py:33
  220.5 7.9 %fusion.64 = f32[512,4096]{1,0:T(8,128)S(1)} fusion(bf16[1024,4096]{1,0:T(8,128)(2,1)} %all-gather.9.cloned.1.call-done, f32[512,1024]{1,0:T(8,128)} %copy-done.2, f32[512]{0:T(512)S(1)} %fusion.82, f32[512]{0:T(512)S(1)} %broadcast_multiply_fusion.1, f32[1024]{0:T(1024)S(1)} %copy-done.62, f32[1024]{0:T(1024)S(1)} %copy-done.56), kind=kOutput, calls=%fused_computation.142 | convolution fusion | flops 4297588736 | bytes 18886656 | tf_op jit(solution)/shard_map/dot_general | solution.py:118
  228.4 3.3 copy-done.63
  231.7 46.7 %fusion.4 = (f32[512,4096]{1,0:T(8,128)}, f32[512,4096]{1,0:T(8,128)}, f32[512,4096]{1,0:T(8,128)}) fusion(f32[4096]{0:T(1024)S(1)} %copy-done.60, f32[512,4096]{1,0:T(8,128)S(1)} %fusion.64, bf16[1024,4096]{1,0:T(8,128)(2,1)S(1)} %copy-done.59, f32[512,1024]{1,0:T(8,128)S(1)} %get-tuple-element.60, f32[1024]{0:T(1024)S(1)} %copy-done.62, ...), kind=kOutput, calls=%fused_computation.18 | convolution fusion | flops 4561829888 | bytes 44068864 | tf_op jit(solution)/shard_map/dot_general | solution.py:118
  278.4 20.9 %all-gather.11.cloned.1.call-done = bf16[4096,1024]{1,0:T(8,128)(2,1)} async-done(((bf16[128,1024]{1,0:T(8,128)(2,1)}), bf16[4096,1024]{1,0:T(8,128)(2,1)}) %all-gather.11.cloned.1.call-update) | async-done | bytes 8388624 | tf_op jit(solution)/shard_map/all_gather | solution.py:34
  299.3 11.0 %fusion.103 = (f32[512]{0:T(512)S(1)}, f32[512,1024]{1,0:T(8,128)S(1)}) fusion(f32[1024]{0:T(1024)S(1)} %copy-done.61, bf16[4096,1024]{1,0:T(8,128)(2,1)} %all-gather.11.cloned.1.call-done, f32[512,4096]{1,0:T(8,128)} %get-tuple-element.43, f32[512,4096]{1,0:T(8,128)} %get-tuple-element.65, f32[4096]{0:T(1024)S(1)} %copy-done.60, f32[1024]{0:T(1024)S(1)} %copy-done.62, ...), kind=kOutput, calls=%fused_computation.199 | convolution fusion | flops 4307025408 | bytes 29394944 | tf_op jit(solution)/shard_map/dot_general | solution.py:125
  310.4 11.0 %fusion.104 = (f32[512]{0:T(512)S(1)}, f32[512,1024]{1,0:T(8,128)S(1)}) fusion(f32[1024]{0:T(1024)S(1)} %copy-done.61, bf16[4096,1024]{1,0:T(8,128)(2,1)} %all-gather.11.cloned.1.call-done, f32[512,4096]{1,0:T(8,128)} %get-tuple-element.44, f32[512,4096]{1,0:T(8,128)} %copy-done.63, f32[4096]{0:T(1024)S(1)} %copy-done.60, f32[1024]{0:T(1024)S(1)} %copy-done.62, ...), kind=kOutput, calls=%fused_computation.200 | convolution fusion | flops 4307025408 | bytes 29394944 | tf_op jit(solution)/shard_map/dot_general | solution.py:125
  321.5 2.5 multiply_reduce_fusion.5
  324.0 3.6 fusion.97
  329.7 15.9 %convert_reduce_fusion = (f32[4096]{0:T(1024)}, bf16[512,4096]{1,0:T(8,128)(2,1)}) fusion(f32[512,4096]{1,0:T(8,128)} %get-tuple-element.44, bf16[4096,1024]{1,0:T(8,128)(2,1)} %all-gather.11.cloned.1.call-done, f32[512,1024]{1,0:T(8,128)} %copy-done.13, f32[512]{0:T(512)S(1)} %negate_multiply_fusion.3, f32[512,4096]{1,0:T(8,128)} %copy-done.63, ...), kind=kOutput, calls=%fused_computation.22 | convolution fusion | flops 4331663360 | bytes 31492096 | tf_op jit(solution)/shard_map/rd,fd->rf/dot_general | solution.py:149
  345.6 15.5 %convert_reduce_fusion.1 = (f32[4096]{0:T(1024)}, bf16[512,4096]{1,0:T(8,128)(2,1)}) fusion(f32[512,4096]{1,0:T(8,128)} %get-tuple-element.43, bf16[4096,1024]{1,0:T(8,128)(2,1)} %all-gather.11.cloned.1.call-done, f32[512,1024]{1,0:T(8,128)S(1)} %get-tuple-element.42, f32[512]{0:T(512)S(1)} %negate_multiply_fusion.5, f32[512,4096]{1,0:T(8,128)} %get-tuple-element.65, ...), kind=kOutput, calls=%fused_computation.23 | convolution fusion | flops 4331663360 | bytes 31492096 | tf_op jit(solution)/shard_map/rd,fd->rf/dot_general | solution.py:149
  361.1 8.4 %add_add_fusion.8 = f32[512,1024]{1,0:T(8,128)S(1)} fusion(f32[512,1024]{1,0:T(8,128)S(1)} %copy-done.14, bf16[512,4096]{1,0:T(8,128)(2,1)} %get-tuple-element.86, bf16[1024,4096]{1,0:T(8,128)(2,1)} %all-gather.9.cloned.1.call-done, f32[512]{0:T(512)S(1)} %negate_multiply_fusion.3), kind=kOutput, calls=%fused_computation.129 | convolution fusion | flops 4296015872 | bytes 16779264 | tf_op jit(solution)/shard_map/rf,df->rd/dot_general | solution.py:153
  369.5 11.8 %fusion.93 = (f32[1024]{0:T(1024)}, f32[512]{0:T(512)S(1)}, f32[512]{0:T(512)S(1)}, f32[1024]{0:T(1024)}, f32[512,1024]{1,0:T(8,128)}) fusion(f32[1024]{0:T(1024)S(1)} %copy-done.56, f32[512,1024]{1,0:T(8,128)S(1)} %get-tuple-element.60, f32[512]{0:T(512)S(1)} %broadcast_multiply_fusion.3, f32[512,1024]{1,0:T(8,128)S(1)} %add_add_fusion.8, ...), kind=kOutput, calls=%fused_computation.189 | convolution fusion | flops 4301255680 | bytes 23091200 | tf_op jit(solution)/shard_map/rf,df->rd/dot_general | solution.py:153
  381.3 4.4 fusion.94
  388.9 9.7 %convert_reduce_fusion.7 = (f32[16,64]{1,0:T(8,128)S(1)}, bf16[16,64,512]{2,1,0:T(8,128)(2,1)}) fusion(bf16[512,16,64]{0,2,1:T(8,128)(2,1)S(1)} %bitcast.102, f32[16,512,512]{1,2,0:T(8,128)} %get-tuple-element.58, f32[16,512]{1,0:T(8,128)} %log_add_fusion.1), kind=kOutput, calls=%fused_computation.97 | convolution fusion | flops 546831360 | bytes 18911232 | tf_op jit(solution)/shard_map/bhqk,bqhe->bkhe/dot_general | solution.py:178
  398.7 13.9 %multiply_reduce_fusion.1 = (f32[16,512]{1,0:T(8,128)}, f32[16,512,512]{1,2,0:T(8,128)}) fusion(f32[16,512,512]{1,2,0:T(8,128)} %get-tuple-element.58, f32[16,512]{1,0:T(8,128)} %log_add_fusion.1, bf16[512,16,64]{0,2,1:T(8,128)(2,1)S(1)} %bitcast.103, bf16[512,16,64]{0,2,1:T(8,128)(2,1)} %bitcast.112), kind=kOutput, calls=%fused_computation.4 | convolution fusion | flops 549445632 | bytes 35717120 | tf_op jit(solution)/shard_map/bqhe,bkhe->bhqk/dot_general | solution.py:165
  412.6 10.8 %multiply_convert_fusion.1 = bf16[16,512,512]{1,2,0:T(8,128)(2,1)} fusion(f32[16,512,512]{1,2,0:T(8,128)} %get-tuple-element.74, f32[16,512,512]{1,2,0:T(8,128)S(1)} %bitcast.97, f32[16,512]{1,0:T(8,128)} %get-tuple-element.73, f32[16,512]{1,0:T(8,128)} %log_add_fusion.1), kind=kLoop, calls=%fused_computation.3 | loop fusion | flops 16777216 | bytes 42008576 | tf_op jit(solution)/shard_map/convert_element_type | solution.py:169
  423.4 7.1 %multiply_convert_fusion.8 = bf16[16,64,512]{2,1,0:T(8,128)(2,1)} fusion(bf16[512,16,64]{0,2,1:T(8,128)(2,1)S(1)} %bitcast.109, bf16[16,512,512]{1,2,0:T(8,128)(2,1)} %multiply_convert_fusion.1), kind=kOutput, calls=%fused_computation.109 | convolution fusion | flops 537919488 | bytes 10485760 | tf_op jit(solution)/shard_map/bhqk,bqhe->bkhe/dot_general | solution.py:175
  430.6 3.0 convert_reduce_fusion.9
  436.3 10.3 %convert_reduce_fusion.6 = (f32[16,64]{1,0:T(8,128)}, bf16[16,64,512]{2,1,0:T(8,128)(2,1)}) fusion(bf16[512,16,64]{0,2,1:T(8,128)(2,1)S(1)} %bitcast.104, f32[16,512,512]{1,2,0:T(8,128)} %get-tuple-element.62, f32[16,512]{1,0:T(8,128)} %log_add_fusion), kind=kOutput, calls=%fused_computation.96 | convolution fusion | flops 546831360 | bytes 18911232 | tf_op jit(solution)/shard_map/bhqk,bqhe->bkhe/dot_general | solution.py:178
  446.5 13.9 %multiply_reduce_fusion = (f32[16,512]{1,0:T(8,128)}, f32[16,512,512]{1,2,0:T(8,128)}) fusion(f32[16,512,512]{1,2,0:T(8,128)} %get-tuple-element.62, f32[16,512]{1,0:T(8,128)} %log_add_fusion, bf16[512,16,64]{0,2,1:T(8,128)(2,1)S(1)} %bitcast.105, bf16[512,16,64]{0,2,1:T(8,128)(2,1)} %bitcast.110), kind=kOutput, calls=%fused_computation.1 | convolution fusion | flops 549445632 | bytes 35717120 | tf_op jit(solution)/shard_map/bqhe,bkhe->bhqk/dot_general | solution.py:165
  460.5 10.6 %multiply_convert_fusion = bf16[16,512,512]{1,2,0:T(8,128)(2,1)} fusion(f32[16,512,512]{1,2,0:T(8,128)} %get-tuple-element.72, f32[16,512,512]{1,2,0:T(8,128)S(1)} %bitcast.95, f32[16,512]{1,0:T(8,128)} %get-tuple-element.71, f32[16,512]{1,0:T(8,128)} %log_add_fusion), kind=kLoop, calls=%fused_computation | loop fusion | flops 16777216 | bytes 42008576 | tf_op jit(solution)/shard_map/convert_element_type | solution.py:169
  471.1 7.2 %multiply_convert_fusion.6 = bf16[16,64,512]{2,1,0:T(8,128)(2,1)} fusion(bf16[512,16,64]{0,2,1:T(8,128)(2,1)S(1)} %bitcast.107, bf16[16,512,512]{1,2,0:T(8,128)(2,1)} %multiply_convert_fusion), kind=kOutput, calls=%fused_computation.101 | convolution fusion | flops 537919488 | bytes 10485760 | tf_op jit(solution)/shard_map/bhqk,bqhe->bkhe/dot_general | solution.py:175
  478.4 2.4 convert_reduce_fusion.8
  481.1 40.2 %all-reduce.7 = (f32[1024]{0:T(1024)S(1)}, f32[1024]{0:T(1024)S(1)}, f32[1024]{0:T(1024)S(1)}, f32[1024]{0:T(1024)S(1)}, f32[4096]{0:T(1024)S(1)}, /*index=5*/f32[1024]{0:T(1024)S(1)}, f32[1024]{0:T(1024)S(1)}) all-reduce(f32[1024]{0:T(1024)S(1)} %add.255, f32[1024]{0:T(1024)S(1)} %add.257, ...), channel_id=2, replica_groups=mesh['dp'=4,'fsdp'=8] {'dp','fsdp'}, use_global_device_ids=true, to_apply=%region_24.25.clone | all-reduce | flops 10240 | bytes 81920
  524.8 2.7 pad_maximum_fusion
  527.6 7.4 %add_convert_fusion.3 = bf16[512,1024]{1,0:T(8,128)(2,1)S(1)} fusion(f32[512,1024]{1,0:T(8,128)S(1)} %copy-done.21, bf16[1024,3072]{1,0:T(8,128)(2,1)} %all-gather.5.cloned.1.call-done, bf16[512,1024]{0,1:T(8,128)(2,1)} %bitcast.116, bf16[512,1024]{0,1:T(8,128)(2,1)} %bitcast.117, bf16[512,1024]{0,1:T(8,128)(2,1)} %bitcast.114, f32[512]{0:T(512)S(1)} %copy-done.49), kind=kOutput, calls=%fused_computation.108 | convolution fusion | flops 3232235520 | bytes 12584960 | tf_op jit(solution)/shard_map/re,de->rd/dot_general | solution.py:190
  535.0 6.5 %add_convert_fusion.2 = bf16[512,1024]{1,0:T(8,128)(2,1)S(1)} fusion(f32[512,1024]{1,0:T(8,128)S(1)} %copy-done.19, bf16[1024,3072]{1,0:T(8,128)(2,1)} %all-gather.5.cloned.1.call-done, bf16[512,1024]{0,1:T(8,128)(2,1)S(1)} %bitcast.118, bf16[512,1024]{0,1:T(8,128)(2,1)S(1)} %bitcast.119, bf16[512,1024]{0,1:T(8,128)(2,1)S(1)} %bitcast.115, ...), kind=kOutput, calls=%fused_computation.100 | convolution fusion | flops 3232235520 | bytes 12584960 | tf_op jit(solution)/shard_map/re,de->rd/dot_general | solution.py:190
  541.5 1.5 pad_maximum_fusion.1
  (201 shorter events, 24.3 us)
Async XLA Ops:
  7.2 76.0 %all-gather.5.cloned.1.call-start = ((), (), s32[]{:S(2)}) async-start(), calls=%async_computation | async-start | bytes 6488064 | tf_op jit(solution)/shard_map/all_gather | solution.py:26
  7.9 133.4 %all-gather.7.cloned.1.call-start = ((), (), s32[]{:S(2)}) async-start(), calls=%async_computation.1 | async-start | bytes 2162688 | tf_op jit(solution)/shard_map/all_gather | solution.py:27
  8.7 211.8 %all-gather.9.cloned.1.call-start = ((), (), s32[]{:S(2)}) async-start(), calls=%async_computation.2 | async-start | bytes 8650752 | tf_op jit(solution)/shard_map/all_gather | solution.py:33
  9.4 289.9 %all-gather.11.cloned.1.call-start = ((), (), s32[]{:S(2)}) async-start(), calls=%async_computation.3 | async-start | bytes 8650752 | tf_op jit(solution)/shard_map/all_gather | solution.py:34
  92.3 53.6 %copy-start.4 = (bf16[512,1024]{0,1:T(8,128)(2,1)}, bf16[512,1024]{0,1:T(8,128)(2,1)S(1)}, u32[]{:S(2)}) copy-start(bf16[512,1024]{0,1:T(8,128)(2,1)S(1)} %copy.71) | copy-start | bytes 3145732
  92.3 9.6 %copy-start.54 = (f32[1024]{0:T(1024)S(1)}, f32[1024]{0:T(1024)}, u32[]{:S(2)}) copy-start(f32[1024]{0:T(1024)} %param.24) | copy-start | bytes 12292
  92.4 9.6 %copy-start.55 = (f32[1024]{0:T(1024)S(1)}, f32[1024]{0:T(1024)}, u32[]{:S(2)}) copy-start(f32[1024]{0:T(1024)} %param.25) | copy-start | bytes 12292
  102.0 13.7 %copy-start.6 = (bf16[512,1024]{0,1:T(8,128)(2,1)}, bf16[512,1024]{0,1:T(8,128)(2,1)S(1)}, u32[]{:S(2)}) copy-start(bf16[512,1024]{0,1:T(8,128)(2,1)S(1)} %copy.67) | copy-start | bytes 3145732
  115.7 7.6 %copy-start.10 = (bf16[512,1024]{0,1:T(8,128)(2,1)}, bf16[512,1024]{0,1:T(8,128)(2,1)S(1)}, u32[]{:S(2)}) copy-start(bf16[512,1024]{0,1:T(8,128)(2,1)S(1)} %copy.66) | copy-start | bytes 3145732
  123.3 9.3 %copy-start.25 = (bf16[512,1024]{0,1:T(8,128)(2,1)S(1)}, bf16[512,1024]{0,1:T(8,128)(2,1)}, u32[]{:S(2)}) copy-start(bf16[512,1024]{0,1:T(8,128)(2,1)} %copy.65) | copy-start | bytes 3145732
  132.5 8.8 %copy-start.31 = (f32[1024]{0:T(1024)S(1)}, f32[1024]{0:T(1024)}, u32[]{:S(2)}) copy-start(f32[1024]{0:T(1024)} %param.26) | copy-start | bytes 12292
  153.7 9.0 %copy-start.24 = (bf16[512,1024]{0,1:T(8,128)(2,1)S(1)}, bf16[512,1024]{0,1:T(8,128)(2,1)}, u32[]{:S(2)}) copy-start(bf16[512,1024]{0,1:T(8,128)(2,1)} %copy.69) | copy-start | bytes 3145732
  162.8 7.7 %copy-start.15 = (bf16[1024,1024]{1,0:T(8,128)(2,1)S(1)}, bf16[1024,1024]{1,0:T(8,128)(2,1)}, u32[]{:S(2)}) copy-start(bf16[1024,1024]{1,0:T(8,128)(2,1)} %all-gather.7.cloned.1.call-done) | copy-start | bytes 6291460
  162.8 7.7 %copy-start.28 = (bf16[1024,1024]{1,0:T(8,128)(2,1)S(1)}, bf16[1024,1024]{1,0:T(8,128)(2,1)}, u32[]{:S(2)}) copy-start(bf16[1024,1024]{1,0:T(8,128)(2,1)} %param.16) | copy-start | bytes 6291460
  170.5 50.0 %copy-start.56 = (f32[1024]{0:T(1024)S(1)}, f32[1024]{0:T(1024)}, u32[]{:S(2)}) copy-start(f32[1024]{0:T(1024)} %param.22) | copy-start | bytes 12292
  170.5 50.0 %copy-start.62 = (f32[1024]{0:T(1024)S(1)}, f32[1024]{0:T(1024)}, u32[]{:S(2)}) copy-start(f32[1024]{0:T(1024)} %param.27) | copy-start | bytes 12292
  173.5 54.9 %copy-start.38 = (f32[512]{0:T(512)}, f32[512]{0:T(512)S(1)}, u32[]{:S(2)}) copy-start(f32[512]{0:T(512)S(1)} %multiply_reduce_fusion.7) | copy-start | bytes 6148
  173.5 58.2 %copy-start.60 = (f32[4096]{0:T(1024)S(1)}, f32[4096]{0:T(1024)}, u32[]{:S(2)}) copy-start(f32[4096]{0:T(1024)} %param.28) | copy-start | bytes 49156
  220.5 11.2 %copy-start.59 = (bf16[1024,4096]{1,0:T(8,128)(2,1)S(1)}, bf16[1024,4096]{1,0:T(8,128)(2,1)}, u32[]{:S(2)}) copy-start(bf16[1024,4096]{1,0:T(8,128)(2,1)} %all-gather.9.cloned.1.call-done) | copy-start | bytes 25165828
  231.7 67.6 %copy-start.61 = (f32[1024]{0:T(1024)S(1)}, f32[1024]{0:T(1024)}, u32[]{:S(2)}) copy-start(f32[1024]{0:T(1024)} %param.29) | copy-start | bytes 12292
  299.3 11.0 %copy-start.3 = (f32[512,1024]{1,0:T(8,128)S(1)}, f32[512,1024]{1,0:T(8,128)}, u32[]{:S(2)}) copy-start(f32[512,1024]{1,0:T(8,128)} %copy-done.2) | copy-start | bytes 6291460
  310.3 11.1 %copy-start.12 = (bf16[1024,1024]{1,0:T(8,128)(2,1)S(1)}, bf16[1024,1024]{1,0:T(8,128)(2,1)}, u32[]{:S(2)}) copy-start(bf16[1024,1024]{1,0:T(8,128)(2,1)} %param.31) | copy-start | bytes 6291460
  310.3 11.1 %copy-start.34 = (f32[512]{0:T(512)S(1)}, f32[512]{0:T(512)}, u32[]{:S(2)}) copy-start(f32[512]{0:T(512)} %fusion.89) | copy-start | bytes 6148
  310.4 11.1 %copy-start.35 = (f32[512]{0:T(512)S(1)}, f32[512]{0:T(512)}, u32[]{:S(2)}) copy-start(f32[512]{0:T(512)} %fusion.88) | copy-start | bytes 6148
  310.4 11.1 %copy-start.40 = (f32[1024]{0:T(1024)S(1)}, f32[1024]{0:T(1024)}, u32[]{:S(2)}) copy-start(f32[1024]{0:T(1024)} %param.23) | copy-start | bytes 12292
  345.6 15.5 %copy-start.14 = (f32[512,1024]{1,0:T(8,128)S(1)}, f32[512,1024]{1,0:T(8,128)}, u32[]{:S(2)}) copy-start(f32[512,1024]{1,0:T(8,128)} %copy-done.13) | copy-start | bytes 6291460
  369.5 11.8 %copy-start.39 = (f32[512]{0:T(512)S(1)}, f32[512]{0:T(512)}, u32[]{:S(2)}) copy-start(f32[512]{0:T(512)} %copy-done.38) | copy-start | bytes 6148
  369.5 11.8 %copy-start.37 = (f32[512]{0:T(512)S(1)}, f32[512]{0:T(512)}, u32[]{:S(2)}) copy-start(f32[512]{0:T(512)} %copy-done.36) | copy-start | bytes 6148
  388.9 23.6 %slice-start.4 = ((s8[16777216]{0:T(1024)(128)(4,1)}), s8[4194304]{0:T(1024)(128)(4,1)S(1)}, s32[]{:S(2)}) async-start(s8[16777216]{0:T(1024)(128)(4,1)} %bitcast.96), calls=%async_computation.8 | async-start | bytes 8388608
  388.9 23.6 %slice-start.5 = ((s8[16777216]{0:T(1024)(128)(4,1)}), s8[4194304]{0:T(1024)(128)(4,1)S(1)}, s32[]{:S(2)}) async-start(s8[16777216]{0:T(1024)(128)(4,1)} %bitcast.96), calls=%async_computation.9 | async-start | bytes 8388608
  398.7 13.9 %slice-start.6 = ((s8[16777216]{0:T(1024)(128)(4,1)}), s8[4194304]{0:T(1024)(128)(4,1)S(1)}, s32[]{:S(2)}) async-start(s8[16777216]{0:T(1024)(128)(4,1)} %bitcast.96), calls=%async_computation.10 | async-start | bytes 8388608
  398.7 13.9 %slice-start.7 = ((s8[16777216]{0:T(1024)(128)(4,1)}), s8[4194304]{0:T(1024)(128)(4,1)S(1)}, s32[]{:S(2)}) async-start(s8[16777216]{0:T(1024)(128)(4,1)} %bitcast.96), calls=%async_computation.11 | async-start | bytes 8388608
  412.6 10.8 %copy-start.11 = (bf16[512,1024]{0,1:T(8,128)(2,1)S(1)}, bf16[512,1024]{0,1:T(8,128)(2,1)}, u32[]{:S(2)}) copy-start(bf16[512,1024]{0,1:T(8,128)(2,1)} %copy-done.10) | copy-start | bytes 3145732
  436.2 24.2 %slice-start = ((s8[16777216]{0:T(1024)(128)(4,1)}), s8[4194304]{0:T(1024)(128)(4,1)S(1)}, s32[]{:S(2)}) async-start(s8[16777216]{0:T(1024)(128)(4,1)} %bitcast.94), calls=%async_computation.4 | async-start | bytes 8388608
  436.3 24.2 %slice-start.1 = ((s8[16777216]{0:T(1024)(128)(4,1)}), s8[4194304]{0:T(1024)(128)(4,1)S(1)}, s32[]{:S(2)}) async-start(s8[16777216]{0:T(1024)(128)(4,1)} %bitcast.94), calls=%async_computation.5 | async-start | bytes 8388608
  446.5 13.9 %slice-start.2 = ((s8[16777216]{0:T(1024)(128)(4,1)}), s8[4194304]{0:T(1024)(128)(4,1)S(1)}, s32[]{:S(2)}) async-start(s8[16777216]{0:T(1024)(128)(4,1)} %bitcast.94), calls=%async_computation.6 | async-start | bytes 8388608
  446.5 13.9 %slice-start.3 = ((s8[16777216]{0:T(1024)(128)(4,1)}), s8[4194304]{0:T(1024)(128)(4,1)S(1)}, s32[]{:S(2)}) async-start(s8[16777216]{0:T(1024)(128)(4,1)} %bitcast.94), calls=%async_computation.7 | async-start | bytes 8388608
  460.4 10.6 %copy-start.9 = (bf16[512,1024]{0,1:T(8,128)(2,1)S(1)}, bf16[512,1024]{0,1:T(8,128)(2,1)}, u32[]{:S(2)}) copy-start(bf16[512,1024]{0,1:T(8,128)(2,1)} %copy.70) | copy-start | bytes 3145732
  471.1 7.2 %copy-start.1 = (bf16[16,512,512]{1,2,0:T(8,128)(2,1)S(1)}, bf16[16,512,512]{1,2,0:T(8,128)(2,1)}, u32[]{:S(2)}) copy-start(bf16[16,512,512]{1,2,0:T(8,128)(2,1)} %multiply_convert_fusion) | copy-start | bytes 25165828
  471.1 7.2 %copy-start.5 = (bf16[512,1024]{0,1:T(8,128)(2,1)S(1)}, bf16[512,1024]{0,1:T(8,128)(2,1)}, u32[]{:S(2)}) copy-start(bf16[512,1024]{0,1:T(8,128)(2,1)} %copy-done.4) | copy-start | bytes 3145732
  478.4 46.4 %copy-start.26 = (bf16[512,1024]{1,0:T(8,128)(2,1)S(1)}, bf16[512,1024]{1,0:T(8,128)(2,1)}, u32[]{:S(2)}) copy-start(bf16[512,1024]{1,0:T(8,128)(2,1)} %get-tuple-element.39) | copy-start | bytes 3145732
  478.4 49.1 %copy-start.21 = (f32[512,1024]{1,0:T(8,128)S(1)}, f32[512,1024]{1,0:T(8,128)}, u32[]{:S(2)}) copy-start(f32[512,1024]{1,0:T(8,128)} %copy-done.20) | copy-start | bytes 6291460
  478.4 49.1 %copy-start.49 = (f32[512]{0:T(512)S(1)}, f32[512]{0:T(512)}, u32[]{:S(2)}) copy-start(f32[512]{0:T(512)} %copy-done.48) | copy-start | bytes 6148
  527.5 7.5 %copy-start.19 = (f32[512,1024]{1,0:T(8,128)S(1)}, f32[512,1024]{1,0:T(8,128)}, u32[]{:S(2)}) copy-start(f32[512,1024]{1,0:T(8,128)} %get-tuple-element.48) | copy-start | bytes 6291460
  527.5 7.5 %copy-start.27 = (bf16[16,64,512]{2,1,0:T(8,128)(2,1)S(1)}, bf16[16,64,512]{2,1,0:T(8,128)(2,1)}, u32[]{:S(2)}) copy-start(bf16[16,64,512]{2,1,0:T(8,128)(2,1)} %get-tuple-element.78) | copy-start | bytes 3145732
  527.5 7.5 %copy-start.29 = (bf16[16,64,512]{2,1,0:T(8,128)(2,1)S(1)}, bf16[16,64,512]{2,1,0:T(8,128)(2,1)}, u32[]{:S(2)}) copy-start(bf16[16,64,512]{2,1,0:T(8,128)(2,1)} %get-tuple-element.82) | copy-start | bytes 3145732
  527.5 7.5 %copy-start.30 = (bf16[16,64,512]{2,1,0:T(8,128)(2,1)S(1)}, bf16[16,64,512]{2,1,0:T(8,128)(2,1)}, u32[]{:S(2)}) copy-start(bf16[16,64,512]{2,1,0:T(8,128)(2,1)} %multiply_convert_fusion.6) | copy-start | bytes 3145732
  527.5 7.5 %copy-start.51 = (f32[512]{0:T(512)S(1)}, f32[512]{0:T(512)}, u32[]{:S(2)}) copy-start(f32[512]{0:T(512)} %copy-done.50) | copy-start | bytes 6148
  (28 other events, 83.8 us)
Sparse Core Ops, SparseCore 0:
  11.0 72.1 all-gather.4
  86.2 55.0 all-gather.6
  144.2 76.2 all-gather.8
  223.3 75.9 all-gather.10
where the time goes:
time: 559 us; the launch traced here: 551 us
  matrix products  261 us (47%)
  waiting for transfers between devices  139 us (25%)
  other arithmetic  68.1 us (12%)
  blocking collectives  40.2 us (7%)
  local copies, waits for them, and re-layouts  27.6 us (5%)
  between operations  15.2 us (3%)
    all_gather x1, waiting for transfers between devices, gather_attention(): lax.all_gather(w_qkv, ('dp', 'fsdp'), axis=0, tiled=True)  68.1 us
    dot_general x2, matrix products, on_device(): jnp.dot(normed_one.astype(jnp.bfloat16), full_in, preferred_element_type=...  54.6 us
    all_gather x1, waiting for transfers between devices, gather_feed(): lax.all_gather(w_in, ('dp', 'fsdp'), axis=0, tiled=True)  46.9 us
    unnamed x1, blocking collectives  40.2 us
    dot_general x2, matrix products, on_device(): jnp.einsum('rd,fd->rf', d_branch, back_down, preferred_element_type=jnp.f...  31.4 us
    dot_general x2, matrix products, on_device(): jnp.einsum('bqhe,bkhe->bhqk', d_context, values, preferred_element_type=j...  27.8 us
    dot_general x2, matrix products, on_device(): jnp.dot(active.astype(jnp.bfloat16), full_down, preferred_element_type=jn...  22 us
    convert_element_type x2, other arithmetic, on_device(): d_scores = (probs_full * (d_probs - row_dot)).astype(jnp.bfloat16)  21.4 us
  transfers between devices with their start and end apart: 4, of which 3 were waited for; matrix products, arithmetic and copies ran while one was open for 26% of the time, Pallas kernels for 0%

commit v1 on v0

v1 whole, which is shorter than its diff:
```python
import functools
import math

import jax
import jax.numpy as jnp
from jax import lax
from jax.experimental import pallas as pl
from jax.experimental.pallas import tpu as pltpu
from jax.sharding import PartitionSpec as P

HD = 64
L = 512
LN_EPS = 1e-12
MIB = 2**20
BF = jnp.bfloat16
F32 = jnp.float32


def params(limit=60, semantics=None):
    return pltpu.CompilerParams(vmem_limit_bytes=limit * MIB, dimension_semantics=semantics)


def dot(left, right, on_left, on_right):
    return lax.dot_general(
        left, right, (((on_left,), (on_right,)), ((), ())), preferred_element_type=F32
    )


def shape_of(dims, kind):
    return jax.ShapeDtypeStruct(dims, kind)


def project_body(x_ref, w_ref, bias_ref, scale_ref, out_ref):
    total = dot(x_ref[...], w_ref[...], 1, 0) + bias_ref[...]
    out_ref[...] = (total * scale_ref[...]).astype(BF)


def project(rows, w_qkv, bias, scale):
    count, width = rows.shape
    wide = w_qkv.shape[1]
    step = 512
    return pl.pallas_call(
        project_body,
        out_shape=shape_of((count, wide), BF),
        grid=(wide // step,),
        in_specs=[
            pl.BlockSpec((count, width), lambda j: (0, 0)),
            pl.BlockSpec((width, step), lambda j: (0, j)),
            pl.BlockSpec((1, step), lambda j: (0, j)),
            pl.BlockSpec((1, step), lambda j: (0, j)),
        ],
        out_specs=pl.BlockSpec((count, step), lambda j: (0, j)),
        compiler_params=params(),
        name="project",
    )(rows, w_qkv, bias, scale)


def lane_halves(kind):
    lane = lax.broadcasted_iota(jnp.int32, (1, 128), 1)
    return [(lane < HD).astype(F32).astype(kind), (lane >= HD).astype(F32).astype(kind)]


QUAD = 256


def attend_body(len_ref, q_ref, k_ref, v_ref, o_ref, e_ref, r_ref):
    length = len_ref[pl.program_id(0)]
    halves = lane_halves(BF)
    lane = lax.broadcasted_iota(jnp.int32, (L, 128), 1)
    row = lax.broadcasted_iota(jnp.int32, (L, 128), 0)
    q_side = jnp.where(lane == 0, 1.0, 0.0).astype(BF)
    k_side = jnp.where((lane == 0) & (row >= length), -1e30, 0.0).astype(BF)
    for pair in range(QUAD // 128):
        part = slice(pair * 128, (pair + 1) * 128)
        q_pair = jnp.concatenate([q_ref[:, part], q_side], axis=1)
        k_pair = k_ref[:, part]
        v_pair = v_ref[:, part]
        powers = []
        for head in range(2):
            k_one = jnp.concatenate([k_pair * halves[head], k_side], axis=1)
            scores = dot(q_pair, k_one, 1, 1)
            peak = jnp.max(scores, axis=1, keepdims=True)
            power = jnp.exp(scores - peak).astype(BF)
            e_ref[2 * pair + head] = power
            powers.append(power)
        right = jnp.concatenate(
            [
                jnp.concatenate([v_pair * half, jnp.broadcast_to(half, (L, 128))], axis=1)
                for half in halves
            ],
            axis=0,
        )
        both = dot(jnp.concatenate(powers, axis=1), right, 1, 0)
        inverse = 1.0 / both[:, 128:]
        r_ref[:, part] = inverse
        o_ref[:, part] = (both[:, :128] * inverse).astype(BF)


def attend(lengths, qkv, width):
    count = qkv.shape[0]
    seqs = count // L
    quads = width // QUAD
    heads = QUAD // HD
    return pl.pallas_call(
        attend_body,
        out_shape=(
            shape_of((count, width), BF),
            shape_of((seqs * width // HD, L, L), BF),
            shape_of((count, width), F32),
        ),
        grid_spec=pltpu.PrefetchScalarGridSpec(
            num_scalar_prefetch=1,
            grid=(seqs, quads),
            in_specs=[
                pl.BlockSpec((L, QUAD), lambda i, j, n: (i, j)),
                pl.BlockSpec((L, QUAD), lambda i, j, n: (i, quads + j)),
                pl.BlockSpec((L, QUAD), lambda i, j, n: (i, 2 * quads + j)),
            ],
            out_specs=[
                pl.BlockSpec((L, QUAD), lambda i, j, n: (i, j)),
                pl.BlockSpec((heads, L, L), lambda i, j, n: (i * quads + j, 0, 0)),
                pl.BlockSpec((L, QUAD), lambda i, j, n: (i, j)),
            ],
        ),
        compiler_params=params(),
        name="attend",
    )(lengths, qkv, qkv, qkv)


def feed_body(x_ref, o_ref, wo_ref, wi_ref, vec_ref, bi_ref, u_ref, s_ref, gl_ref, gp_ref, ub_ref):
    @pl.when(pl.program_id(1) == 0)
    def _():
        joined = dot(o_ref[...], wo_ref[...], 1, 0) + vec_ref[0:1, :] + x_ref[...].astype(F32)
        centered = joined - jnp.mean(joined, axis=1, keepdims=True)
        spread = lax.rsqrt(jnp.mean(centered * centered, axis=1, keepdims=True) + LN_EPS)
        normed = centered * spread * vec_ref[1:2, :] + vec_ref[2:3, :]
        u_ref[...] = normed
        s_ref[...] = jnp.broadcast_to(spread, s_ref.shape)
        ub_ref[...] = normed.astype(BF)

    step = 256
    for part in range(gl_ref.shape[1] // step):
        cols = slice(part * step, (part + 1) * step)
        pre = dot(ub_ref[...], wi_ref[:, cols], 1, 0) + bi_ref[:, cols]
        phi = 0.5 + 0.5 * lax.erf(pre * math.sqrt(0.5))
        slope = phi + pre * jnp.exp(-0.5 * pre * pre) * (1.0 / math.sqrt(2.0 * math.pi))
        gl_ref[:, cols] = (pre * phi).astype(BF)
        gp_ref[:, cols] = slope.astype(BF)


def feed(rows, context, w_out, w_in, vectors, bias_in):
    count, width = rows.shape
    wide = w_in.shape[1]
    step = 1024
    return pl.pallas_call(
        feed_body,
        out_shape=(
            shape_of((count, width), F32),
            shape_of((count, 128), F32),
            shape_of((count, wide), BF),
            shape_of((count, wide), BF),
        ),
        grid=(count // L, wide // step),
        in_specs=[
            pl.BlockSpec((L, width), lambda i, j: (i, 0)),
            pl.BlockSpec((L, width), lambda i, j: (i, 0)),
            pl.BlockSpec((width, width), lambda i, j: (0, 0)),
            pl.BlockSpec((width, step), lambda i, j: (0, j)),
            pl.BlockSpec((8, width), lambda i, j: (0, 0)),
            pl.BlockSpec((1, step), lambda i, j: (0, j)),
        ],
        out_specs=[
            pl.BlockSpec((L, width), lambda i, j: (i, 0)),
            pl.BlockSpec((L, 128), lambda i, j: (i, 0)),
            pl.BlockSpec((L, step), lambda i, j: (i, j)),
            pl.BlockSpec((L, step), lambda i, j: (i, j)),
        ],
        scratch_shapes=[pltpu.VMEM((L, width), BF)],
        compiler_params=params(),
        name="feed",
    )(rows, context, w_out, w_in, vectors, bias_in)


ROWS = 256


def turn_body(
    len_ref, gl_ref, gp_ref, u_ref, s_ref, r_ref, c_ref, wd_any, wi_any, wo_any, vec_ref,
    y_ref, dh_ref, do_ref, gv_ref, gi_ref, wd_ref, wi_ref, wo_ref, sems,
):
    index = pl.program_id(0)
    width = u_ref.shape[1]
    wide = gl_ref.shape[1]
    parts = 4
    step = wide // parts
    down = [
        pltpu.make_async_copy(
            wd_any.at[pl.ds(part * step, step)], wd_ref.at[pl.ds(part * step, step)], sems.at[part]
        )
        for part in range(parts)
    ]
    whole_in = pltpu.make_async_copy(wi_any, wi_ref, sems.at[parts])
    whole_out = pltpu.make_async_copy(wo_any, wo_ref, sems.at[parts + 1])

    @pl.when(index == 0)
    def _():
        for copy in down:
            copy.start()
        whole_in.start()
        whole_out.start()
        gv_ref[...] = jnp.zeros_like(gv_ref)
        gi_ref[...] = jnp.zeros_like(gi_ref)

    gain_one, beta_one, gain_two, beta_two, bias_down = (vec_ref[n : n + 1, :] for n in range(1, 6))
    normed = u_ref[...]
    total = normed + bias_down
    for part in range(parts):
        pl.when(index == 0)(down[part].wait)
        rows = slice(part * step, (part + 1) * step)
        total = total + dot(gl_ref[:, rows], wd_ref[rows, :], 1, 0)
    centered = total - jnp.mean(total, axis=1, keepdims=True)
    spread = lax.rsqrt(jnp.mean(centered * centered, axis=1, keepdims=True) + LN_EPS)
    hat = centered * spread
    y_ref[...] = (hat * gain_two + beta_two).astype(BF)
    per_seq = L // ROWS
    first = lax.rem(index, per_seq) * ROWS
    live = lax.broadcasted_iota(jnp.int32, (ROWS, 1), 0) + first < len_ref[index // per_seq]
    dy = jnp.where(live, c_ref[...].astype(F32), 0.0)
    gv_ref[4:5, :] += jnp.sum(dy, axis=0, keepdims=True)
    scaled = dy * gain_two
    d_two = spread * (
        scaled
        - jnp.mean(scaled, axis=1, keepdims=True)
        - hat * jnp.mean(scaled * hat, axis=1, keepdims=True)
    )
    d_branch = d_two.astype(BF)
    gv_ref[3:4, :] += jnp.sum(d_branch.astype(F32), axis=0, keepdims=True)
    pl.when(index == 0)(whole_in.wait)
    total = d_two
    half = step // 2
    for part in range(2 * parts):
        rows = slice(part * half, (part + 1) * half)
        d_hidden = dot(d_branch, wd_ref[rows, :], 1, 1) * gp_ref[:, rows].astype(F32)
        d_hidden = d_hidden.astype(BF)
        gi_ref[:, rows] += jnp.sum(d_hidden.astype(F32), axis=0, keepdims=True)
        total = total + dot(d_hidden, wi_ref[:, rows], 1, 1)
    gv_ref[2:3, :] += jnp.sum(total, axis=0, keepdims=True)
    scaled = total * gain_one
    hat = (normed - beta_one) * (1.0 / gain_one)
    d_one = s_ref[:, 0:1] * (
        scaled
        - jnp.mean(scaled, axis=1, keepdims=True)
        - hat * jnp.mean(scaled * hat, axis=1, keepdims=True)
    )
    dh_ref[...] = d_one
    d_att = d_one.astype(BF)
    gv_ref[1:2, :] += jnp.sum(d_att.astype(F32), axis=0, keepdims=True)
    pl.when(index == 0)(whole_out.wait)
    d_context = dot(d_att, wo_ref[...], 1, 1).astype(BF).astype(F32)
    gv_ref[0:1, :] += jnp.sum(d_context, axis=0, keepdims=True)
    do_ref[...] = (d_context * r_ref[...]).astype(BF)


def turn(lengths, gl, gp, normed, spread, inverse, cotangent, w_down, w_in, w_out, vectors):
    count, width = normed.shape
    wide = gl.shape[1]
    block = lambda cols: pl.BlockSpec((ROWS, cols), lambda i, n: (i, 0))
    anywhere = pl.BlockSpec(memory_space=pl.ANY)
    return pl.pallas_call(
        turn_body,
        out_shape=(
            shape_of((count, width), BF),
            shape_of((count, width), F32),
            shape_of((count, width), BF),
            shape_of((8, width), F32),
            shape_of((1, wide), F32),
        ),
        grid_spec=pltpu.PrefetchScalarGridSpec(
            num_scalar_prefetch=1,
            grid=(count // ROWS,),
            in_specs=[
                block(wide), block(wide), block(width), block(128), block(width), block(width),
                anywhere, anywhere, anywhere, pl.BlockSpec((8, width), lambda i, n: (0, 0)),
            ],
            out_specs=[
                block(width), block(width), block(width),
                pl.BlockSpec((8, width), lambda i, n: (0, 0)),
                pl.BlockSpec((1, wide), lambda i, n: (0, 0)),
            ],
            scratch_shapes=[
                pltpu.VMEM(w_down.shape, BF),
                pltpu.VMEM(w_in.shape, BF),
                pltpu.VMEM(w_out.shape, BF),
                pltpu.SemaphoreType.DMA((6,)),
            ],
        ),
        compiler_params=params(),
        name="turn",
    )(lengths, gl, gp, normed, spread, inverse, cotangent, w_down, w_in, w_out, vectors)


def back_body(
    q_ref, k_ref, v_ref, o_ref, do_ref, e_ref, dh_ref, w_any, dx_ref, gq_ref, all_ref, w_ref, sem
):
    seq, quad = pl.program_id(0), pl.program_id(1)
    quads = pl.num_programs(1)
    width = dh_ref.shape[1]
    whole = pltpu.make_async_copy(w_any, w_ref, sem)

    @pl.when((seq == 0) & (quad == 0))
    def _():
        whole.start()
        gq_ref[...] = jnp.zeros_like(gq_ref)

    halves = lane_halves(BF)
    halves_wide = lane_halves(F32)
    lane = lax.broadcasted_iota(jnp.int32, (L, 128), 1)
    for pair in range(QUAD // 128):
        part = slice(pair * 128, (pair + 1) * 128)
        q_pair, k_pair, v_pair, do_pair = (r[:, part] for r in (q_ref, k_ref, v_ref, do_ref))
        products = do_pair.astype(F32) * o_ref[:, part].astype(F32)
        shifts = [jnp.sum(products * half, axis=1, keepdims=True) for half in halves_wide]
        rough = [shift.astype(BF).astype(F32) for shift in shifts]
        side = jnp.where(
            lane == 0,
            -rough[0],
            jnp.where(
                lane == 1,
                rough[0] - shifts[0],
                jnp.where(lane == 2, -rough[1], jnp.where(lane == 3, rough[1] - shifts[1], 0.0)),
            ),
        ).astype(BF)
        left = jnp.concatenate([do_pair, side], axis=1)
        q_turned = q_pair.T
        do_turned = do_pair.T
        d_scores, d_keys, d_values = [], [], []
        for head in range(2):
            rows = slice(head * HD, (head + 1) * HD)
            power = e_ref[2 * pair + head]
            marks = jnp.where(lane // 2 == head, 1.0, 0.0).astype(BF)
            right = jnp.concatenate([v_pair * halves[head], marks], axis=1)
            d_score = (power.astype(F32) * dot(left, right, 1, 1)).astype(BF)
            d_scores.append(d_score)
            d_keys.append(dot(q_turned[rows], d_score, 1, 0))
            d_values.append(dot(do_turned[rows], power, 1, 0))
        right = jnp.concatenate([k_pair * half for half in halves], axis=0)
        d_query = (dot(jnp.concatenate(d_scores, axis=1), right, 1, 0) * (HD**-0.5)).astype(BF)
        cols = pl.multiple_of(quad * QUAD + pair * 128, 128)
        gq_ref[:, pl.ds(cols, 128)] += jnp.sum(d_query.astype(F32), axis=0, keepdims=True)
        all_ref[:, pl.ds(cols, 128)] = d_query
        all_ref[:, pl.ds(width + cols, 128)] = jnp.concatenate(d_keys, axis=0).T.astype(BF)
        all_ref[:, pl.ds(2 * width + cols, 128)] = jnp.concatenate(d_values, axis=0).T.astype(BF)

    pl.when((seq == 0) & (quad == quads - 1))(whole.wait)

    @pl.when(quad == quads - 1)
    def _():
        dx_ref[...] = (dh_ref[...] + dot(all_ref[...], w_ref[...], 1, 1)).astype(BF)


def back(qkv, context, d_context, powers, d_joined, w_qkv):
    count, width = d_joined.shape
    quads = width // QUAD
    heads = QUAD // HD
    col = lambda n: pl.BlockSpec((L, QUAD), lambda i, j: (i, n * quads + j))
    return pl.pallas_call(
        back_body,
        out_shape=(shape_of((count, width), BF), shape_of((1, width), F32)),
        grid=(count // L, quads),
        in_specs=[
            col(0), col(1), col(2), col(0), col(0),
            pl.BlockSpec((heads, L, L), lambda i, j: (i * quads + j, 0, 0)),
            pl.BlockSpec((L, width), lambda i, j: (i, 0)),
            pl.BlockSpec(memory_space=pl.ANY),
        ],
        out_specs=[
            pl.BlockSpec((L, width), lambda i, j: (i, 0)),
            pl.BlockSpec((1, width), lambda i, j: (0, 0)),
        ],
        scratch_shapes=[
            pltpu.VMEM((L, 3 * width), BF),
            pltpu.VMEM(w_qkv.shape, BF),
            pltpu.SemaphoreType.DMA,
        ],
        compiler_params=params(),
        name="back",
    )(qkv, qkv, qkv, context, d_context, powers, d_joined, w_qkv)


BOTH = ("dp", "fsdp")


def on_device(
    tokens, lengths, w_qkv, w_out, w_in, w_down, gain_one, gain_two,
    bias_q, bias_v, bias_out, beta_one, bias_in, bias_down, beta_two, cotangent,
):
    width = w_out.shape[1]
    full_qkv = lax.all_gather(w_qkv, BOTH, axis=0, tiled=True)
    full_out = lax.all_gather(w_out, BOTH, axis=0, tiled=True)
    full_in = lax.all_gather(w_in, BOTH, axis=0, tiled=True)
    full_down = lax.all_gather(w_down, BOTH, axis=0, tiled=True)
    score_scale = HD**-0.5
    ones = jnp.ones((width,), F32)
    zeros = jnp.zeros((width,), F32)
    bias = jnp.concatenate([bias_q, zeros, bias_v])[None]
    scale = jnp.concatenate([ones * score_scale, ones, ones])[None]
    vectors = jnp.stack([bias_out, gain_one, beta_one, gain_two, beta_two, bias_down, zeros, zeros])
    qkv = project(tokens, full_qkv, bias, scale)
    context, powers, inverse = attend(lengths, qkv, width)
    normed, spread, gl, gp = feed(tokens, context, full_out, full_in, vectors, bias_in[None])
    output, d_joined, d_context, sums, sum_in = turn(
        lengths, gl, gp, normed, spread, inverse, cotangent, full_down, full_in, full_out, vectors
    )
    input_grad, sum_q = back(qkv, context, d_context, powers, d_joined, full_qkv)
    parts = (sum_q[0], sums[0], sums[1], sums[2], sum_in[0], sums[3], sums[4])
    shares = lax.psum_scatter(parts, BOTH, scatter_dimension=0, tiled=True)
    return (output, input_grad, *shares)


def solution(mesh):
    split, rows, copied = P(BOTH), P(BOTH, None), P()
    in_specs = (rows, split, rows, rows, rows, rows, *([copied] * 9), rows)
    out_specs = (rows, rows, *([split] * 7))
    return jax.shard_map(
        on_device, mesh=mesh, in_specs=in_specs, out_specs=out_specs, check_vma=False
    )
```

time: 559 us -> 433 us (0.77); the launches traced: 551 us -> 432 us
  matrix products: 261 us -> 0 us
  Pallas kernels: 0 us -> 138 us
  waiting for transfers between devices: 139 us -> 233 us
  other arithmetic: 68.1 us -> 1.3 us
  local copies, waits for them, and re-layouts: 27.6 us -> 6.53 us
    dot_general x28 -> x0, matrix products: 261 us -> none  [the longest x2 54.6 us: on_device(): jnp.dot(normed_one.astype(jnp.bfloat16), full_in, preferred_element_type=...]
    pallas_call x0 -> x5, Pallas kernels: none -> 138 us  [the longest x1 48.1 us: turn(): pl.pallas_call(turn_body, out_shape=(shape_of((count, width), BF), shape_...]
    all_gather x4, waiting for transfers between devices: 136 us -> 230 us  [the longest x1 79.1 us: on_device(): full_in = lax.all_gather(w_in, BOTH, axis=0, tiled=True)]
    reduce_sum x11 -> x0, other arithmetic: 31 us -> none  [the longest x2 17 us: on_device(): denominator = jnp.sum(powers, axis=-1, keepdims=True)]
    convert_element_type x5 -> x0, other arithmetic: 30.2 us -> none  [the longest x2 21.4 us: on_device(): d_scores = (probs_full * (d_probs - row_dot)).astype(jnp.bfloat16)]
    unnamed x151 -> x9, local copies, waits for them, and re-layouts: 16.3 us -> 4.08 us
    convert_element_type x6 -> x0, local copies, waits for them, and re-layouts: 8.43 us -> none  [the longest x2 3.75 us: on_device(): queries = (projected[:, :model_width] + bias_q).astype(jnp.bfloat16).resh...]
  transfers between devices with their start and end apart: 4 -> 4, of which waited for: 3 -> 4; matrix products, arithmetic and copies ran while one was open for 26% -> 1% of each run, Pallas kernels for 0% -> 13%
where the time goes in v1:
time: 433 us; the launch traced here: 432 us
  waiting for transfers between devices  233 us (54%)
  Pallas kernels  138 us (32%)
  blocking collectives  40 us (9%)
  between operations  13.8 us (3%)
  local copies, waits for them, and re-layouts  6.53 us (2%)
    all_gather x1, waiting for transfers between devices, on_device(): full_in = lax.all_gather(w_in, BOTH, axis=0, tiled=True)  79.1 us
    all_gather x1, waiting for transfers between devices, on_device(): full_qkv = lax.all_gather(w_qkv, BOTH, axis=0, tiled=True)  70.5 us
    all_gather x1, waiting for transfers between devices, on_device(): full_down = lax.all_gather(w_down, BOTH, axis=0, tiled=True)  51.5 us
    pallas_call x1, Pallas kernels, turn(): pl.pallas_call(turn_body, out_shape=(shape_of((count, width), BF), shape_...  48.1 us
    unnamed x1, blocking collectives  40 us
    pallas_call x1, Pallas kernels, back(): pl.pallas_call(back_body, out_shape=(shape_of((count, width), BF), shape_...  33.3 us
    all_gather x1, waiting for transfers between devices, on_device(): full_out = lax.all_gather(w_out, BOTH, axis=0, tiled=True)  29.2 us
    pallas_call x1, Pallas kernels, feed(): pl.pallas_call(feed_body, out_shape=(shape_of((count, width), F32), shape...  27.4 us
  transfers between devices with their start and end apart: 4, of which 4 were waited for; matrix products, arithmetic and copies ran while one was open for 1% of the time, Pallas kernels for 13%

profile of v1, /device:TPU:0, one launch (start us, length us, event | category | flops | bytes accessed | tf_op | source)
XLA Modules:
  0.0 432.2 jit_solution(9490031112978088238)
XLA Ops:
  7.2 0.0 all-gather.5.cloned.1.call-start
  7.2 0.7 all-gather.5.cloned.1.call-update
  7.9 0.0 all-gather.7.cloned.1.call-start
  8.0 0.7 all-gather.7.cloned.1.call-update
  8.7 0.0 all-gather.9.cloned.1.call-start
  8.7 0.7 all-gather.9.cloned.1.call-update
  9.4 0.0 all-gather.11.cloned.1.call-start
  9.4 0.5 all-gather.11.cloned.1.call-update
  10.0 1.4 stack.31.vec_ref
  11.4 1.3 pad_maximum_fusion
  12.7 70.5 %all-gather.5.cloned.1.call-done.w_ref.w_any = bf16[1024,3072]{1,0:T(8,128)(2,1)} async-done(((bf16[32,3072]{1,0:T(8,128)(2,1)}), bf16[1024,3072]{1,0:T(8,128)(2,1)}) %all-gather.5.cloned.1.call-update) | async-done | bytes 6291472 | tf_op jit(solution)/shard_map/all_gather | solution.py:398
  83.2 11.4 %project.1.q_ref.k_ref.v_ref = bf16[1024,3072]{1,0:T(8,128)(2,1)} custom-call(bf16[1024,1024]{1,0:T(8,128)(2,1)} %x_ref.3, bf16[1024,3072]{1,0:T(8,128)(2,1)} %all-gather.5.cloned.1.call-done.w_ref.w_any, f32[1,3072]{1,0:T(1,128)} %bitcast.15, f32[1,3072]{1,0:T(1,128)} %constant.0.clone.1.scale_ref), custom_call_target="tpu_custom_call" | custom-call | tf_op jit(solution)/shard_map/project/pallas_call | solution.py:42
  94.6 17.4 %attend.1 = (bf16[1024,1024]{1,0:T(8,128)(2,1)}, bf16[32,512,512]{2,1,0:T(8,128)(2,1)}, f32[1024,1024]{1,0:T(8,128)}) custom-call(s32[2]{0:T(128)} %len_ref.3, bf16[1024,3072]{1,0:T(8,128)(2,1)} %project.1.q_ref.k_ref.v_ref, bf16[1024,3072]{1,0:T(8,128)(2,1)} %project.1.q_ref.k_ref.v_ref, bf16[1024,3072]{1,0:T(8,128)(2,1)} %project.1.q_ref.k_ref.v_ref), custom_call_target="tpu_custom_call" | custom-call | tf_op jit(solution)/shard_map/attend/pallas_call | solution.py:104
  112.0 29.2 %all-gather.7.cloned.1.call-done.wo_ref.wo_any = bf16[1024,1024]{1,0:T(8,128)(2,1)} async-done(((bf16[32,1024]{1,0:T(8,128)(2,1)}), bf16[1024,1024]{1,0:T(8,128)(2,1)}) %all-gather.7.cloned.1.call-update) | async-done | bytes 2097168 | tf_op jit(solution)/shard_map/all_gather | solution.py:399
  141.2 79.1 %all-gather.9.cloned.1.call-done.wi_ref.wi_any = bf16[1024,4096]{1,0:T(8,128)(2,1)} async-done(((bf16[32,4096]{1,0:T(8,128)(2,1)}), bf16[1024,4096]{1,0:T(8,128)(2,1)}) %all-gather.9.cloned.1.call-update) | async-done | bytes 8388624 | tf_op jit(solution)/shard_map/all_gather | solution.py:400
  220.3 27.4 %feed.1 = (f32[1024,1024]{1,0:T(8,128)}, f32[1024,128]{1,0:T(8,128)}, bf16[1024,4096]{1,0:T(8,128)(2,1)}, bf16[1024,4096]{1,0:T(8,128)(2,1)}) custom-call(bf16[1024,1024]{1,0:T(8,128)(2,1)} %x_ref.3, bf16[1024,1024]{1,0:T(8,128)(2,1)} %get-tuple-element.23.o_ref, bf16[1024,1024]{1,0:T(8,128)(2,1)} %all-gather.7.cloned.1.call-done.wo_ref.wo_any, ...), custom_call_target="tpu_custom_call" | custom-call | tf_op jit(solution)/shard_map/feed/pallas_call | solution.py:155
  247.7 51.5 %all-gather.11.cloned.1.call-done.wd_any = bf16[4096,1024]{1,0:T(8,128)(2,1)} async-done(((bf16[128,1024]{1,0:T(8,128)(2,1)}), bf16[4096,1024]{1,0:T(8,128)(2,1)}) %all-gather.11.cloned.1.call-update) | async-done | bytes 8388624 | tf_op jit(solution)/shard_map/all_gather | solution.py:401
  299.2 48.1 %turn.1 = (bf16[1024,1024]{1,0:T(8,128)(2,1)}, f32[1024,1024]{1,0:T(8,128)}, bf16[1024,1024]{1,0:T(8,128)(2,1)}, f32[8,1024]{1,0:T(8,128)}, f32[1,4096]{1,0:T(1,128)}) custom-call(s32[2]{0:T(128)} %len_ref.3, bf16[1024,4096]{1,0:T(8,128)(2,1)} %get-tuple-element.24.gl_ref, bf16[1024,4096]{1,0:T(8,128)(2,1)} %get-tuple-element.25.gp_ref, ...), custom_call_target="tpu_custom_call" | custom-call | tf_op jit(solution)/shard_map/turn/pallas_call | solution.py:269
  347.3 1.0 fusion
  348.4 0.0 copy-start
  348.4 33.3 %back.1 = (bf16[1024,1024]{1,0:T(8,128)(2,1)}, f32[1,1024]{1,0:T(1,128)}) custom-call(bf16[1024,3072]{1,0:T(8,128)(2,1)} %project.1.q_ref.k_ref.v_ref, bf16[1024,3072]{1,0:T(8,128)(2,1)} %project.1.q_ref.k_ref.v_ref, bf16[1024,3072]{1,0:T(8,128)(2,1)} %project.1.q_ref.k_ref.v_ref, bf16[1024,1024]{1,0:T(8,128)(2,1)} %get-tuple-element.23.o_ref, ...), custom_call_target="tpu_custom_call" | custom-call | tf_op jit(solution)/shard_map/back/pallas_call | solution.py:366
  381.6 0.0 copy-done
  381.6 40.0 %all-reduce.7 = (f32[1024]{0:T(1024)S(1)}, f32[1024]{0:T(1024)S(1)}, f32[1024]{0:T(1024)S(1)}, f32[1024]{0:T(1024)S(1)}, f32[4096]{0:T(1024)S(1)}, /*index=5*/f32[1024]{0:T(1024)S(1)}, f32[1024]{0:T(1024)S(1)}) all-reduce(f32[1024]{0:T(1024)} %bitcast.29, f32[1024]{0:T(1024)S(1)} %bitcast.20, ...), channel_id=2, replica_groups=mesh['dp'=4,'fsdp'=8] {'dp','fsdp'}, use_global_device_ids=true, to_apply=%region_0.0.clone | all-reduce | flops 10240 | bytes 81920
  421.6 0.6 dynamic-slice
  422.2 0.6 dynamic-slice.1
  422.8 0.6 dynamic-slice.2
  423.4 0.6 dynamic-slice.3
  424.0 0.6 dynamic-slice.5
  424.5 0.6 dynamic-slice.6
  425.1 0.6 dynamic-slice.4
  (2 shorter events, 0.0 us)
Async XLA Ops:
  7.2 76.0 %all-gather.5.cloned.1.call-start = ((), (), s32[]{:S(2)}) async-start(), calls=%async_computation | async-start | bytes 6488064 | tf_op jit(solution)/shard_map/all_gather | solution.py:398
  7.9 133.3 %all-gather.7.cloned.1.call-start = ((), (), s32[]{:S(2)}) async-start(), calls=%async_computation.1 | async-start | bytes 2162688 | tf_op jit(solution)/shard_map/all_gather | solution.py:399
  8.7 211.7 %all-gather.9.cloned.1.call-start = ((), (), s32[]{:S(2)}) async-start(), calls=%async_computation.2 | async-start | bytes 8650752 | tf_op jit(solution)/shard_map/all_gather | solution.py:400
  9.4 289.8 %all-gather.11.cloned.1.call-start = ((), (), s32[]{:S(2)}) async-start(), calls=%async_computation.3 | async-start | bytes 8650752 | tf_op jit(solution)/shard_map/all_gather | solution.py:401
  348.4 33.3 %copy-start = (f32[1,4096]{1,0:T(1,128)S(1)}, f32[1,4096]{1,0:T(1,128)}, u32[]{:S(2)}) copy-start(f32[1,4096]{1,0:T(1,128)} %get-tuple-element.36) | copy-start | bytes 49156
Sparse Core Ops, SparseCore 0:
  11.0 72.1 all-gather.4
  86.2 54.9 all-gather.6
  144.2 76.1 all-gather.8
  223.2 76.0 all-gather.10

commit v2 on v1

v2 whole, which is shorter than its diff:
```python
import functools
import math

import jax
import jax.numpy as jnp
from jax import lax
from jax.experimental import pallas as pl
from jax.experimental.pallas import tpu as pltpu
from jax.sharding import PartitionSpec as P

HD = 64
L = 512
LN_EPS = 1e-12
MIB = 2**20
BF = jnp.bfloat16
F32 = jnp.float32


def params(limit=60, semantics=None):
    return pltpu.CompilerParams(vmem_limit_bytes=limit * MIB, dimension_semantics=semantics)


def dot(left, right, on_left, on_right):
    return lax.dot_general(
        left, right, (((on_left,), (on_right,)), ((), ())), preferred_element_type=F32
    )


def shape_of(dims, kind):
    return jax.ShapeDtypeStruct(dims, kind)


def cost(flops):
    return pl.CostEstimate(flops=flops, bytes_accessed=0, transcendentals=0)


def issue(sources, buf, sem, place, height):
    plane_at, z_at, core_at = place
    cols = buf.shape[1]
    for source, tag in sources:
        if tag is None:
            pltpu.make_async_copy(source, buf, sem).start()
            continue
        chip, zs, first, turned = tag
        tall = source.shape[0] // len(zs)
        for step, z in enumerate(zs):
            row = ((plane_at ^ chip) * 8 + (z_at ^ z) * 2 + (core_at ^ turned)) * height
            for block in range(height // tall):
                pltpu.make_async_copy(
                    source.at[pl.ds(step * tall, tall), pl.ds(first + block * cols, cols)],
                    buf.at[pl.ds(pl.multiple_of(row + block * tall, tall), tall)],
                    sem,
                ).start()


def settle(buf, sem):
    pltpu.make_async_copy(buf, buf, sem).wait()


def tagged(refs, tags):
    return list(zip(refs, tags))


def tags_of(sources):
    return [tag for _, tag in sources]


def arrays_of(sources):
    return [array for array, _ in sources]


def place_of(scalars, seqs):
    return scalars[seqs], scalars[seqs + 1], scalars[seqs + 2]


ANYWHERE = pl.BlockSpec(memory_space=pl.ANY)

def pack_body(qkv_ref, out_ref, in_ref, down_ref, own_ref, feed_ref):
    height = qkv_ref.shape[0]
    at = 0
    for ref in (qkv_ref, out_ref, in_ref):
        own_ref[:, at : at + ref.shape[1]] = ref[...]
        at += ref.shape[1]
    for first in range(0, down_ref.shape[0], height):
        own_ref[:, at : at + down_ref.shape[1]] = down_ref[first : first + height, :]
        at += down_ref.shape[1]
    feed_ref[:, : out_ref.shape[1]] = out_ref[...]
    feed_ref[:, out_ref.shape[1] :] = in_ref[...]


def pack(w_qkv, w_out, w_in, w_down):
    height = w_qkv.shape[0]
    feed_wide = w_out.shape[1] + w_in.shape[1]
    wide = w_qkv.shape[1] + feed_wide + w_down.shape[0] // height * w_down.shape[1]
    return pl.pallas_call(
        pack_body,
        out_shape=(shape_of((height, wide), BF), shape_of((height, feed_wide), BF)),
        compiler_params=params(20),
        name="pack",
    )(w_qkv, w_out, w_in, w_down)


def project_body(seqs, tags, len_ref, x_ref, bias_ref, scale_ref, *refs):
    sources, (out_ref, buf, sem) = tagged(refs, tags), refs[len(tags) :]

    @pl.when(pl.program_id(0) == 0)
    def _():
        issue(sources, buf, sem, place_of(len_ref, seqs), buf.shape[0] // 32)
        settle(buf, sem)

    step = out_ref.shape[1]
    cols = pl.ds(pl.multiple_of(pl.program_id(0) * step, step), step)
    total = dot(x_ref[...], buf[:, cols], 1, 0) + bias_ref[...]
    out_ref[...] = (total * scale_ref[...]).astype(BF)


def project(scalars, seqs, rows, sources, bias, scale):
    count, width = rows.shape
    wide = bias.shape[1]
    step = 1024
    return pl.pallas_call(
        functools.partial(project_body, seqs, tags_of(sources)),
        out_shape=shape_of((count, wide), BF),
        grid_spec=pltpu.PrefetchScalarGridSpec(
            num_scalar_prefetch=1,
            grid=(wide // step,),
            in_specs=[
                pl.BlockSpec((count, width), lambda j, n: (0, 0)),
                pl.BlockSpec((1, step), lambda j, n: (0, j)),
                pl.BlockSpec((1, step), lambda j, n: (0, j)),
                *([ANYWHERE] * len(sources)),
            ],
            out_specs=pl.BlockSpec((count, step), lambda j, n: (0, j)),
            scratch_shapes=[pltpu.VMEM((width, wide), BF), pltpu.SemaphoreType.DMA],
        ),
        compiler_params=params(),
        cost_estimate=cost(2 * count * width * wide),
        name="project",
    )(scalars, rows, bias, scale, *arrays_of(sources))


def lane_halves(kind):
    lane = lax.broadcasted_iota(jnp.int32, (1, 128), 1)
    return [(lane < HD).astype(F32).astype(kind), (lane >= HD).astype(F32).astype(kind)]


QUAD = 256


def attend_body(seq, len_ref, q_ref, k_ref, v_ref, *refs):
    o_ref, e_ref, r_ref = refs[-3:]
    length = len_ref[seq]
    halves = lane_halves(BF)
    lane = lax.broadcasted_iota(jnp.int32, (L, 128), 1)
    row = lax.broadcasted_iota(jnp.int32, (L, 128), 0)
    q_side = jnp.where(lane == 0, 1.0, 0.0).astype(BF)
    k_side = jnp.where((lane == 0) & (row >= length), -1e30, 0.0).astype(BF)
    for pair in range(QUAD // 128):
        part = slice(pair * 128, (pair + 1) * 128)
        q_pair = jnp.concatenate([q_ref[:, part], q_side], axis=1)
        k_pair = k_ref[:, part]
        v_pair = v_ref[:, part]
        powers = []
        for head in range(2):
            k_one = jnp.concatenate([k_pair * halves[head], k_side], axis=1)
            scores = dot(q_pair, k_one, 1, 1)
            peak = jnp.max(scores, axis=1, keepdims=True)
            power = jnp.exp(scores - peak).astype(BF)
            e_ref[2 * pair + head] = power
            powers.append(power)
        right = jnp.concatenate(
            [
                jnp.concatenate([v_pair * half, jnp.broadcast_to(half, (L, 128))], axis=1)
                for half in halves
            ],
            axis=0,
        )
        both = dot(jnp.concatenate(powers, axis=1), right, 1, 0)
        inverse = 1.0 / both[:, 128:]
        r_ref[:, part] = inverse
        o_ref[:, part] = (both[:, :128] * inverse).astype(BF)


def attend(scalars, qkv, width, seq, earlier):
    count = qkv.shape[0]
    quads = width // QUAD
    heads = QUAD // HD
    return pl.pallas_call(
        functools.partial(attend_body, seq),
        out_shape=(
            shape_of((count, width), BF),
            shape_of((count // L * width // HD, L, L), BF),
            shape_of((count, width), F32),
        ),
        grid_spec=pltpu.PrefetchScalarGridSpec(
            num_scalar_prefetch=1,
            grid=(quads,),
            in_specs=[
                pl.BlockSpec((L, QUAD), lambda j, n: (seq, j)),
                pl.BlockSpec((L, QUAD), lambda j, n: (seq, quads + j)),
                pl.BlockSpec((L, QUAD), lambda j, n: (seq, 2 * quads + j)),
                *([ANYWHERE] * len(earlier)),
            ],
            out_specs=[
                pl.BlockSpec((L, QUAD), lambda j, n: (seq, j)),
                pl.BlockSpec((heads, L, L), lambda j, n: (seq * quads + j, 0, 0)),
                pl.BlockSpec((L, QUAD), lambda j, n: (seq, j)),
            ],
        ),
        compiler_params=params(),
        input_output_aliases={4 + n: n for n in range(len(earlier))},
        cost_estimate=cost(16 * L * width * L),
        name="attend",
    )(scalars, qkv, qkv, qkv, *earlier)


ROWS = 256


def feed_body(seqs, tags, len_ref, x_ref, o_ref, vec_ref, bi_ref, *refs):
    sources, (u_ref, s_ref, gl_ref, gp_ref, buf, sem) = tagged(refs, tags), refs[-6:]

    @pl.when(pl.program_id(0) == 0)
    def _():
        issue(sources, buf, sem, place_of(len_ref, seqs), buf.shape[0] // 32)
        settle(buf, sem)

    width = x_ref.shape[1]
    joined = dot(o_ref[...], buf[:, :width], 1, 0) + vec_ref[0:1, :] + x_ref[...].astype(F32)
    centered = joined - jnp.mean(joined, axis=1, keepdims=True)
    spread = lax.rsqrt(jnp.mean(centered * centered, axis=1, keepdims=True) + LN_EPS)
    normed = centered * spread * vec_ref[1:2, :] + vec_ref[2:3, :]
    u_ref[...] = normed
    s_ref[...] = jnp.broadcast_to(spread, s_ref.shape)
    rounded = normed.astype(BF)
    step = 512
    for part in range(gl_ref.shape[1] // step):
        cols = slice(part * step, (part + 1) * step)
        pre = dot(rounded, buf[:, width + part * step : width + (part + 1) * step], 1, 0)
        pre = pre + bi_ref[:, cols]
        phi = 0.5 + 0.5 * lax.erf(pre * math.sqrt(0.5))
        slope = phi + pre * jnp.exp(-0.5 * pre * pre) * (1.0 / math.sqrt(2.0 * math.pi))
        gl_ref[:, cols] = (pre * phi).astype(BF)
        gp_ref[:, cols] = slope.astype(BF)


def feed(scalars, seqs, rows, context, sources, vectors, bias_in, seq, earlier):
    count, width = rows.shape
    wide = bias_in.shape[1]
    steps = L // ROWS
    block = lambda cols: pl.BlockSpec((ROWS, cols), lambda i, n: (seq * steps + i, 0))
    return pl.pallas_call(
        functools.partial(feed_body, seqs, tags_of(sources)),
        out_shape=(
            shape_of((count, width), F32),
            shape_of((count, 128), F32),
            shape_of((count, wide), BF),
            shape_of((count, wide), BF),
        ),
        grid_spec=pltpu.PrefetchScalarGridSpec(
            num_scalar_prefetch=1,
            grid=(steps,),
            in_specs=[
                block(width),
                block(width),
                pl.BlockSpec((8, width), lambda i, n: (0, 0)),
                pl.BlockSpec((1, wide), lambda i, n: (0, 0)),
                *([ANYWHERE] * (len(sources) + len(earlier))),
            ],
            out_specs=[block(width), block(128), block(wide), block(wide)],
            scratch_shapes=[pltpu.VMEM((width, width + wide), BF), pltpu.SemaphoreType.DMA],
        ),
        compiler_params=params(),
        input_output_aliases={5 + len(sources) + n: n for n in range(len(earlier))},
        cost_estimate=cost(2 * L * width * (width + wide)),
        name="feed",
    )(scalars, rows, context, vectors, bias_in, *arrays_of(sources), *earlier)


def turn_body(
    seqs, feed_tags, down_tags, len_ref, gl_ref, gp_ref, u_ref, s_ref, r_ref, c_ref, vec_ref, *refs
):
    feeds, downs = tagged(refs, feed_tags), tagged(refs[len(feed_tags) :], down_tags)
    y_ref, dh_ref, do_ref, gv_ref, gi_ref, buf, down, sems = refs[-8:]
    index = pl.program_id(0)
    width = u_ref.shape[1]
    wide = gl_ref.shape[1]
    parts = 4
    step = wide // parts

    @pl.when(index == 0)
    def _():
        place = place_of(len_ref, seqs)
        issue(downs, down, sems.at[0], place, wide // 32)
        issue(feeds, buf, sems.at[1], place, width // 32)
        gv_ref[...] = jnp.zeros_like(gv_ref)
        gi_ref[...] = jnp.zeros_like(gi_ref)
        settle(down, sems.at[0])

    gain_one, beta_one, gain_two, beta_two, bias_down = (vec_ref[n : n + 1, :] for n in range(1, 6))
    normed = u_ref[...]
    total = normed + bias_down
    for part in range(parts):
        rows = slice(part * step, (part + 1) * step)
        total = total + dot(gl_ref[:, rows], down[rows, :], 1, 0)
    centered = total - jnp.mean(total, axis=1, keepdims=True)
    spread = lax.rsqrt(jnp.mean(centered * centered, axis=1, keepdims=True) + LN_EPS)
    hat = centered * spread
    y_ref[...] = (hat * gain_two + beta_two).astype(BF)
    per_seq = L // ROWS
    first = lax.rem(index, per_seq) * ROWS
    live = lax.broadcasted_iota(jnp.int32, (ROWS, 1), 0) + first < len_ref[index // per_seq]
    dy = jnp.where(live, c_ref[...].astype(F32), 0.0)
    gv_ref[4:5, :] += jnp.sum(dy, axis=0, keepdims=True)
    scaled = dy * gain_two
    d_two = spread * (
        scaled
        - jnp.mean(scaled, axis=1, keepdims=True)
        - hat * jnp.mean(scaled * hat, axis=1, keepdims=True)
    )
    d_branch = d_two.astype(BF)
    gv_ref[3:4, :] += jnp.sum(d_branch.astype(F32), axis=0, keepdims=True)
    pl.when(index == 0)(functools.partial(settle, buf, sems.at[1]))
    total = d_two
    half = step // 2
    for part in range(2 * parts):
        rows = slice(part * half, (part + 1) * half)
        d_hidden = dot(d_branch, down[rows, :], 1, 1) * gp_ref[:, rows].astype(F32)
        d_hidden = d_hidden.astype(BF)
        gi_ref[:, rows] += jnp.sum(d_hidden.astype(F32), axis=0, keepdims=True)
        total = total + dot(d_hidden, buf[:, width + part * half : width + (part + 1) * half], 1, 1)
    gv_ref[2:3, :] += jnp.sum(total, axis=0, keepdims=True)
    scaled = total * gain_one
    hat = (normed - beta_one) * (1.0 / gain_one)
    d_one = s_ref[:, 0:1] * (
        scaled
        - jnp.mean(scaled, axis=1, keepdims=True)
        - hat * jnp.mean(scaled * hat, axis=1, keepdims=True)
    )
    dh_ref[...] = d_one
    d_att = d_one.astype(BF)
    gv_ref[1:2, :] += jnp.sum(d_att.astype(F32), axis=0, keepdims=True)
    d_context = dot(d_att, buf[:, :width], 1, 1).astype(BF).astype(F32)
    gv_ref[0:1, :] += jnp.sum(d_context, axis=0, keepdims=True)
    do_ref[...] = (d_context * r_ref[...]).astype(BF)


def turn(scalars, seqs, gl, gp, normed, spread, inverse, cotangent, feeds, downs, vectors):
    count, width = normed.shape
    wide = gl.shape[1]
    block = lambda cols: pl.BlockSpec((ROWS, cols), lambda i, n: (i, 0))
    return pl.pallas_call(
        functools.partial(turn_body, seqs, tags_of(feeds), tags_of(downs)),
        out_shape=(
            shape_of((count, width), BF),
            shape_of((count, width), F32),
            shape_of((count, width), BF),
            shape_of((8, width), F32),
            shape_of((1, wide), F32),
        ),
        grid_spec=pltpu.PrefetchScalarGridSpec(
            num_scalar_prefetch=1,
            grid=(count // ROWS,),
            in_specs=[
                block(wide),
                block(wide),
                block(width),
                block(128),
                block(width),
                block(width),
                pl.BlockSpec((8, width), lambda i, n: (0, 0)),
                *([ANYWHERE] * (len(feeds) + len(downs))),
            ],
            out_specs=[
                block(width),
                block(width),
                block(width),
                pl.BlockSpec((8, width), lambda i, n: (0, 0)),
                pl.BlockSpec((1, wide), lambda i, n: (0, 0)),
            ],
            scratch_shapes=[
                pltpu.VMEM((width, width + wide), BF),
                pltpu.VMEM((wide, width), BF),
                pltpu.SemaphoreType.DMA((2,)),
            ],
        ),
        compiler_params=params(),
        cost_estimate=cost(2 * count * width * (width + 3 * wide)),
        name="turn",
    )(scalars, gl, gp, normed, spread, inverse, cotangent, vectors, *arrays_of(feeds), *arrays_of(downs))


def back_body(
    seqs, tags, len_ref, q_ref, k_ref, v_ref, o_ref, do_ref, e_ref, dh_ref, *refs
):
    sources, (dx_ref, gq_ref, all_ref, w_ref, sem) = tagged(refs, tags), refs[len(tags) :]
    seq, quad = pl.program_id(0), pl.program_id(1)
    quads = pl.num_programs(1)
    width = dh_ref.shape[1]

    @pl.when((seq == 0) & (quad == 0))
    def _():
        issue(sources, w_ref, sem, place_of(len_ref, seqs), width // 32)
        gq_ref[...] = jnp.zeros_like(gq_ref)

    halves = lane_halves(BF)
    halves_wide = lane_halves(F32)
    lane = lax.broadcasted_iota(jnp.int32, (L, 128), 1)
    for pair in range(QUAD // 128):
        part = slice(pair * 128, (pair + 1) * 128)
        q_pair, k_pair, v_pair, do_pair = (r[:, part] for r in (q_ref, k_ref, v_ref, do_ref))
        products = do_pair.astype(F32) * o_ref[:, part].astype(F32)
        shifts = [jnp.sum(products * half, axis=1, keepdims=True) for half in halves_wide]
        rough = [shift.astype(BF).astype(F32) for shift in shifts]
        side = jnp.where(
            lane == 0,
            -rough[0],
            jnp.where(
                lane == 1,
                rough[0] - shifts[0],
                jnp.where(lane == 2, -rough[1], jnp.where(lane == 3, rough[1] - shifts[1], 0.0)),
            ),
        ).astype(BF)
        left = jnp.concatenate([do_pair, side], axis=1)
        q_turned = q_pair.T
        do_turned = do_pair.T
        d_scores, d_keys, d_values = [], [], []
        for head in range(2):
            rows = slice(head * HD, (head + 1) * HD)
            power = e_ref[2 * pair + head]
            marks = jnp.where(lane // 2 == head, 1.0, 0.0).astype(BF)
            right = jnp.concatenate([v_pair * halves[head], marks], axis=1)
            d_score = (power.astype(F32) * dot(left, right, 1, 1)).astype(BF)
            d_scores.append(d_score)
            d_keys.append(dot(q_turned[rows], d_score, 1, 0))
            d_values.append(dot(do_turned[rows], power, 1, 0))
        right = jnp.concatenate([k_pair * half for half in halves], axis=0)
        d_query = (dot(jnp.concatenate(d_scores, axis=1), right, 1, 0) * (HD**-0.5)).astype(BF)
        cols = pl.multiple_of(quad * QUAD + pair * 128, 128)
        gq_ref[:, pl.ds(cols, 128)] += jnp.sum(d_query.astype(F32), axis=0, keepdims=True)
        all_ref[:, pl.ds(cols, 128)] = d_query
        all_ref[:, pl.ds(width + cols, 128)] = jnp.concatenate(d_keys, axis=0).T.astype(BF)
        all_ref[:, pl.ds(2 * width + cols, 128)] = jnp.concatenate(d_values, axis=0).T.astype(BF)

    pl.when((seq == 0) & (quad == quads - 1))(functools.partial(settle, w_ref, sem))

    @pl.when(quad == quads - 1)
    def _():
        dx_ref[...] = (dh_ref[...] + dot(all_ref[...], w_ref[...], 1, 1)).astype(BF)


def back(scalars, seqs, qkv, context, d_context, powers, d_joined, sources):
    count, width = d_joined.shape
    quads = width // QUAD
    heads = QUAD // HD
    col = lambda n: pl.BlockSpec((L, QUAD), lambda i, j, s: (i, n * quads + j))
    return pl.pallas_call(
        functools.partial(back_body, seqs, tags_of(sources)),
        out_shape=(shape_of((count, width), BF), shape_of((1, width), F32)),
        grid_spec=pltpu.PrefetchScalarGridSpec(
            num_scalar_prefetch=1,
            grid=(seqs, quads),
            in_specs=[
                col(0),
                col(1),
                col(2),
                col(0),
                col(0),
                pl.BlockSpec((heads, L, L), lambda i, j, s: (i * quads + j, 0, 0)),
                pl.BlockSpec((L, width), lambda i, j, s: (i, 0)),
                *([ANYWHERE] * len(sources)),
            ],
            out_specs=[
                pl.BlockSpec((L, width), lambda i, j, s: (i, 0)),
                pl.BlockSpec((1, width), lambda i, j, s: (0, 0)),
            ],
            scratch_shapes=[
                pltpu.VMEM((L, 3 * width), BF),
                pltpu.VMEM((width, 3 * width), BF),
                pltpu.SemaphoreType.DMA,
            ],
        ),
        compiler_params=params(),
        cost_estimate=cost(2 * count * width * 3 * width + 20 * count * width * L),
        name="back",
    )(scalars, qkv, qkv, qkv, context, d_context, powers, d_joined, *arrays_of(sources))


BOTH = ("dp", "fsdp")


def hop(block, axis, flip):
    size = lax.axis_size(axis)
    return lax.ppermute(block, axis, [(i, i ^ flip) for i in range(size)])


def over_x(block):
    return hop(block, "dp", 1)


def over_y(block):
    return hop(block, "dp", 2)


def over_core(block):
    return hop(block, "fsdp", 1)


def over_z(block, k):
    return hop(block, "fsdp", 2 * k)


def after(value, *earlier):
    return lax.optimization_barrier((value, *earlier))[0]


MOVES = {
    "x": over_x,
    "y": over_y,
    "c": over_core,
    "1": functools.partial(over_z, k=1),
    "2": functools.partial(over_z, k=2),
    "3": functools.partial(over_z, k=3),
}


def stage(lanes, blocks, *earlier):
    blocks = after(tuple(blocks), *earlier)
    return lax.optimization_barrier(tuple(MOVES[lane](block) for lane, block in zip(lanes, blocks)))


def both(mine, others):
    return [(array, (*tag, 0)) for array, tag in mine] + [
        (array, (*tag, 1)) for array, (_, tag) in zip(others, mine)
    ]


def stack(*blocks):
    return jnp.concatenate(blocks, axis=0)


def whole(array):
    return [(array, None)]


def reduce_shares(block, slots):
    dp, fsdp = lax.axis_size("dp"), lax.axis_size("fsdp")
    block = block.reshape(dp, fsdp, slots)
    for axis, dim in (("dp", 0), ("fsdp", 0)):
        size = lax.axis_size(axis)
        at = lax.axis_index(axis)
        pick = lambda k: lax.dynamic_index_in_dim(block, at ^ k, 0, keepdims=False)
        block = functools.reduce(
            lambda left, right: left + right, [pick(0)] + [hop(pick(k), axis, k) for k in range(1, size)]
        )
    return block


def on_device(
    tokens, lengths, w_qkv, w_out, w_in, w_down, gain_one, gain_two,
    bias_q, bias_v, bias_out, beta_one, bias_in, bias_down, beta_two, cotangent,
):
    width = w_out.shape[1]
    seqs = lengths.shape[0]
    chip = lax.axis_index("fsdp")
    scalars = jnp.concatenate(
        [lengths, jnp.stack([lax.axis_index("dp"), chip // 2, chip % 2]).astype(jnp.int32)]
    )
    score_scale = HD**-0.5
    ones = jnp.ones((width,), F32)
    zeros = jnp.zeros((width,), F32)
    bias = jnp.concatenate([bias_q, zeros, bias_v])[None]
    scale = jnp.concatenate([ones * score_scale, ones, ones])[None]
    vectors = jnp.stack([bias_out, gain_one, beta_one, gain_two, beta_two, bias_down, zeros, zeros])
    special = (lax.axis_size("dp"), lax.axis_size("fsdp")) == (4, 8)
    if special:
        own, w_feed = pack(w_qkv, w_out, w_in, w_down)
        at_feed = w_qkv.shape[1]
        at_down = at_feed + w_feed.shape[1]
        z_one, z_two, z_three, near_x, near_y = stage("123xy", (w_qkv, w_qkv, w_qkv, own, own))
        far = stack(z_one, z_two, z_three)
        x_far, y_far, feed_two, own_core, near_x_core = stage(
            "xy2cc", (far, far, w_feed, own, near_x)
        )
        left = stack(near_x[:, :at_feed], x_far[:32])
        crossed, crossed_more, feed_one, near_y_core, far_core = stage(
            "yx1cc", (left, y_far[32:], w_feed, near_y, far), feed_two, own_core, near_x_core
        )
        x_far_core, y_far_core, crossed_core, crossed_more_core = stage(
            "cccc", (x_far, y_far, crossed, crossed_more), feed_one, near_y_core, far_core
        )
        near = (own, near_x, near_y)
        near_core = (own_core, near_x_core, near_y_core)
        rest = (1, 2, 3)
        qkv_parts = both(
            [
                *((array, (chip, (0,), 0)) for chip, array in enumerate(near)),
                (far, (0, rest, 0)),
                (x_far, (1, rest, 0)),
                (y_far, (2, rest, 0)),
                (crossed, (3, (0, 1), 0)),
                (crossed_more, (3, (2, 3), 0)),
            ],
            [*near_core, far_core, x_far_core, y_far_core, crossed_core, crossed_more_core],
        )
        pair = stack(feed_one, feed_two)
        x_pair, y_pair, feed_three, pair_core = stage(
            "xy3c", (pair, pair, w_feed, pair), y_far_core, crossed_core, crossed_more_core
        )
        first = after(tokens, pair)
    else:
        first = tokens
        w_feed = jnp.concatenate([w_out, w_in], axis=1)
        qkv_parts = whole(lax.all_gather(w_qkv, BOTH, axis=0, tiled=True))
        feed_parts = whole(lax.all_gather(w_feed, BOTH, axis=0, tiled=True))
        down_parts = whole(lax.all_gather(w_down, BOTH, axis=0, tiled=True))
    qkv = project(scalars, seqs, first, qkv_parts, bias, scale)
    if special:
        x_last, y_last, cross_down, down_one, down_two = stage(
            "xyy12", (feed_three, feed_three, near_x[:, at_down:], w_down, w_down), qkv, pair_core
        )
    attended = []
    for seq in range(seqs):
        if special and seq == 1:
            x_last, y_last, *attended = after((x_last, y_last, *attended), cross_down, down_one)
            left = stack(near_x[:, at_feed:at_down], x_pair[:32])
            crossed, crossed_more, down_three, x_pair_core, y_pair_core = stage(
                "yx3cc", (left, stack(y_pair[32:], y_last), w_down, x_pair, y_pair), x_last, *attended
            )
        attended = attend(scalars, qkv, width, seq, attended)
    context, powers, inverse = attended
    if special:
        cores = stage(
            "ccccc", (feed_three, x_last, y_last, crossed, crossed_more), context, down_three
        )
        feed_parts = both(
            [
                *((array, (chip, (0,), at_feed)) for chip, array in enumerate(near)),
                (pair, (0, (1, 2), 0)),
                (x_pair, (1, (1, 2), 0)),
                (y_pair, (2, (1, 2), 0)),
                (feed_three, (0, (3,), 0)),
                (x_last, (1, (3,), 0)),
                (y_last, (2, (3,), 0)),
                (crossed, (3, (0, 1), 0)),
                (crossed_more, (3, (2, 3), 0)),
            ],
            [*near_core, pair_core, x_pair_core, y_pair_core, *cores],
        )
        far = stack(down_one, down_two, down_three)
        x_far, y_far, *diagonal = stage(
            "xy123", (far, far, cross_down, cross_down, cross_down), *cores
        )
    fed = []
    for seq in range(seqs):
        fed = feed(scalars, seqs, tokens, context, feed_parts, vectors, bias_in[None], seq, fed)
        if special and seq == 0:
            x_far, cross_down, *fed = after((x_far, cross_down, *fed), y_far, *diagonal)
    normed, spread, gl, gp = fed
    if special:
        mine = [
            (after(far, x_far), (0, rest, 0)),
            (x_far, (1, rest, 0)),
            (y_far, (2, rest, 0)),
            (cross_down, (3, (0,), 0)),
            *((block, (3, (k,), 0)) for block, k in zip(diagonal, rest)),
        ]
        down_parts = both(
            [*((array, (chip, (0,), at_down)) for chip, array in enumerate(near)), *mine],
            [*near_core, *(over_core(block) for block, _ in mine)],
        )
    output, d_joined, d_context, sums, sum_in = turn(
        scalars, seqs, gl, gp, normed, spread, inverse, cotangent, feed_parts, down_parts, vectors
    )
    input_grad, sum_q = back(scalars, seqs, qkv, context, d_context, powers, d_joined, qkv_parts)
    devices = lax.axis_size("dp") * lax.axis_size("fsdp")
    parts = (sum_q[0], sums[0], sums[1], sums[2], sum_in[0], sums[3], sums[4])
    rows = jnp.concatenate([part.reshape(devices, -1) for part in parts], axis=1)
    mine = reduce_shares(rows, rows.shape[1])
    shares, at = [], 0
    for part in parts:
        shares.append(mine[at : at + part.shape[0] // devices])
        at += part.shape[0] // devices
    return (output, input_grad, *shares)


def solution(mesh):
    split, rows, copied = P(BOTH), P(BOTH, None), P()
    in_specs = (rows, split, rows, rows, rows, rows, *([copied] * 9), rows)
    out_specs = (rows, rows, *([split] * 7))
    return jax.shard_map(
        on_device, mesh=mesh, in_specs=in_specs, out_specs=out_specs, check_vma=False
    )
```

time: 433 us -> 287 us (0.66)
  waiting for transfers between devices: 233 us -> 50.2 us
  starting transfers between devices: 0.15 us -> 55.6 us
  blocking collectives: 40 us -> 0 us
  local copies, waits for them, and re-layouts: 6.53 us -> 24.3 us
  between operations: 13.8 us -> 1.4 us
  Pallas kernels: 138 us -> 150 us
    all_gather x4 -> x0, waiting for transfers between devices: 230 us -> none  [the longest x1 79.1 us: on_device(): full_in = lax.all_gather(w_in, BOTH, axis=0, tiled=True)]
    ppermute x0 -> x60, starting transfers between devices: none -> 55.6 us  [hop(): return lax.ppermute(block, axis, [(i, i ^ flip) for i in range(size)])]
    ppermute x0 -> x60, waiting for transfers between devices: none -> 50.2 us  [hop(): return lax.ppermute(block, axis, [(i, i ^ flip) for i in range(size)])]
    unnamed x1 -> x0, blocking collectives: 40 us -> none
    pallas_call x5 -> x8, Pallas kernels: 138 us -> 150 us  [the longest x1 46.4 us: turn(): pl.pallas_call(functools.partial(turn_body, seqs, tags_of(feeds), tags_of...]
    unnamed x9 -> x107, local copies, waits for them, and re-layouts: 4.08 us -> 15.5 us
  transfers between devices with their start and end apart: 4 -> 60, of which waited for: 4 -> 15; matrix products, arithmetic and copies ran while one was open for 1% -> 3% of each run, Pallas kernels for 13% -> 24%
where the time goes in v2:
time: 287 us; the launch traced here: 286 us
  Pallas kernels  150 us (52%)
  starting transfers between devices  55.6 us (19%)
  waiting for transfers between devices  50.2 us (17%)
  local copies, waits for them, and re-layouts  24.3 us (8%)
  other arithmetic  4.26 us (1%)
    ppermute x60, starting transfers between devices, hop(): return lax.ppermute(block, axis, [(i, i ^ flip) for i in range(size)])  55.6 us
    ppermute x60, waiting for transfers between devices, hop(): return lax.ppermute(block, axis, [(i, i ^ flip) for i in range(size)])  50.2 us
    pallas_call x1, Pallas kernels, turn(): pl.pallas_call(functools.partial(turn_body, seqs, tags_of(feeds), tags_of...  46.4 us
    pallas_call x2, Pallas kernels, feed(): pl.pallas_call(functools.partial(feed_body, seqs, tags_of(sources)), out_...  35.6 us
    pallas_call x1, Pallas kernels, back(): pl.pallas_call(functools.partial(back_body, seqs, tags_of(sources)), out_...  34.1 us
    pallas_call x2, Pallas kernels, attend(): pl.pallas_call(functools.partial(attend_body, seq), out_shape=(shape_of((...  20.4 us
    unnamed x107, local copies, waits for them, and re-layouts  15.5 us
    pallas_call x1, Pallas kernels, project(): pl.pallas_call(functools.partial(project_body, seqs, tags_of(sources)), o...  14 us
  transfers between devices with their start and end apart: 60, of which 15 were waited for; matrix products, arithmetic and copies ran while one was open for 3% of the time, Pallas kernels for 24%

profile of v2, /device:TPU:0, one launch (start us, length us, event | category | flops | bytes accessed | tf_op | source)
XLA Modules:
  0.0 286.3 jit_solution(15751222438602851654)
XLA Ops:
  0.7 0.9 copy-done.1
  1.6 0.9 copy-done.2
  4.4 3.0 %collective-permute-start.3 = (bf16[32,12288]{1,0:T(8,128)(2,1)S(1)}, bf16[32,12288]{1,0:T(8,128)(2,1)S(1)}, u32[]{:S(2)}, u32[]{:S(2)}) collective-permute-start(bf16[32,12288]{1,0:T(8,128)(2,1)S(1)} %get-tuple-element.145.refs_0_.refs_22_), channel_id=1, source_target_pairs={{0,8},{8,0},{16,24},{24,16},{1,9},{9,1},{17,25},{25,17},{2,10},{10... | collective-permute-start | bytes 2359304 | tf_op jit(solution)/shard_map/ppermute | solution.py:494
  7.4 1.5 collective-permute-start.4
  8.9 1.6 collective-permute-start
  10.5 2.6 collective-permute-start.1
  13.3 4.6 %collective-permute-done = bf16[32,3072]{1,0:T(8,128)(2,1)S(1)} collective-permute-done((bf16[32,3072]{1,0:T(8,128)(2,1)S(1)}, bf16[32,3072]{1,0:T(8,128)(2,1)S(1)}, u32[]{:S(2)}, u32[]{:S(2)}) %collective-permute-start) | collective-permute-done | bytes 196640 | tf_op jit(solution)/shard_map/ppermute | solution.py:494
  17.9 9.8 %collective-permute-done.1 = bf16[32,3072]{1,0:T(8,128)(2,1)S(1)} collective-permute-done((bf16[32,3072]{1,0:T(8,128)(2,1)S(1)}, bf16[32,3072]{1,0:T(8,128)(2,1)S(1)}, u32[]{:S(2)}, u32[]{:S(2)}) %collective-permute-start.1) | collective-permute-done | bytes 196640 | tf_op jit(solution)/shard_map/ppermute | solution.py:494
  31.4 3.8 %collective-permute-start.7 = (bf16[32,5120]{1,0:T(8,128)(2,1)S(1)}, bf16[32,5120]{1,0:T(8,128)(2,1)}, u32[]{:S(2)}, u32[]{:S(2)}) collective-permute-start(bf16[32,5120]{1,0:T(8,128)(2,1)S(1)} %get-tuple-element.174), channel_id=1, source_target_pairs={{0,4},{1,5},{2,6},{3,7},{4,0},{5,1},{6,2},{7,3},{8,12},{9,13},{10,... | collective-permute-start | bytes 983048 | tf_op jit(solution)/shard_map/ppermute | solution.py:494
  35.2 14.4 %collective-permute-done.7 = bf16[32,5120]{1,0:T(8,128)(2,1)} collective-permute-done((bf16[32,5120]{1,0:T(8,128)(2,1)S(1)}, bf16[32,5120]{1,0:T(8,128)(2,1)}, u32[]{:S(2)}, u32[]{:S(2)}) %collective-permute-start.7) | collective-permute-done | bytes 327712 | tf_op jit(solution)/shard_map/ppermute | solution.py:494
  49.7 1.1 copy-done.12
  51.7 1.8 slice.59
  54.7 1.5 collective-permute-start.10
  56.2 1.5 collective-permute-start.11
  58.3 8.5 %collective-permute-done.12 = bf16[32,5120]{1,0:T(8,128)(2,1)} collective-permute-done((bf16[32,5120]{1,0:T(8,128)(2,1)S(1)}, bf16[32,5120]{1,0:T(8,128)(2,1)}, u32[]{:S(2)}, u32[]{:S(2)}) %collective-permute-start.12) | collective-permute-done | bytes 327712 | tf_op jit(solution)/shard_map/ppermute | solution.py:494
  68.2 1.0 constant_dynamic-update-slice_fusion.4
  69.9 1.0 constant_dynamic-update-slice_fusion.3.refs_3_
  72.7 1.5 collective-permute-start.19
  76.0 2.2 collective-permute-start.21
  78.2 14.0 %project.1.q_ref.k_ref.v_ref = bf16[1024,3072]{1,0:T(8,128)(2,1)} custom-call(s32[5]{0:T(128)} %pad_add_fusion.len_ref, bf16[1024,1024]{1,0:T(8,128)(2,1)} %x_ref.4, f32[1,3072]{1,0:T(1,128)} %bitcast.27, f32[1,3072]{1,0:T(1,128)} %constant.70.clone.1.scale_ref, bf16[32,12288]{1,0:T(8,128)(2,1)} %copy-done, bf16[32,12288]{1,0:T(8,128)(2,1)} %copy-done.6, ...), custom_call_target="tpu_custom_call" | custom-call | flops 6442450944 | tf_op jit(solution)/shard_map/project/pallas_call | solution.py:121
  93.6 1.3 collective-permute-start.25
  95.8 1.4 collective-permute-start.27
  97.2 10.2 %attend.2 = (bf16[1024,1024]{1,0:T(8,128)(2,1)}, bf16[32,512,512]{2,1,0:T(8,128)(2,1)}, f32[1024,1024]{1,0:T(8,128)}) custom-call(s32[5]{0:T(128)} %pad_add_fusion.len_ref, bf16[1024,3072]{1,0:T(8,128)(2,1)} %project.1.q_ref.k_ref.v_ref, bf16[1024,3072]{1,0:T(8,128)(2,1)} %project.1.q_ref.k_ref.v_ref, bf16[1024,3072]{1,0:T(8,128)(2,1)} %project.1.q_ref.k_ref.v_ref), custom_call_target="tpu_custom_call" | custom-call | flops 4294967296 | tf_op jit(solution)/shard_map/attend/pallas_call | solution.py:188
  110.0 0.9 pad_maximum_fusion
  110.9 1.6 collective-permute-start.28
  113.8 2.4 collective-permute-start.30
  116.2 10.2 %attend.3 = (bf16[1024,1024]{1,0:T(8,128)(2,1)}, bf16[32,512,512]{2,1,0:T(8,128)(2,1)}, f32[1024,1024]{1,0:T(8,128)}) custom-call(s32[5]{0:T(128)} %pad_add_fusion.len_ref, bf16[1024,3072]{1,0:T(8,128)(2,1)} %project.1.q_ref.k_ref.v_ref, bf16[1024,3072]{1,0:T(8,128)(2,1)} %project.1.q_ref.k_ref.v_ref, ...), custom_call_target="tpu_custom_call", output_to_operand_aliasing={{0}: (4, {}), {1}: (5, {}), {2}: (6, {})} | custom-call | flops 4294967296 | tf_op jit(solution)/shard_map/attend/pallas_call | solution.py:188
  127.6 1.7 constant_dynamic-update-slice_fusion.7
  129.3 1.7 constant_dynamic-update-slice_fusion.6
  131.0 1.7 constant_dynamic-update-slice_fusion.5.refs_25_
  132.7 1.4 collective-permute-start.38
  134.1 1.3 collective-permute-start.39
  136.8 1.6 collective-permute-start.41
  138.4 2.1 collective-permute-start.42
  140.5 17.8 %feed.2 = (f32[1024,1024]{1,0:T(8,128)}, f32[1024,128]{1,0:T(8,128)}, bf16[1024,4096]{1,0:T(8,128)(2,1)}, bf16[1024,4096]{1,0:T(8,128)(2,1)}) custom-call(s32[5]{0:T(128)} %pad_add_fusion.len_ref, bf16[1024,1024]{1,0:T(8,128)(2,1)} %x_ref.4, bf16[1024,1024]{1,0:T(8,128)(2,1)} %get-tuple-element.193.o_ref, f32[8,1024]{1,0:T(8,128)} %stack.43.vec_ref, ...), custom_call_target="tpu_custom_call" | custom-call | flops 5368709120 | tf_op jit(solution)/shard_map/feed/pallas_call | solution.py:252
  159.7 4.3 %collective-permute-done.46.refs_38_ = bf16[32,4096]{1,0:T(8,128)(2,1)S(1)} collective-permute-done((bf16[32,4096]{1,0:T(8,128)(2,1)}, bf16[32,4096]{1,0:T(8,128)(2,1)S(1)}, u32[]{:S(2)}, u32[]{:S(2)}) %collective-permute-start.46) | collective-permute-done | bytes 262176 | tf_op jit(solution)/shard_map/ppermute | solution.py:494
  164.5 17.7 %feed.3 = (f32[1024,1024]{1,0:T(8,128)}, f32[1024,128]{1,0:T(8,128)}, bf16[1024,4096]{1,0:T(8,128)(2,1)}, bf16[1024,4096]{1,0:T(8,128)(2,1)}) custom-call(s32[5]{0:T(128)} %pad_add_fusion.len_ref, bf16[1024,1024]{1,0:T(8,128)(2,1)} %x_ref.4, ...), custom_call_target="tpu_custom_call", output_to_operand_aliasing={{0}: (27, {}), {1}: (28, {}), {2}: (29, {}), {3}: (30, {})} | custom-call | flops 5368709120 | tf_op jit(solution)/shard_map/feed/pallas_call | solution.py:252
  183.9 46.4 %turn.1 = (bf16[1024,1024]{1,0:T(8,128)(2,1)}, f32[1024,1024]{1,0:T(8,128)}, bf16[1024,1024]{1,0:T(8,128)(2,1)}, f32[8,1024]{1,0:T(8,128)}, f32[1,4096]{1,0:T(1,128)}) custom-call(s32[5]{0:T(128)} %pad_add_fusion.len_ref, bf16[1024,4096]{1,0:T(8,128)(2,1)} %get-tuple-element.237.gl_ref, bf16[1024,4096]{1,0:T(8,128)(2,1)} %get-tuple-element.238.gp_ref, ...), custom_call_target="tpu_custom_call" | custom-call | flops 27917287424 | tf_op jit(solution)/shard_map/turn/pallas_call | solution.py:352
  230.3 34.1 %back.1 = (bf16[1024,1024]{1,0:T(8,128)(2,1)}, f32[1,1024]{1,0:T(1,128)}) custom-call(s32[5]{0:T(128)} %pad_add_fusion.len_ref, bf16[1024,3072]{1,0:T(8,128)(2,1)} %project.1.q_ref.k_ref.v_ref, bf16[1024,3072]{1,0:T(8,128)(2,1)} %project.1.q_ref.k_ref.v_ref, bf16[1024,3072]{1,0:T(8,128)(2,1)} %project.1.q_ref.k_ref.v_ref, ...), custom_call_target="tpu_custom_call" | custom-call | flops 17179869184 | tf_op jit(solution)/shard_map/back/pallas_call | solution.py:457
  264.9 1.3 reduce.39
  266.9 1.9 collective-permute-start.52
  269.4 1.1 collective-permute-start.50
  270.4 1.1 collective-permute-done.52
  271.5 1.0 collective-permute-done.51
  273.6 1.7 collective-permute-start.58
  275.4 4.7 %collective-permute-start.57 = (f32[320]{0:T(512)S(1)}, f32[320]{0:T(512)S(1)}, u32[]{:S(2)}, u32[]{:S(2)}) collective-permute-start(f32[320]{0:T(512)S(1)} %get-tuple-element.261), channel_id=1, source_target_pairs={{0,5},{1,4},{2,7},{3,6},{4,1},{5,0},{6,3},{7,2},{8,13},{9,12},{10,... | collective-permute-start | bytes 3848 | tf_op jit(solution)/shard_map/ppermute | solution.py:494
  280.1 1.5 collective-permute-start.55
  282.6 2.0 collective-permute-done.56
  (220 shorter events, 31.6 us)
Async XLA Ops:
  4.4 23.3 %collective-permute-start.3 = (bf16[32,12288]{1,0:T(8,128)(2,1)S(1)}, bf16[32,12288]{1,0:T(8,128)(2,1)S(1)}, u32[]{:S(2)}, u32[]{:S(2)}) collective-permute-start(bf16[32,12288]{1,0:T(8,128)(2,1)S(1)} %get-tuple-element.145.refs_0_.refs_22_), channel_id=1, source_target_pairs={{0,8},{8,0},{16,24},{24,16},{1,9},{9,1},{17,25},{25,17},{2,10},{10... | collective-permute-start | bytes 2359304 | tf_op jit(solution)/shard_map/ppermute | solution.py:494
  7.4 20.3 %collective-permute-start.4 = (bf16[32,12288]{1,0:T(8,128)(2,1)S(1)}, bf16[32,12288]{1,0:T(8,128)(2,1)S(1)}, u32[]{:S(2)}, u32[]{:S(2)}) collective-permute-start(bf16[32,12288]{1,0:T(8,128)(2,1)S(1)} %get-tuple-element.145.refs_0_.refs_22_), channel_id=1, source_target_pairs={{0,16},{8,24},{16,0},{24,8},{1,17},{9,25},{17,1},{25,9},{2,18},{10... | collective-permute-start | bytes 2359304 | tf_op jit(solution)/shard_map/ppermute | solution.py:494
  8.9 9.0 %collective-permute-start = (bf16[32,3072]{1,0:T(8,128)(2,1)S(1)}, bf16[32,3072]{1,0:T(8,128)(2,1)S(1)}, u32[]{:S(2)}, u32[]{:S(2)}) collective-permute-start(bf16[32,3072]{1,0:T(8,128)(2,1)S(1)} %copy-done.4), channel_id=1, source_target_pairs={{0,2},{1,3},{2,0},{3,1},{4,6},{5,7},{6,4},{7,5},{8,10},{9,11},{10,... | collective-permute-start | bytes 589832 | tf_op jit(solution)/shard_map/ppermute | solution.py:494
  10.5 17.2 %collective-permute-start.1 = (bf16[32,3072]{1,0:T(8,128)(2,1)S(1)}, bf16[32,3072]{1,0:T(8,128)(2,1)S(1)}, u32[]{:S(2)}, u32[]{:S(2)}) collective-permute-start(bf16[32,3072]{1,0:T(8,128)(2,1)S(1)} %copy-done.4), channel_id=1, source_target_pairs={{0,4},{1,5},{2,6},{3,7},{4,0},{5,1},{6,2},{7,3},{8,12},{9,13},{10,... | collective-permute-start | bytes 589832 | tf_op jit(solution)/shard_map/ppermute | solution.py:494
  13.1 14.6 %collective-permute-start.2 = (bf16[32,3072]{1,0:T(8,128)(2,1)S(1)}, bf16[32,3072]{1,0:T(8,128)(2,1)S(1)}, u32[]{:S(2)}, u32[]{:S(2)}) collective-permute-start(bf16[32,3072]{1,0:T(8,128)(2,1)S(1)} %copy-done.4), channel_id=1, source_target_pairs={{0,6},{1,7},{2,4},{3,5},{4,2},{5,3},{6,0},{7,1},{8,14},{9,15},{10,... | collective-permute-start | bytes 589832 | tf_op jit(solution)/shard_map/ppermute | solution.py:494
  29.8 19.8 %collective-permute-start.8 = (bf16[32,12288]{1,0:T(8,128)(2,1)S(1)}, bf16[32,12288]{1,0:T(8,128)(2,1)S(1)}, u32[]{:S(2)}, u32[]{:S(2)}) collective-permute-start(bf16[32,12288]{1,0:T(8,128)(2,1)S(1)} %get-tuple-element.145.refs_0_.refs_22_), channel_id=1, source_target_pairs={{0,1},{1,0},{2,3},{3,2},{4,5},{5,4},{6,7},{7,6},{8,9},{9,8},{10,11... | collective-permute-start | bytes 2359304 | tf_op jit(solution)/shard_map/ppermute | solution.py:494
  29.9 19.8 %collective-permute-start.9 = (bf16[32,12288]{1,0:T(8,128)(2,1)S(1)}, bf16[32,12288]{1,0:T(8,128)(2,1)S(1)}, u32[]{:S(2)}, u32[]{:S(2)}) collective-permute-start(bf16[32,12288]{1,0:T(8,128)(2,1)S(1)} %collective-permute-done.3.refs_1_.refs_23_), channel_id=1, source_target_pairs={{0,1},{1,0},{2,3},{3,2},{4,5},{5,4},{6,7},{7,6},{8,9},{9,8},{10,11... | collective-permute-start | bytes 2359304 | tf_op jit(solution)/shard_map/ppermute | solution.py:494
  30.4 19.3 %collective-permute-start.5 = (bf16[96,3072]{1,0:T(8,128)(2,1)}, bf16[96,3072]{1,0:T(8,128)(2,1)S(1)}, u32[]{:S(2)}, u32[]{:S(2)}) collective-permute-start(bf16[96,3072]{1,0:T(8,128)(2,1)} %constant_dynamic-update-slice_fusion.refs_3_), channel_id=1, source_target_pairs={{0,8},{8,0},{16,24},{24,16},{1,9},{9,1},{17,25},{25,17},{2,10},{10... | collective-permute-start | bytes 1769480 | tf_op jit(solution)/shard_map/ppermute | solution.py:494
  30.9 18.7 %collective-permute-start.6 = (bf16[96,3072]{1,0:T(8,128)(2,1)}, bf16[96,3072]{1,0:T(8,128)(2,1)}, u32[]{:S(2)}, u32[]{:S(2)}) collective-permute-start(bf16[96,3072]{1,0:T(8,128)(2,1)} %constant_dynamic-update-slice_fusion.refs_3_), channel_id=1, source_target_pairs={{0,16},{8,24},{16,0},{24,8},{1,17},{9,25},{17,1},{25,9},{2,18},{10... | collective-permute-start | bytes 1769480 | tf_op jit(solution)/shard_map/ppermute | solution.py:494
  31.4 18.2 %collective-permute-start.7 = (bf16[32,5120]{1,0:T(8,128)(2,1)S(1)}, bf16[32,5120]{1,0:T(8,128)(2,1)}, u32[]{:S(2)}, u32[]{:S(2)}) collective-permute-start(bf16[32,5120]{1,0:T(8,128)(2,1)S(1)} %get-tuple-element.174), channel_id=1, source_target_pairs={{0,4},{1,5},{2,6},{3,7},{4,0},{5,1},{6,2},{7,3},{8,12},{9,13},{10,... | collective-permute-start | bytes 983048 | tf_op jit(solution)/shard_map/ppermute | solution.py:494
  54.2 13.1 %collective-permute-start.13 = (bf16[32,12288]{1,0:T(8,128)(2,1)S(1)}, bf16[32,12288]{1,0:T(8,128)(2,1)S(1)}, u32[]{:S(2)}, u32[]{:S(2)}) collective-permute-start(bf16[32,12288]{1,0:T(8,128)(2,1)S(1)} %collective-permute-done.4.refs_2_.refs_24_), channel_id=1, source_target_pairs={{0,1},{1,0},{2,3},{3,2},{4,5},{5,4},{6,7},{7,6},{8,9},{9,8},{10,11... | collective-permute-start | bytes 2359304 | tf_op jit(solution)/shard_map/ppermute | solution.py:494
  54.2 13.1 %collective-permute-start.14 = (bf16[96,3072]{1,0:T(8,128)(2,1)}, bf16[96,3072]{1,0:T(8,128)(2,1)}, u32[]{:S(2)}, u32[]{:S(2)}) collective-permute-start(bf16[96,3072]{1,0:T(8,128)(2,1)} %constant_dynamic-update-slice_fusion.refs_3_), channel_id=1, source_target_pairs={{0,1},{1,0},{2,3},{3,2},{4,5},{5,4},{6,7},{7,6},{8,9},{9,8},{10,11... | collective-permute-start | bytes 1769480 | tf_op jit(solution)/shard_map/ppermute | solution.py:494
  54.7 12.2 %collective-permute-start.10 = (bf16[64,3072]{1,0:T(8,128)(2,1)}, bf16[64,3072]{1,0:T(8,128)(2,1)}, u32[]{:S(2)}, u32[]{:S(2)}) collective-permute-start(bf16[64,3072]{1,0:T(8,128)(2,1)} %pad_maximum_fusion.2), channel_id=1, source_target_pairs={{0,16},{8,24},{16,0},{24,8},{1,17},{9,25},{17,1},{25,9},{2,18},{10... | collective-permute-start | bytes 1179656 | tf_op jit(solution)/shard_map/ppermute | solution.py:494
  56.2 11.1 %collective-permute-start.11 = (bf16[64,3072]{1,0:T(8,128)(2,1)}, bf16[64,3072]{1,0:T(8,128)(2,1)}, u32[]{:S(2)}, u32[]{:S(2)}) collective-permute-start(bf16[64,3072]{1,0:T(8,128)(2,1)} %slice.59), channel_id=1, source_target_pairs={{0,8},{8,0},{16,24},{24,16},{1,9},{9,1},{17,25},{25,17},{2,10},{10... | collective-permute-start | bytes 1179656 | tf_op jit(solution)/shard_map/ppermute | solution.py:494
  57.7 9.2 %collective-permute-start.12 = (bf16[32,5120]{1,0:T(8,128)(2,1)S(1)}, bf16[32,5120]{1,0:T(8,128)(2,1)}, u32[]{:S(2)}, u32[]{:S(2)}) collective-permute-start(bf16[32,5120]{1,0:T(8,128)(2,1)S(1)} %get-tuple-element.174), channel_id=1, source_target_pairs={{0,2},{1,3},{2,0},{3,1},{4,6},{5,7},{6,4},{7,5},{8,10},{9,11},{10,... | collective-permute-start | bytes 983048 | tf_op jit(solution)/shard_map/ppermute | solution.py:494
  72.7 19.6 %collective-permute-start.19 = (bf16[64,5120]{1,0:T(8,128)(2,1)S(1)}, bf16[64,5120]{1,0:T(8,128)(2,1)S(1)}, u32[]{:S(2)}, u32[]{:S(2)}) collective-permute-start(bf16[64,5120]{1,0:T(8,128)(2,1)S(1)} %constant_dynamic-update-slice_fusion.3.refs_3_), channel_id=1, source_target_pairs={{0,8},{8,0},{16,24},{24,16},{1,9},{9,1},{17,25},{25,17},{2,10},{10... | collective-permute-start | bytes 1966088 | tf_op jit(solution)/shard_map/ppermute | solution.py:494
  74.2 18.1 %collective-permute-start.20 = (bf16[64,5120]{1,0:T(8,128)(2,1)S(1)}, bf16[64,5120]{1,0:T(8,128)(2,1)S(1)}, u32[]{:S(2)}, u32[]{:S(2)}) collective-permute-start(bf16[64,5120]{1,0:T(8,128)(2,1)S(1)} %constant_dynamic-update-slice_fusion.3.refs_3_), channel_id=1, source_target_pairs={{0,16},{8,24},{16,0},{24,8},{1,17},{9,25},{17,1},{25,9},{2,18},{10... | collective-permute-start | bytes 1966088 | tf_op jit(solution)/shard_map/ppermute | solution.py:494
  74.7 17.6 %collective-permute-start.22 = (bf16[64,5120]{1,0:T(8,128)(2,1)S(1)}, bf16[64,5120]{1,0:T(8,128)(2,1)}, u32[]{:S(2)}, u32[]{:S(2)}) collective-permute-start(bf16[64,5120]{1,0:T(8,128)(2,1)S(1)} %constant_dynamic-update-slice_fusion.3.refs_3_), channel_id=1, source_target_pairs={{0,1},{1,0},{2,3},{3,2},{4,5},{5,4},{6,7},{7,6},{8,9},{9,8},{10,11... | collective-permute-start | bytes 1966088 | tf_op jit(solution)/shard_map/ppermute | solution.py:494
  76.0 16.2 %collective-permute-start.21 = (bf16[32,5120]{1,0:T(8,128)(2,1)S(1)}, bf16[32,5120]{1,0:T(8,128)(2,1)S(1)}, u32[]{:S(2)}, u32[]{:S(2)}) collective-permute-start(bf16[32,5120]{1,0:T(8,128)(2,1)S(1)} %get-tuple-element.174), channel_id=1, source_target_pairs={{0,6},{1,7},{2,4},{3,5},{4,2},{5,3},{6,0},{7,1},{8,14},{9,15},{10,... | collective-permute-start | bytes 983048 | tf_op jit(solution)/shard_map/ppermute | solution.py:494
  92.3 16.8 %collective-permute-start.23 = (bf16[32,5120]{1,0:T(8,128)(2,1)S(1)}, bf16[32,5120]{1,0:T(8,128)(2,1)S(1)}, u32[]{:S(2)}, u32[]{:S(2)}) collective-permute-start(bf16[32,5120]{1,0:T(8,128)(2,1)S(1)} %collective-permute-done.21.refs_6_), channel_id=1, source_target_pairs={{0,8},{8,0},{16,24},{24,16},{1,9},{9,1},{17,25},{25,17},{2,10},{10... | collective-permute-start | bytes 983048 | tf_op jit(solution)/shard_map/ppermute | solution.py:494
  92.9 16.2 %collective-permute-start.24 = (bf16[32,5120]{1,0:T(8,128)(2,1)S(1)}, bf16[32,5120]{1,0:T(8,128)(2,1)S(1)}, u32[]{:S(2)}, u32[]{:S(2)}) collective-permute-start(bf16[32,5120]{1,0:T(8,128)(2,1)S(1)} %collective-permute-done.21.refs_6_), channel_id=1, source_target_pairs={{0,16},{8,24},{16,0},{24,8},{1,17},{9,25},{17,1},{25,9},{2,18},{10... | collective-permute-start | bytes 983048 | tf_op jit(solution)/shard_map/ppermute | solution.py:494
  93.6 14.6 %collective-permute-start.25 = (bf16[32,4096]{1,0:T(8,128)(2,1)}, bf16[32,4096]{1,0:T(8,128)(2,1)}, u32[]{:S(2)}, u32[]{:S(2)}) collective-permute-start(bf16[32,4096]{1,0:T(8,128)(2,1)} %slice.60), channel_id=1, source_target_pairs={{0,16},{8,24},{16,0},{24,8},{1,17},{9,25},{17,1},{25,9},{2,18},{10... | collective-permute-start | bytes 786440 | tf_op jit(solution)/shard_map/ppermute | solution.py:494
  95.0 13.2 %collective-permute-start.26 = (bf16[128,1024]{1,0:T(8,128)(2,1)S(1)}, bf16[128,1024]{1,0:T(8,128)(2,1)}, u32[]{:S(2)}, u32[]{:S(2)}) collective-permute-start(bf16[128,1024]{1,0:T(8,128)(2,1)S(1)} %copy-done.3), channel_id=1, source_target_pairs={{0,2},{1,3},{2,0},{3,1},{4,6},{5,7},{6,4},{7,5},{8,10},{9,11},{10,... | collective-permute-start | bytes 786440 | tf_op jit(solution)/shard_map/ppermute | solution.py:494
  95.8 13.4 %collective-permute-start.27 = (bf16[128,1024]{1,0:T(8,128)(2,1)S(1)}, bf16[128,1024]{1,0:T(8,128)(2,1)S(1)}, u32[]{:S(2)}, u32[]{:S(2)}) collective-permute-start(bf16[128,1024]{1,0:T(8,128)(2,1)S(1)} %copy-done.3), channel_id=1, source_target_pairs={{0,4},{1,5},{2,6},{3,7},{4,0},{5,1},{6,2},{7,3},{8,12},{9,13},{10,... | collective-permute-start | bytes 786440 | tf_op jit(solution)/shard_map/ppermute | solution.py:494
  110.9 15.4 %collective-permute-start.28 = (bf16[64,5120]{1,0:T(8,128)(2,1)}, bf16[64,5120]{1,0:T(8,128)(2,1)S(1)}, u32[]{:S(2)}, u32[]{:S(2)}) collective-permute-start(bf16[64,5120]{1,0:T(8,128)(2,1)} %get-tuple-element.198), channel_id=1, source_target_pairs={{0,16},{8,24},{16,0},{24,8},{1,17},{9,25},{17,1},{25,9},{2,18},{10... | collective-permute-start | bytes 1966088 | tf_op jit(solution)/shard_map/ppermute | solution.py:494
  112.5 13.9 %collective-permute-start.29 = (bf16[64,5120]{1,0:T(8,128)(2,1)S(1)}, bf16[64,5120]{1,0:T(8,128)(2,1)}, u32[]{:S(2)}, u32[]{:S(2)}) collective-permute-start(bf16[64,5120]{1,0:T(8,128)(2,1)S(1)} %get-tuple-element.199), channel_id=1, source_target_pairs={{0,8},{8,0},{16,24},{24,16},{1,9},{9,1},{17,25},{25,17},{2,10},{10... | collective-permute-start | bytes 1966088 | tf_op jit(solution)/shard_map/ppermute | solution.py:494
  113.3 13.1 %collective-permute-start.31 = (bf16[64,5120]{1,0:T(8,128)(2,1)S(1)}, bf16[64,5120]{1,0:T(8,128)(2,1)}, u32[]{:S(2)}, u32[]{:S(2)}) collective-permute-start(bf16[64,5120]{1,0:T(8,128)(2,1)S(1)} %collective-permute-done.19.refs_4_), channel_id=1, source_target_pairs={{0,1},{1,0},{2,3},{3,2},{4,5},{5,4},{6,7},{7,6},{8,9},{9,8},{10,11... | collective-permute-start | bytes 1966088 | tf_op jit(solution)/shard_map/ppermute | solution.py:494
  113.3 13.1 %collective-permute-start.32 = (bf16[64,5120]{1,0:T(8,128)(2,1)S(1)}, bf16[64,5120]{1,0:T(8,128)(2,1)}, u32[]{:S(2)}, u32[]{:S(2)}) collective-permute-start(bf16[64,5120]{1,0:T(8,128)(2,1)S(1)} %collective-permute-done.20.refs_5_), channel_id=1, source_target_pairs={{0,1},{1,0},{2,3},{3,2},{4,5},{5,4},{6,7},{7,6},{8,9},{9,8},{10,11... | collective-permute-start | bytes 1966088 | tf_op jit(solution)/shard_map/ppermute | solution.py:494
  113.8 12.6 %collective-permute-start.30 = (bf16[128,1024]{1,0:T(8,128)(2,1)S(1)}, bf16[128,1024]{1,0:T(8,128)(2,1)}, u32[]{:S(2)}, u32[]{:S(2)}) collective-permute-start(bf16[128,1024]{1,0:T(8,128)(2,1)S(1)} %copy-done.3), channel_id=1, source_target_pairs={{0,6},{1,7},{2,4},{3,5},{4,2},{5,3},{6,0},{7,1},{8,14},{9,15},{10,... | collective-permute-start | bytes 786440 | tf_op jit(solution)/shard_map/ppermute | solution.py:494
  126.4 6.2 %collective-permute-start.36 = (bf16[64,5120]{1,0:T(8,128)(2,1)S(1)}, bf16[64,5120]{1,0:T(8,128)(2,1)S(1)}, u32[]{:S(2)}, u32[]{:S(2)}) collective-permute-start(bf16[64,5120]{1,0:T(8,128)(2,1)S(1)} %collective-permute-done.28.refs_9_), channel_id=1, source_target_pairs={{0,1},{1,0},{2,3},{3,2},{4,5},{5,4},{6,7},{7,6},{8,9},{9,8},{10,11... | collective-permute-start | bytes 1966088 | tf_op jit(solution)/shard_map/ppermute | solution.py:494
  126.5 6.2 %collective-permute-start.37 = (bf16[64,5120]{1,0:T(8,128)(2,1)}, bf16[64,5120]{1,0:T(8,128)(2,1)S(1)}, u32[]{:S(2)}, u32[]{:S(2)}) collective-permute-start(bf16[64,5120]{1,0:T(8,128)(2,1)} %collective-permute-done.29.refs_10_), channel_id=1, source_target_pairs={{0,1},{1,0},{2,3},{3,2},{4,5},{5,4},{6,7},{7,6},{8,9},{9,8},{10,11... | collective-permute-start | bytes 1966088 | tf_op jit(solution)/shard_map/ppermute | solution.py:494
  127.0 5.6 %collective-permute-start.33 = (bf16[32,5120]{1,0:T(8,128)(2,1)S(1)}, bf16[32,5120]{1,0:T(8,128)(2,1)S(1)}, u32[]{:S(2)}, u32[]{:S(2)}) collective-permute-start(bf16[32,5120]{1,0:T(8,128)(2,1)S(1)} %copy-done.19), channel_id=1, source_target_pairs={{0,1},{1,0},{2,3},{3,2},{4,5},{5,4},{6,7},{7,6},{8,9},{9,8},{10,11... | collective-permute-start | bytes 983048 | tf_op jit(solution)/shard_map/ppermute | solution.py:494
  127.1 5.5 %collective-permute-start.34 = (bf16[32,5120]{1,0:T(8,128)(2,1)}, bf16[32,5120]{1,0:T(8,128)(2,1)S(1)}, u32[]{:S(2)}, u32[]{:S(2)}) collective-permute-start(bf16[32,5120]{1,0:T(8,128)(2,1)} %copy-done.20), channel_id=1, source_target_pairs={{0,1},{1,0},{2,3},{3,2},{4,5},{5,4},{6,7},{7,6},{8,9},{9,8},{10,11... | collective-permute-start | bytes 983048 | tf_op jit(solution)/shard_map/ppermute | solution.py:494
  127.5 5.1 %collective-permute-start.35 = (bf16[32,5120]{1,0:T(8,128)(2,1)S(1)}, bf16[32,5120]{1,0:T(8,128)(2,1)S(1)}, u32[]{:S(2)}, u32[]{:S(2)}) collective-permute-start(bf16[32,5120]{1,0:T(8,128)(2,1)S(1)} %collective-permute-done.24.refs_8_), channel_id=1, source_target_pairs={{0,1},{1,0},{2,3},{3,2},{4,5},{5,4},{6,7},{7,6},{8,9},{9,8},{10,11... | collective-permute-start | bytes 983048 | tf_op jit(solution)/shard_map/ppermute | solution.py:494
  132.7 25.7 %collective-permute-start.38 = (bf16[384,1024]{1,0:T(8,128)(2,1)}, bf16[384,1024]{1,0:T(8,128)(2,1)}, u32[]{:S(2)}, u32[]{:S(2)}) collective-permute-start(bf16[384,1024]{1,0:T(8,128)(2,1)} %constant_dynamic-update-slice_fusion.5.refs_25_), channel_id=1, source_target_pairs={{0,8},{8,0},{16,24},{24,16},{1,9},{9,1},{17,25},{25,17},{2,10},{10... | collective-permute-start | bytes 2359304 | tf_op jit(solution)/shard_map/ppermute | solution.py:494
  134.1 24.3 %collective-permute-start.39 = (bf16[384,1024]{1,0:T(8,128)(2,1)}, bf16[384,1024]{1,0:T(8,128)(2,1)}, u32[]{:S(2)}, u32[]{:S(2)}) collective-permute-start(bf16[384,1024]{1,0:T(8,128)(2,1)} %constant_dynamic-update-slice_fusion.5.refs_25_), channel_id=1, source_target_pairs={{0,16},{8,24},{16,0},{24,8},{1,17},{9,25},{17,1},{25,9},{2,18},{10... | collective-permute-start | bytes 2359304 | tf_op jit(solution)/shard_map/ppermute | solution.py:494
  136.1 22.3 %collective-permute-start.40 = (bf16[32,4096]{1,0:T(8,128)(2,1)}, bf16[32,4096]{1,0:T(8,128)(2,1)S(1)}, u32[]{:S(2)}, u32[]{:S(2)}) collective-permute-start(bf16[32,4096]{1,0:T(8,128)(2,1)} %collective-permute-done.25.refs_28_), channel_id=1, source_target_pairs={{0,2},{1,3},{2,0},{3,1},{4,6},{5,7},{6,4},{7,5},{8,10},{9,11},{10,... | collective-permute-start | bytes 786440 | tf_op jit(solution)/shard_map/ppermute | solution.py:494
  136.8 21.6 %collective-permute-start.41 = (bf16[32,4096]{1,0:T(8,128)(2,1)}, bf16[32,4096]{1,0:T(8,128)(2,1)S(1)}, u32[]{:S(2)}, u32[]{:S(2)}) collective-permute-start(bf16[32,4096]{1,0:T(8,128)(2,1)} %collective-permute-done.25.refs_28_), channel_id=1, source_target_pairs={{0,4},{1,5},{2,6},{3,7},{4,0},{5,1},{6,2},{7,3},{8,12},{9,13},{10,... | collective-permute-start | bytes 786440 | tf_op jit(solution)/shard_map/ppermute | solution.py:494
  138.4 20.0 %collective-permute-start.42 = (bf16[32,4096]{1,0:T(8,128)(2,1)}, bf16[32,4096]{1,0:T(8,128)(2,1)S(1)}, u32[]{:S(2)}, u32[]{:S(2)}) collective-permute-start(bf16[32,4096]{1,0:T(8,128)(2,1)} %collective-permute-done.25.refs_28_), channel_id=1, source_target_pairs={{0,6},{1,7},{2,4},{3,5},{4,2},{5,3},{6,0},{7,1},{8,14},{9,15},{10,... | collective-permute-start | bytes 786440 | tf_op jit(solution)/shard_map/ppermute | solution.py:494
  158.4 23.9 %collective-permute-start.43 = (bf16[384,1024]{1,0:T(8,128)(2,1)}, bf16[384,1024]{1,0:T(8,128)(2,1)S(1)}, u32[]{:S(2)}, u32[]{:S(2)}) collective-permute-start(bf16[384,1024]{1,0:T(8,128)(2,1)} %constant_dynamic-update-slice_fusion.5.refs_25_), channel_id=1, source_target_pairs={{0,1},{1,0},{2,3},{3,2},{4,5},{5,4},{6,7},{7,6},{8,9},{9,8},{10,11... | collective-permute-start | bytes 2359304 | tf_op jit(solution)/shard_map/ppermute | solution.py:494
  158.5 23.8 %collective-permute-start.44 = (bf16[384,1024]{1,0:T(8,128)(2,1)}, bf16[384,1024]{1,0:T(8,128)(2,1)S(1)}, u32[]{:S(2)}, u32[]{:S(2)}) collective-permute-start(bf16[384,1024]{1,0:T(8,128)(2,1)} %collective-permute-done.38.refs_26_), channel_id=1, source_target_pairs={{0,1},{1,0},{2,3},{3,2},{4,5},{5,4},{6,7},{7,6},{8,9},{9,8},{10,11... | collective-permute-start | bytes 2359304 | tf_op jit(solution)/shard_map/ppermute | solution.py:494
  159.0 23.4 %collective-permute-start.45 = (bf16[384,1024]{1,0:T(8,128)(2,1)}, bf16[384,1024]{1,0:T(8,128)(2,1)S(1)}, u32[]{:S(2)}, u32[]{:S(2)}) collective-permute-start(bf16[384,1024]{1,0:T(8,128)(2,1)} %collective-permute-done.39.refs_27_), channel_id=1, source_target_pairs={{0,1},{1,0},{2,3},{3,2},{4,5},{5,4},{6,7},{7,6},{8,9},{9,8},{10,11... | collective-permute-start | bytes 2359304 | tf_op jit(solution)/shard_map/ppermute | solution.py:494
  159.1 4.9 %collective-permute-start.46 = (bf16[32,4096]{1,0:T(8,128)(2,1)}, bf16[32,4096]{1,0:T(8,128)(2,1)S(1)}, u32[]{:S(2)}, u32[]{:S(2)}) collective-permute-start(bf16[32,4096]{1,0:T(8,128)(2,1)} %collective-permute-done.25.refs_28_), channel_id=1, source_target_pairs={{0,1},{1,0},{2,3},{3,2},{4,5},{5,4},{6,7},{7,6},{8,9},{9,8},{10,11... | collective-permute-start | bytes 786440 | tf_op jit(solution)/shard_map/ppermute | solution.py:494
  164.0 18.3 %collective-permute-start.48 = (bf16[32,4096]{1,0:T(8,128)(2,1)}, bf16[32,4096]{1,0:T(8,128)(2,1)S(1)}, u32[]{:S(2)}, u32[]{:S(2)}) collective-permute-start(bf16[32,4096]{1,0:T(8,128)(2,1)} %copy-done.45), channel_id=1, source_target_pairs={{0,1},{1,0},{2,3},{3,2},{4,5},{5,4},{6,7},{7,6},{8,9},{9,8},{10,11... | collective-permute-start | bytes 786440 | tf_op jit(solution)/shard_map/ppermute | solution.py:494
  164.2 18.2 %collective-permute-start.49 = (bf16[32,4096]{1,0:T(8,128)(2,1)}, bf16[32,4096]{1,0:T(8,128)(2,1)S(1)}, u32[]{:S(2)}, u32[]{:S(2)}) collective-permute-start(bf16[32,4096]{1,0:T(8,128)(2,1)} %copy-done.46), channel_id=1, source_target_pairs={{0,1},{1,0},{2,3},{3,2},{4,5},{5,4},{6,7},{7,6},{8,9},{9,8},{10,11... | collective-permute-start | bytes 786440 | tf_op jit(solution)/shard_map/ppermute | solution.py:494
  273.1 8.5 %collective-permute-start.59 = (f32[320]{0:T(512)S(1)}, f32[320]{0:T(512)S(1)}, u32[]{:S(2)}, u32[]{:S(2)}) collective-permute-start(f32[320]{0:T(512)S(1)} %get-tuple-element.259), channel_id=1, source_target_pairs={{0,7},{1,6},{2,5},{3,4},{4,3},{5,2},{6,1},{7,0},{8,15},{9,14},{10,... | collective-permute-start | bytes 3848 | tf_op jit(solution)/shard_map/ppermute | solution.py:494
  273.6 8.8 %collective-permute-start.58 = (f32[320]{0:T(512)S(1)}, f32[320]{0:T(512)S(1)}, u32[]{:S(2)}, u32[]{:S(2)}) collective-permute-start(f32[320]{0:T(512)S(1)} %get-tuple-element.260), channel_id=1, source_target_pairs={{0,6},{1,7},{2,4},{3,5},{4,2},{5,3},{6,0},{7,1},{8,14},{9,15},{10,... | collective-permute-start | bytes 3848 | tf_op jit(solution)/shard_map/ppermute | solution.py:494
  275.4 7.2 %collective-permute-start.57 = (f32[320]{0:T(512)S(1)}, f32[320]{0:T(512)S(1)}, u32[]{:S(2)}, u32[]{:S(2)}) collective-permute-start(f32[320]{0:T(512)S(1)} %get-tuple-element.261), channel_id=1, source_target_pairs={{0,5},{1,4},{2,7},{3,6},{4,1},{5,0},{6,3},{7,2},{8,13},{9,12},{10,... | collective-permute-start | bytes 3848 | tf_op jit(solution)/shard_map/ppermute | solution.py:494
  (63 other events, 853.4 us)

commit v3 on v2

--- a/solution.py
+++ b/solution.py
@@ -34,12 +34,12 @@
     return pl.CostEstimate(flops=flops, bytes_accessed=0, transcendentals=0)
 
 
-def issue(sources, buf, sem, place, height):
+def issue(sources, buf, sem, place, height, window=0):
     plane_at, z_at, core_at = place
     cols = buf.shape[1]
     for source, tag in sources:
         if tag is None:
-            pltpu.make_async_copy(source, buf, sem).start()
+            pltpu.make_async_copy(source.at[:, pl.ds(window, cols)], buf, sem).start()
             continue
         chip, zs, first, turned = tag
         tall = source.shape[0] // len(zs)
@@ -47,7 +47,7 @@
             row = ((plane_at ^ chip) * 8 + (z_at ^ z) * 2 + (core_at ^ turned)) * height
             for block in range(height // tall):
                 pltpu.make_async_copy(
-                    source.at[pl.ds(step * tall, tall), pl.ds(first + block * cols, cols)],
+                    source.at[pl.ds(step * tall, tall), pl.ds(first + window + block * cols, cols)],
                     buf.at[pl.ds(pl.multiple_of(row + block * tall, tall), tall)],
                     sem,
                 ).start()
@@ -100,24 +100,44 @@
     )(w_qkv, w_out, w_in, w_down)
 
 
+def glue_body(plans, count, *refs):
+    sources, targets = refs[:count], refs[count:]
+    for plan, target in zip(plans, targets):
+        at = 0
+        for number, top, rows, left in plan:
+            target[at : at + rows, :] = sources[number][top : top + rows, left : left + target.shape[1]]
+            at += rows
+
+
+def glue(arrays, *plans):
+    return pl.pallas_call(
+        functools.partial(glue_body, [plan[1:] for plan in plans], len(arrays)),
+        out_shape=[shape_of((sum(w[2] for w in plan[1:]), plan[0]), BF) for plan in plans],
+        compiler_params=params(20),
+        name="glue",
+    )(*arrays)
+
+
 def project_body(seqs, tags, len_ref, x_ref, bias_ref, scale_ref, *refs):
-    sources, (out_ref, buf, sem) = tagged(refs, tags), refs[len(tags) :]
-
-    @pl.when(pl.program_id(0) == 0)
+    sources, (out_ref, buf, sems) = tagged(refs, tags), refs[len(tags) :]
+    here = pl.program_id(0)
+    step = out_ref.shape[1]
+
+    @pl.when(here == 0)
     def _():
-        issue(sources, buf, sem, place_of(len_ref, seqs), buf.shape[0] // 32)
-        settle(buf, sem)
-
-    step = out_ref.shape[1]
-    cols = pl.ds(pl.multiple_of(pl.program_id(0) * step, step), step)
-    total = dot(x_ref[...], buf[:, cols], 1, 0) + bias_ref[...]
+        place = place_of(len_ref, seqs)
+        for part in range(buf.shape[0]):
+            issue(sources, buf.at[part], sems.at[part], place, buf.shape[1] // 32, part * step)
+
+    settle(buf.at[here], sems.at[here])
+    total = dot(x_ref[...], buf[here], 1, 0) + bias_ref[...]
     out_ref[...] = (total * scale_ref[...]).astype(BF)
 
 
 def project(scalars, seqs, rows, sources, bias, scale):
     count, width = rows.shape
     wide = bias.shape[1]
-    step = 1024
+    step = PROJECT
     return pl.pallas_call(
         functools.partial(project_body, seqs, tags_of(sources)),
         out_shape=shape_of((count, wide), BF),
@@ -131,12 +151,18 @@
                 *([ANYWHERE] * len(sources)),
             ],
             out_specs=pl.BlockSpec((count, step), lambda j, n: (0, j)),
-            scratch_shapes=[pltpu.VMEM((width, wide), BF), pltpu.SemaphoreType.DMA],
+            scratch_shapes=[
+                pltpu.VMEM((wide // step, width, step), BF),
+                pltpu.SemaphoreType.DMA((wide // step,)),
+            ],
         ),
         compiler_params=params(),
         cost_estimate=cost(2 * count * width * wide),
         name="project",
     )(scalars, rows, bias, scale, *arrays_of(sources))
+
+
+PROJECT = 512
 
 
 def lane_halves(kind):
@@ -215,42 +241,48 @@
 
 
 ROWS = 256
-
-
-def feed_body(seqs, tags, len_ref, x_ref, o_ref, vec_ref, bi_ref, *refs):
-    sources, (u_ref, s_ref, gl_ref, gp_ref, buf, sem) = tagged(refs, tags), refs[-6:]
+FEED = 512
+
+
+def hidden(rounded, buf, bi_ref, gl_ref, gp_ref):
+    for part in range(gl_ref.shape[1] // FEED):
+        cols = slice(part * FEED, (part + 1) * FEED)
+        pre = dot(rounded, buf[:, cols], 1, 0) + bi_ref[:, cols]
+        phi = 0.5 + 0.5 * lax.erf(pre * math.sqrt(0.5))
+        power = (-0.5 / math.log(2.0)) * pre * pre - 0.5 * math.log2(2.0 * math.pi)
+        gl_ref[:, cols] = (pre * phi).astype(BF)
+        gp_ref[:, cols] = (phi + pre * jnp.exp2(power)).astype(BF)
+
+
+def join_body(seqs, tags, len_ref, x_ref, o_ref, vec_ref, bi_ref, *refs):
+    sources = tagged(refs, tags)
+    u_ref, s_ref, gl_ref, gp_ref, out, buf, sems = refs[-7:]
+    width = x_ref.shape[1]
 
     @pl.when(pl.program_id(0) == 0)
     def _():
-        issue(sources, buf, sem, place_of(len_ref, seqs), buf.shape[0] // 32)
-        settle(buf, sem)
-
-    width = x_ref.shape[1]
-    joined = dot(o_ref[...], buf[:, :width], 1, 0) + vec_ref[0:1, :] + x_ref[...].astype(F32)
+        place = place_of(len_ref, seqs)
+        issue(sources, out, sems.at[0], place, width // 32)
+        issue(sources, buf, sems.at[1], place, width // 32, width)
+        settle(out, sems.at[0])
+
+    joined = dot(o_ref[...], out[...], 1, 0) + vec_ref[0:1, :] + x_ref[...].astype(F32)
     centered = joined - jnp.mean(joined, axis=1, keepdims=True)
     spread = lax.rsqrt(jnp.mean(centered * centered, axis=1, keepdims=True) + LN_EPS)
     normed = centered * spread * vec_ref[1:2, :] + vec_ref[2:3, :]
     u_ref[...] = normed
     s_ref[...] = jnp.broadcast_to(spread, s_ref.shape)
     rounded = normed.astype(BF)
-    step = 512
-    for part in range(gl_ref.shape[1] // step):
-        cols = slice(part * step, (part + 1) * step)
-        pre = dot(rounded, buf[:, width + part * step : width + (part + 1) * step], 1, 0)
-        pre = pre + bi_ref[:, cols]
-        phi = 0.5 + 0.5 * lax.erf(pre * math.sqrt(0.5))
-        slope = phi + pre * jnp.exp(-0.5 * pre * pre) * (1.0 / math.sqrt(2.0 * math.pi))
-        gl_ref[:, cols] = (pre * phi).astype(BF)
-        gp_ref[:, cols] = slope.astype(BF)
-
-
-def feed(scalars, seqs, rows, context, sources, vectors, bias_in, seq, earlier):
+    pl.when(pl.program_id(0) == 0)(functools.partial(settle, buf, sems.at[1]))
+    hidden(rounded, buf, bi_ref, gl_ref, gp_ref)
+
+
+def join(scalars, seqs, rows, context, sources, vectors, bias_in):
     count, width = rows.shape
     wide = bias_in.shape[1]
-    steps = L // ROWS
-    block = lambda cols: pl.BlockSpec((ROWS, cols), lambda i, n: (seq * steps + i, 0))
+    block = lambda cols: pl.BlockSpec((ROWS, cols), lambda i, n: (i, 0))
     return pl.pallas_call(
-        functools.partial(feed_body, seqs, tags_of(sources)),
+        functools.partial(join_body, seqs, tags_of(sources)),
         out_shape=(
             shape_of((count, width), F32),
             shape_of((count, 128), F32),
@@ -259,57 +291,69 @@
         ),
         grid_spec=pltpu.PrefetchScalarGridSpec(
             num_scalar_prefetch=1,
-            grid=(steps,),
+            grid=(count // ROWS,),
             in_specs=[
                 block(width),
                 block(width),
                 pl.BlockSpec((8, width), lambda i, n: (0, 0)),
                 pl.BlockSpec((1, wide), lambda i, n: (0, 0)),
-                *([ANYWHERE] * (len(sources) + len(earlier))),
+                *([ANYWHERE] * len(sources)),
             ],
             out_specs=[block(width), block(128), block(wide), block(wide)],
-            scratch_shapes=[pltpu.VMEM((width, width + wide), BF), pltpu.SemaphoreType.DMA],
+            scratch_shapes=[
+                pltpu.VMEM((width, width), BF),
+                pltpu.VMEM((width, wide), BF),
+                pltpu.SemaphoreType.DMA((2,)),
+            ],
         ),
         compiler_params=params(),
-        input_output_aliases={5 + len(sources) + n: n for n in range(len(earlier))},
-        cost_estimate=cost(2 * L * width * (width + wide)),
-        name="feed",
-    )(scalars, rows, context, vectors, bias_in, *arrays_of(sources), *earlier)
+        cost_estimate=cost(2 * count * width * (width + wide)),
+        name="join",
+    )(scalars, rows, context, vectors, bias_in, *arrays_of(sources))
 
 
 def turn_body(
-    seqs, feed_tags, down_tags, len_ref, gl_ref, gp_ref, u_ref, s_ref, r_ref, c_ref, vec_ref, *refs
+    seqs, feed_tags, down_tags, len_ref, gl_ref, u_ref, s_ref, c_ref, vec_ref, gp_any, r_any, *refs
 ):
     feeds, downs = tagged(refs, feed_tags), tagged(refs[len(feed_tags) :], down_tags)
-    y_ref, dh_ref, do_ref, gv_ref, gi_ref, buf, down, sems = refs[-8:]
+    y_ref, dh_ref, do_ref, gv_ref, gi_ref, out, buf, down, gp_ref, r_ref, sems, gp_sems = refs[-12:]
     index = pl.program_id(0)
+    first = index == 0
     width = u_ref.shape[1]
     wide = gl_ref.shape[1]
     parts = 4
     step = wide // parts
-
-    @pl.when(index == 0)
+    steps = gp_ref.shape[0]
+    slopes = [
+        pltpu.make_async_copy(gp_any.at[pl.ds(n * ROWS, ROWS)], gp_ref.at[n], gp_sems.at[n])
+        for n in range(steps)
+    ]
+    inverse = pltpu.make_async_copy(r_any, r_ref, sems.at[3])
+
+    @pl.when(first)
     def _():
         place = place_of(len_ref, seqs)
         issue(downs, down, sems.at[0], place, wide // 32)
-        issue(feeds, buf, sems.at[1], place, width // 32)
+        slopes[0].start()
+        issue(feeds, buf, sems.at[1], place, width // 32, width)
+        issue(feeds, out, sems.at[2], place, width // 32)
+        for copy in slopes[1:]:
+            copy.start()
+        inverse.start()
         gv_ref[...] = jnp.zeros_like(gv_ref)
         gi_ref[...] = jnp.zeros_like(gi_ref)
         settle(down, sems.at[0])
 
     gain_one, beta_one, gain_two, beta_two, bias_down = (vec_ref[n : n + 1, :] for n in range(1, 6))
     normed = u_ref[...]
-    total = normed + bias_down
-    for part in range(parts):
-        rows = slice(part * step, (part + 1) * step)
-        total = total + dot(gl_ref[:, rows], down[rows, :], 1, 0)
+    total = normed + bias_down + dot(gl_ref[...], down[...], 1, 0)
     centered = total - jnp.mean(total, axis=1, keepdims=True)
     spread = lax.rsqrt(jnp.mean(centered * centered, axis=1, keepdims=True) + LN_EPS)
     hat = centered * spread
     y_ref[...] = (hat * gain_two + beta_two).astype(BF)
     per_seq = L // ROWS
-    first = lax.rem(index, per_seq) * ROWS
-    live = lax.broadcasted_iota(jnp.int32, (ROWS, 1), 0) + first < len_ref[index // per_seq]
+    start = lax.rem(index, per_seq) * ROWS
+    live = lax.broadcasted_iota(jnp.int32, (ROWS, 1), 0) + start < len_ref[index // per_seq]
     dy = jnp.where(live, c_ref[...].astype(F32), 0.0)
     gv_ref[4:5, :] += jnp.sum(dy, axis=0, keepdims=True)
     scaled = dy * gain_two
@@ -320,15 +364,16 @@
     )
     d_branch = d_two.astype(BF)
     gv_ref[3:4, :] += jnp.sum(d_branch.astype(F32), axis=0, keepdims=True)
-    pl.when(index == 0)(functools.partial(settle, buf, sems.at[1]))
+    pl.when(first)(functools.partial(settle, buf, sems.at[1]))
+    for n in range(steps):
+        pl.when(index == n)(slopes[n].wait)
     total = d_two
-    half = step // 2
-    for part in range(2 * parts):
-        rows = slice(part * half, (part + 1) * half)
-        d_hidden = dot(d_branch, down[rows, :], 1, 1) * gp_ref[:, rows].astype(F32)
+    for part in range(parts):
+        rows = slice(part * step, (part + 1) * step)
+        d_hidden = dot(d_branch, down[rows, :], 1, 1) * gp_ref[index, :, rows].astype(F32)
         d_hidden = d_hidden.astype(BF)
         gi_ref[:, rows] += jnp.sum(d_hidden.astype(F32), axis=0, keepdims=True)
-        total = total + dot(d_hidden, buf[:, width + part * half : width + (part + 1) * half], 1, 1)
+        total = total + dot(d_hidden, buf[:, rows], 1, 1)
     gv_ref[2:3, :] += jnp.sum(total, axis=0, keepdims=True)
     scaled = total * gain_one
     hat = (normed - beta_one) * (1.0 / gain_one)
@@ -340,14 +385,22 @@
     dh_ref[...] = d_one
     d_att = d_one.astype(BF)
     gv_ref[1:2, :] += jnp.sum(d_att.astype(F32), axis=0, keepdims=True)
-    d_context = dot(d_att, buf[:, :width], 1, 1).astype(BF).astype(F32)
+
+    @pl.when(first)
+    def _():
+        settle(out, sems.at[2])
+        inverse.wait()
+
+    d_context = dot(d_att, out[...], 1, 1).astype(BF).astype(F32)
     gv_ref[0:1, :] += jnp.sum(d_context, axis=0, keepdims=True)
-    do_ref[...] = (d_context * r_ref[...]).astype(BF)
+    rows = pl.ds(pl.multiple_of(index * ROWS, ROWS), ROWS)
+    do_ref[...] = (d_context * r_ref[rows, :]).astype(BF)
 
 
 def turn(scalars, seqs, gl, gp, normed, spread, inverse, cotangent, feeds, downs, vectors):
     count, width = normed.shape
     wide = gl.shape[1]
+    steps = count // ROWS
     block = lambda cols: pl.BlockSpec((ROWS, cols), lambda i, n: (i, 0))
     return pl.pallas_call(
         functools.partial(turn_body, seqs, tags_of(feeds), tags_of(downs)),
@@ -360,16 +413,14 @@
         ),
         grid_spec=pltpu.PrefetchScalarGridSpec(
             num_scalar_prefetch=1,
-            grid=(count // ROWS,),
+            grid=(steps,),
             in_specs=[
-                block(wide),
                 block(wide),
                 block(width),
                 block(128),
                 block(width),
-                block(width),
                 pl.BlockSpec((8, width), lambda i, n: (0, 0)),
-                *([ANYWHERE] * (len(feeds) + len(downs))),
+                *([ANYWHERE] * (2 + len(feeds) + len(downs))),
             ],
             out_specs=[
                 block(width),
@@ -379,15 +430,21 @@
                 pl.BlockSpec((1, wide), lambda i, n: (0, 0)),
             ],
             scratch_shapes=[
-                pltpu.VMEM((width, width + wide), BF),
+                pltpu.VMEM((width, width), BF),
+                pltpu.VMEM((width, wide), BF),
                 pltpu.VMEM((wide, width), BF),
-                pltpu.SemaphoreType.DMA((2,)),
+                pltpu.VMEM((steps, ROWS, wide), BF),
+                pltpu.VMEM((count, width), F32),
+                pltpu.SemaphoreType.DMA((4,)),
+                pltpu.SemaphoreType.DMA((steps,)),
             ],
         ),
         compiler_params=params(),
         cost_estimate=cost(2 * count * width * (width + 3 * wide)),
         name="turn",
-    )(scalars, gl, gp, normed, spread, inverse, cotangent, vectors, *arrays_of(feeds), *arrays_of(downs))
+    )(
+        scalars, gl, normed, spread, cotangent, vectors, gp, inverse, *arrays_of(feeds), *arrays_of(downs)
+    )
 
 
 def back_body(
@@ -535,25 +592,8 @@
     ]
 
 
-def stack(*blocks):
-    return jnp.concatenate(blocks, axis=0)
-
-
 def whole(array):
     return [(array, None)]
-
-
-def reduce_shares(block, slots):
-    dp, fsdp = lax.axis_size("dp"), lax.axis_size("fsdp")
-    block = block.reshape(dp, fsdp, slots)
-    for axis, dim in (("dp", 0), ("fsdp", 0)):
-        size = lax.axis_size(axis)
-        at = lax.axis_index(axis)
-        pick = lambda k: lax.dynamic_index_in_dim(block, at ^ k, 0, keepdims=False)
-        block = functools.reduce(
-            lambda left, right: left + right, [pick(0)] + [hop(pick(k), axis, k) for k in range(1, size)]
-        )
-    return block
 
 
 def on_device(
@@ -578,13 +618,20 @@
         at_feed = w_qkv.shape[1]
         at_down = at_feed + w_feed.shape[1]
         z_one, z_two, z_three, near_x, near_y = stage("123xy", (w_qkv, w_qkv, w_qkv, own, own))
-        far = stack(z_one, z_two, z_three)
+        tall, cols_feed = w_qkv.shape[0], w_feed.shape[1]
+        (far,) = glue(
+            (z_one, z_two, z_three), (at_feed, *((n, 0, tall, 0) for n in range(3)))
+        )
         x_far, y_far, feed_two, own_core, near_x_core = stage(
             "xy2cc", (far, far, w_feed, own, near_x)
         )
-        left = stack(near_x[:, :at_feed], x_far[:32])
+        left, right = glue(
+            (near_x, x_far, y_far),
+            (at_feed, (0, 0, tall, 0), (1, 0, tall, 0)),
+            (at_feed, (2, tall, 2 * tall, 0)),
+        )
         crossed, crossed_more, feed_one, near_y_core, far_core = stage(
-            "yx1cc", (left, y_far[32:], w_feed, near_y, far), feed_two, own_core, near_x_core
+            "yx1cc", (left, right, w_feed, near_y, far), feed_two, own_core, near_x_core
         )
         x_far_core, y_far_core, crossed_core, crossed_more_core = stage(
             "cccc", (x_far, y_far, crossed, crossed_more), feed_one, near_y_core, far_core
@@ -603,7 +650,11 @@
             ],
             [*near_core, far_core, x_far_core, y_far_core, crossed_core, crossed_more_core],
         )
-        pair = stack(feed_one, feed_two)
+        pair, near_x_down = glue(
+            (feed_one, feed_two, near_x),
+            (cols_feed, (0, 0, tall, 0), (1, 0, tall, 0)),
+            (w_down.shape[0] // tall * width, (2, 0, tall, at_down)),
+        )
         x_pair, y_pair, feed_three, pair_core = stage(
             "xy3c", (pair, pair, w_feed, pair), y_far_core, crossed_core, crossed_more_core
         )
@@ -617,15 +668,19 @@
     qkv = project(scalars, seqs, first, qkv_parts, bias, scale)
     if special:
         x_last, y_last, cross_down, down_one, down_two = stage(
-            "xyy12", (feed_three, feed_three, near_x[:, at_down:], w_down, w_down), qkv, pair_core
+            "xyy12", (feed_three, feed_three, near_x_down, w_down, w_down), qkv, pair_core
         )
     attended = []
     for seq in range(seqs):
         if special and seq == 1:
             x_last, y_last, *attended = after((x_last, y_last, *attended), cross_down, down_one)
-            left = stack(near_x[:, at_feed:at_down], x_pair[:32])
+            left, right = glue(
+                (near_x, x_pair, y_pair, y_last),
+                (cols_feed, (0, 0, tall, at_feed), (1, 0, tall, 0)),
+                (cols_feed, (2, tall, tall, 0), (3, 0, tall, 0)),
+            )
             crossed, crossed_more, down_three, x_pair_core, y_pair_core = stage(
-                "yx3cc", (left, stack(y_pair[32:], y_last), w_down, x_pair, y_pair), x_last, *attended
+                "yx3cc", (left, right, w_down, x_pair, y_pair), x_last, *attended
             )
         attended = attend(scalars, qkv, width, seq, attended)
     context, powers, inverse = attended
@@ -647,16 +702,18 @@
             ],
             [*near_core, pair_core, x_pair_core, y_pair_core, *cores],
         )
-        far = stack(down_one, down_two, down_three)
+        (far,) = glue(
+            (down_one, down_two, down_three),
+            (width, *((n, 0, w_down.shape[0], 0) for n in range(3))),
+        )
         x_far, y_far, *diagonal = stage(
             "xy123", (far, far, cross_down, cross_down, cross_down), *cores
         )
-    fed = []
-    for seq in range(seqs):
-        fed = feed(scalars, seqs, tokens, context, feed_parts, vectors, bias_in[None], seq, fed)
-        if special and seq == 0:
-            x_far, cross_down, *fed = after((x_far, cross_down, *fed), y_far, *diagonal)
-    normed, spread, gl, gp = fed
+    normed, spread, gl, gp = join(
+        scalars, seqs, tokens, context, feed_parts, vectors, bias_in[None]
+    )
+    if special:
+        x_far, cross_down, gl = after((x_far, cross_down, gl), y_far, *diagonal)
     if special:
         mine = [
             (after(far, x_far), (0, rest, 0)),
@@ -676,11 +733,13 @@
     devices = lax.axis_size("dp") * lax.axis_size("fsdp")
     parts = (sum_q[0], sums[0], sums[1], sums[2], sum_in[0], sums[3], sums[4])
     rows = jnp.concatenate([part.reshape(devices, -1) for part in parts], axis=1)
-    mine = reduce_shares(rows, rows.shape[1])
+    mine = jnp.sum(lax.all_to_all(rows, BOTH, 0, 0, tiled=True), axis=0)
+    small = width // devices
+    sizes = (small, small, small, small, sum_in.shape[1] // devices, small, small)
     shares, at = [], 0
-    for part in parts:
-        shares.append(mine[at : at + part.shape[0] // devices])
-        at += part.shape[0] // devices
+    for size in sizes:
+        shares.append(mine[at : at + size])
+        at += size
     return (output, input_grad, *shares)
 
 

time: 287 us -> 259 us (0.902)
  local copies, waits for them, and re-layouts: 24.3 us -> 9.63 us
  starting transfers between devices: 55.6 us -> 41.2 us
  blocking collectives: 0 us -> 10.3 us
  Pallas kernels: 150 us -> 141 us
    ppermute x60 -> x50, starting transfers between devices: 55.6 us -> 41.2 us  [hop(): return lax.ppermute(block, axis, [(i, i ^ flip) for i in range(size)])]
    all_to_all x0 -> x1, blocking collectives: none -> 10.3 us  [on_device(): mine = jnp.sum(lax.all_to_all(rows, BOTH, 0, 0, tiled=True), axis=0)]
    unnamed x107 -> x90, local copies, waits for them, and re-layouts: 15.5 us -> 6.75 us
    pallas_call x2 -> x6, Pallas kernels: 35.6 us -> 28.3 us  [the longest x1 26 us: join(): pl.pallas_call(functools.partial(join_body, seqs, tags_of(sources)), out_...]
    concatenate x3 -> x0, local copies, waits for them, and re-layouts: 3.35 us -> none  [stack(): return jnp.concatenate(blocks, axis=0)]
    ppermute x60 -> x50, waiting for transfers between devices: 50.2 us -> 51.6 us  [hop(): return lax.ppermute(block, axis, [(i, i ^ flip) for i in range(size)])]
  transfers between devices with their start and end apart: 60 -> 50, of which waited for: 15 -> 15; matrix products, arithmetic and copies ran while one was open for 3% -> 1% of each run, Pallas kernels for 24% -> 23%
where the time goes in v3:
time: 259 us; the launch traced here: 258 us
  Pallas kernels  141 us (54%)
  waiting for transfers between devices  51.6 us (20%)
  starting transfers between devices  41.2 us (16%)
  blocking collectives  10.3 us (4%)
  local copies, waits for them, and re-layouts  9.63 us (4%)
  other arithmetic  3.29 us (1%)
    ppermute x50, waiting for transfers between devices, hop(): return lax.ppermute(block, axis, [(i, i ^ flip) for i in range(size)])  51.6 us
    pallas_call x1, Pallas kernels, turn(): pl.pallas_call(functools.partial(turn_body, seqs, tags_of(feeds), tags_of...  44.3 us
    ppermute x50, starting transfers between devices, hop(): return lax.ppermute(block, axis, [(i, i ^ flip) for i in range(size)])  41.2 us
    pallas_call x1, Pallas kernels, back(): pl.pallas_call(functools.partial(back_body, seqs, tags_of(sources)), out_...  34.1 us
    pallas_call x1, Pallas kernels, join(): pl.pallas_call(functools.partial(join_body, seqs, tags_of(sources)), out_...  26 us
    pallas_call x2, Pallas kernels, attend(): pl.pallas_call(functools.partial(attend_body, seq), out_shape=(shape_of((...  20.4 us
    pallas_call x1, Pallas kernels, project(): pl.pallas_call(functools.partial(project_body, seqs, tags_of(sources)), o...  12.6 us
    all_to_all x1, blocking collectives, on_device(): mine = jnp.sum(lax.all_to_all(rows, BOTH, 0, 0, tiled=True), axis=0)  10.3 us
  transfers between devices with their start and end apart: 50, of which 15 were waited for; matrix products, arithmetic and copies ran while one was open for 1% of the time, Pallas kernels for 23%

profile of v3, /device:TPU:0, one launch (start us, length us, event | category | flops | bytes accessed | tf_op | source)
XLA Modules:
  0.0 258.0 jit_solution(14066320625617004901)
XLA Ops:
  0.7 0.9 copy-done.9
  1.6 0.9 copy-done.10
  2.5 0.8 copy-done.12
  3.4 1.0 pack.1
  4.4 3.0 %collective-permute-start.3 = (bf16[32,12288]{1,0:T(8,128)(2,1)S(1)}, bf16[32,12288]{1,0:T(8,128)(2,1)S(1)}, u32[]{:S(2)}, u32[]{:S(2)}) collective-permute-start(bf16[32,12288]{1,0:T(8,128)(2,1)S(1)} %get-tuple-element.144.refs_0_.refs_22_), channel_id=1, source_target_pairs={{0,8},{8,0},{16,24},{24,16},{1,9},{9,1},{17,25},{25,17},{2,10},{10... | collective-permute-start | bytes 2359304 | tf_op jit(solution)/shard_map/ppermute | solution.py:551
  7.4 1.5 collective-permute-start.4
  8.9 1.6 collective-permute-start
  10.5 2.6 %collective-permute-start.1 = (bf16[32,3072]{1,0:T(8,128)(2,1)}, bf16[32,3072]{1,0:T(8,128)(2,1)S(1)}, u32[]{:S(2)}, u32[]{:S(2)}) collective-permute-start(bf16[32,3072]{1,0:T(8,128)(2,1)} %qkv_ref.1), channel_id=1, source_target_pairs={{0,4},{1,5},{2,6},{3,7},{4,0},{5,1},{6,2},{7,3},{8,12},{9,13},{10,... | collective-permute-start | bytes 589832 | tf_op jit(solution)/shard_map/ppermute | solution.py:551
  13.3 4.8 %collective-permute-done.refs_0_ = bf16[32,3072]{1,0:T(8,128)(2,1)S(1)} collective-permute-done((bf16[32,3072]{1,0:T(8,128)(2,1)}, bf16[32,3072]{1,0:T(8,128)(2,1)S(1)}, u32[]{:S(2)}, u32[]{:S(2)}) %collective-permute-start) | collective-permute-done | bytes 196640 | tf_op jit(solution)/shard_map/ppermute | solution.py:551
  18.1 9.8 %collective-permute-done.1.refs_1_ = bf16[32,3072]{1,0:T(8,128)(2,1)S(1)} collective-permute-done((bf16[32,3072]{1,0:T(8,128)(2,1)}, bf16[32,3072]{1,0:T(8,128)(2,1)S(1)}, u32[]{:S(2)}, u32[]{:S(2)}) %collective-permute-start.1) | collective-permute-done | bytes 196640 | tf_op jit(solution)/shard_map/ppermute | solution.py:551
  29.6 3.8 %collective-permute-start.7 = (bf16[32,5120]{1,0:T(8,128)(2,1)S(1)}, bf16[32,5120]{1,0:T(8,128)(2,1)S(1)}, u32[]{:S(2)}, u32[]{:S(2)}) collective-permute-start(bf16[32,5120]{1,0:T(8,128)(2,1)S(1)} %get-tuple-element.174), channel_id=1, source_target_pairs={{0,4},{1,5},{2,6},{3,7},{4,0},{5,1},{6,2},{7,3},{8,12},{9,13},{10,... | collective-permute-start | bytes 983048 | tf_op jit(solution)/shard_map/ppermute | solution.py:551
  33.4 14.4 %collective-permute-done.7.refs_1_ = bf16[32,5120]{1,0:T(8,128)(2,1)S(1)} collective-permute-done((bf16[32,5120]{1,0:T(8,128)(2,1)S(1)}, bf16[32,5120]{1,0:T(8,128)(2,1)S(1)}, u32[]{:S(2)}, u32[]{:S(2)}) %collective-permute-start.7) | collective-permute-done | bytes 327712 | tf_op jit(solution)/shard_map/ppermute | solution.py:551
  47.8 0.9 copy-done.25
  49.4 1.5 collective-permute-start.10
  50.9 1.5 collective-permute-start.11
  52.4 9.1 %collective-permute-done.12.refs_0_ = bf16[32,5120]{1,0:T(8,128)(2,1)S(1)} collective-permute-done((bf16[32,5120]{1,0:T(8,128)(2,1)S(1)}, bf16[32,5120]{1,0:T(8,128)(2,1)S(1)}, u32[]{:S(2)}, u32[]{:S(2)}) %collective-permute-start.12) | collective-permute-done | bytes 327712 | tf_op jit(solution)/shard_map/ppermute | solution.py:551
  63.0 1.3 pad_maximum_fusion
  64.3 0.9 glue.7
  65.4 0.8 collective-permute-done.18.refs_15_
  66.3 1.6 collective-permute-start.19
  68.9 2.0 collective-permute-start.21
  70.9 12.6 %project.1.q_ref.k_ref.v_ref = bf16[1024,3072]{1,0:T(8,128)(2,1)} custom-call(s32[5]{0:T(128)} %pad_add_fusion.len_ref, bf16[1024,1024]{1,0:T(8,128)(2,1)} %x_ref.2, f32[1,3072]{1,0:T(1,128)} %bitcast.13, f32[1,3072]{1,0:T(1,128)} %constant.37.clone.1.scale_ref, bf16[32,12288]{1,0:T(8,128)(2,1)} %copy-done.13, bf16[32,12288]{1,0:T(8,128)(2,1)} %copy-done, ...), custom_call_target="tpu_custom_call" | custom-call | flops 6442450944 | tf_op jit(solution)/shard_map/project/pallas_call | solution.py:141
  83.6 1.0 collective-permute-done.20.refs_2_.refs_5_
  85.7 1.5 collective-permute-start.25
  87.2 1.9 collective-permute-start.26
  89.6 10.2 %attend.2 = (bf16[1024,1024]{1,0:T(8,128)(2,1)}, bf16[32,512,512]{2,1,0:T(8,128)(2,1)}, f32[1024,1024]{1,0:T(8,128)}) custom-call(s32[5]{0:T(128)} %pad_add_fusion.len_ref, bf16[1024,3072]{1,0:T(8,128)(2,1)} %project.1.q_ref.k_ref.v_ref, bf16[1024,3072]{1,0:T(8,128)(2,1)} %project.1.q_ref.k_ref.v_ref, bf16[1024,3072]{1,0:T(8,128)(2,1)} %project.1.q_ref.k_ref.v_ref), custom_call_target="tpu_custom_call" | custom-call | flops 4294967296 | tf_op jit(solution)/shard_map/attend/pallas_call | solution.py:214
  99.8 2.7 %collective-permute-done.27.refs_1_ = bf16[128,1024]{1,0:T(8,128)(2,1)S(1)} collective-permute-done((bf16[128,1024]{1,0:T(8,128)(2,1)S(1)}, bf16[128,1024]{1,0:T(8,128)(2,1)S(1)}, u32[]{:S(2)}, u32[]{:S(2)}) %collective-permute-start.27) | collective-permute-done | bytes 262176 | tf_op jit(solution)/shard_map/ppermute | solution.py:551
  102.5 1.2 glue.8
  103.8 1.6 collective-permute-start.28
  106.4 1.9 collective-permute-start.30
  108.4 10.2 %attend.3 = (bf16[1024,1024]{1,0:T(8,128)(2,1)}, bf16[32,512,512]{2,1,0:T(8,128)(2,1)}, f32[1024,1024]{1,0:T(8,128)}) custom-call(s32[5]{0:T(128)} %pad_add_fusion.len_ref, bf16[1024,3072]{1,0:T(8,128)(2,1)} %project.1.q_ref.k_ref.v_ref, bf16[1024,3072]{1,0:T(8,128)(2,1)} %project.1.q_ref.k_ref.v_ref, ...), custom_call_target="tpu_custom_call", output_to_operand_aliasing={{0}: (4, {}), {1}: (5, {}), {2}: (6, {})} | custom-call | flops 4294967296 | tf_op jit(solution)/shard_map/attend/pallas_call | solution.py:214
  120.6 2.0 collective-permute-done.33.refs_17_
  122.6 0.8 collective-permute-done.34.refs_18_
  123.4 0.7 copy-done.37
  124.1 0.9 collective-permute-start.38
  125.0 1.1 collective-permute-start.39
  126.1 1.6 collective-permute-start.40
  127.8 0.8 collective-permute-start.41
  128.6 2.0 collective-permute-start.42
  130.5 26.0 %join.1 = (f32[1024,1024]{1,0:T(8,128)}, f32[1024,128]{1,0:T(8,128)}, bf16[1024,4096]{1,0:T(8,128)(2,1)}, bf16[1024,4096]{1,0:T(8,128)(2,1)}) custom-call(s32[5]{0:T(128)} %pad_add_fusion.len_ref, bf16[1024,1024]{1,0:T(8,128)(2,1)} %x_ref.2, bf16[1024,1024]{1,0:T(8,128)(2,1)} %get-tuple-element.211.o_ref, f32[8,1024]{1,0:T(8,128)} %stack.43.vec_ref, ...), custom_call_target="tpu_custom_call" | custom-call | flops 10737418240 | tf_op jit(solution)/shard_map/join/pallas_call | solution.py:284
  157.8 3.8 %collective-permute-done.46.refs_38_ = bf16[32,4096]{1,0:T(8,128)(2,1)S(1)} collective-permute-done((bf16[32,4096]{1,0:T(8,128)(2,1)S(1)}, bf16[32,4096]{1,0:T(8,128)(2,1)S(1)}, u32[]{:S(2)}, u32[]{:S(2)}) %collective-permute-start.46) | collective-permute-done | bytes 262176 | tf_op jit(solution)/shard_map/ppermute | solution.py:551
  162.1 1.2 collective-permute-done.48.refs_40_
  163.8 0.9 copy-done.30
  164.6 0.9 copy-done.31
  165.6 44.3 %turn.1 = (bf16[1024,1024]{1,0:T(8,128)(2,1)}, f32[1024,1024]{1,0:T(8,128)}, bf16[1024,1024]{1,0:T(8,128)(2,1)}, f32[8,1024]{1,0:T(8,128)}, f32[1,4096]{1,0:T(1,128)}) custom-call(s32[5]{0:T(128)} %pad_add_fusion.len_ref, bf16[1024,4096]{1,0:T(8,128)(2,1)} %get-tuple-element.235.gl_ref, f32[1024,1024]{1,0:T(8,128)} %get-tuple-element.236.u_ref, ...), custom_call_target="tpu_custom_call" | custom-call | flops 27917287424 | tf_op jit(solution)/shard_map/turn/pallas_call | solution.py:405
  210.0 34.1 %back.1 = (bf16[1024,1024]{1,0:T(8,128)(2,1)}, f32[1,1024]{1,0:T(1,128)}) custom-call(s32[5]{0:T(128)} %pad_add_fusion.len_ref, bf16[1024,3072]{1,0:T(8,128)(2,1)} %project.1.q_ref.k_ref.v_ref, bf16[1024,3072]{1,0:T(8,128)(2,1)} %project.1.q_ref.k_ref.v_ref, bf16[1024,3072]{1,0:T(8,128)(2,1)} %project.1.q_ref.k_ref.v_ref, ...), custom_call_target="tpu_custom_call" | custom-call | flops 17179869184 | tf_op jit(solution)/shard_map/back/pallas_call | solution.py:514
  244.5 1.3 reduce.24
  246.5 10.3 %all_to_all.9 = f32[32,1,320]{2,1,0:T(1,128)S(1)} all-to-all(f32[32,1,320]{2,1,0:T(1,128)S(1)} %all_to_all.6), channel_id=1, replica_groups=mesh['dp'=4,'fsdp'=8] {'dp','fsdp'}, dimensions={0} | all-to-all | bytes 81920 | tf_op jit(solution)/shard_map/all_to_all | solution.py:736
  (174 shorter events, 14.3 us)
Async XLA Ops:
  4.4 23.5 %collective-permute-start.3 = (bf16[32,12288]{1,0:T(8,128)(2,1)S(1)}, bf16[32,12288]{1,0:T(8,128)(2,1)S(1)}, u32[]{:S(2)}, u32[]{:S(2)}) collective-permute-start(bf16[32,12288]{1,0:T(8,128)(2,1)S(1)} %get-tuple-element.144.refs_0_.refs_22_), channel_id=1, source_target_pairs={{0,8},{8,0},{16,24},{24,16},{1,9},{9,1},{17,25},{25,17},{2,10},{10... | collective-permute-start | bytes 2359304 | tf_op jit(solution)/shard_map/ppermute | solution.py:551
  7.4 20.5 %collective-permute-start.4 = (bf16[32,12288]{1,0:T(8,128)(2,1)S(1)}, bf16[32,12288]{1,0:T(8,128)(2,1)S(1)}, u32[]{:S(2)}, u32[]{:S(2)}) collective-permute-start(bf16[32,12288]{1,0:T(8,128)(2,1)S(1)} %get-tuple-element.144.refs_0_.refs_22_), channel_id=1, source_target_pairs={{0,16},{8,24},{16,0},{24,8},{1,17},{9,25},{17,1},{25,9},{2,18},{10... | collective-permute-start | bytes 2359304 | tf_op jit(solution)/shard_map/ppermute | solution.py:551
  8.9 9.2 %collective-permute-start = (bf16[32,3072]{1,0:T(8,128)(2,1)}, bf16[32,3072]{1,0:T(8,128)(2,1)S(1)}, u32[]{:S(2)}, u32[]{:S(2)}) collective-permute-start(bf16[32,3072]{1,0:T(8,128)(2,1)} %qkv_ref.1), channel_id=1, source_target_pairs={{0,2},{1,3},{2,0},{3,1},{4,6},{5,7},{6,4},{7,5},{8,10},{9,11},{10,... | collective-permute-start | bytes 589832 | tf_op jit(solution)/shard_map/ppermute | solution.py:551
  10.5 17.4 %collective-permute-start.1 = (bf16[32,3072]{1,0:T(8,128)(2,1)}, bf16[32,3072]{1,0:T(8,128)(2,1)S(1)}, u32[]{:S(2)}, u32[]{:S(2)}) collective-permute-start(bf16[32,3072]{1,0:T(8,128)(2,1)} %qkv_ref.1), channel_id=1, source_target_pairs={{0,4},{1,5},{2,6},{3,7},{4,0},{5,1},{6,2},{7,3},{8,12},{9,13},{10,... | collective-permute-start | bytes 589832 | tf_op jit(solution)/shard_map/ppermute | solution.py:551
  13.1 14.8 %collective-permute-start.2 = (bf16[32,3072]{1,0:T(8,128)(2,1)}, bf16[32,3072]{1,0:T(8,128)(2,1)S(1)}, u32[]{:S(2)}, u32[]{:S(2)}) collective-permute-start(bf16[32,3072]{1,0:T(8,128)(2,1)} %qkv_ref.1), channel_id=1, source_target_pairs={{0,6},{1,7},{2,4},{3,5},{4,2},{5,3},{6,0},{7,1},{8,14},{9,15},{10,... | collective-permute-start | bytes 589832 | tf_op jit(solution)/shard_map/ppermute | solution.py:551
  28.0 19.8 %collective-permute-start.8 = (bf16[32,12288]{1,0:T(8,128)(2,1)S(1)}, bf16[32,12288]{1,0:T(8,128)(2,1)S(1)}, u32[]{:S(2)}, u32[]{:S(2)}) collective-permute-start(bf16[32,12288]{1,0:T(8,128)(2,1)S(1)} %get-tuple-element.144.refs_0_.refs_22_), channel_id=1, source_target_pairs={{0,1},{1,0},{2,3},{3,2},{4,5},{5,4},{6,7},{7,6},{8,9},{9,8},{10,11... | collective-permute-start | bytes 2359304 | tf_op jit(solution)/shard_map/ppermute | solution.py:551
  28.1 20.7 %collective-permute-start.9 = (bf16[32,12288]{1,0:T(8,128)(2,1)S(1)}, bf16[32,12288]{1,0:T(8,128)(2,1)}, u32[]{:S(2)}, u32[]{:S(2)}) collective-permute-start(bf16[32,12288]{1,0:T(8,128)(2,1)S(1)} %collective-permute-done.3.refs_0_.refs_2_.refs_1_.refs_23_), channel_id=1, source_target_pairs={{0,1},{1,0},{2,3},{3,2},{4,5},{5,4},{6,7},{7,6},{8,9},{9,8},{10,11... | collective-permute-start | bytes 2359304 | tf_op jit(solution)/shard_map/ppermute | solution.py:551
  28.6 19.2 %collective-permute-start.5 = (bf16[96,3072]{1,0:T(8,128)(2,1)S(1)}, bf16[96,3072]{1,0:T(8,128)(2,1)S(1)}, u32[]{:S(2)}, u32[]{:S(2)}) collective-permute-start(bf16[96,3072]{1,0:T(8,128)(2,1)S(1)} %glue.5.refs_3_), channel_id=1, source_target_pairs={{0,8},{8,0},{16,24},{24,16},{1,9},{9,1},{17,25},{25,17},{2,10},{10... | collective-permute-start | bytes 1769480 | tf_op jit(solution)/shard_map/ppermute | solution.py:551
  29.1 18.7 %collective-permute-start.6 = (bf16[96,3072]{1,0:T(8,128)(2,1)S(1)}, bf16[96,3072]{1,0:T(8,128)(2,1)S(1)}, u32[]{:S(2)}, u32[]{:S(2)}) collective-permute-start(bf16[96,3072]{1,0:T(8,128)(2,1)S(1)} %glue.5.refs_3_), channel_id=1, source_target_pairs={{0,16},{8,24},{16,0},{24,8},{1,17},{9,25},{17,1},{25,9},{2,18},{10... | collective-permute-start | bytes 1769480 | tf_op jit(solution)/shard_map/ppermute | solution.py:551
  29.6 18.2 %collective-permute-start.7 = (bf16[32,5120]{1,0:T(8,128)(2,1)S(1)}, bf16[32,5120]{1,0:T(8,128)(2,1)S(1)}, u32[]{:S(2)}, u32[]{:S(2)}) collective-permute-start(bf16[32,5120]{1,0:T(8,128)(2,1)S(1)} %get-tuple-element.174), channel_id=1, source_target_pairs={{0,4},{1,5},{2,6},{3,7},{4,0},{5,1},{6,2},{7,3},{8,12},{9,13},{10,... | collective-permute-start | bytes 983048 | tf_op jit(solution)/shard_map/ppermute | solution.py:551
  48.8 13.0 %collective-permute-start.13 = (bf16[32,12288]{1,0:T(8,128)(2,1)S(1)}, bf16[32,12288]{1,0:T(8,128)(2,1)S(1)}, u32[]{:S(2)}, u32[]{:S(2)}) collective-permute-start(bf16[32,12288]{1,0:T(8,128)(2,1)S(1)} %collective-permute-done.4.refs_2_.refs_24_), channel_id=1, source_target_pairs={{0,1},{1,0},{2,3},{3,2},{4,5},{5,4},{6,7},{7,6},{8,9},{9,8},{10,11... | collective-permute-start | bytes 2359304 | tf_op jit(solution)/shard_map/ppermute | solution.py:551
  48.9 12.9 %collective-permute-start.14 = (bf16[96,3072]{1,0:T(8,128)(2,1)S(1)}, bf16[96,3072]{1,0:T(8,128)(2,1)S(1)}, u32[]{:S(2)}, u32[]{:S(2)}) collective-permute-start(bf16[96,3072]{1,0:T(8,128)(2,1)S(1)} %glue.5.refs_3_), channel_id=1, source_target_pairs={{0,1},{1,0},{2,3},{3,2},{4,5},{5,4},{6,7},{7,6},{8,9},{9,8},{10,11... | collective-permute-start | bytes 1769480 | tf_op jit(solution)/shard_map/ppermute | solution.py:551
  49.4 12.1 %collective-permute-start.10 = (bf16[64,3072]{1,0:T(8,128)(2,1)S(1)}, bf16[64,3072]{1,0:T(8,128)(2,1)}, u32[]{:S(2)}, u32[]{:S(2)}) collective-permute-start(bf16[64,3072]{1,0:T(8,128)(2,1)S(1)} %get-tuple-element.154), channel_id=1, source_target_pairs={{0,16},{8,24},{16,0},{24,8},{1,17},{9,25},{17,1},{25,9},{2,18},{10... | collective-permute-start | bytes 1179656 | tf_op jit(solution)/shard_map/ppermute | solution.py:551
  50.9 10.9 %collective-permute-start.11 = (bf16[64,3072]{1,0:T(8,128)(2,1)S(1)}, bf16[64,3072]{1,0:T(8,128)(2,1)}, u32[]{:S(2)}, u32[]{:S(2)}) collective-permute-start(bf16[64,3072]{1,0:T(8,128)(2,1)S(1)} %get-tuple-element.155), channel_id=1, source_target_pairs={{0,8},{8,0},{16,24},{24,16},{1,9},{9,1},{17,25},{25,17},{2,10},{10... | collective-permute-start | bytes 1179656 | tf_op jit(solution)/shard_map/ppermute | solution.py:551
  52.4 9.1 %collective-permute-start.12 = (bf16[32,5120]{1,0:T(8,128)(2,1)S(1)}, bf16[32,5120]{1,0:T(8,128)(2,1)S(1)}, u32[]{:S(2)}, u32[]{:S(2)}) collective-permute-start(bf16[32,5120]{1,0:T(8,128)(2,1)S(1)} %get-tuple-element.174), channel_id=1, source_target_pairs={{0,2},{1,3},{2,0},{3,1},{4,6},{5,7},{6,4},{7,5},{8,10},{9,11},{10,... | collective-permute-start | bytes 983048 | tf_op jit(solution)/shard_map/ppermute | solution.py:551
  61.9 4.4 %collective-permute-start.15 = (bf16[96,3072]{1,0:T(8,128)(2,1)S(1)}, bf16[96,3072]{1,0:T(8,128)(2,1)}, u32[]{:S(2)}, u32[]{:S(2)}) collective-permute-start(bf16[96,3072]{1,0:T(8,128)(2,1)S(1)} %collective-permute-done.5.refs_1_.refs_4_), channel_id=1, source_target_pairs={{0,1},{1,0},{2,3},{3,2},{4,5},{5,4},{6,7},{7,6},{8,9},{9,8},{10,11... | collective-permute-start | bytes 1769480 | tf_op jit(solution)/shard_map/ppermute | solution.py:551
  62.0 4.3 %collective-permute-start.16 = (bf16[96,3072]{1,0:T(8,128)(2,1)S(1)}, bf16[96,3072]{1,0:T(8,128)(2,1)}, u32[]{:S(2)}, u32[]{:S(2)}) collective-permute-start(bf16[96,3072]{1,0:T(8,128)(2,1)S(1)} %collective-permute-done.6.refs_2_.refs_5_), channel_id=1, source_target_pairs={{0,1},{1,0},{2,3},{3,2},{4,5},{5,4},{6,7},{7,6},{8,9},{9,8},{10,11... | collective-permute-start | bytes 1769480 | tf_op jit(solution)/shard_map/ppermute | solution.py:551
  62.5 3.0 %collective-permute-start.17 = (bf16[64,3072]{1,0:T(8,128)(2,1)}, bf16[64,3072]{1,0:T(8,128)(2,1)}, u32[]{:S(2)}, u32[]{:S(2)}) collective-permute-start(bf16[64,3072]{1,0:T(8,128)(2,1)} %collective-permute-done.10.refs_6_), channel_id=1, source_target_pairs={{0,1},{1,0},{2,3},{3,2},{4,5},{5,4},{6,7},{7,6},{8,9},{9,8},{10,11... | collective-permute-start | bytes 1179656 | tf_op jit(solution)/shard_map/ppermute | solution.py:551
  63.0 3.3 %collective-permute-start.18 = (bf16[64,3072]{1,0:T(8,128)(2,1)}, bf16[64,3072]{1,0:T(8,128)(2,1)}, u32[]{:S(2)}, u32[]{:S(2)}) collective-permute-start(bf16[64,3072]{1,0:T(8,128)(2,1)} %collective-permute-done.11.refs_7_), channel_id=1, source_target_pairs={{0,1},{1,0},{2,3},{3,2},{4,5},{5,4},{6,7},{7,6},{8,9},{9,8},{10,11... | collective-permute-start | bytes 1179656 | tf_op jit(solution)/shard_map/ppermute | solution.py:551
  66.3 17.3 %collective-permute-start.19 = (bf16[64,5120]{1,0:T(8,128)(2,1)}, bf16[64,5120]{1,0:T(8,128)(2,1)S(1)}, u32[]{:S(2)}, u32[]{:S(2)}) collective-permute-start(bf16[64,5120]{1,0:T(8,128)(2,1)} %get-tuple-element.175.refs_3_), channel_id=1, source_target_pairs={{0,8},{8,0},{16,24},{24,16},{1,9},{9,1},{17,25},{25,17},{2,10},{10... | collective-permute-start | bytes 1966088 | tf_op jit(solution)/shard_map/ppermute | solution.py:551
  67.8 16.7 %collective-permute-start.20 = (bf16[64,5120]{1,0:T(8,128)(2,1)}, bf16[64,5120]{1,0:T(8,128)(2,1)S(1)}, u32[]{:S(2)}, u32[]{:S(2)}) collective-permute-start(bf16[64,5120]{1,0:T(8,128)(2,1)} %get-tuple-element.175.refs_3_), channel_id=1, source_target_pairs={{0,16},{8,24},{16,0},{24,8},{1,17},{9,25},{17,1},{25,9},{2,18},{10... | collective-permute-start | bytes 1966088 | tf_op jit(solution)/shard_map/ppermute | solution.py:551
  68.3 16.2 %collective-permute-start.22 = (bf16[64,5120]{1,0:T(8,128)(2,1)}, bf16[64,5120]{1,0:T(8,128)(2,1)}, u32[]{:S(2)}, u32[]{:S(2)}) collective-permute-start(bf16[64,5120]{1,0:T(8,128)(2,1)} %get-tuple-element.175.refs_3_), channel_id=1, source_target_pairs={{0,1},{1,0},{2,3},{3,2},{4,5},{5,4},{6,7},{7,6},{8,9},{9,8},{10,11... | collective-permute-start | bytes 1966088 | tf_op jit(solution)/shard_map/ppermute | solution.py:551
  68.9 14.6 %collective-permute-start.21 = (bf16[32,5120]{1,0:T(8,128)(2,1)}, bf16[32,5120]{1,0:T(8,128)(2,1)}, u32[]{:S(2)}, u32[]{:S(2)}) collective-permute-start(bf16[32,5120]{1,0:T(8,128)(2,1)} %copy-done.14), channel_id=1, source_target_pairs={{0,6},{1,7},{2,4},{3,5},{4,2},{5,3},{6,0},{7,1},{8,14},{9,15},{10,... | collective-permute-start | bytes 983048 | tf_op jit(solution)/shard_map/ppermute | solution.py:551
  84.6 17.9 %collective-permute-start.23 = (bf16[32,5120]{1,0:T(8,128)(2,1)}, bf16[32,5120]{1,0:T(8,128)(2,1)S(1)}, u32[]{:S(2)}, u32[]{:S(2)}) collective-permute-start(bf16[32,5120]{1,0:T(8,128)(2,1)} %collective-permute-done.21.refs_6_), channel_id=1, source_target_pairs={{0,8},{8,0},{16,24},{24,16},{1,9},{9,1},{17,25},{25,17},{2,10},{10... | collective-permute-start | bytes 983048 | tf_op jit(solution)/shard_map/ppermute | solution.py:551
  85.1 17.3 %collective-permute-start.24 = (bf16[32,5120]{1,0:T(8,128)(2,1)}, bf16[32,5120]{1,0:T(8,128)(2,1)S(1)}, u32[]{:S(2)}, u32[]{:S(2)}) collective-permute-start(bf16[32,5120]{1,0:T(8,128)(2,1)} %collective-permute-done.21.refs_6_), channel_id=1, source_target_pairs={{0,16},{8,24},{16,0},{24,8},{1,17},{9,25},{17,1},{25,9},{2,18},{10... | collective-permute-start | bytes 983048 | tf_op jit(solution)/shard_map/ppermute | solution.py:551
  85.7 14.1 %collective-permute-start.25 = (bf16[32,4096]{1,0:T(8,128)(2,1)S(1)}, bf16[32,4096]{1,0:T(8,128)(2,1)S(1)}, u32[]{:S(2)}, u32[]{:S(2)}) collective-permute-start(bf16[32,4096]{1,0:T(8,128)(2,1)S(1)} %get-tuple-element.183), channel_id=1, source_target_pairs={{0,16},{8,24},{16,0},{24,8},{1,17},{9,25},{17,1},{25,9},{2,18},{10... | collective-permute-start | bytes 786440 | tf_op jit(solution)/shard_map/ppermute | solution.py:551
  87.2 12.6 %collective-permute-start.26 = (bf16[128,1024]{1,0:T(8,128)(2,1)S(1)}, bf16[128,1024]{1,0:T(8,128)(2,1)S(1)}, u32[]{:S(2)}, u32[]{:S(2)}) collective-permute-start(bf16[128,1024]{1,0:T(8,128)(2,1)S(1)} %copy-done.11), channel_id=1, source_target_pairs={{0,2},{1,3},{2,0},{3,1},{4,6},{5,7},{6,4},{7,5},{8,10},{9,11},{10,... | collective-permute-start | bytes 786440 | tf_op jit(solution)/shard_map/ppermute | solution.py:551
  89.1 13.4 %collective-permute-start.27 = (bf16[128,1024]{1,0:T(8,128)(2,1)S(1)}, bf16[128,1024]{1,0:T(8,128)(2,1)S(1)}, u32[]{:S(2)}, u32[]{:S(2)}) collective-permute-start(bf16[128,1024]{1,0:T(8,128)(2,1)S(1)} %copy-done.11), channel_id=1, source_target_pairs={{0,4},{1,5},{2,6},{3,7},{4,0},{5,1},{6,2},{7,3},{8,12},{9,13},{10,... | collective-permute-start | bytes 786440 | tf_op jit(solution)/shard_map/ppermute | solution.py:551
  103.8 14.8 %collective-permute-start.28 = (bf16[64,5120]{1,0:T(8,128)(2,1)}, bf16[64,5120]{1,0:T(8,128)(2,1)}, u32[]{:S(2)}, u32[]{:S(2)}) collective-permute-start(bf16[64,5120]{1,0:T(8,128)(2,1)} %get-tuple-element.203), channel_id=1, source_target_pairs={{0,16},{8,24},{16,0},{24,8},{1,17},{9,25},{17,1},{25,9},{2,18},{10... | collective-permute-start | bytes 1966088 | tf_op jit(solution)/shard_map/ppermute | solution.py:551
  105.4 13.3 %collective-permute-start.29 = (bf16[64,5120]{1,0:T(8,128)(2,1)}, bf16[64,5120]{1,0:T(8,128)(2,1)}, u32[]{:S(2)}, u32[]{:S(2)}) collective-permute-start(bf16[64,5120]{1,0:T(8,128)(2,1)} %get-tuple-element.204), channel_id=1, source_target_pairs={{0,8},{8,0},{16,24},{24,16},{1,9},{9,1},{17,25},{25,17},{2,10},{10... | collective-permute-start | bytes 1966088 | tf_op jit(solution)/shard_map/ppermute | solution.py:551
  105.9 12.7 %collective-permute-start.31 = (bf16[64,5120]{1,0:T(8,128)(2,1)S(1)}, bf16[64,5120]{1,0:T(8,128)(2,1)S(1)}, u32[]{:S(2)}, u32[]{:S(2)}) collective-permute-start(bf16[64,5120]{1,0:T(8,128)(2,1)S(1)} %collective-permute-done.19.refs_1_.refs_4_), channel_id=1, source_target_pairs={{0,1},{1,0},{2,3},{3,2},{4,5},{5,4},{6,7},{7,6},{8,9},{9,8},{10,11... | collective-permute-start | bytes 1966088 | tf_op jit(solution)/shard_map/ppermute | solution.py:551
  105.9 12.7 %collective-permute-start.32 = (bf16[64,5120]{1,0:T(8,128)(2,1)S(1)}, bf16[64,5120]{1,0:T(8,128)(2,1)}, u32[]{:S(2)}, u32[]{:S(2)}) collective-permute-start(bf16[64,5120]{1,0:T(8,128)(2,1)S(1)} %collective-permute-done.20.refs_2_.refs_5_), channel_id=1, source_target_pairs={{0,1},{1,0},{2,3},{3,2},{4,5},{5,4},{6,7},{7,6},{8,9},{9,8},{10,11... | collective-permute-start | bytes 1966088 | tf_op jit(solution)/shard_map/ppermute | solution.py:551
  106.4 12.2 %collective-permute-start.30 = (bf16[128,1024]{1,0:T(8,128)(2,1)S(1)}, bf16[128,1024]{1,0:T(8,128)(2,1)S(1)}, u32[]{:S(2)}, u32[]{:S(2)}) collective-permute-start(bf16[128,1024]{1,0:T(8,128)(2,1)S(1)} %copy-done.11), channel_id=1, source_target_pairs={{0,6},{1,7},{2,4},{3,5},{4,2},{5,3},{6,0},{7,1},{8,14},{9,15},{10,... | collective-permute-start | bytes 786440 | tf_op jit(solution)/shard_map/ppermute | solution.py:551
  118.6 4.7 %collective-permute-start.36 = (bf16[64,5120]{1,0:T(8,128)(2,1)}, bf16[64,5120]{1,0:T(8,128)(2,1)S(1)}, u32[]{:S(2)}, u32[]{:S(2)}) collective-permute-start(bf16[64,5120]{1,0:T(8,128)(2,1)} %collective-permute-done.28.refs_9_), channel_id=1, source_target_pairs={{0,1},{1,0},{2,3},{3,2},{4,5},{5,4},{6,7},{7,6},{8,9},{9,8},{10,11... | collective-permute-start | bytes 1966088 | tf_op jit(solution)/shard_map/ppermute | solution.py:551
  118.7 4.7 %collective-permute-start.37 = (bf16[64,5120]{1,0:T(8,128)(2,1)}, bf16[64,5120]{1,0:T(8,128)(2,1)}, u32[]{:S(2)}, u32[]{:S(2)}) collective-permute-start(bf16[64,5120]{1,0:T(8,128)(2,1)} %collective-permute-done.29.refs_10_), channel_id=1, source_target_pairs={{0,1},{1,0},{2,3},{3,2},{4,5},{5,4},{6,7},{7,6},{8,9},{9,8},{10,11... | collective-permute-start | bytes 1966088 | tf_op jit(solution)/shard_map/ppermute | solution.py:551
  119.2 3.4 %collective-permute-start.33 = (bf16[32,5120]{1,0:T(8,128)(2,1)}, bf16[32,5120]{1,0:T(8,128)(2,1)S(1)}, u32[]{:S(2)}, u32[]{:S(2)}) collective-permute-start(bf16[32,5120]{1,0:T(8,128)(2,1)} %collective-permute-done.21.refs_6_), channel_id=1, source_target_pairs={{0,1},{1,0},{2,3},{3,2},{4,5},{5,4},{6,7},{7,6},{8,9},{9,8},{10,11... | collective-permute-start | bytes 983048 | tf_op jit(solution)/shard_map/ppermute | solution.py:551
  119.3 4.1 %collective-permute-start.34 = (bf16[32,5120]{1,0:T(8,128)(2,1)}, bf16[32,5120]{1,0:T(8,128)(2,1)S(1)}, u32[]{:S(2)}, u32[]{:S(2)}) collective-permute-start(bf16[32,5120]{1,0:T(8,128)(2,1)} %copy-done.35), channel_id=1, source_target_pairs={{0,1},{1,0},{2,3},{3,2},{4,5},{5,4},{6,7},{7,6},{8,9},{9,8},{10,11... | collective-permute-start | bytes 983048 | tf_op jit(solution)/shard_map/ppermute | solution.py:551
  119.7 3.6 %collective-permute-start.35 = (bf16[32,5120]{1,0:T(8,128)(2,1)S(1)}, bf16[32,5120]{1,0:T(8,128)(2,1)}, u32[]{:S(2)}, u32[]{:S(2)}) collective-permute-start(bf16[32,5120]{1,0:T(8,128)(2,1)S(1)} %collective-permute-done.24.refs_3_.refs_8_), channel_id=1, source_target_pairs={{0,1},{1,0},{2,3},{3,2},{4,5},{5,4},{6,7},{7,6},{8,9},{9,8},{10,11... | collective-permute-start | bytes 983048 | tf_op jit(solution)/shard_map/ppermute | solution.py:551
  124.1 32.4 %collective-permute-start.38 = (bf16[384,1024]{1,0:T(8,128)(2,1)S(1)}, bf16[384,1024]{1,0:T(8,128)(2,1)S(1)}, u32[]{:S(2)}, u32[]{:S(2)}) collective-permute-start(bf16[384,1024]{1,0:T(8,128)(2,1)S(1)} %glue.9.refs_25_), channel_id=1, source_target_pairs={{0,8},{8,0},{16,24},{24,16},{1,9},{9,1},{17,25},{25,17},{2,10},{10... | collective-permute-start | bytes 2359304 | tf_op jit(solution)/shard_map/ppermute | solution.py:551
  125.0 31.6 %collective-permute-start.39 = (bf16[384,1024]{1,0:T(8,128)(2,1)S(1)}, bf16[384,1024]{1,0:T(8,128)(2,1)S(1)}, u32[]{:S(2)}, u32[]{:S(2)}) collective-permute-start(bf16[384,1024]{1,0:T(8,128)(2,1)S(1)} %glue.9.refs_25_), channel_id=1, source_target_pairs={{0,16},{8,24},{16,0},{24,8},{1,17},{9,25},{17,1},{25,9},{2,18},{10... | collective-permute-start | bytes 2359304 | tf_op jit(solution)/shard_map/ppermute | solution.py:551
  126.1 30.4 %collective-permute-start.40 = (bf16[32,4096]{1,0:T(8,128)(2,1)}, bf16[32,4096]{1,0:T(8,128)(2,1)S(1)}, u32[]{:S(2)}, u32[]{:S(2)}) collective-permute-start(bf16[32,4096]{1,0:T(8,128)(2,1)} %copy-done.38), channel_id=1, source_target_pairs={{0,2},{1,3},{2,0},{3,1},{4,6},{5,7},{6,4},{7,5},{8,10},{9,11},{10,... | collective-permute-start | bytes 786440 | tf_op jit(solution)/shard_map/ppermute | solution.py:551
  127.8 28.8 %collective-permute-start.41 = (bf16[32,4096]{1,0:T(8,128)(2,1)}, bf16[32,4096]{1,0:T(8,128)(2,1)}, u32[]{:S(2)}, u32[]{:S(2)}) collective-permute-start(bf16[32,4096]{1,0:T(8,128)(2,1)} %copy-done.38), channel_id=1, source_target_pairs={{0,4},{1,5},{2,6},{3,7},{4,0},{5,1},{6,2},{7,3},{8,12},{9,13},{10,... | collective-permute-start | bytes 786440 | tf_op jit(solution)/shard_map/ppermute | solution.py:551
  128.6 28.0 %collective-permute-start.42 = (bf16[32,4096]{1,0:T(8,128)(2,1)}, bf16[32,4096]{1,0:T(8,128)(2,1)}, u32[]{:S(2)}, u32[]{:S(2)}) collective-permute-start(bf16[32,4096]{1,0:T(8,128)(2,1)} %copy-done.38), channel_id=1, source_target_pairs={{0,6},{1,7},{2,4},{3,5},{4,2},{5,3},{6,0},{7,1},{8,14},{9,15},{10,... | collective-permute-start | bytes 786440 | tf_op jit(solution)/shard_map/ppermute | solution.py:551
  156.6 7.1 %collective-permute-start.43 = (bf16[384,1024]{1,0:T(8,128)(2,1)S(1)}, bf16[384,1024]{1,0:T(8,128)(2,1)S(1)}, u32[]{:S(2)}, u32[]{:S(2)}) collective-permute-start(bf16[384,1024]{1,0:T(8,128)(2,1)S(1)} %glue.9.refs_25_), channel_id=1, source_target_pairs={{0,1},{1,0},{2,3},{3,2},{4,5},{5,4},{6,7},{7,6},{8,9},{9,8},{10,11... | collective-permute-start | bytes 2359304 | tf_op jit(solution)/shard_map/ppermute | solution.py:551
  156.7 7.0 %collective-permute-start.44 = (bf16[384,1024]{1,0:T(8,128)(2,1)S(1)}, bf16[384,1024]{1,0:T(8,128)(2,1)S(1)}, u32[]{:S(2)}, u32[]{:S(2)}) collective-permute-start(bf16[384,1024]{1,0:T(8,128)(2,1)S(1)} %collective-permute-done.38.refs_26_), channel_id=1, source_target_pairs={{0,1},{1,0},{2,3},{3,2},{4,5},{5,4},{6,7},{7,6},{8,9},{9,8},{10,11... | collective-permute-start | bytes 2359304 | tf_op jit(solution)/shard_map/ppermute | solution.py:551
  157.2 6.5 %collective-permute-start.45 = (bf16[384,1024]{1,0:T(8,128)(2,1)S(1)}, bf16[384,1024]{1,0:T(8,128)(2,1)S(1)}, u32[]{:S(2)}, u32[]{:S(2)}) collective-permute-start(bf16[384,1024]{1,0:T(8,128)(2,1)S(1)} %collective-permute-done.39.refs_27_), channel_id=1, source_target_pairs={{0,1},{1,0},{2,3},{3,2},{4,5},{5,4},{6,7},{7,6},{8,9},{9,8},{10,11... | collective-permute-start | bytes 2359304 | tf_op jit(solution)/shard_map/ppermute | solution.py:551
  157.3 4.3 %collective-permute-start.46 = (bf16[32,4096]{1,0:T(8,128)(2,1)S(1)}, bf16[32,4096]{1,0:T(8,128)(2,1)S(1)}, u32[]{:S(2)}, u32[]{:S(2)}) collective-permute-start(bf16[32,4096]{1,0:T(8,128)(2,1)S(1)} %copy-done.39), channel_id=1, source_target_pairs={{0,1},{1,0},{2,3},{3,2},{4,5},{5,4},{6,7},{7,6},{8,9},{9,8},{10,11... | collective-permute-start | bytes 786440 | tf_op jit(solution)/shard_map/ppermute | solution.py:551
  157.7 4.3 %collective-permute-start.47 = (bf16[32,4096]{1,0:T(8,128)(2,1)S(1)}, bf16[32,4096]{1,0:T(8,128)(2,1)S(1)}, u32[]{:S(2)}, u32[]{:S(2)}) collective-permute-start(bf16[32,4096]{1,0:T(8,128)(2,1)S(1)} %collective-permute-done.40.refs_29_), channel_id=1, source_target_pairs={{0,1},{1,0},{2,3},{3,2},{4,5},{5,4},{6,7},{7,6},{8,9},{9,8},{10,11... | collective-permute-start | bytes 786440 | tf_op jit(solution)/shard_map/ppermute | solution.py:551
  (47 other events, 759.8 us)

commit v4 on v3

--- a/solution.py
+++ b/solution.py
@@ -75,17 +75,21 @@
 
 ANYWHERE = pl.BlockSpec(memory_space=pl.ANY)
 
-def pack_body(qkv_ref, out_ref, in_ref, down_ref, own_ref, feed_ref):
+def pack_body(qkv_ref, out_ref, in_ref, down_ref, own_ref, feed_ref, sem):
     height = qkv_ref.shape[0]
-    at = 0
+    copies, at = [], 0
     for ref in (qkv_ref, out_ref, in_ref):
-        own_ref[:, at : at + ref.shape[1]] = ref[...]
+        copies.append(pltpu.make_async_copy(ref, own_ref.at[:, pl.ds(at, ref.shape[1])], sem))
         at += ref.shape[1]
     for first in range(0, down_ref.shape[0], height):
-        own_ref[:, at : at + down_ref.shape[1]] = down_ref[first : first + height, :]
+        window = down_ref.at[pl.ds(first, height)]
+        copies.append(pltpu.make_async_copy(window, own_ref.at[:, pl.ds(at, down_ref.shape[1])], sem))
         at += down_ref.shape[1]
-    feed_ref[:, : out_ref.shape[1]] = out_ref[...]
-    feed_ref[:, out_ref.shape[1] :] = in_ref[...]
+    for copy in copies:
+        copy.start()
+    settle(own_ref, sem)
+    first = qkv_ref.shape[1]
+    feed_ref[...] = own_ref[:, first : first + feed_ref.shape[1]]
 
 
 def pack(w_qkv, w_out, w_in, w_down):
@@ -95,7 +99,9 @@
     return pl.pallas_call(
         pack_body,
         out_shape=(shape_of((height, wide), BF), shape_of((height, feed_wide), BF)),
-        compiler_params=params(20),
+        in_specs=[ANYWHERE] * 4,
+        scratch_shapes=[pltpu.SemaphoreType.DMA],
+        compiler_params=params(),
         name="pack",
     )(w_qkv, w_out, w_in, w_down)
 
@@ -312,11 +318,14 @@
     )(scalars, rows, context, vectors, bias_in, *arrays_of(sources))
 
 
+TURN = 256
+
+
 def turn_body(
-    seqs, feed_tags, down_tags, len_ref, gl_ref, u_ref, s_ref, c_ref, vec_ref, gp_any, r_any, *refs
+    seqs, feed_tags, down_tags, len_ref, gl_ref, u_ref, s_ref, c_ref, vec_ref, gp_any, *refs
 ):
     feeds, downs = tagged(refs, feed_tags), tagged(refs[len(feed_tags) :], down_tags)
-    y_ref, dh_ref, do_ref, gv_ref, gi_ref, out, buf, down, gp_ref, r_ref, sems, gp_sems = refs[-12:]
+    y_ref, dh_ref, do_ref, gv_ref, gi_ref, out, buf, down, gp_ref, sems, gp_sems = refs[-11:]
     index = pl.program_id(0)
     first = index == 0
     width = u_ref.shape[1]
@@ -325,10 +334,9 @@
     step = wide // parts
     steps = gp_ref.shape[0]
     slopes = [
-        pltpu.make_async_copy(gp_any.at[pl.ds(n * ROWS, ROWS)], gp_ref.at[n], gp_sems.at[n])
+        pltpu.make_async_copy(gp_any.at[pl.ds(n * TURN, TURN)], gp_ref.at[n], gp_sems.at[n])
         for n in range(steps)
     ]
-    inverse = pltpu.make_async_copy(r_any, r_ref, sems.at[3])
 
     @pl.when(first)
     def _():
@@ -339,7 +347,6 @@
         issue(feeds, out, sems.at[2], place, width // 32)
         for copy in slopes[1:]:
             copy.start()
-        inverse.start()
         gv_ref[...] = jnp.zeros_like(gv_ref)
         gi_ref[...] = jnp.zeros_like(gi_ref)
         settle(down, sems.at[0])
@@ -351,9 +358,9 @@
     spread = lax.rsqrt(jnp.mean(centered * centered, axis=1, keepdims=True) + LN_EPS)
     hat = centered * spread
     y_ref[...] = (hat * gain_two + beta_two).astype(BF)
-    per_seq = L // ROWS
-    start = lax.rem(index, per_seq) * ROWS
-    live = lax.broadcasted_iota(jnp.int32, (ROWS, 1), 0) + start < len_ref[index // per_seq]
+    per_seq = L // TURN
+    start = lax.rem(index, per_seq) * TURN
+    live = lax.broadcasted_iota(jnp.int32, (TURN, 1), 0) + start < len_ref[index // per_seq]
     dy = jnp.where(live, c_ref[...].astype(F32), 0.0)
     gv_ref[4:5, :] += jnp.sum(dy, axis=0, keepdims=True)
     scaled = dy * gain_two
@@ -386,22 +393,17 @@
     d_att = d_one.astype(BF)
     gv_ref[1:2, :] += jnp.sum(d_att.astype(F32), axis=0, keepdims=True)
 
-    @pl.when(first)
-    def _():
-        settle(out, sems.at[2])
-        inverse.wait()
-
-    d_context = dot(d_att, out[...], 1, 1).astype(BF).astype(F32)
-    gv_ref[0:1, :] += jnp.sum(d_context, axis=0, keepdims=True)
-    rows = pl.ds(pl.multiple_of(index * ROWS, ROWS), ROWS)
-    do_ref[...] = (d_context * r_ref[rows, :]).astype(BF)
-
-
-def turn(scalars, seqs, gl, gp, normed, spread, inverse, cotangent, feeds, downs, vectors):
+    pl.when(first)(functools.partial(settle, out, sems.at[2]))
+    d_context = dot(d_att, out[...], 1, 1).astype(BF)
+    do_ref[...] = d_context
+    gv_ref[0:1, :] += jnp.sum(d_context.astype(F32), axis=0, keepdims=True)
+
+
+def turn(scalars, seqs, gl, gp, normed, spread, cotangent, feeds, downs, vectors):
     count, width = normed.shape
     wide = gl.shape[1]
-    steps = count // ROWS
-    block = lambda cols: pl.BlockSpec((ROWS, cols), lambda i, n: (i, 0))
+    steps = count // TURN
+    block = lambda cols: pl.BlockSpec((TURN, cols), lambda i, n: (i, 0))
     return pl.pallas_call(
         functools.partial(turn_body, seqs, tags_of(feeds), tags_of(downs)),
         out_shape=(
@@ -420,7 +422,7 @@
                 block(128),
                 block(width),
                 pl.BlockSpec((8, width), lambda i, n: (0, 0)),
-                *([ANYWHERE] * (2 + len(feeds) + len(downs))),
+                *([ANYWHERE] * (1 + len(feeds) + len(downs))),
             ],
             out_specs=[
                 block(width),
@@ -433,9 +435,8 @@
                 pltpu.VMEM((width, width), BF),
                 pltpu.VMEM((width, wide), BF),
                 pltpu.VMEM((wide, width), BF),
-                pltpu.VMEM((steps, ROWS, wide), BF),
-                pltpu.VMEM((count, width), F32),
-                pltpu.SemaphoreType.DMA((4,)),
+                pltpu.VMEM((steps, TURN, wide), BF),
+                pltpu.SemaphoreType.DMA((3,)),
                 pltpu.SemaphoreType.DMA((steps,)),
             ],
         ),
@@ -443,12 +444,15 @@
         cost_estimate=cost(2 * count * width * (width + 3 * wide)),
         name="turn",
     )(
-        scalars, gl, normed, spread, cotangent, vectors, gp, inverse, *arrays_of(feeds), *arrays_of(downs)
+        scalars, gl, normed, spread, cotangent, vectors, gp, *arrays_of(feeds), *arrays_of(downs)
     )
 
 
+WIDE = 512
+
+
 def back_body(
-    seqs, tags, len_ref, q_ref, k_ref, v_ref, o_ref, do_ref, e_ref, dh_ref, *refs
+    seqs, tags, len_ref, q_ref, k_ref, v_ref, o_ref, do_ref, r_ref, e_ref, dh_ref, *refs
 ):
     sources, (dx_ref, gq_ref, all_ref, w_ref, sem) = tagged(refs, tags), refs[len(tags) :]
     seq, quad = pl.program_id(0), pl.program_id(1)
@@ -463,9 +467,10 @@
     halves = lane_halves(BF)
     halves_wide = lane_halves(F32)
     lane = lax.broadcasted_iota(jnp.int32, (L, 128), 1)
-    for pair in range(QUAD // 128):
+    for pair in range(WIDE // 128):
         part = slice(pair * 128, (pair + 1) * 128)
-        q_pair, k_pair, v_pair, do_pair = (r[:, part] for r in (q_ref, k_ref, v_ref, do_ref))
+        q_pair, k_pair, v_pair = (r[:, part] for r in (q_ref, k_ref, v_ref))
+        do_pair = (do_ref[:, part].astype(F32) * r_ref[:, part]).astype(BF)
         products = do_pair.astype(F32) * o_ref[:, part].astype(F32)
         shifts = [jnp.sum(products * half, axis=1, keepdims=True) for half in halves_wide]
         rough = [shift.astype(BF).astype(F32) for shift in shifts]
@@ -493,7 +498,7 @@
             d_values.append(dot(do_turned[rows], power, 1, 0))
         right = jnp.concatenate([k_pair * half for half in halves], axis=0)
         d_query = (dot(jnp.concatenate(d_scores, axis=1), right, 1, 0) * (HD**-0.5)).astype(BF)
-        cols = pl.multiple_of(quad * QUAD + pair * 128, 128)
+        cols = pl.multiple_of(quad * WIDE + pair * 128, 128)
         gq_ref[:, pl.ds(cols, 128)] += jnp.sum(d_query.astype(F32), axis=0, keepdims=True)
         all_ref[:, pl.ds(cols, 128)] = d_query
         all_ref[:, pl.ds(width + cols, 128)] = jnp.concatenate(d_keys, axis=0).T.astype(BF)
@@ -506,11 +511,11 @@
         dx_ref[...] = (dh_ref[...] + dot(all_ref[...], w_ref[...], 1, 1)).astype(BF)
 
 
-def back(scalars, seqs, qkv, context, d_context, powers, d_joined, sources):
+def back(scalars, seqs, qkv, context, d_context, inverse, powers, d_joined, sources):
     count, width = d_joined.shape
-    quads = width // QUAD
-    heads = QUAD // HD
-    col = lambda n: pl.BlockSpec((L, QUAD), lambda i, j, s: (i, n * quads + j))
+    quads = width // WIDE
+    heads = WIDE // HD
+    col = lambda n: pl.BlockSpec((L, WIDE), lambda i, j, s: (i, n * quads + j))
     return pl.pallas_call(
         functools.partial(back_body, seqs, tags_of(sources)),
         out_shape=(shape_of((count, width), BF), shape_of((1, width), F32)),
@@ -523,6 +528,7 @@
                 col(2),
                 col(0),
                 col(0),
+                col(0),
                 pl.BlockSpec((heads, L, L), lambda i, j, s: (i * quads + j, 0, 0)),
                 pl.BlockSpec((L, width), lambda i, j, s: (i, 0)),
                 *([ANYWHERE] * len(sources)),
@@ -540,7 +546,7 @@
         compiler_params=params(),
         cost_estimate=cost(2 * count * width * 3 * width + 20 * count * width * L),
         name="back",
-    )(scalars, qkv, qkv, qkv, context, d_context, powers, d_joined, *arrays_of(sources))
+    )(scalars, qkv, qkv, qkv, context, d_context, inverse, powers, d_joined, *arrays_of(sources))
 
 
 BOTH = ("dp", "fsdp")
@@ -549,6 +555,10 @@
 def hop(block, axis, flip):
     size = lax.axis_size(axis)
     return lax.ppermute(block, axis, [(i, i ^ flip) for i in range(size)])
+
+
+def after_all(*values):
+    return lax.optimization_barrier(values)
 
 
 def over_x(block):
@@ -619,6 +629,7 @@
         at_down = at_feed + w_feed.shape[1]
         z_one, z_two, z_three, near_x, near_y = stage("123xy", (w_qkv, w_qkv, w_qkv, own, own))
         tall, cols_feed = w_qkv.shape[0], w_feed.shape[1]
+        z_one, scalars, bias, scale, vectors = after_all(z_one, scalars, bias, scale, vectors)
         (far,) = glue(
             (z_one, z_two, z_three), (at_feed, *((n, 0, tall, 0) for n in range(3)))
         )
@@ -727,9 +738,9 @@
             [*near_core, *(over_core(block) for block, _ in mine)],
         )
     output, d_joined, d_context, sums, sum_in = turn(
-        scalars, seqs, gl, gp, normed, spread, inverse, cotangent, feed_parts, down_parts, vectors
+        scalars, seqs, gl, gp, normed, spread, cotangent, feed_parts, down_parts, vectors
     )
-    input_grad, sum_q = back(scalars, seqs, qkv, context, d_context, powers, d_joined, qkv_parts)
+    input_grad, sum_q = back(scalars, seqs, qkv, context, d_context, inverse, powers, d_joined, qkv_parts)
     devices = lax.axis_size("dp") * lax.axis_size("fsdp")
     parts = (sum_q[0], sums[0], sums[1], sums[2], sum_in[0], sums[3], sums[4])
     rows = jnp.concatenate([part.reshape(devices, -1) for part in parts], axis=1)

time: 259 us -> 254 us (0.981)
  waiting for transfers between devices: 51.6 us -> 48.8 us
    ppermute x50, waiting for transfers between devices: 51.6 us -> 48.8 us  [hop(): return lax.ppermute(block, axis, [(i, i ^ flip) for i in range(size)])]
    unnamed x90 -> x76, local copies, waits for them, and re-layouts: 6.75 us -> 4.85 us
  transfers between devices with their start and end apart: 50 -> 50, of which waited for: 15 -> 16; matrix products, arithmetic and copies ran while one was open for 1% -> 2% of each run, Pallas kernels for 23% -> 24%
where the time goes in v4:
time: 254 us; the launch traced here: 253 us
  Pallas kernels  139 us (55%)
  waiting for transfers between devices  48.8 us (19%)
  starting transfers between devices  41.7 us (16%)
  blocking collectives  10.1 us (4%)
  local copies, waits for them, and re-layouts  8.51 us (3%)
  other arithmetic  3.94 us (2%)
    ppermute x50, waiting for transfers between devices, hop(): return lax.ppermute(block, axis, [(i, i ^ flip) for i in range(size)])  48.8 us
    pallas_call x1, Pallas kernels, turn(): pl.pallas_call(functools.partial(turn_body, seqs, tags_of(feeds), tags_of...  44.2 us
    ppermute x50, starting transfers between devices, hop(): return lax.ppermute(block, axis, [(i, i ^ flip) for i in range(size)])  41.7 us
    pallas_call x1, Pallas kernels, back(): pl.pallas_call(functools.partial(back_body, seqs, tags_of(sources)), out_...  31.9 us
    pallas_call x1, Pallas kernels, join(): pl.pallas_call(functools.partial(join_body, seqs, tags_of(sources)), out_...  25.8 us
    pallas_call x2, Pallas kernels, attend(): pl.pallas_call(functools.partial(attend_body, seq), out_shape=(shape_of((...  20.5 us
    pallas_call x1, Pallas kernels, project(): pl.pallas_call(functools.partial(project_body, seqs, tags_of(sources)), o...  12.4 us
    all_to_all x1, blocking collectives, on_device(): mine = jnp.sum(lax.all_to_all(rows, BOTH, 0, 0, tiled=True), axis=0)  10.1 us
  transfers between devices with their start and end apart: 50, of which 16 were waited for; matrix products, arithmetic and copies ran while one was open for 2% of the time, Pallas kernels for 24%

profile of v4, /device:TPU:0, one launch (start us, length us, event | category | flops | bytes accessed | tf_op | source)
XLA Modules:
  0.0 253.2 jit_solution(4144308249624870179)
XLA Ops:
  0.6 2.1 pack.1
  2.7 3.0 %collective-permute-start.3 = (bf16[32,12288]{1,0:T(8,128)(2,1)}, bf16[32,12288]{1,0:T(8,128)(2,1)S(1)}, u32[]{:S(2)}, u32[]{:S(2)}) collective-permute-start(bf16[32,12288]{1,0:T(8,128)(2,1)} %get-tuple-element.151.refs_0_.refs_22_), channel_id=1, source_target_pairs={{0,8},{8,0},{16,24},{24,16},{1,9},{9,1},{17,25},{25,17},{2,10},{10... | collective-permute-start | bytes 2359304 | tf_op jit(solution)/shard_map/ppermute | solution.py:557
  5.7 1.5 collective-permute-start.4
  7.3 1.6 collective-permute-start
  8.8 2.6 %collective-permute-start.1 = (bf16[32,3072]{1,0:T(8,128)(2,1)}, bf16[32,3072]{1,0:T(8,128)(2,1)S(1)}, u32[]{:S(2)}, u32[]{:S(2)}) collective-permute-start(bf16[32,3072]{1,0:T(8,128)(2,1)} %qkv_ref.1), channel_id=1, source_target_pairs={{0,4},{1,5},{2,6},{3,7},{4,0},{5,1},{6,2},{7,3},{8,12},{9,13},{10,... | collective-permute-start | bytes 589832 | tf_op jit(solution)/shard_map/ppermute | solution.py:557
  11.7 1.4 stack.43.vec_ref
  13.1 1.2 pad_add_fusion.len_ref
  14.3 1.3 pad_maximum_fusion
  15.6 0.8 collective-permute-done.refs_0_
  16.4 9.8 %collective-permute-done.1.refs_1_ = bf16[32,3072]{1,0:T(8,128)(2,1)S(1)} collective-permute-done((bf16[32,3072]{1,0:T(8,128)(2,1)}, bf16[32,3072]{1,0:T(8,128)(2,1)S(1)}, u32[]{:S(2)}, u32[]{:S(2)}) %collective-permute-start.1) | collective-permute-done | bytes 196640 | tf_op jit(solution)/shard_map/ppermute | solution.py:557
  27.9 3.8 %collective-permute-start.7 = (bf16[32,5120]{1,0:T(8,128)(2,1)}, bf16[32,5120]{1,0:T(8,128)(2,1)S(1)}, u32[]{:S(2)}, u32[]{:S(2)}) collective-permute-start(bf16[32,5120]{1,0:T(8,128)(2,1)} %get-tuple-element.181), channel_id=1, source_target_pairs={{0,4},{1,5},{2,6},{3,7},{4,0},{5,1},{6,2},{7,3},{8,12},{9,13},{10,... | collective-permute-start | bytes 983048 | tf_op jit(solution)/shard_map/ppermute | solution.py:557
  31.7 14.6 %collective-permute-done.7.refs_1_ = bf16[32,5120]{1,0:T(8,128)(2,1)S(1)} collective-permute-done((bf16[32,5120]{1,0:T(8,128)(2,1)}, bf16[32,5120]{1,0:T(8,128)(2,1)S(1)}, u32[]{:S(2)}, u32[]{:S(2)}) %collective-permute-start.7) | collective-permute-done | bytes 327712 | tf_op jit(solution)/shard_map/ppermute | solution.py:557
  46.4 1.0 copy-done.11
  48.0 1.5 collective-permute-start.10
  49.5 1.5 collective-permute-start.11
  51.0 9.3 %collective-permute-done.12.refs_0_ = bf16[32,5120]{1,0:T(8,128)(2,1)S(1)} collective-permute-done((bf16[32,5120]{1,0:T(8,128)(2,1)}, bf16[32,5120]{1,0:T(8,128)(2,1)S(1)}, u32[]{:S(2)}, u32[]{:S(2)}) %collective-permute-start.12) | collective-permute-done | bytes 327712 | tf_op jit(solution)/shard_map/ppermute | solution.py:557
  61.5 0.9 glue.7
  62.4 1.5 collective-permute-done.17.refs_14_
  64.6 1.5 collective-permute-start.19
  66.6 2.4 collective-permute-start.21
  69.0 12.4 %project.1.q_ref.k_ref.v_ref = bf16[1024,3072]{1,0:T(8,128)(2,1)} custom-call(s32[5]{0:T(128)} %pad_add_fusion.len_ref, bf16[1024,1024]{1,0:T(8,128)(2,1)} %x_ref.2, f32[1,3072]{1,0:T(1,128)} %bitcast.13, f32[1,3072]{1,0:T(1,128)} %constant.37.clone.1.scale_ref, bf16[32,12288]{1,0:T(8,128)(2,1)} %get-tuple-element.151.refs_0_.refs_22_, ...), custom_call_target="tpu_custom_call" | custom-call | flops 6442450944 | tf_op jit(solution)/shard_map/project/pallas_call | solution.py:147
  81.6 1.2 collective-permute-done.20.refs_2_.refs_5_
  82.8 1.0 collective-permute-start.23
  84.3 1.5 collective-permute-start.25
  85.8 1.3 collective-permute-start.26
  87.1 0.8 collective-permute-start.27
  87.9 10.3 %attend.2 = (bf16[1024,1024]{1,0:T(8,128)(2,1)}, bf16[32,512,512]{2,1,0:T(8,128)(2,1)}, f32[1024,1024]{1,0:T(8,128)}) custom-call(s32[5]{0:T(128)} %pad_add_fusion.len_ref, bf16[1024,3072]{1,0:T(8,128)(2,1)} %project.1.q_ref.k_ref.v_ref, bf16[1024,3072]{1,0:T(8,128)(2,1)} %project.1.q_ref.k_ref.v_ref, bf16[1024,3072]{1,0:T(8,128)(2,1)} %project.1.q_ref.k_ref.v_ref), custom_call_target="tpu_custom_call" | custom-call | flops 4294967296 | tf_op jit(solution)/shard_map/attend/pallas_call | solution.py:220
  98.3 2.3 collective-permute-done.27.refs_1_
  100.6 0.9 glue.8
  101.6 1.5 collective-permute-start.28
  103.1 0.6 collective-permute-start.29
  104.3 1.6 collective-permute-start.30
  105.9 10.2 %attend.3 = (bf16[1024,1024]{1,0:T(8,128)(2,1)}, bf16[32,512,512]{2,1,0:T(8,128)(2,1)}, f32[1024,1024]{1,0:T(8,128)}) custom-call(s32[5]{0:T(128)} %pad_add_fusion.len_ref, bf16[1024,3072]{1,0:T(8,128)(2,1)} %project.1.q_ref.k_ref.v_ref, bf16[1024,3072]{1,0:T(8,128)(2,1)} %project.1.q_ref.k_ref.v_ref, ...), custom_call_target="tpu_custom_call", output_to_operand_aliasing={{0}: (4, {}), {1}: (5, {}), {2}: (6, {})} | custom-call | flops 4294967296 | tf_op jit(solution)/shard_map/attend/pallas_call | solution.py:220
  117.4 2.7 %collective-permute-done.33.refs_17_ = bf16[32,5120]{1,0:T(8,128)(2,1)S(1)} collective-permute-done((bf16[32,5120]{1,0:T(8,128)(2,1)}, bf16[32,5120]{1,0:T(8,128)(2,1)S(1)}, u32[]{:S(2)}, u32[]{:S(2)}) %collective-permute-start.33) | collective-permute-done | bytes 327712 | tf_op jit(solution)/shard_map/ppermute | solution.py:557
  120.1 0.8 collective-permute-done.34.refs_18_
  120.9 0.7 copy-done.28
  121.8 1.1 collective-permute-start.38
  122.9 1.4 collective-permute-start.39
  124.4 1.9 collective-permute-start.40
  126.5 2.3 collective-permute-start.42
  128.7 25.8 %join.1 = (f32[1024,1024]{1,0:T(8,128)}, f32[1024,128]{1,0:T(8,128)}, bf16[1024,4096]{1,0:T(8,128)(2,1)}, bf16[1024,4096]{1,0:T(8,128)(2,1)}) custom-call(s32[5]{0:T(128)} %pad_add_fusion.len_ref, bf16[1024,1024]{1,0:T(8,128)(2,1)} %x_ref.2, bf16[1024,1024]{1,0:T(8,128)(2,1)} %get-tuple-element.220.o_ref, f32[8,1024]{1,0:T(8,128)} %stack.43.vec_ref, ...), custom_call_target="tpu_custom_call" | custom-call | flops 10737418240 | tf_op jit(solution)/shard_map/join/pallas_call | solution.py:290
  156.6 2.2 collective-permute-done.46.refs_38_
  159.6 1.7 collective-permute-done.48.refs_40_
  161.8 0.9 copy-done.17
  163.2 44.2 %turn.1 = (bf16[1024,1024]{1,0:T(8,128)(2,1)}, f32[1024,1024]{1,0:T(8,128)}, bf16[1024,1024]{1,0:T(8,128)(2,1)}, f32[8,1024]{1,0:T(8,128)}, f32[1,4096]{1,0:T(1,128)}) custom-call(s32[5]{0:T(128)} %pad_add_fusion.len_ref, bf16[1024,4096]{1,0:T(8,128)(2,1)} %get-tuple-element.245.gl_ref, f32[1024,1024]{1,0:T(8,128)} %get-tuple-element.246.u_ref, ...), custom_call_target="tpu_custom_call" | custom-call | flops 27917287424 | tf_op jit(solution)/shard_map/turn/pallas_call | solution.py:407
  207.5 31.9 %back.1 = (bf16[1024,1024]{1,0:T(8,128)(2,1)}, f32[1,1024]{1,0:T(1,128)}) custom-call(s32[5]{0:T(128)} %pad_add_fusion.len_ref, bf16[1024,3072]{1,0:T(8,128)(2,1)} %project.1.q_ref.k_ref.v_ref, bf16[1024,3072]{1,0:T(8,128)(2,1)} %project.1.q_ref.k_ref.v_ref, bf16[1024,3072]{1,0:T(8,128)(2,1)} %project.1.q_ref.k_ref.v_ref, ...), custom_call_target="tpu_custom_call" | custom-call | flops 17179869184 | tf_op jit(solution)/shard_map/back/pallas_call | solution.py:519
  240.0 1.3 reduce.24
  241.9 10.1 %all_to_all.9 = f32[32,1,320]{2,1,0:T(1,128)S(1)} all-to-all(f32[32,1,320]{2,1,0:T(1,128)S(1)} %all_to_all.6), channel_id=1, replica_groups=mesh['dp'=4,'fsdp'=8] {'dp','fsdp'}, dimensions={0} | all-to-all | bytes 81920 | tf_op jit(solution)/shard_map/all_to_all | solution.py:747
  (160 shorter events, 13.9 us)
Async XLA Ops:
  2.7 23.5 %collective-permute-start.3 = (bf16[32,12288]{1,0:T(8,128)(2,1)}, bf16[32,12288]{1,0:T(8,128)(2,1)S(1)}, u32[]{:S(2)}, u32[]{:S(2)}) collective-permute-start(bf16[32,12288]{1,0:T(8,128)(2,1)} %get-tuple-element.151.refs_0_.refs_22_), channel_id=1, source_target_pairs={{0,8},{8,0},{16,24},{24,16},{1,9},{9,1},{17,25},{25,17},{2,10},{10... | collective-permute-start | bytes 2359304 | tf_op jit(solution)/shard_map/ppermute | solution.py:557
  5.7 20.5 %collective-permute-start.4 = (bf16[32,12288]{1,0:T(8,128)(2,1)}, bf16[32,12288]{1,0:T(8,128)(2,1)}, u32[]{:S(2)}, u32[]{:S(2)}) collective-permute-start(bf16[32,12288]{1,0:T(8,128)(2,1)} %get-tuple-element.151.refs_0_.refs_22_), channel_id=1, source_target_pairs={{0,16},{8,24},{16,0},{24,8},{1,17},{9,25},{17,1},{25,9},{2,18},{10... | collective-permute-start | bytes 2359304 | tf_op jit(solution)/shard_map/ppermute | solution.py:557
  7.3 9.2 %collective-permute-start = (bf16[32,3072]{1,0:T(8,128)(2,1)}, bf16[32,3072]{1,0:T(8,128)(2,1)S(1)}, u32[]{:S(2)}, u32[]{:S(2)}) collective-permute-start(bf16[32,3072]{1,0:T(8,128)(2,1)} %qkv_ref.1), channel_id=1, source_target_pairs={{0,2},{1,3},{2,0},{3,1},{4,6},{5,7},{6,4},{7,5},{8,10},{9,11},{10,... | collective-permute-start | bytes 589832 | tf_op jit(solution)/shard_map/ppermute | solution.py:557
  8.8 17.4 %collective-permute-start.1 = (bf16[32,3072]{1,0:T(8,128)(2,1)}, bf16[32,3072]{1,0:T(8,128)(2,1)S(1)}, u32[]{:S(2)}, u32[]{:S(2)}) collective-permute-start(bf16[32,3072]{1,0:T(8,128)(2,1)} %qkv_ref.1), channel_id=1, source_target_pairs={{0,4},{1,5},{2,6},{3,7},{4,0},{5,1},{6,2},{7,3},{8,12},{9,13},{10,... | collective-permute-start | bytes 589832 | tf_op jit(solution)/shard_map/ppermute | solution.py:557
  11.4 14.8 %collective-permute-start.2 = (bf16[32,3072]{1,0:T(8,128)(2,1)}, bf16[32,3072]{1,0:T(8,128)(2,1)S(1)}, u32[]{:S(2)}, u32[]{:S(2)}) collective-permute-start(bf16[32,3072]{1,0:T(8,128)(2,1)} %qkv_ref.1), channel_id=1, source_target_pairs={{0,6},{1,7},{2,4},{3,5},{4,2},{5,3},{6,0},{7,1},{8,14},{9,15},{10,... | collective-permute-start | bytes 589832 | tf_op jit(solution)/shard_map/ppermute | solution.py:557
  26.3 20.0 %collective-permute-start.8 = (bf16[32,12288]{1,0:T(8,128)(2,1)}, bf16[32,12288]{1,0:T(8,128)(2,1)S(1)}, u32[]{:S(2)}, u32[]{:S(2)}) collective-permute-start(bf16[32,12288]{1,0:T(8,128)(2,1)} %get-tuple-element.151.refs_0_.refs_22_), channel_id=1, source_target_pairs={{0,1},{1,0},{2,3},{3,2},{4,5},{5,4},{6,7},{7,6},{8,9},{9,8},{10,11... | collective-permute-start | bytes 2359304 | tf_op jit(solution)/shard_map/ppermute | solution.py:557
  26.4 21.0 %collective-permute-start.9 = (bf16[32,12288]{1,0:T(8,128)(2,1)S(1)}, bf16[32,12288]{1,0:T(8,128)(2,1)}, u32[]{:S(2)}, u32[]{:S(2)}) collective-permute-start(bf16[32,12288]{1,0:T(8,128)(2,1)S(1)} %collective-permute-done.3.refs_0_.refs_2_.refs_1_.refs_23_), channel_id=1, source_target_pairs={{0,1},{1,0},{2,3},{3,2},{4,5},{5,4},{6,7},{7,6},{8,9},{9,8},{10,11... | collective-permute-start | bytes 2359304 | tf_op jit(solution)/shard_map/ppermute | solution.py:557
  26.9 19.5 %collective-permute-start.5 = (bf16[96,3072]{1,0:T(8,128)(2,1)S(1)}, bf16[96,3072]{1,0:T(8,128)(2,1)S(1)}, u32[]{:S(2)}, u32[]{:S(2)}) collective-permute-start(bf16[96,3072]{1,0:T(8,128)(2,1)S(1)} %glue.5.refs_3_), channel_id=1, source_target_pairs={{0,8},{8,0},{16,24},{24,16},{1,9},{9,1},{17,25},{25,17},{2,10},{10... | collective-permute-start | bytes 1769480 | tf_op jit(solution)/shard_map/ppermute | solution.py:557
  27.4 18.9 %collective-permute-start.6 = (bf16[96,3072]{1,0:T(8,128)(2,1)S(1)}, bf16[96,3072]{1,0:T(8,128)(2,1)S(1)}, u32[]{:S(2)}, u32[]{:S(2)}) collective-permute-start(bf16[96,3072]{1,0:T(8,128)(2,1)S(1)} %glue.5.refs_3_), channel_id=1, source_target_pairs={{0,16},{8,24},{16,0},{24,8},{1,17},{9,25},{17,1},{25,9},{2,18},{10... | collective-permute-start | bytes 1769480 | tf_op jit(solution)/shard_map/ppermute | solution.py:557
  27.9 18.4 %collective-permute-start.7 = (bf16[32,5120]{1,0:T(8,128)(2,1)}, bf16[32,5120]{1,0:T(8,128)(2,1)S(1)}, u32[]{:S(2)}, u32[]{:S(2)}) collective-permute-start(bf16[32,5120]{1,0:T(8,128)(2,1)} %get-tuple-element.181), channel_id=1, source_target_pairs={{0,4},{1,5},{2,6},{3,7},{4,0},{5,1},{6,2},{7,3},{8,12},{9,13},{10,... | collective-permute-start | bytes 983048 | tf_op jit(solution)/shard_map/ppermute | solution.py:557
  47.4 13.0 %collective-permute-start.13 = (bf16[32,12288]{1,0:T(8,128)(2,1)}, bf16[32,12288]{1,0:T(8,128)(2,1)S(1)}, u32[]{:S(2)}, u32[]{:S(2)}) collective-permute-start(bf16[32,12288]{1,0:T(8,128)(2,1)} %collective-permute-done.4.refs_2_.refs_24_), channel_id=1, source_target_pairs={{0,1},{1,0},{2,3},{3,2},{4,5},{5,4},{6,7},{7,6},{8,9},{9,8},{10,11... | collective-permute-start | bytes 2359304 | tf_op jit(solution)/shard_map/ppermute | solution.py:557
  47.5 12.9 %collective-permute-start.14 = (bf16[96,3072]{1,0:T(8,128)(2,1)S(1)}, bf16[96,3072]{1,0:T(8,128)(2,1)S(1)}, u32[]{:S(2)}, u32[]{:S(2)}) collective-permute-start(bf16[96,3072]{1,0:T(8,128)(2,1)S(1)} %glue.5.refs_3_), channel_id=1, source_target_pairs={{0,1},{1,0},{2,3},{3,2},{4,5},{5,4},{6,7},{7,6},{8,9},{9,8},{10,11... | collective-permute-start | bytes 1769480 | tf_op jit(solution)/shard_map/ppermute | solution.py:557
  48.0 12.4 %collective-permute-start.10 = (bf16[64,3072]{1,0:T(8,128)(2,1)S(1)}, bf16[64,3072]{1,0:T(8,128)(2,1)S(1)}, u32[]{:S(2)}, u32[]{:S(2)}) collective-permute-start(bf16[64,3072]{1,0:T(8,128)(2,1)S(1)} %get-tuple-element.161), channel_id=1, source_target_pairs={{0,16},{8,24},{16,0},{24,8},{1,17},{9,25},{17,1},{25,9},{2,18},{10... | collective-permute-start | bytes 1179656 | tf_op jit(solution)/shard_map/ppermute | solution.py:557
  49.5 10.8 %collective-permute-start.11 = (bf16[64,3072]{1,0:T(8,128)(2,1)S(1)}, bf16[64,3072]{1,0:T(8,128)(2,1)S(1)}, u32[]{:S(2)}, u32[]{:S(2)}) collective-permute-start(bf16[64,3072]{1,0:T(8,128)(2,1)S(1)} %get-tuple-element.162), channel_id=1, source_target_pairs={{0,8},{8,0},{16,24},{24,16},{1,9},{9,1},{17,25},{25,17},{2,10},{10... | collective-permute-start | bytes 1179656 | tf_op jit(solution)/shard_map/ppermute | solution.py:557
  51.0 9.3 %collective-permute-start.12 = (bf16[32,5120]{1,0:T(8,128)(2,1)}, bf16[32,5120]{1,0:T(8,128)(2,1)S(1)}, u32[]{:S(2)}, u32[]{:S(2)}) collective-permute-start(bf16[32,5120]{1,0:T(8,128)(2,1)} %get-tuple-element.181), channel_id=1, source_target_pairs={{0,2},{1,3},{2,0},{3,1},{4,6},{5,7},{6,4},{7,5},{8,10},{9,11},{10,... | collective-permute-start | bytes 983048 | tf_op jit(solution)/shard_map/ppermute | solution.py:557
  60.4 4.0 %collective-permute-start.15 = (bf16[96,3072]{1,0:T(8,128)(2,1)S(1)}, bf16[96,3072]{1,0:T(8,128)(2,1)S(1)}, u32[]{:S(2)}, u32[]{:S(2)}) collective-permute-start(bf16[96,3072]{1,0:T(8,128)(2,1)S(1)} %collective-permute-done.5.refs_1_.refs_4_), channel_id=1, source_target_pairs={{0,1},{1,0},{2,3},{3,2},{4,5},{5,4},{6,7},{7,6},{8,9},{9,8},{10,11... | collective-permute-start | bytes 1769480 | tf_op jit(solution)/shard_map/ppermute | solution.py:557
  60.5 4.0 %collective-permute-start.16 = (bf16[96,3072]{1,0:T(8,128)(2,1)S(1)}, bf16[96,3072]{1,0:T(8,128)(2,1)S(1)}, u32[]{:S(2)}, u32[]{:S(2)}) collective-permute-start(bf16[96,3072]{1,0:T(8,128)(2,1)S(1)} %collective-permute-done.6.refs_2_.refs_5_), channel_id=1, source_target_pairs={{0,1},{1,0},{2,3},{3,2},{4,5},{5,4},{6,7},{7,6},{8,9},{9,8},{10,11... | collective-permute-start | bytes 1769480 | tf_op jit(solution)/shard_map/ppermute | solution.py:557
  61.0 2.9 %collective-permute-start.17 = (bf16[64,3072]{1,0:T(8,128)(2,1)S(1)}, bf16[64,3072]{1,0:T(8,128)(2,1)S(1)}, u32[]{:S(2)}, u32[]{:S(2)}) collective-permute-start(bf16[64,3072]{1,0:T(8,128)(2,1)S(1)} %collective-permute-done.10.refs_6_), channel_id=1, source_target_pairs={{0,1},{1,0},{2,3},{3,2},{4,5},{5,4},{6,7},{7,6},{8,9},{9,8},{10,11... | collective-permute-start | bytes 1179656 | tf_op jit(solution)/shard_map/ppermute | solution.py:557
  61.5 2.9 %collective-permute-start.18 = (bf16[64,3072]{1,0:T(8,128)(2,1)S(1)}, bf16[64,3072]{1,0:T(8,128)(2,1)S(1)}, u32[]{:S(2)}, u32[]{:S(2)}) collective-permute-start(bf16[64,3072]{1,0:T(8,128)(2,1)S(1)} %collective-permute-done.11.refs_7_), channel_id=1, source_target_pairs={{0,1},{1,0},{2,3},{3,2},{4,5},{5,4},{6,7},{7,6},{8,9},{9,8},{10,11... | collective-permute-start | bytes 1179656 | tf_op jit(solution)/shard_map/ppermute | solution.py:557
  64.6 17.0 %collective-permute-start.19 = (bf16[64,5120]{1,0:T(8,128)(2,1)}, bf16[64,5120]{1,0:T(8,128)(2,1)S(1)}, u32[]{:S(2)}, u32[]{:S(2)}) collective-permute-start(bf16[64,5120]{1,0:T(8,128)(2,1)} %get-tuple-element.182.refs_3_), channel_id=1, source_target_pairs={{0,8},{8,0},{16,24},{24,16},{1,9},{9,1},{17,25},{25,17},{2,10},{10... | collective-permute-start | bytes 1966088 | tf_op jit(solution)/shard_map/ppermute | solution.py:557
  66.1 16.7 %collective-permute-start.20 = (bf16[64,5120]{1,0:T(8,128)(2,1)}, bf16[64,5120]{1,0:T(8,128)(2,1)S(1)}, u32[]{:S(2)}, u32[]{:S(2)}) collective-permute-start(bf16[64,5120]{1,0:T(8,128)(2,1)} %get-tuple-element.182.refs_3_), channel_id=1, source_target_pairs={{0,16},{8,24},{16,0},{24,8},{1,17},{9,25},{17,1},{25,9},{2,18},{10... | collective-permute-start | bytes 1966088 | tf_op jit(solution)/shard_map/ppermute | solution.py:557
  66.6 16.2 %collective-permute-start.22 = (bf16[64,5120]{1,0:T(8,128)(2,1)}, bf16[64,5120]{1,0:T(8,128)(2,1)}, u32[]{:S(2)}, u32[]{:S(2)}) collective-permute-start(bf16[64,5120]{1,0:T(8,128)(2,1)} %get-tuple-element.182.refs_3_), channel_id=1, source_target_pairs={{0,1},{1,0},{2,3},{3,2},{4,5},{5,4},{6,7},{7,6},{8,9},{9,8},{10,11... | collective-permute-start | bytes 1966088 | tf_op jit(solution)/shard_map/ppermute | solution.py:557
  66.6 14.8 %collective-permute-start.21 = (bf16[32,5120]{1,0:T(8,128)(2,1)}, bf16[32,5120]{1,0:T(8,128)(2,1)}, u32[]{:S(2)}, u32[]{:S(2)}) collective-permute-start(bf16[32,5120]{1,0:T(8,128)(2,1)} %get-tuple-element.181), channel_id=1, source_target_pairs={{0,6},{1,7},{2,4},{3,5},{4,2},{5,3},{6,0},{7,1},{8,14},{9,15},{10,... | collective-permute-start | bytes 983048 | tf_op jit(solution)/shard_map/ppermute | solution.py:557
  82.8 17.8 %collective-permute-start.23 = (bf16[32,5120]{1,0:T(8,128)(2,1)}, bf16[32,5120]{1,0:T(8,128)(2,1)}, u32[]{:S(2)}, u32[]{:S(2)}) collective-permute-start(bf16[32,5120]{1,0:T(8,128)(2,1)} %collective-permute-done.21.refs_6_), channel_id=1, source_target_pairs={{0,8},{8,0},{16,24},{24,16},{1,9},{9,1},{17,25},{25,17},{2,10},{10... | collective-permute-start | bytes 983048 | tf_op jit(solution)/shard_map/ppermute | solution.py:557
  83.8 16.8 %collective-permute-start.24 = (bf16[32,5120]{1,0:T(8,128)(2,1)}, bf16[32,5120]{1,0:T(8,128)(2,1)S(1)}, u32[]{:S(2)}, u32[]{:S(2)}) collective-permute-start(bf16[32,5120]{1,0:T(8,128)(2,1)} %collective-permute-done.21.refs_6_), channel_id=1, source_target_pairs={{0,16},{8,24},{16,0},{24,8},{1,17},{9,25},{17,1},{25,9},{2,18},{10... | collective-permute-start | bytes 983048 | tf_op jit(solution)/shard_map/ppermute | solution.py:557
  84.3 14.0 %collective-permute-start.25 = (bf16[32,4096]{1,0:T(8,128)(2,1)S(1)}, bf16[32,4096]{1,0:T(8,128)(2,1)S(1)}, u32[]{:S(2)}, u32[]{:S(2)}) collective-permute-start(bf16[32,4096]{1,0:T(8,128)(2,1)S(1)} %get-tuple-element.192), channel_id=1, source_target_pairs={{0,16},{8,24},{16,0},{24,8},{1,17},{9,25},{17,1},{25,9},{2,18},{10... | collective-permute-start | bytes 786440 | tf_op jit(solution)/shard_map/ppermute | solution.py:557
  85.8 12.5 %collective-permute-start.26 = (bf16[128,1024]{1,0:T(8,128)(2,1)}, bf16[128,1024]{1,0:T(8,128)(2,1)S(1)}, u32[]{:S(2)}, u32[]{:S(2)}) collective-permute-start(bf16[128,1024]{1,0:T(8,128)(2,1)} %down_ref.1), channel_id=1, source_target_pairs={{0,2},{1,3},{2,0},{3,1},{4,6},{5,7},{6,4},{7,5},{8,10},{9,11},{10,... | collective-permute-start | bytes 786440 | tf_op jit(solution)/shard_map/ppermute | solution.py:557
  87.1 13.5 %collective-permute-start.27 = (bf16[128,1024]{1,0:T(8,128)(2,1)}, bf16[128,1024]{1,0:T(8,128)(2,1)S(1)}, u32[]{:S(2)}, u32[]{:S(2)}) collective-permute-start(bf16[128,1024]{1,0:T(8,128)(2,1)} %down_ref.1), channel_id=1, source_target_pairs={{0,4},{1,5},{2,6},{3,7},{4,0},{5,1},{6,2},{7,3},{8,12},{9,13},{10,... | collective-permute-start | bytes 786440 | tf_op jit(solution)/shard_map/ppermute | solution.py:557
  101.6 14.5 %collective-permute-start.28 = (bf16[64,5120]{1,0:T(8,128)(2,1)}, bf16[64,5120]{1,0:T(8,128)(2,1)}, u32[]{:S(2)}, u32[]{:S(2)}) collective-permute-start(bf16[64,5120]{1,0:T(8,128)(2,1)} %get-tuple-element.212), channel_id=1, source_target_pairs={{0,16},{8,24},{16,0},{24,8},{1,17},{9,25},{17,1},{25,9},{2,18},{10... | collective-permute-start | bytes 1966088 | tf_op jit(solution)/shard_map/ppermute | solution.py:557
  103.1 13.0 %collective-permute-start.29 = (bf16[64,5120]{1,0:T(8,128)(2,1)S(1)}, bf16[64,5120]{1,0:T(8,128)(2,1)}, u32[]{:S(2)}, u32[]{:S(2)}) collective-permute-start(bf16[64,5120]{1,0:T(8,128)(2,1)S(1)} %get-tuple-element.213), channel_id=1, source_target_pairs={{0,8},{8,0},{16,24},{24,16},{1,9},{9,1},{17,25},{25,17},{2,10},{10... | collective-permute-start | bytes 1966088 | tf_op jit(solution)/shard_map/ppermute | solution.py:557
  103.7 12.3 %collective-permute-start.31 = (bf16[64,5120]{1,0:T(8,128)(2,1)S(1)}, bf16[64,5120]{1,0:T(8,128)(2,1)S(1)}, u32[]{:S(2)}, u32[]{:S(2)}) collective-permute-start(bf16[64,5120]{1,0:T(8,128)(2,1)S(1)} %collective-permute-done.19.refs_1_.refs_4_), channel_id=1, source_target_pairs={{0,1},{1,0},{2,3},{3,2},{4,5},{5,4},{6,7},{7,6},{8,9},{9,8},{10,11... | collective-permute-start | bytes 1966088 | tf_op jit(solution)/shard_map/ppermute | solution.py:557
  103.8 12.4 %collective-permute-start.32 = (bf16[64,5120]{1,0:T(8,128)(2,1)S(1)}, bf16[64,5120]{1,0:T(8,128)(2,1)}, u32[]{:S(2)}, u32[]{:S(2)}) collective-permute-start(bf16[64,5120]{1,0:T(8,128)(2,1)S(1)} %collective-permute-done.20.refs_2_.refs_5_), channel_id=1, source_target_pairs={{0,1},{1,0},{2,3},{3,2},{4,5},{5,4},{6,7},{7,6},{8,9},{9,8},{10,11... | collective-permute-start | bytes 1966088 | tf_op jit(solution)/shard_map/ppermute | solution.py:557
  104.3 11.8 %collective-permute-start.30 = (bf16[128,1024]{1,0:T(8,128)(2,1)}, bf16[128,1024]{1,0:T(8,128)(2,1)S(1)}, u32[]{:S(2)}, u32[]{:S(2)}) collective-permute-start(bf16[128,1024]{1,0:T(8,128)(2,1)} %down_ref.1), channel_id=1, source_target_pairs={{0,6},{1,7},{2,4},{3,5},{4,2},{5,3},{6,0},{7,1},{8,14},{9,15},{10,... | collective-permute-start | bytes 786440 | tf_op jit(solution)/shard_map/ppermute | solution.py:557
  116.1 4.7 %collective-permute-start.36 = (bf16[64,5120]{1,0:T(8,128)(2,1)}, bf16[64,5120]{1,0:T(8,128)(2,1)S(1)}, u32[]{:S(2)}, u32[]{:S(2)}) collective-permute-start(bf16[64,5120]{1,0:T(8,128)(2,1)} %collective-permute-done.28.refs_9_), channel_id=1, source_target_pairs={{0,1},{1,0},{2,3},{3,2},{4,5},{5,4},{6,7},{7,6},{8,9},{9,8},{10,11... | collective-permute-start | bytes 1966088 | tf_op jit(solution)/shard_map/ppermute | solution.py:557
  116.2 5.4 %collective-permute-start.37 = (bf16[64,5120]{1,0:T(8,128)(2,1)}, bf16[64,5120]{1,0:T(8,128)(2,1)}, u32[]{:S(2)}, u32[]{:S(2)}) collective-permute-start(bf16[64,5120]{1,0:T(8,128)(2,1)} %collective-permute-done.29.refs_10_), channel_id=1, source_target_pairs={{0,1},{1,0},{2,3},{3,2},{4,5},{5,4},{6,7},{7,6},{8,9},{9,8},{10,11... | collective-permute-start | bytes 1966088 | tf_op jit(solution)/shard_map/ppermute | solution.py:557
  116.7 3.4 %collective-permute-start.33 = (bf16[32,5120]{1,0:T(8,128)(2,1)}, bf16[32,5120]{1,0:T(8,128)(2,1)S(1)}, u32[]{:S(2)}, u32[]{:S(2)}) collective-permute-start(bf16[32,5120]{1,0:T(8,128)(2,1)} %collective-permute-done.21.refs_6_), channel_id=1, source_target_pairs={{0,1},{1,0},{2,3},{3,2},{4,5},{5,4},{6,7},{7,6},{8,9},{9,8},{10,11... | collective-permute-start | bytes 983048 | tf_op jit(solution)/shard_map/ppermute | solution.py:557
  116.8 4.1 %collective-permute-start.34 = (bf16[32,5120]{1,0:T(8,128)(2,1)}, bf16[32,5120]{1,0:T(8,128)(2,1)S(1)}, u32[]{:S(2)}, u32[]{:S(2)}) collective-permute-start(bf16[32,5120]{1,0:T(8,128)(2,1)} %collective-permute-done.23.refs_7_), channel_id=1, source_target_pairs={{0,1},{1,0},{2,3},{3,2},{4,5},{5,4},{6,7},{7,6},{8,9},{9,8},{10,11... | collective-permute-start | bytes 983048 | tf_op jit(solution)/shard_map/ppermute | solution.py:557
  117.2 3.6 %collective-permute-start.35 = (bf16[32,5120]{1,0:T(8,128)(2,1)S(1)}, bf16[32,5120]{1,0:T(8,128)(2,1)S(1)}, u32[]{:S(2)}, u32[]{:S(2)}) collective-permute-start(bf16[32,5120]{1,0:T(8,128)(2,1)S(1)} %collective-permute-done.24.refs_3_.refs_8_), channel_id=1, source_target_pairs={{0,1},{1,0},{2,3},{3,2},{4,5},{5,4},{6,7},{7,6},{8,9},{9,8},{10,11... | collective-permute-start | bytes 983048 | tf_op jit(solution)/shard_map/ppermute | solution.py:557
  121.8 32.9 %collective-permute-start.38 = (bf16[384,1024]{1,0:T(8,128)(2,1)S(1)}, bf16[384,1024]{1,0:T(8,128)(2,1)S(1)}, u32[]{:S(2)}, u32[]{:S(2)}) collective-permute-start(bf16[384,1024]{1,0:T(8,128)(2,1)S(1)} %glue.9.refs_25_), channel_id=1, source_target_pairs={{0,8},{8,0},{16,24},{24,16},{1,9},{9,1},{17,25},{25,17},{2,10},{10... | collective-permute-start | bytes 2359304 | tf_op jit(solution)/shard_map/ppermute | solution.py:557
  122.9 31.7 %collective-permute-start.39 = (bf16[384,1024]{1,0:T(8,128)(2,1)S(1)}, bf16[384,1024]{1,0:T(8,128)(2,1)S(1)}, u32[]{:S(2)}, u32[]{:S(2)}) collective-permute-start(bf16[384,1024]{1,0:T(8,128)(2,1)S(1)} %glue.9.refs_25_), channel_id=1, source_target_pairs={{0,16},{8,24},{16,0},{24,8},{1,17},{9,25},{17,1},{25,9},{2,18},{10... | collective-permute-start | bytes 2359304 | tf_op jit(solution)/shard_map/ppermute | solution.py:557
  124.4 30.2 %collective-permute-start.40 = (bf16[32,4096]{1,0:T(8,128)(2,1)}, bf16[32,4096]{1,0:T(8,128)(2,1)S(1)}, u32[]{:S(2)}, u32[]{:S(2)}) collective-permute-start(bf16[32,4096]{1,0:T(8,128)(2,1)} %copy-done.30), channel_id=1, source_target_pairs={{0,2},{1,3},{2,0},{3,1},{4,6},{5,7},{6,4},{7,5},{8,10},{9,11},{10,... | collective-permute-start | bytes 786440 | tf_op jit(solution)/shard_map/ppermute | solution.py:557
  126.2 28.4 %collective-permute-start.41 = (bf16[32,4096]{1,0:T(8,128)(2,1)}, bf16[32,4096]{1,0:T(8,128)(2,1)S(1)}, u32[]{:S(2)}, u32[]{:S(2)}) collective-permute-start(bf16[32,4096]{1,0:T(8,128)(2,1)} %copy-done.30), channel_id=1, source_target_pairs={{0,4},{1,5},{2,6},{3,7},{4,0},{5,1},{6,2},{7,3},{8,12},{9,13},{10,... | collective-permute-start | bytes 786440 | tf_op jit(solution)/shard_map/ppermute | solution.py:557
  126.5 28.2 %collective-permute-start.42 = (bf16[32,4096]{1,0:T(8,128)(2,1)}, bf16[32,4096]{1,0:T(8,128)(2,1)S(1)}, u32[]{:S(2)}, u32[]{:S(2)}) collective-permute-start(bf16[32,4096]{1,0:T(8,128)(2,1)} %copy-done.30), channel_id=1, source_target_pairs={{0,6},{1,7},{2,4},{3,5},{4,2},{5,3},{6,0},{7,1},{8,14},{9,15},{10,... | collective-permute-start | bytes 786440 | tf_op jit(solution)/shard_map/ppermute | solution.py:557
  155.5 6.3 %collective-permute-start.43 = (bf16[384,1024]{1,0:T(8,128)(2,1)S(1)}, bf16[384,1024]{1,0:T(8,128)(2,1)S(1)}, u32[]{:S(2)}, u32[]{:S(2)}) collective-permute-start(bf16[384,1024]{1,0:T(8,128)(2,1)S(1)} %glue.9.refs_25_), channel_id=1, source_target_pairs={{0,1},{1,0},{2,3},{3,2},{4,5},{5,4},{6,7},{7,6},{8,9},{9,8},{10,11... | collective-permute-start | bytes 2359304 | tf_op jit(solution)/shard_map/ppermute | solution.py:557
  155.5 6.3 %collective-permute-start.44 = (bf16[384,1024]{1,0:T(8,128)(2,1)S(1)}, bf16[384,1024]{1,0:T(8,128)(2,1)S(1)}, u32[]{:S(2)}, u32[]{:S(2)}) collective-permute-start(bf16[384,1024]{1,0:T(8,128)(2,1)S(1)} %collective-permute-done.38.refs_26_), channel_id=1, source_target_pairs={{0,1},{1,0},{2,3},{3,2},{4,5},{5,4},{6,7},{7,6},{8,9},{9,8},{10,11... | collective-permute-start | bytes 2359304 | tf_op jit(solution)/shard_map/ppermute | solution.py:557
  156.0 5.8 %collective-permute-start.45 = (bf16[384,1024]{1,0:T(8,128)(2,1)S(1)}, bf16[384,1024]{1,0:T(8,128)(2,1)S(1)}, u32[]{:S(2)}, u32[]{:S(2)}) collective-permute-start(bf16[384,1024]{1,0:T(8,128)(2,1)S(1)} %collective-permute-done.39.refs_27_), channel_id=1, source_target_pairs={{0,1},{1,0},{2,3},{3,2},{4,5},{5,4},{6,7},{7,6},{8,9},{9,8},{10,11... | collective-permute-start | bytes 2359304 | tf_op jit(solution)/shard_map/ppermute | solution.py:557
  156.1 2.7 %collective-permute-start.46 = (bf16[32,4096]{1,0:T(8,128)(2,1)}, bf16[32,4096]{1,0:T(8,128)(2,1)S(1)}, u32[]{:S(2)}, u32[]{:S(2)}) collective-permute-start(bf16[32,4096]{1,0:T(8,128)(2,1)} %copy-done.30), channel_id=1, source_target_pairs={{0,1},{1,0},{2,3},{3,2},{4,5},{5,4},{6,7},{7,6},{8,9},{9,8},{10,11... | collective-permute-start | bytes 786440 | tf_op jit(solution)/shard_map/ppermute | solution.py:557
  156.5 3.0 %collective-permute-start.47 = (bf16[32,4096]{1,0:T(8,128)(2,1)}, bf16[32,4096]{1,0:T(8,128)(2,1)S(1)}, u32[]{:S(2)}, u32[]{:S(2)}) collective-permute-start(bf16[32,4096]{1,0:T(8,128)(2,1)} %copy-done.31), channel_id=1, source_target_pairs={{0,1},{1,0},{2,3},{3,2},{4,5},{5,4},{6,7},{7,6},{8,9},{9,8},{10,11... | collective-permute-start | bytes 786440 | tf_op jit(solution)/shard_map/ppermute | solution.py:557
  (40 other events, 390.0 us)

commit v5 on v4

--- a/solution.py
+++ b/solution.py
@@ -452,12 +452,16 @@
 
 
 def back_body(
-    seqs, tags, len_ref, q_ref, k_ref, v_ref, o_ref, do_ref, r_ref, e_ref, dh_ref, *refs
+    seqs, tags, len_ref, q_ref, k_ref, v_ref, o_ref, do_ref, r_ref, e_ref, dh_any, *refs
 ):
-    sources, (dx_ref, gq_ref, all_ref, w_ref, sem) = tagged(refs, tags), refs[len(tags) :]
+    sources = tagged(refs, tags)
+    dx_ref, gq_ref, all_ref, w_ref, dh_ref, sem, dh_sem = refs[len(tags) :]
     seq, quad = pl.program_id(0), pl.program_id(1)
     quads = pl.num_programs(1)
-    width = dh_ref.shape[1]
+    width = dx_ref.shape[1]
+    rows = pl.ds(pl.multiple_of(seq * L, L), L)
+    joined = pltpu.make_async_copy(dh_any.at[rows], dh_ref, dh_sem)
+    pl.when(quad == 0)(joined.start)
 
     @pl.when((seq == 0) & (quad == 0))
     def _():
@@ -508,6 +512,7 @@
 
     @pl.when(quad == quads - 1)
     def _():
+        joined.wait()
         dx_ref[...] = (dh_ref[...] + dot(all_ref[...], w_ref[...], 1, 1)).astype(BF)
 
 
@@ -530,8 +535,7 @@
                 col(0),
                 col(0),
                 pl.BlockSpec((heads, L, L), lambda i, j, s: (i * quads + j, 0, 0)),
-                pl.BlockSpec((L, width), lambda i, j, s: (i, 0)),
-                *([ANYWHERE] * len(sources)),
+                *([ANYWHERE] * (1 + len(sources))),
             ],
             out_specs=[
                 pl.BlockSpec((L, width), lambda i, j, s: (i, 0)),
@@ -540,6 +544,8 @@
             scratch_shapes=[
                 pltpu.VMEM((L, 3 * width), BF),
                 pltpu.VMEM((width, 3 * width), BF),
+                pltpu.VMEM((L, width), F32),
+                pltpu.SemaphoreType.DMA,
                 pltpu.SemaphoreType.DMA,
             ],
         ),
@@ -627,7 +633,7 @@
         own, w_feed = pack(w_qkv, w_out, w_in, w_down)
         at_feed = w_qkv.shape[1]
         at_down = at_feed + w_feed.shape[1]
-        z_one, z_two, z_three, near_x, near_y = stage("123xy", (w_qkv, w_qkv, w_qkv, own, own))
+        z_two, z_three, z_one, near_x, near_y = stage("231xy", (w_qkv, w_qkv, w_qkv, own, own))
         tall, cols_feed = w_qkv.shape[0], w_feed.shape[1]
         z_one, scalars, bias, scale, vectors = after_all(z_one, scalars, bias, scale, vectors)
         (far,) = glue(
@@ -678,8 +684,8 @@
         down_parts = whole(lax.all_gather(w_down, BOTH, axis=0, tiled=True))
     qkv = project(scalars, seqs, first, qkv_parts, bias, scale)
     if special:
-        x_last, y_last, cross_down, down_one, down_two = stage(
-            "xyy12", (feed_three, feed_three, near_x_down, w_down, w_down), qkv, pair_core
+        x_last, y_last, down_two, down_one, cross_down = stage(
+            "xy21y", (feed_three, feed_three, w_down, w_down, near_x_down), qkv, pair_core
         )
     attended = []
     for seq in range(seqs):
@@ -718,7 +724,7 @@
             (width, *((n, 0, w_down.shape[0], 0) for n in range(3))),
         )
         x_far, y_far, *diagonal = stage(
-            "xy123", (far, far, cross_down, cross_down, cross_down), *cores
+            "xy231", (far, far, cross_down, cross_down, cross_down), *cores
         )
     normed, spread, gl, gp = join(
         scalars, seqs, tokens, context, feed_parts, vectors, bias_in[None]
@@ -731,7 +737,7 @@
             (x_far, (1, rest, 0)),
             (y_far, (2, rest, 0)),
             (cross_down, (3, (0,), 0)),
-            *((block, (3, (k,), 0)) for block, k in zip(diagonal, rest)),
+            *((block, (3, (k,), 0)) for block, k in zip(diagonal, (2, 3, 1))),
         ]
         down_parts = both(
             [*((array, (chip, (0,), at_down)) for chip, array in enumerate(near)), *mine],

time: 254 us -> 253 us (level)
  no operation moved by 1% of the time
where the time goes in v5:
time: 253 us; the launch traced here: 252 us
  Pallas kernels  138 us (55%)
  waiting for transfers between devices  47.4 us (19%)
  starting transfers between devices  42.4 us (17%)
  blocking collectives  10.3 us (4%)
  local copies, waits for them, and re-layouts  8.51 us (3%)
  other arithmetic  3.94 us (2%)
    ppermute x50, waiting for transfers between devices, hop(): return lax.ppermute(block, axis, [(i, i ^ flip) for i in range(size)])  47.4 us
    pallas_call x1, Pallas kernels, turn(): pl.pallas_call(functools.partial(turn_body, seqs, tags_of(feeds), tags_of...  44.2 us
    ppermute x50, starting transfers between devices, hop(): return lax.ppermute(block, axis, [(i, i ^ flip) for i in range(size)])  42.4 us
    pallas_call x1, Pallas kernels, back(): pl.pallas_call(functools.partial(back_body, seqs, tags_of(sources)), out_...  31.4 us
    pallas_call x1, Pallas kernels, join(): pl.pallas_call(functools.partial(join_body, seqs, tags_of(sources)), out_...  25.8 us
    pallas_call x2, Pallas kernels, attend(): pl.pallas_call(functools.partial(attend_body, seq), out_shape=(shape_of((...  20.5 us
    pallas_call x1, Pallas kernels, project(): pl.pallas_call(functools.partial(project_body, seqs, tags_of(sources)), o...  12.4 us
    all_to_all x1, blocking collectives, on_device(): mine = jnp.sum(lax.all_to_all(rows, BOTH, 0, 0, tiled=True), axis=0)  10.3 us
  transfers between devices with their start and end apart: 50, of which 16 were waited for; matrix products, arithmetic and copies ran while one was open for 2% of the time, Pallas kernels for 24%

profile of v5, /device:TPU:0, one launch (start us, length us, event | category | flops | bytes accessed | tf_op | source)
XLA Modules:
  0.0 252.1 jit_solution(12103171285579980661)
XLA Ops:
  0.6 2.1 pack.1
  2.7 3.0 %collective-permute-start.3 = (bf16[32,12288]{1,0:T(8,128)(2,1)}, bf16[32,12288]{1,0:T(8,128)(2,1)S(1)}, u32[]{:S(2)}, u32[]{:S(2)}) collective-permute-start(bf16[32,12288]{1,0:T(8,128)(2,1)} %get-tuple-element.151.refs_0_.refs_22_), channel_id=1, source_target_pairs={{0,8},{8,0},{16,24},{24,16},{1,9},{9,1},{17,25},{25,17},{2,10},{10... | collective-permute-start | bytes 2359304 | tf_op jit(solution)/shard_map/ppermute | solution.py:563
  5.7 1.5 collective-permute-start.4
  7.3 2.6 %collective-permute-start = (bf16[32,3072]{1,0:T(8,128)(2,1)}, bf16[32,3072]{1,0:T(8,128)(2,1)S(1)}, u32[]{:S(2)}, u32[]{:S(2)}) collective-permute-start(bf16[32,3072]{1,0:T(8,128)(2,1)} %qkv_ref.1), channel_id=1, source_target_pairs={{0,4},{1,5},{2,6},{3,7},{4,0},{5,1},{6,2},{7,3},{8,12},{9,13},{10,... | collective-permute-start | bytes 589832 | tf_op jit(solution)/shard_map/ppermute | solution.py:563
  9.9 1.3 collective-permute-start.1
  11.4 1.4 stack.43.vec_ref
  12.9 1.2 pad_add_fusion.len_ref
  14.1 1.3 pad_maximum_fusion
  15.4 8.7 %collective-permute-done.refs_1_ = bf16[32,3072]{1,0:T(8,128)(2,1)S(1)} collective-permute-done((bf16[32,3072]{1,0:T(8,128)(2,1)}, bf16[32,3072]{1,0:T(8,128)(2,1)S(1)}, u32[]{:S(2)}, u32[]{:S(2)}) %collective-permute-start) | collective-permute-done | bytes 196640 | tf_op jit(solution)/shard_map/ppermute | solution.py:563
  24.3 0.8 collective-permute-done.4.refs_2_.refs_24_
  26.1 1.7 collective-permute-start.6
  27.8 3.7 %collective-permute-start.7 = (bf16[32,5120]{1,0:T(8,128)(2,1)}, bf16[32,5120]{1,0:T(8,128)(2,1)S(1)}, u32[]{:S(2)}, u32[]{:S(2)}) collective-permute-start(bf16[32,5120]{1,0:T(8,128)(2,1)} %get-tuple-element.181), channel_id=1, source_target_pairs={{0,4},{1,5},{2,6},{3,7},{4,0},{5,1},{6,2},{7,3},{8,12},{9,13},{10,... | collective-permute-start | bytes 983048 | tf_op jit(solution)/shard_map/ppermute | solution.py:563
  31.4 14.6 %collective-permute-done.7.refs_1_ = bf16[32,5120]{1,0:T(8,128)(2,1)S(1)} collective-permute-done((bf16[32,5120]{1,0:T(8,128)(2,1)}, bf16[32,5120]{1,0:T(8,128)(2,1)S(1)}, u32[]{:S(2)}, u32[]{:S(2)}) %collective-permute-start.7) | collective-permute-done | bytes 327712 | tf_op jit(solution)/shard_map/ppermute | solution.py:563
  46.1 1.0 copy-done.11
  47.7 1.5 collective-permute-start.10
  49.2 1.5 collective-permute-start.11
  50.7 9.3 %collective-permute-done.12.refs_0_ = bf16[32,5120]{1,0:T(8,128)(2,1)S(1)} collective-permute-done((bf16[32,5120]{1,0:T(8,128)(2,1)}, bf16[32,5120]{1,0:T(8,128)(2,1)S(1)}, u32[]{:S(2)}, u32[]{:S(2)}) %collective-permute-start.12) | collective-permute-done | bytes 327712 | tf_op jit(solution)/shard_map/ppermute | solution.py:563
  61.2 0.9 glue.7
  62.1 1.5 collective-permute-done.17.refs_14_
  64.4 1.5 collective-permute-start.19
  66.4 2.6 %collective-permute-start.21 = (bf16[32,5120]{1,0:T(8,128)(2,1)}, bf16[32,5120]{1,0:T(8,128)(2,1)}, u32[]{:S(2)}, u32[]{:S(2)}) collective-permute-start(bf16[32,5120]{1,0:T(8,128)(2,1)} %get-tuple-element.181), channel_id=1, source_target_pairs={{0,6},{1,7},{2,4},{3,5},{4,2},{5,3},{6,0},{7,1},{8,14},{9,15},{10,... | collective-permute-start | bytes 983048 | tf_op jit(solution)/shard_map/ppermute | solution.py:563
  69.0 12.4 %project.1.q_ref.k_ref.v_ref = bf16[1024,3072]{1,0:T(8,128)(2,1)} custom-call(s32[5]{0:T(128)} %pad_add_fusion.len_ref, bf16[1024,1024]{1,0:T(8,128)(2,1)} %x_ref.2, f32[1,3072]{1,0:T(1,128)} %bitcast.13, f32[1,3072]{1,0:T(1,128)} %constant.37.clone.1.scale_ref, bf16[32,12288]{1,0:T(8,128)(2,1)} %get-tuple-element.151.refs_0_.refs_22_, ...), custom_call_target="tpu_custom_call" | custom-call | flops 6442450944 | tf_op jit(solution)/shard_map/project/pallas_call | solution.py:147
  81.5 1.1 collective-permute-done.20.refs_2_.refs_5_
  82.5 1.0 collective-permute-start.23
  84.0 2.4 collective-permute-start.25
  86.4 0.8 collective-permute-start.26
  87.2 0.8 collective-permute-start.27
  87.9 10.3 %attend.2 = (bf16[1024,1024]{1,0:T(8,128)(2,1)}, bf16[32,512,512]{2,1,0:T(8,128)(2,1)}, f32[1024,1024]{1,0:T(8,128)}) custom-call(s32[5]{0:T(128)} %pad_add_fusion.len_ref, bf16[1024,3072]{1,0:T(8,128)(2,1)} %project.1.q_ref.k_ref.v_ref, bf16[1024,3072]{1,0:T(8,128)(2,1)} %project.1.q_ref.k_ref.v_ref, bf16[1024,3072]{1,0:T(8,128)(2,1)} %project.1.q_ref.k_ref.v_ref), custom_call_target="tpu_custom_call" | custom-call | flops 4294967296 | tf_op jit(solution)/shard_map/attend/pallas_call | solution.py:220
  98.3 1.0 glue.8
  99.2 1.5 collective-permute-start.28
  100.7 0.9 collective-permute-start.29
  102.1 1.3 collective-permute-start.30
  103.4 10.2 %attend.3 = (bf16[1024,1024]{1,0:T(8,128)(2,1)}, bf16[32,512,512]{2,1,0:T(8,128)(2,1)}, f32[1024,1024]{1,0:T(8,128)}) custom-call(s32[5]{0:T(128)} %pad_add_fusion.len_ref, bf16[1024,3072]{1,0:T(8,128)(2,1)} %project.1.q_ref.k_ref.v_ref, bf16[1024,3072]{1,0:T(8,128)(2,1)} %project.1.q_ref.k_ref.v_ref, ...), custom_call_target="tpu_custom_call", output_to_operand_aliasing={{0}: (4, {}), {1}: (5, {}), {2}: (6, {})} | custom-call | flops 4294967296 | tf_op jit(solution)/shard_map/attend/pallas_call | solution.py:220
  113.6 1.1 collective-permute-done.28.refs_9_
  114.7 1.1 collective-permute-done.29.refs_10_
  117.1 2.7 %collective-permute-done.33.refs_17_ = bf16[32,5120]{1,0:T(8,128)(2,1)S(1)} collective-permute-done((bf16[32,5120]{1,0:T(8,128)(2,1)}, bf16[32,5120]{1,0:T(8,128)(2,1)S(1)}, u32[]{:S(2)}, u32[]{:S(2)}) %collective-permute-start.33) | collective-permute-done | bytes 327712 | tf_op jit(solution)/shard_map/ppermute | solution.py:563
  119.8 0.8 collective-permute-done.34.refs_18_
  120.6 0.7 copy-done.28
  122.7 3.5 %collective-permute-start.40 = (bf16[32,4096]{1,0:T(8,128)(2,1)}, bf16[32,4096]{1,0:T(8,128)(2,1)S(1)}, u32[]{:S(2)}, u32[]{:S(2)}) collective-permute-start(bf16[32,4096]{1,0:T(8,128)(2,1)} %copy-done.30), channel_id=1, source_target_pairs={{0,4},{1,5},{2,6},{3,7},{4,0},{5,1},{6,2},{7,3},{8,12},{9,13},{10,... | collective-permute-start | bytes 786440 | tf_op jit(solution)/shard_map/ppermute | solution.py:563
  126.1 1.9 collective-permute-start.41
  128.0 25.8 %join.1 = (f32[1024,1024]{1,0:T(8,128)}, f32[1024,128]{1,0:T(8,128)}, bf16[1024,4096]{1,0:T(8,128)(2,1)}, bf16[1024,4096]{1,0:T(8,128)(2,1)}) custom-call(s32[5]{0:T(128)} %pad_add_fusion.len_ref, bf16[1024,1024]{1,0:T(8,128)(2,1)} %x_ref.2, bf16[1024,1024]{1,0:T(8,128)(2,1)} %get-tuple-element.220.o_ref, f32[8,1024]{1,0:T(8,128)} %stack.43.vec_ref, ...), custom_call_target="tpu_custom_call" | custom-call | flops 10737418240 | tf_op jit(solution)/shard_map/join/pallas_call | solution.py:290
  155.9 2.2 collective-permute-done.46.refs_38_
  158.9 1.7 collective-permute-done.48.refs_40_
  161.1 0.9 copy-done.17
  162.5 44.2 %turn.1 = (bf16[1024,1024]{1,0:T(8,128)(2,1)}, f32[1024,1024]{1,0:T(8,128)}, bf16[1024,1024]{1,0:T(8,128)(2,1)}, f32[8,1024]{1,0:T(8,128)}, f32[1,4096]{1,0:T(1,128)}) custom-call(s32[5]{0:T(128)} %pad_add_fusion.len_ref, bf16[1024,4096]{1,0:T(8,128)(2,1)} %get-tuple-element.245.gl_ref, f32[1024,1024]{1,0:T(8,128)} %get-tuple-element.246.u_ref, ...), custom_call_target="tpu_custom_call" | custom-call | flops 27917287424 | tf_op jit(solution)/shard_map/turn/pallas_call | solution.py:407
  206.8 31.4 %back.1 = (bf16[1024,1024]{1,0:T(8,128)(2,1)}, f32[1,1024]{1,0:T(1,128)}) custom-call(s32[5]{0:T(128)} %pad_add_fusion.len_ref, bf16[1024,3072]{1,0:T(8,128)(2,1)} %project.1.q_ref.k_ref.v_ref, bf16[1024,3072]{1,0:T(8,128)(2,1)} %project.1.q_ref.k_ref.v_ref, bf16[1024,3072]{1,0:T(8,128)(2,1)} %project.1.q_ref.k_ref.v_ref, ...), custom_call_target="tpu_custom_call" | custom-call | flops 17179869184 | tf_op jit(solution)/shard_map/back/pallas_call | solution.py:524
  238.7 1.3 reduce.24
  240.6 10.3 %all_to_all.9 = f32[32,1,320]{2,1,0:T(1,128)S(1)} all-to-all(f32[32,1,320]{2,1,0:T(1,128)S(1)} %all_to_all.6), channel_id=1, replica_groups=mesh['dp'=4,'fsdp'=8] {'dp','fsdp'}, dimensions={0} | all-to-all | bytes 81920 | tf_op jit(solution)/shard_map/all_to_all | solution.py:753
  (160 shorter events, 14.0 us)
Async XLA Ops:
  2.7 21.5 %collective-permute-start.3 = (bf16[32,12288]{1,0:T(8,128)(2,1)}, bf16[32,12288]{1,0:T(8,128)(2,1)S(1)}, u32[]{:S(2)}, u32[]{:S(2)}) collective-permute-start(bf16[32,12288]{1,0:T(8,128)(2,1)} %get-tuple-element.151.refs_0_.refs_22_), channel_id=1, source_target_pairs={{0,8},{8,0},{16,24},{24,16},{1,9},{9,1},{17,25},{25,17},{2,10},{10... | collective-permute-start | bytes 2359304 | tf_op jit(solution)/shard_map/ppermute | solution.py:563
  5.7 19.3 %collective-permute-start.4 = (bf16[32,12288]{1,0:T(8,128)(2,1)}, bf16[32,12288]{1,0:T(8,128)(2,1)}, u32[]{:S(2)}, u32[]{:S(2)}) collective-permute-start(bf16[32,12288]{1,0:T(8,128)(2,1)} %get-tuple-element.151.refs_0_.refs_22_), channel_id=1, source_target_pairs={{0,16},{8,24},{16,0},{24,8},{1,17},{9,25},{17,1},{25,9},{2,18},{10... | collective-permute-start | bytes 2359304 | tf_op jit(solution)/shard_map/ppermute | solution.py:563
  7.3 16.8 %collective-permute-start = (bf16[32,3072]{1,0:T(8,128)(2,1)}, bf16[32,3072]{1,0:T(8,128)(2,1)S(1)}, u32[]{:S(2)}, u32[]{:S(2)}) collective-permute-start(bf16[32,3072]{1,0:T(8,128)(2,1)} %qkv_ref.1), channel_id=1, source_target_pairs={{0,4},{1,5},{2,6},{3,7},{4,0},{5,1},{6,2},{7,3},{8,12},{9,13},{10,... | collective-permute-start | bytes 589832 | tf_op jit(solution)/shard_map/ppermute | solution.py:563
  9.9 14.3 %collective-permute-start.1 = (bf16[32,3072]{1,0:T(8,128)(2,1)}, bf16[32,3072]{1,0:T(8,128)(2,1)S(1)}, u32[]{:S(2)}, u32[]{:S(2)}) collective-permute-start(bf16[32,3072]{1,0:T(8,128)(2,1)} %qkv_ref.1), channel_id=1, source_target_pairs={{0,6},{1,7},{2,4},{3,5},{4,2},{5,3},{6,0},{7,1},{8,14},{9,15},{10,... | collective-permute-start | bytes 589832 | tf_op jit(solution)/shard_map/ppermute | solution.py:563
  11.2 13.0 %collective-permute-start.2 = (bf16[32,3072]{1,0:T(8,128)(2,1)}, bf16[32,3072]{1,0:T(8,128)(2,1)S(1)}, u32[]{:S(2)}, u32[]{:S(2)}) collective-permute-start(bf16[32,3072]{1,0:T(8,128)(2,1)} %qkv_ref.1), channel_id=1, source_target_pairs={{0,2},{1,3},{2,0},{3,1},{4,6},{5,7},{6,4},{7,5},{8,10},{9,11},{10,... | collective-permute-start | bytes 589832 | tf_op jit(solution)/shard_map/ppermute | solution.py:563
  25.1 21.0 %collective-permute-start.8 = (bf16[32,12288]{1,0:T(8,128)(2,1)}, bf16[32,12288]{1,0:T(8,128)(2,1)S(1)}, u32[]{:S(2)}, u32[]{:S(2)}) collective-permute-start(bf16[32,12288]{1,0:T(8,128)(2,1)} %get-tuple-element.151.refs_0_.refs_22_), channel_id=1, source_target_pairs={{0,1},{1,0},{2,3},{3,2},{4,5},{5,4},{6,7},{7,6},{8,9},{9,8},{10,11... | collective-permute-start | bytes 2359304 | tf_op jit(solution)/shard_map/ppermute | solution.py:563
  25.2 21.9 %collective-permute-start.9 = (bf16[32,12288]{1,0:T(8,128)(2,1)S(1)}, bf16[32,12288]{1,0:T(8,128)(2,1)}, u32[]{:S(2)}, u32[]{:S(2)}) collective-permute-start(bf16[32,12288]{1,0:T(8,128)(2,1)S(1)} %collective-permute-done.3.refs_0_.refs_2_.refs_1_.refs_23_), channel_id=1, source_target_pairs={{0,1},{1,0},{2,3},{3,2},{4,5},{5,4},{6,7},{7,6},{8,9},{9,8},{10,11... | collective-permute-start | bytes 2359304 | tf_op jit(solution)/shard_map/ppermute | solution.py:563
  25.7 20.4 %collective-permute-start.5 = (bf16[96,3072]{1,0:T(8,128)(2,1)S(1)}, bf16[96,3072]{1,0:T(8,128)(2,1)S(1)}, u32[]{:S(2)}, u32[]{:S(2)}) collective-permute-start(bf16[96,3072]{1,0:T(8,128)(2,1)S(1)} %glue.5.refs_3_), channel_id=1, source_target_pairs={{0,8},{8,0},{16,24},{24,16},{1,9},{9,1},{17,25},{25,17},{2,10},{10... | collective-permute-start | bytes 1769480 | tf_op jit(solution)/shard_map/ppermute | solution.py:563
  26.1 20.0 %collective-permute-start.6 = (bf16[96,3072]{1,0:T(8,128)(2,1)S(1)}, bf16[96,3072]{1,0:T(8,128)(2,1)S(1)}, u32[]{:S(2)}, u32[]{:S(2)}) collective-permute-start(bf16[96,3072]{1,0:T(8,128)(2,1)S(1)} %glue.5.refs_3_), channel_id=1, source_target_pairs={{0,16},{8,24},{16,0},{24,8},{1,17},{9,25},{17,1},{25,9},{2,18},{10... | collective-permute-start | bytes 1769480 | tf_op jit(solution)/shard_map/ppermute | solution.py:563
  27.8 18.3 %collective-permute-start.7 = (bf16[32,5120]{1,0:T(8,128)(2,1)}, bf16[32,5120]{1,0:T(8,128)(2,1)S(1)}, u32[]{:S(2)}, u32[]{:S(2)}) collective-permute-start(bf16[32,5120]{1,0:T(8,128)(2,1)} %get-tuple-element.181), channel_id=1, source_target_pairs={{0,4},{1,5},{2,6},{3,7},{4,0},{5,1},{6,2},{7,3},{8,12},{9,13},{10,... | collective-permute-start | bytes 983048 | tf_op jit(solution)/shard_map/ppermute | solution.py:563
  47.1 13.0 %collective-permute-start.13 = (bf16[32,12288]{1,0:T(8,128)(2,1)}, bf16[32,12288]{1,0:T(8,128)(2,1)S(1)}, u32[]{:S(2)}, u32[]{:S(2)}) collective-permute-start(bf16[32,12288]{1,0:T(8,128)(2,1)} %collective-permute-done.4.refs_2_.refs_24_), channel_id=1, source_target_pairs={{0,1},{1,0},{2,3},{3,2},{4,5},{5,4},{6,7},{7,6},{8,9},{9,8},{10,11... | collective-permute-start | bytes 2359304 | tf_op jit(solution)/shard_map/ppermute | solution.py:563
  47.2 12.9 %collective-permute-start.14 = (bf16[96,3072]{1,0:T(8,128)(2,1)S(1)}, bf16[96,3072]{1,0:T(8,128)(2,1)S(1)}, u32[]{:S(2)}, u32[]{:S(2)}) collective-permute-start(bf16[96,3072]{1,0:T(8,128)(2,1)S(1)} %glue.5.refs_3_), channel_id=1, source_target_pairs={{0,1},{1,0},{2,3},{3,2},{4,5},{5,4},{6,7},{7,6},{8,9},{9,8},{10,11... | collective-permute-start | bytes 1769480 | tf_op jit(solution)/shard_map/ppermute | solution.py:563
  47.7 12.4 %collective-permute-start.10 = (bf16[64,3072]{1,0:T(8,128)(2,1)S(1)}, bf16[64,3072]{1,0:T(8,128)(2,1)S(1)}, u32[]{:S(2)}, u32[]{:S(2)}) collective-permute-start(bf16[64,3072]{1,0:T(8,128)(2,1)S(1)} %get-tuple-element.161), channel_id=1, source_target_pairs={{0,16},{8,24},{16,0},{24,8},{1,17},{9,25},{17,1},{25,9},{2,18},{10... | collective-permute-start | bytes 1179656 | tf_op jit(solution)/shard_map/ppermute | solution.py:563
  49.2 10.8 %collective-permute-start.11 = (bf16[64,3072]{1,0:T(8,128)(2,1)S(1)}, bf16[64,3072]{1,0:T(8,128)(2,1)S(1)}, u32[]{:S(2)}, u32[]{:S(2)}) collective-permute-start(bf16[64,3072]{1,0:T(8,128)(2,1)S(1)} %get-tuple-element.162), channel_id=1, source_target_pairs={{0,8},{8,0},{16,24},{24,16},{1,9},{9,1},{17,25},{25,17},{2,10},{10... | collective-permute-start | bytes 1179656 | tf_op jit(solution)/shard_map/ppermute | solution.py:563
  50.7 9.3 %collective-permute-start.12 = (bf16[32,5120]{1,0:T(8,128)(2,1)}, bf16[32,5120]{1,0:T(8,128)(2,1)S(1)}, u32[]{:S(2)}, u32[]{:S(2)}) collective-permute-start(bf16[32,5120]{1,0:T(8,128)(2,1)} %get-tuple-element.181), channel_id=1, source_target_pairs={{0,2},{1,3},{2,0},{3,1},{4,6},{5,7},{6,4},{7,5},{8,10},{9,11},{10,... | collective-permute-start | bytes 983048 | tf_op jit(solution)/shard_map/ppermute | solution.py:563
  60.1 4.0 %collective-permute-start.15 = (bf16[96,3072]{1,0:T(8,128)(2,1)S(1)}, bf16[96,3072]{1,0:T(8,128)(2,1)S(1)}, u32[]{:S(2)}, u32[]{:S(2)}) collective-permute-start(bf16[96,3072]{1,0:T(8,128)(2,1)S(1)} %collective-permute-done.5.refs_1_.refs_4_), channel_id=1, source_target_pairs={{0,1},{1,0},{2,3},{3,2},{4,5},{5,4},{6,7},{7,6},{8,9},{9,8},{10,11... | collective-permute-start | bytes 1769480 | tf_op jit(solution)/shard_map/ppermute | solution.py:563
  60.2 4.0 %collective-permute-start.16 = (bf16[96,3072]{1,0:T(8,128)(2,1)S(1)}, bf16[96,3072]{1,0:T(8,128)(2,1)S(1)}, u32[]{:S(2)}, u32[]{:S(2)}) collective-permute-start(bf16[96,3072]{1,0:T(8,128)(2,1)S(1)} %collective-permute-done.6.refs_2_.refs_5_), channel_id=1, source_target_pairs={{0,1},{1,0},{2,3},{3,2},{4,5},{5,4},{6,7},{7,6},{8,9},{9,8},{10,11... | collective-permute-start | bytes 1769480 | tf_op jit(solution)/shard_map/ppermute | solution.py:563
  60.7 2.9 %collective-permute-start.17 = (bf16[64,3072]{1,0:T(8,128)(2,1)S(1)}, bf16[64,3072]{1,0:T(8,128)(2,1)S(1)}, u32[]{:S(2)}, u32[]{:S(2)}) collective-permute-start(bf16[64,3072]{1,0:T(8,128)(2,1)S(1)} %collective-permute-done.10.refs_6_), channel_id=1, source_target_pairs={{0,1},{1,0},{2,3},{3,2},{4,5},{5,4},{6,7},{7,6},{8,9},{9,8},{10,11... | collective-permute-start | bytes 1179656 | tf_op jit(solution)/shard_map/ppermute | solution.py:563
  61.2 2.9 %collective-permute-start.18 = (bf16[64,3072]{1,0:T(8,128)(2,1)S(1)}, bf16[64,3072]{1,0:T(8,128)(2,1)S(1)}, u32[]{:S(2)}, u32[]{:S(2)}) collective-permute-start(bf16[64,3072]{1,0:T(8,128)(2,1)S(1)} %collective-permute-done.11.refs_7_), channel_id=1, source_target_pairs={{0,1},{1,0},{2,3},{3,2},{4,5},{5,4},{6,7},{7,6},{8,9},{9,8},{10,11... | collective-permute-start | bytes 1179656 | tf_op jit(solution)/shard_map/ppermute | solution.py:563
  64.4 17.1 %collective-permute-start.19 = (bf16[64,5120]{1,0:T(8,128)(2,1)}, bf16[64,5120]{1,0:T(8,128)(2,1)S(1)}, u32[]{:S(2)}, u32[]{:S(2)}) collective-permute-start(bf16[64,5120]{1,0:T(8,128)(2,1)} %get-tuple-element.182.refs_3_), channel_id=1, source_target_pairs={{0,8},{8,0},{16,24},{24,16},{1,9},{9,1},{17,25},{25,17},{2,10},{10... | collective-permute-start | bytes 1966088 | tf_op jit(solution)/shard_map/ppermute | solution.py:563
  65.8 16.7 %collective-permute-start.20 = (bf16[64,5120]{1,0:T(8,128)(2,1)}, bf16[64,5120]{1,0:T(8,128)(2,1)S(1)}, u32[]{:S(2)}, u32[]{:S(2)}) collective-permute-start(bf16[64,5120]{1,0:T(8,128)(2,1)} %get-tuple-element.182.refs_3_), channel_id=1, source_target_pairs={{0,16},{8,24},{16,0},{24,8},{1,17},{9,25},{17,1},{25,9},{2,18},{10... | collective-permute-start | bytes 1966088 | tf_op jit(solution)/shard_map/ppermute | solution.py:563
  66.3 16.2 %collective-permute-start.22 = (bf16[64,5120]{1,0:T(8,128)(2,1)}, bf16[64,5120]{1,0:T(8,128)(2,1)}, u32[]{:S(2)}, u32[]{:S(2)}) collective-permute-start(bf16[64,5120]{1,0:T(8,128)(2,1)} %get-tuple-element.182.refs_3_), channel_id=1, source_target_pairs={{0,1},{1,0},{2,3},{3,2},{4,5},{5,4},{6,7},{7,6},{8,9},{9,8},{10,11... | collective-permute-start | bytes 1966088 | tf_op jit(solution)/shard_map/ppermute | solution.py:563
  66.4 15.1 %collective-permute-start.21 = (bf16[32,5120]{1,0:T(8,128)(2,1)}, bf16[32,5120]{1,0:T(8,128)(2,1)}, u32[]{:S(2)}, u32[]{:S(2)}) collective-permute-start(bf16[32,5120]{1,0:T(8,128)(2,1)} %get-tuple-element.181), channel_id=1, source_target_pairs={{0,6},{1,7},{2,4},{3,5},{4,2},{5,3},{6,0},{7,1},{8,14},{9,15},{10,... | collective-permute-start | bytes 983048 | tf_op jit(solution)/shard_map/ppermute | solution.py:563
  82.5 15.7 %collective-permute-start.23 = (bf16[32,5120]{1,0:T(8,128)(2,1)}, bf16[32,5120]{1,0:T(8,128)(2,1)}, u32[]{:S(2)}, u32[]{:S(2)}) collective-permute-start(bf16[32,5120]{1,0:T(8,128)(2,1)} %collective-permute-done.21.refs_6_), channel_id=1, source_target_pairs={{0,8},{8,0},{16,24},{24,16},{1,9},{9,1},{17,25},{25,17},{2,10},{10... | collective-permute-start | bytes 983048 | tf_op jit(solution)/shard_map/ppermute | solution.py:563
  83.5 14.7 %collective-permute-start.24 = (bf16[32,5120]{1,0:T(8,128)(2,1)}, bf16[32,5120]{1,0:T(8,128)(2,1)S(1)}, u32[]{:S(2)}, u32[]{:S(2)}) collective-permute-start(bf16[32,5120]{1,0:T(8,128)(2,1)} %collective-permute-done.21.refs_6_), channel_id=1, source_target_pairs={{0,16},{8,24},{16,0},{24,8},{1,17},{9,25},{17,1},{25,9},{2,18},{10... | collective-permute-start | bytes 983048 | tf_op jit(solution)/shard_map/ppermute | solution.py:563
  84.0 14.2 %collective-permute-start.25 = (bf16[128,1024]{1,0:T(8,128)(2,1)}, bf16[128,1024]{1,0:T(8,128)(2,1)S(1)}, u32[]{:S(2)}, u32[]{:S(2)}) collective-permute-start(bf16[128,1024]{1,0:T(8,128)(2,1)} %down_ref.1), channel_id=1, source_target_pairs={{0,4},{1,5},{2,6},{3,7},{4,0},{5,1},{6,2},{7,3},{8,12},{9,13},{10,... | collective-permute-start | bytes 786440 | tf_op jit(solution)/shard_map/ppermute | solution.py:563
  86.4 11.8 %collective-permute-start.26 = (bf16[128,1024]{1,0:T(8,128)(2,1)}, bf16[128,1024]{1,0:T(8,128)(2,1)S(1)}, u32[]{:S(2)}, u32[]{:S(2)}) collective-permute-start(bf16[128,1024]{1,0:T(8,128)(2,1)} %down_ref.1), channel_id=1, source_target_pairs={{0,2},{1,3},{2,0},{3,1},{4,6},{5,7},{6,4},{7,5},{8,10},{9,11},{10,... | collective-permute-start | bytes 786440 | tf_op jit(solution)/shard_map/ppermute | solution.py:563
  87.2 11.0 %collective-permute-start.27 = (bf16[32,4096]{1,0:T(8,128)(2,1)S(1)}, bf16[32,4096]{1,0:T(8,128)(2,1)S(1)}, u32[]{:S(2)}, u32[]{:S(2)}) collective-permute-start(bf16[32,4096]{1,0:T(8,128)(2,1)S(1)} %get-tuple-element.194), channel_id=1, source_target_pairs={{0,16},{8,24},{16,0},{24,8},{1,17},{9,25},{17,1},{25,9},{2,18},{10... | collective-permute-start | bytes 786440 | tf_op jit(solution)/shard_map/ppermute | solution.py:563
  99.2 15.5 %collective-permute-start.28 = (bf16[64,5120]{1,0:T(8,128)(2,1)}, bf16[64,5120]{1,0:T(8,128)(2,1)}, u32[]{:S(2)}, u32[]{:S(2)}) collective-permute-start(bf16[64,5120]{1,0:T(8,128)(2,1)} %get-tuple-element.212), channel_id=1, source_target_pairs={{0,16},{8,24},{16,0},{24,8},{1,17},{9,25},{17,1},{25,9},{2,18},{10... | collective-permute-start | bytes 1966088 | tf_op jit(solution)/shard_map/ppermute | solution.py:563
  100.7 15.1 %collective-permute-start.29 = (bf16[64,5120]{1,0:T(8,128)(2,1)S(1)}, bf16[64,5120]{1,0:T(8,128)(2,1)}, u32[]{:S(2)}, u32[]{:S(2)}) collective-permute-start(bf16[64,5120]{1,0:T(8,128)(2,1)S(1)} %get-tuple-element.213), channel_id=1, source_target_pairs={{0,8},{8,0},{16,24},{24,16},{1,9},{9,1},{17,25},{25,17},{2,10},{10... | collective-permute-start | bytes 1966088 | tf_op jit(solution)/shard_map/ppermute | solution.py:563
  101.6 14.2 %collective-permute-start.31 = (bf16[64,5120]{1,0:T(8,128)(2,1)S(1)}, bf16[64,5120]{1,0:T(8,128)(2,1)S(1)}, u32[]{:S(2)}, u32[]{:S(2)}) collective-permute-start(bf16[64,5120]{1,0:T(8,128)(2,1)S(1)} %collective-permute-done.19.refs_1_.refs_4_), channel_id=1, source_target_pairs={{0,1},{1,0},{2,3},{3,2},{4,5},{5,4},{6,7},{7,6},{8,9},{9,8},{10,11... | collective-permute-start | bytes 1966088 | tf_op jit(solution)/shard_map/ppermute | solution.py:563
  101.6 14.2 %collective-permute-start.32 = (bf16[64,5120]{1,0:T(8,128)(2,1)S(1)}, bf16[64,5120]{1,0:T(8,128)(2,1)}, u32[]{:S(2)}, u32[]{:S(2)}) collective-permute-start(bf16[64,5120]{1,0:T(8,128)(2,1)S(1)} %collective-permute-done.20.refs_2_.refs_5_), channel_id=1, source_target_pairs={{0,1},{1,0},{2,3},{3,2},{4,5},{5,4},{6,7},{7,6},{8,9},{9,8},{10,11... | collective-permute-start | bytes 1966088 | tf_op jit(solution)/shard_map/ppermute | solution.py:563
  102.1 11.5 %collective-permute-start.30 = (bf16[128,1024]{1,0:T(8,128)(2,1)}, bf16[128,1024]{1,0:T(8,128)(2,1)S(1)}, u32[]{:S(2)}, u32[]{:S(2)}) collective-permute-start(bf16[128,1024]{1,0:T(8,128)(2,1)} %down_ref.1), channel_id=1, source_target_pairs={{0,6},{1,7},{2,4},{3,5},{4,2},{5,3},{6,0},{7,1},{8,14},{9,15},{10,... | collective-permute-start | bytes 786440 | tf_op jit(solution)/shard_map/ppermute | solution.py:563
  115.9 4.7 %collective-permute-start.36 = (bf16[64,5120]{1,0:T(8,128)(2,1)}, bf16[64,5120]{1,0:T(8,128)(2,1)S(1)}, u32[]{:S(2)}, u32[]{:S(2)}) collective-permute-start(bf16[64,5120]{1,0:T(8,128)(2,1)} %collective-permute-done.28.refs_9_), channel_id=1, source_target_pairs={{0,1},{1,0},{2,3},{3,2},{4,5},{5,4},{6,7},{7,6},{8,9},{9,8},{10,11... | collective-permute-start | bytes 1966088 | tf_op jit(solution)/shard_map/ppermute | solution.py:563
  115.9 5.4 %collective-permute-start.37 = (bf16[64,5120]{1,0:T(8,128)(2,1)}, bf16[64,5120]{1,0:T(8,128)(2,1)}, u32[]{:S(2)}, u32[]{:S(2)}) collective-permute-start(bf16[64,5120]{1,0:T(8,128)(2,1)} %collective-permute-done.29.refs_10_), channel_id=1, source_target_pairs={{0,1},{1,0},{2,3},{3,2},{4,5},{5,4},{6,7},{7,6},{8,9},{9,8},{10,11... | collective-permute-start | bytes 1966088 | tf_op jit(solution)/shard_map/ppermute | solution.py:563
  116.4 3.4 %collective-permute-start.33 = (bf16[32,5120]{1,0:T(8,128)(2,1)}, bf16[32,5120]{1,0:T(8,128)(2,1)S(1)}, u32[]{:S(2)}, u32[]{:S(2)}) collective-permute-start(bf16[32,5120]{1,0:T(8,128)(2,1)} %collective-permute-done.21.refs_6_), channel_id=1, source_target_pairs={{0,1},{1,0},{2,3},{3,2},{4,5},{5,4},{6,7},{7,6},{8,9},{9,8},{10,11... | collective-permute-start | bytes 983048 | tf_op jit(solution)/shard_map/ppermute | solution.py:563
  116.5 4.1 %collective-permute-start.34 = (bf16[32,5120]{1,0:T(8,128)(2,1)}, bf16[32,5120]{1,0:T(8,128)(2,1)S(1)}, u32[]{:S(2)}, u32[]{:S(2)}) collective-permute-start(bf16[32,5120]{1,0:T(8,128)(2,1)} %collective-permute-done.23.refs_7_), channel_id=1, source_target_pairs={{0,1},{1,0},{2,3},{3,2},{4,5},{5,4},{6,7},{7,6},{8,9},{9,8},{10,11... | collective-permute-start | bytes 983048 | tf_op jit(solution)/shard_map/ppermute | solution.py:563
  116.9 3.6 %collective-permute-start.35 = (bf16[32,5120]{1,0:T(8,128)(2,1)S(1)}, bf16[32,5120]{1,0:T(8,128)(2,1)S(1)}, u32[]{:S(2)}, u32[]{:S(2)}) collective-permute-start(bf16[32,5120]{1,0:T(8,128)(2,1)S(1)} %collective-permute-done.24.refs_3_.refs_8_), channel_id=1, source_target_pairs={{0,1},{1,0},{2,3},{3,2},{4,5},{5,4},{6,7},{7,6},{8,9},{9,8},{10,11... | collective-permute-start | bytes 983048 | tf_op jit(solution)/shard_map/ppermute | solution.py:563
  121.5 32.4 %collective-permute-start.38 = (bf16[384,1024]{1,0:T(8,128)(2,1)S(1)}, bf16[384,1024]{1,0:T(8,128)(2,1)S(1)}, u32[]{:S(2)}, u32[]{:S(2)}) collective-permute-start(bf16[384,1024]{1,0:T(8,128)(2,1)S(1)} %glue.9.refs_25_), channel_id=1, source_target_pairs={{0,8},{8,0},{16,24},{24,16},{1,9},{9,1},{17,25},{25,17},{2,10},{10... | collective-permute-start | bytes 2359304 | tf_op jit(solution)/shard_map/ppermute | solution.py:563
  122.2 31.8 %collective-permute-start.39 = (bf16[384,1024]{1,0:T(8,128)(2,1)S(1)}, bf16[384,1024]{1,0:T(8,128)(2,1)S(1)}, u32[]{:S(2)}, u32[]{:S(2)}) collective-permute-start(bf16[384,1024]{1,0:T(8,128)(2,1)S(1)} %glue.9.refs_25_), channel_id=1, source_target_pairs={{0,16},{8,24},{16,0},{24,8},{1,17},{9,25},{17,1},{25,9},{2,18},{10... | collective-permute-start | bytes 2359304 | tf_op jit(solution)/shard_map/ppermute | solution.py:563
  122.7 31.2 %collective-permute-start.40 = (bf16[32,4096]{1,0:T(8,128)(2,1)}, bf16[32,4096]{1,0:T(8,128)(2,1)S(1)}, u32[]{:S(2)}, u32[]{:S(2)}) collective-permute-start(bf16[32,4096]{1,0:T(8,128)(2,1)} %copy-done.30), channel_id=1, source_target_pairs={{0,4},{1,5},{2,6},{3,7},{4,0},{5,1},{6,2},{7,3},{8,12},{9,13},{10,... | collective-permute-start | bytes 786440 | tf_op jit(solution)/shard_map/ppermute | solution.py:563
  126.1 27.8 %collective-permute-start.41 = (bf16[32,4096]{1,0:T(8,128)(2,1)}, bf16[32,4096]{1,0:T(8,128)(2,1)S(1)}, u32[]{:S(2)}, u32[]{:S(2)}) collective-permute-start(bf16[32,4096]{1,0:T(8,128)(2,1)} %copy-done.30), channel_id=1, source_target_pairs={{0,6},{1,7},{2,4},{3,5},{4,2},{5,3},{6,0},{7,1},{8,14},{9,15},{10,... | collective-permute-start | bytes 786440 | tf_op jit(solution)/shard_map/ppermute | solution.py:563
  128.0 25.9 %collective-permute-start.42 = (bf16[32,4096]{1,0:T(8,128)(2,1)}, bf16[32,4096]{1,0:T(8,128)(2,1)S(1)}, u32[]{:S(2)}, u32[]{:S(2)}) collective-permute-start(bf16[32,4096]{1,0:T(8,128)(2,1)} %copy-done.30), channel_id=1, source_target_pairs={{0,2},{1,3},{2,0},{3,1},{4,6},{5,7},{6,4},{7,5},{8,10},{9,11},{10,... | collective-permute-start | bytes 786440 | tf_op jit(solution)/shard_map/ppermute | solution.py:563
  154.8 6.3 %collective-permute-start.43 = (bf16[384,1024]{1,0:T(8,128)(2,1)S(1)}, bf16[384,1024]{1,0:T(8,128)(2,1)S(1)}, u32[]{:S(2)}, u32[]{:S(2)}) collective-permute-start(bf16[384,1024]{1,0:T(8,128)(2,1)S(1)} %glue.9.refs_25_), channel_id=1, source_target_pairs={{0,1},{1,0},{2,3},{3,2},{4,5},{5,4},{6,7},{7,6},{8,9},{9,8},{10,11... | collective-permute-start | bytes 2359304 | tf_op jit(solution)/shard_map/ppermute | solution.py:563
  154.8 6.3 %collective-permute-start.44 = (bf16[384,1024]{1,0:T(8,128)(2,1)S(1)}, bf16[384,1024]{1,0:T(8,128)(2,1)S(1)}, u32[]{:S(2)}, u32[]{:S(2)}) collective-permute-start(bf16[384,1024]{1,0:T(8,128)(2,1)S(1)} %collective-permute-done.38.refs_26_), channel_id=1, source_target_pairs={{0,1},{1,0},{2,3},{3,2},{4,5},{5,4},{6,7},{7,6},{8,9},{9,8},{10,11... | collective-permute-start | bytes 2359304 | tf_op jit(solution)/shard_map/ppermute | solution.py:563
  155.3 5.8 %collective-permute-start.45 = (bf16[384,1024]{1,0:T(8,128)(2,1)S(1)}, bf16[384,1024]{1,0:T(8,128)(2,1)S(1)}, u32[]{:S(2)}, u32[]{:S(2)}) collective-permute-start(bf16[384,1024]{1,0:T(8,128)(2,1)S(1)} %collective-permute-done.39.refs_27_), channel_id=1, source_target_pairs={{0,1},{1,0},{2,3},{3,2},{4,5},{5,4},{6,7},{7,6},{8,9},{9,8},{10,11... | collective-permute-start | bytes 2359304 | tf_op jit(solution)/shard_map/ppermute | solution.py:563
  155.3 2.7 %collective-permute-start.46 = (bf16[32,4096]{1,0:T(8,128)(2,1)}, bf16[32,4096]{1,0:T(8,128)(2,1)S(1)}, u32[]{:S(2)}, u32[]{:S(2)}) collective-permute-start(bf16[32,4096]{1,0:T(8,128)(2,1)} %copy-done.30), channel_id=1, source_target_pairs={{0,1},{1,0},{2,3},{3,2},{4,5},{5,4},{6,7},{7,6},{8,9},{9,8},{10,11... | collective-permute-start | bytes 786440 | tf_op jit(solution)/shard_map/ppermute | solution.py:563
  155.8 3.0 %collective-permute-start.47 = (bf16[32,4096]{1,0:T(8,128)(2,1)}, bf16[32,4096]{1,0:T(8,128)(2,1)S(1)}, u32[]{:S(2)}, u32[]{:S(2)}) collective-permute-start(bf16[32,4096]{1,0:T(8,128)(2,1)} %copy-done.31), channel_id=1, source_target_pairs={{0,1},{1,0},{2,3},{3,2},{4,5},{5,4},{6,7},{7,6},{8,9},{9,8},{10,11... | collective-permute-start | bytes 786440 | tf_op jit(solution)/shard_map/ppermute | solution.py:563
  (40 other events, 385.7 us)

commit v6 on v5

--- a/solution.py
+++ b/solution.py
@@ -748,15 +748,12 @@
     )
     input_grad, sum_q = back(scalars, seqs, qkv, context, d_context, inverse, powers, d_joined, qkv_parts)
     devices = lax.axis_size("dp") * lax.axis_size("fsdp")
-    parts = (sum_q[0], sums[0], sums[1], sums[2], sum_in[0], sums[3], sums[4])
-    rows = jnp.concatenate([part.reshape(devices, -1) for part in parts], axis=1)
+    small = jnp.concatenate([sum_q, sums[:5]], axis=0).reshape(6, devices, -1).transpose(1, 0, 2)
+    rows = jnp.concatenate([sum_in.reshape(devices, -1), small.reshape(devices, -1)], axis=1)
     mine = jnp.sum(lax.all_to_all(rows, BOTH, 0, 0, tiled=True), axis=0)
-    small = width // devices
-    sizes = (small, small, small, small, sum_in.shape[1] // devices, small, small)
-    shares, at = [], 0
-    for size in sizes:
-        shares.append(mine[at : at + size])
-        at += size
+    wide = sum_in.shape[1] // devices
+    six = mine[wide:].reshape(6, -1)
+    shares = (six[0], six[1], six[2], six[3], mine[:wide], six[4], six[5])
     return (output, input_grad, *shares)
 
 

time: 253 us -> 252 us (level)
  no operation moved by 1% of the time
where the time goes in v6:
time: 252 us; the launch traced here: 251 us
  Pallas kernels  138 us (55%)
  waiting for transfers between devices  46.4 us (18%)
  starting transfers between devices  44.1 us (18%)
  blocking collectives  11 us (4%)
  local copies, waits for them, and re-layouts  6.8 us (3%)
  other arithmetic  3.3 us (1%)
    ppermute x50, waiting for transfers between devices, hop(): return lax.ppermute(block, axis, [(i, i ^ flip) for i in range(size)])  46.4 us
    pallas_call x1, Pallas kernels, turn(): pl.pallas_call(functools.partial(turn_body, seqs, tags_of(feeds), tags_of...  44.2 us
    ppermute x50, starting transfers between devices, hop(): return lax.ppermute(block, axis, [(i, i ^ flip) for i in range(size)])  44.1 us
    pallas_call x1, Pallas kernels, back(): pl.pallas_call(functools.partial(back_body, seqs, tags_of(sources)), out_...  31.4 us
    pallas_call x1, Pallas kernels, join(): pl.pallas_call(functools.partial(join_body, seqs, tags_of(sources)), out_...  25.9 us
    pallas_call x2, Pallas kernels, attend(): pl.pallas_call(functools.partial(attend_body, seq), out_shape=(shape_of((...  20.4 us
    pallas_call x1, Pallas kernels, project(): pl.pallas_call(functools.partial(project_body, seqs, tags_of(sources)), o...  12.4 us
    all_to_all x1, blocking collectives, on_device(): mine = jnp.sum(lax.all_to_all(rows, BOTH, 0, 0, tiled=True), axis=0)  11 us
  transfers between devices with their start and end apart: 50, of which 16 were waited for; matrix products, arithmetic and copies ran while one was open for 2% of the time, Pallas kernels for 24%

profile of v6, /device:TPU:0, one launch (start us, length us, event | category | flops | bytes accessed | tf_op | source)
XLA Modules:
  0.0 251.1 jit_solution(12827818463749820603)
XLA Ops:
  0.6 2.1 pack.1
  2.7 3.0 %collective-permute-start.3 = (bf16[32,12288]{1,0:T(8,128)(2,1)}, bf16[32,12288]{1,0:T(8,128)(2,1)S(1)}, u32[]{:S(2)}, u32[]{:S(2)}) collective-permute-start(bf16[32,12288]{1,0:T(8,128)(2,1)} %get-tuple-element.151.refs_0_.refs_22_), channel_id=1, source_target_pairs={{0,8},{8,0},{16,24},{24,16},{1,9},{9,1},{17,25},{25,17},{2,10},{10... | collective-permute-start | bytes 2359304 | tf_op jit(solution)/shard_map/ppermute | solution.py:563
  5.7 1.5 collective-permute-start.4
  7.3 2.6 %collective-permute-start = (bf16[32,3072]{1,0:T(8,128)(2,1)}, bf16[32,3072]{1,0:T(8,128)(2,1)S(1)}, u32[]{:S(2)}, u32[]{:S(2)}) collective-permute-start(bf16[32,3072]{1,0:T(8,128)(2,1)} %qkv_ref.1), channel_id=1, source_target_pairs={{0,4},{1,5},{2,6},{3,7},{4,0},{5,1},{6,2},{7,3},{8,12},{9,13},{10,... | collective-permute-start | bytes 589832 | tf_op jit(solution)/shard_map/ppermute | solution.py:563
  9.9 1.3 collective-permute-start.1
  11.4 1.4 stack.43.vec_ref
  12.9 1.2 pad_add_fusion.len_ref
  14.1 1.3 pad_maximum_fusion.1
  15.4 8.7 %collective-permute-done.refs_1_ = bf16[32,3072]{1,0:T(8,128)(2,1)S(1)} collective-permute-done((bf16[32,3072]{1,0:T(8,128)(2,1)}, bf16[32,3072]{1,0:T(8,128)(2,1)S(1)}, u32[]{:S(2)}, u32[]{:S(2)}) %collective-permute-start) | collective-permute-done | bytes 196640 | tf_op jit(solution)/shard_map/ppermute | solution.py:563
  24.3 0.8 collective-permute-done.4.refs_2_.refs_24_
  26.1 1.7 collective-permute-start.6
  27.8 3.7 %collective-permute-start.7 = (bf16[32,5120]{1,0:T(8,128)(2,1)}, bf16[32,5120]{1,0:T(8,128)(2,1)S(1)}, u32[]{:S(2)}, u32[]{:S(2)}) collective-permute-start(bf16[32,5120]{1,0:T(8,128)(2,1)} %get-tuple-element.181), channel_id=1, source_target_pairs={{0,4},{1,5},{2,6},{3,7},{4,0},{5,1},{6,2},{7,3},{8,12},{9,13},{10,... | collective-permute-start | bytes 983048 | tf_op jit(solution)/shard_map/ppermute | solution.py:563
  31.4 14.6 %collective-permute-done.7.refs_1_ = bf16[32,5120]{1,0:T(8,128)(2,1)S(1)} collective-permute-done((bf16[32,5120]{1,0:T(8,128)(2,1)}, bf16[32,5120]{1,0:T(8,128)(2,1)S(1)}, u32[]{:S(2)}, u32[]{:S(2)}) %collective-permute-start.7) | collective-permute-done | bytes 327712 | tf_op jit(solution)/shard_map/ppermute | solution.py:563
  46.1 0.9 copy-done.11
  47.7 1.5 collective-permute-start.10
  49.2 1.5 collective-permute-start.11
  50.7 9.3 %collective-permute-done.12.refs_0_ = bf16[32,5120]{1,0:T(8,128)(2,1)S(1)} collective-permute-done((bf16[32,5120]{1,0:T(8,128)(2,1)}, bf16[32,5120]{1,0:T(8,128)(2,1)S(1)}, u32[]{:S(2)}, u32[]{:S(2)}) %collective-permute-start.12) | collective-permute-done | bytes 327712 | tf_op jit(solution)/shard_map/ppermute | solution.py:563
  61.2 0.9 glue.7
  62.1 1.4 collective-permute-done.17.refs_14_
  64.3 1.5 collective-permute-start.19
  66.3 2.6 %collective-permute-start.21 = (bf16[32,5120]{1,0:T(8,128)(2,1)}, bf16[32,5120]{1,0:T(8,128)(2,1)}, u32[]{:S(2)}, u32[]{:S(2)}) collective-permute-start(bf16[32,5120]{1,0:T(8,128)(2,1)} %get-tuple-element.181), channel_id=1, source_target_pairs={{0,6},{1,7},{2,4},{3,5},{4,2},{5,3},{6,0},{7,1},{8,14},{9,15},{10,... | collective-permute-start | bytes 983048 | tf_op jit(solution)/shard_map/ppermute | solution.py:563
  69.0 12.4 %project.1.q_ref.k_ref.v_ref = bf16[1024,3072]{1,0:T(8,128)(2,1)} custom-call(s32[5]{0:T(128)} %pad_add_fusion.len_ref, bf16[1024,1024]{1,0:T(8,128)(2,1)} %x_ref.2, f32[1,3072]{1,0:T(1,128)} %bitcast.21, f32[1,3072]{1,0:T(1,128)} %constant.37.clone.1.scale_ref, bf16[32,12288]{1,0:T(8,128)(2,1)} %get-tuple-element.151.refs_0_.refs_22_, ...), custom_call_target="tpu_custom_call" | custom-call | flops 6442450944 | tf_op jit(solution)/shard_map/project/pallas_call | solution.py:147
  81.4 1.1 collective-permute-done.20.refs_2_.refs_5_
  82.5 2.0 collective-permute-start.25
  84.7 1.5 collective-permute-start.27
  86.2 0.9 collective-permute-start.23
  87.1 0.8 collective-permute-start.24
  87.9 10.3 %attend.2 = (bf16[1024,1024]{1,0:T(8,128)(2,1)}, bf16[32,512,512]{2,1,0:T(8,128)(2,1)}, f32[1024,1024]{1,0:T(8,128)}) custom-call(s32[5]{0:T(128)} %pad_add_fusion.len_ref, bf16[1024,3072]{1,0:T(8,128)(2,1)} %project.1.q_ref.k_ref.v_ref, bf16[1024,3072]{1,0:T(8,128)(2,1)} %project.1.q_ref.k_ref.v_ref, bf16[1024,3072]{1,0:T(8,128)(2,1)} %project.1.q_ref.k_ref.v_ref), custom_call_target="tpu_custom_call" | custom-call | flops 4294967296 | tf_op jit(solution)/shard_map/attend/pallas_call | solution.py:220
  98.2 0.9 collective-permute-done.24.refs_3_.refs_8_
  99.1 0.9 glue.8
  100.1 0.7 collective-permute-start.28
  100.8 1.3 collective-permute-start.29
  102.6 2.2 collective-permute-start.30
  104.7 10.2 %attend.3 = (bf16[1024,1024]{1,0:T(8,128)(2,1)}, bf16[32,512,512]{2,1,0:T(8,128)(2,1)}, f32[1024,1024]{1,0:T(8,128)}) custom-call(s32[5]{0:T(128)} %pad_add_fusion.len_ref, bf16[1024,3072]{1,0:T(8,128)(2,1)} %project.1.q_ref.k_ref.v_ref, bf16[1024,3072]{1,0:T(8,128)(2,1)} %project.1.q_ref.k_ref.v_ref, ...), custom_call_target="tpu_custom_call", output_to_operand_aliasing={{0}: (4, {}), {1}: (5, {}), {2}: (6, {})} | custom-call | flops 4294967296 | tf_op jit(solution)/shard_map/attend/pallas_call | solution.py:220
  116.6 3.0 %collective-permute-done.33.refs_17_ = bf16[32,5120]{1,0:T(8,128)(2,1)S(1)} collective-permute-done((bf16[32,5120]{1,0:T(8,128)(2,1)}, bf16[32,5120]{1,0:T(8,128)(2,1)S(1)}, u32[]{:S(2)}, u32[]{:S(2)}) %collective-permute-start.33) | collective-permute-done | bytes 327712 | tf_op jit(solution)/shard_map/ppermute | solution.py:563
  120.1 3.9 %collective-permute-start.40 = (bf16[32,4096]{1,0:T(8,128)(2,1)}, bf16[32,4096]{1,0:T(8,128)(2,1)S(1)}, u32[]{:S(2)}, u32[]{:S(2)}) collective-permute-start(bf16[32,4096]{1,0:T(8,128)(2,1)} %copy-done.31), channel_id=1, source_target_pairs={{0,4},{1,5},{2,6},{3,7},{4,0},{5,1},{6,2},{7,3},{8,12},{9,13},{10,... | collective-permute-start | bytes 786440 | tf_op jit(solution)/shard_map/ppermute | solution.py:563
  124.0 1.5 collective-permute-start.41
  125.6 0.8 collective-permute-start.38
  126.3 1.5 collective-permute-start.39
  127.8 25.9 %join.1 = (f32[1024,1024]{1,0:T(8,128)}, f32[1024,128]{1,0:T(8,128)}, bf16[1024,4096]{1,0:T(8,128)(2,1)}, bf16[1024,4096]{1,0:T(8,128)(2,1)}) custom-call(s32[5]{0:T(128)} %pad_add_fusion.len_ref, bf16[1024,1024]{1,0:T(8,128)(2,1)} %x_ref.2, bf16[1024,1024]{1,0:T(8,128)(2,1)} %get-tuple-element.220.o_ref, f32[8,1024]{1,0:T(8,128)} %stack.43.vec_ref, ...), custom_call_target="tpu_custom_call" | custom-call | flops 10737418240 | tf_op jit(solution)/shard_map/join/pallas_call | solution.py:290
  153.7 0.6 copy-done.32
  155.7 2.1 collective-permute-done.47.refs_39_
  158.8 1.7 collective-permute-done.49.refs_41_
  160.9 0.9 copy-done.17
  162.3 44.2 %turn.1 = (bf16[1024,1024]{1,0:T(8,128)(2,1)}, f32[1024,1024]{1,0:T(8,128)}, bf16[1024,1024]{1,0:T(8,128)(2,1)}, f32[8,1024]{1,0:T(8,128)}, f32[1,4096]{1,0:T(1,128)}) custom-call(s32[5]{0:T(128)} %pad_add_fusion.len_ref, bf16[1024,4096]{1,0:T(8,128)(2,1)} %get-tuple-element.245.gl_ref, f32[1024,1024]{1,0:T(8,128)} %get-tuple-element.246.u_ref, ...), custom_call_target="tpu_custom_call" | custom-call | flops 27917287424 | tf_op jit(solution)/shard_map/turn/pallas_call | solution.py:407
  206.6 31.4 %back.1 = (bf16[1024,1024]{1,0:T(8,128)(2,1)}, f32[1,1024]{1,0:T(1,128)}) custom-call(s32[5]{0:T(128)} %pad_add_fusion.len_ref, bf16[1024,3072]{1,0:T(8,128)(2,1)} %project.1.q_ref.k_ref.v_ref, bf16[1024,3072]{1,0:T(8,128)(2,1)} %project.1.q_ref.k_ref.v_ref, bf16[1024,3072]{1,0:T(8,128)(2,1)} %project.1.q_ref.k_ref.v_ref, ...), custom_call_target="tpu_custom_call" | custom-call | flops 17179869184 | tf_op jit(solution)/shard_map/back/pallas_call | solution.py:524
  237.9 0.7 pad_maximum_fusion
  238.9 11.0 %all_to_all.9 = f32[32,1,320]{2,1,0:T(1,128)S(1)} all-to-all(f32[32,1,320]{2,1,0:T(1,128)S(1)} %copy.30), channel_id=1, replica_groups=mesh['dp'=4,'fsdp'=8] {'dp','fsdp'}, dimensions={0} | all-to-all | bytes 81920 | tf_op jit(solution)/shard_map/all_to_all | solution.py:753
  (157 shorter events, 11.8 us)
Async XLA Ops:
  2.7 21.5 %collective-permute-start.3 = (bf16[32,12288]{1,0:T(8,128)(2,1)}, bf16[32,12288]{1,0:T(8,128)(2,1)S(1)}, u32[]{:S(2)}, u32[]{:S(2)}) collective-permute-start(bf16[32,12288]{1,0:T(8,128)(2,1)} %get-tuple-element.151.refs_0_.refs_22_), channel_id=1, source_target_pairs={{0,8},{8,0},{16,24},{24,16},{1,9},{9,1},{17,25},{25,17},{2,10},{10... | collective-permute-start | bytes 2359304 | tf_op jit(solution)/shard_map/ppermute | solution.py:563
  5.7 19.3 %collective-permute-start.4 = (bf16[32,12288]{1,0:T(8,128)(2,1)}, bf16[32,12288]{1,0:T(8,128)(2,1)}, u32[]{:S(2)}, u32[]{:S(2)}) collective-permute-start(bf16[32,12288]{1,0:T(8,128)(2,1)} %get-tuple-element.151.refs_0_.refs_22_), channel_id=1, source_target_pairs={{0,16},{8,24},{16,0},{24,8},{1,17},{9,25},{17,1},{25,9},{2,18},{10... | collective-permute-start | bytes 2359304 | tf_op jit(solution)/shard_map/ppermute | solution.py:563
  7.3 16.8 %collective-permute-start = (bf16[32,3072]{1,0:T(8,128)(2,1)}, bf16[32,3072]{1,0:T(8,128)(2,1)S(1)}, u32[]{:S(2)}, u32[]{:S(2)}) collective-permute-start(bf16[32,3072]{1,0:T(8,128)(2,1)} %qkv_ref.1), channel_id=1, source_target_pairs={{0,4},{1,5},{2,6},{3,7},{4,0},{5,1},{6,2},{7,3},{8,12},{9,13},{10,... | collective-permute-start | bytes 589832 | tf_op jit(solution)/shard_map/ppermute | solution.py:563
  9.9 14.3 %collective-permute-start.1 = (bf16[32,3072]{1,0:T(8,128)(2,1)}, bf16[32,3072]{1,0:T(8,128)(2,1)S(1)}, u32[]{:S(2)}, u32[]{:S(2)}) collective-permute-start(bf16[32,3072]{1,0:T(8,128)(2,1)} %qkv_ref.1), channel_id=1, source_target_pairs={{0,6},{1,7},{2,4},{3,5},{4,2},{5,3},{6,0},{7,1},{8,14},{9,15},{10,... | collective-permute-start | bytes 589832 | tf_op jit(solution)/shard_map/ppermute | solution.py:563
  11.2 13.0 %collective-permute-start.2 = (bf16[32,3072]{1,0:T(8,128)(2,1)}, bf16[32,3072]{1,0:T(8,128)(2,1)S(1)}, u32[]{:S(2)}, u32[]{:S(2)}) collective-permute-start(bf16[32,3072]{1,0:T(8,128)(2,1)} %qkv_ref.1), channel_id=1, source_target_pairs={{0,2},{1,3},{2,0},{3,1},{4,6},{5,7},{6,4},{7,5},{8,10},{9,11},{10,... | collective-permute-start | bytes 589832 | tf_op jit(solution)/shard_map/ppermute | solution.py:563
  25.1 21.0 %collective-permute-start.8 = (bf16[32,12288]{1,0:T(8,128)(2,1)}, bf16[32,12288]{1,0:T(8,128)(2,1)S(1)}, u32[]{:S(2)}, u32[]{:S(2)}) collective-permute-start(bf16[32,12288]{1,0:T(8,128)(2,1)} %get-tuple-element.151.refs_0_.refs_22_), channel_id=1, source_target_pairs={{0,1},{1,0},{2,3},{3,2},{4,5},{5,4},{6,7},{7,6},{8,9},{9,8},{10,11... | collective-permute-start | bytes 2359304 | tf_op jit(solution)/shard_map/ppermute | solution.py:563
  25.2 21.8 %collective-permute-start.9 = (bf16[32,12288]{1,0:T(8,128)(2,1)S(1)}, bf16[32,12288]{1,0:T(8,128)(2,1)}, u32[]{:S(2)}, u32[]{:S(2)}) collective-permute-start(bf16[32,12288]{1,0:T(8,128)(2,1)S(1)} %collective-permute-done.3.refs_0_.refs_2_.refs_1_.refs_23_), channel_id=1, source_target_pairs={{0,1},{1,0},{2,3},{3,2},{4,5},{5,4},{6,7},{7,6},{8,9},{9,8},{10,11... | collective-permute-start | bytes 2359304 | tf_op jit(solution)/shard_map/ppermute | solution.py:563
  25.7 20.4 %collective-permute-start.5 = (bf16[96,3072]{1,0:T(8,128)(2,1)S(1)}, bf16[96,3072]{1,0:T(8,128)(2,1)S(1)}, u32[]{:S(2)}, u32[]{:S(2)}) collective-permute-start(bf16[96,3072]{1,0:T(8,128)(2,1)S(1)} %glue.5.refs_3_), channel_id=1, source_target_pairs={{0,8},{8,0},{16,24},{24,16},{1,9},{9,1},{17,25},{25,17},{2,10},{10... | collective-permute-start | bytes 1769480 | tf_op jit(solution)/shard_map/ppermute | solution.py:563
  26.1 20.0 %collective-permute-start.6 = (bf16[96,3072]{1,0:T(8,128)(2,1)S(1)}, bf16[96,3072]{1,0:T(8,128)(2,1)S(1)}, u32[]{:S(2)}, u32[]{:S(2)}) collective-permute-start(bf16[96,3072]{1,0:T(8,128)(2,1)S(1)} %glue.5.refs_3_), channel_id=1, source_target_pairs={{0,16},{8,24},{16,0},{24,8},{1,17},{9,25},{17,1},{25,9},{2,18},{10... | collective-permute-start | bytes 1769480 | tf_op jit(solution)/shard_map/ppermute | solution.py:563
  27.8 18.3 %collective-permute-start.7 = (bf16[32,5120]{1,0:T(8,128)(2,1)}, bf16[32,5120]{1,0:T(8,128)(2,1)S(1)}, u32[]{:S(2)}, u32[]{:S(2)}) collective-permute-start(bf16[32,5120]{1,0:T(8,128)(2,1)} %get-tuple-element.181), channel_id=1, source_target_pairs={{0,4},{1,5},{2,6},{3,7},{4,0},{5,1},{6,2},{7,3},{8,12},{9,13},{10,... | collective-permute-start | bytes 983048 | tf_op jit(solution)/shard_map/ppermute | solution.py:563
  47.1 13.0 %collective-permute-start.13 = (bf16[32,12288]{1,0:T(8,128)(2,1)}, bf16[32,12288]{1,0:T(8,128)(2,1)S(1)}, u32[]{:S(2)}, u32[]{:S(2)}) collective-permute-start(bf16[32,12288]{1,0:T(8,128)(2,1)} %collective-permute-done.4.refs_2_.refs_24_), channel_id=1, source_target_pairs={{0,1},{1,0},{2,3},{3,2},{4,5},{5,4},{6,7},{7,6},{8,9},{9,8},{10,11... | collective-permute-start | bytes 2359304 | tf_op jit(solution)/shard_map/ppermute | solution.py:563
  47.2 12.9 %collective-permute-start.14 = (bf16[96,3072]{1,0:T(8,128)(2,1)S(1)}, bf16[96,3072]{1,0:T(8,128)(2,1)S(1)}, u32[]{:S(2)}, u32[]{:S(2)}) collective-permute-start(bf16[96,3072]{1,0:T(8,128)(2,1)S(1)} %glue.5.refs_3_), channel_id=1, source_target_pairs={{0,1},{1,0},{2,3},{3,2},{4,5},{5,4},{6,7},{7,6},{8,9},{9,8},{10,11... | collective-permute-start | bytes 1769480 | tf_op jit(solution)/shard_map/ppermute | solution.py:563
  47.7 12.4 %collective-permute-start.10 = (bf16[64,3072]{1,0:T(8,128)(2,1)S(1)}, bf16[64,3072]{1,0:T(8,128)(2,1)S(1)}, u32[]{:S(2)}, u32[]{:S(2)}) collective-permute-start(bf16[64,3072]{1,0:T(8,128)(2,1)S(1)} %get-tuple-element.161), channel_id=1, source_target_pairs={{0,16},{8,24},{16,0},{24,8},{1,17},{9,25},{17,1},{25,9},{2,18},{10... | collective-permute-start | bytes 1179656 | tf_op jit(solution)/shard_map/ppermute | solution.py:563
  49.2 10.8 %collective-permute-start.11 = (bf16[64,3072]{1,0:T(8,128)(2,1)S(1)}, bf16[64,3072]{1,0:T(8,128)(2,1)S(1)}, u32[]{:S(2)}, u32[]{:S(2)}) collective-permute-start(bf16[64,3072]{1,0:T(8,128)(2,1)S(1)} %get-tuple-element.162), channel_id=1, source_target_pairs={{0,8},{8,0},{16,24},{24,16},{1,9},{9,1},{17,25},{25,17},{2,10},{10... | collective-permute-start | bytes 1179656 | tf_op jit(solution)/shard_map/ppermute | solution.py:563
  50.7 9.3 %collective-permute-start.12 = (bf16[32,5120]{1,0:T(8,128)(2,1)}, bf16[32,5120]{1,0:T(8,128)(2,1)S(1)}, u32[]{:S(2)}, u32[]{:S(2)}) collective-permute-start(bf16[32,5120]{1,0:T(8,128)(2,1)} %get-tuple-element.181), channel_id=1, source_target_pairs={{0,2},{1,3},{2,0},{3,1},{4,6},{5,7},{6,4},{7,5},{8,10},{9,11},{10,... | collective-permute-start | bytes 983048 | tf_op jit(solution)/shard_map/ppermute | solution.py:563
  60.1 4.0 %collective-permute-start.15 = (bf16[96,3072]{1,0:T(8,128)(2,1)S(1)}, bf16[96,3072]{1,0:T(8,128)(2,1)S(1)}, u32[]{:S(2)}, u32[]{:S(2)}) collective-permute-start(bf16[96,3072]{1,0:T(8,128)(2,1)S(1)} %collective-permute-done.5.refs_1_.refs_4_), channel_id=1, source_target_pairs={{0,1},{1,0},{2,3},{3,2},{4,5},{5,4},{6,7},{7,6},{8,9},{9,8},{10,11... | collective-permute-start | bytes 1769480 | tf_op jit(solution)/shard_map/ppermute | solution.py:563
  60.2 4.0 %collective-permute-start.16 = (bf16[96,3072]{1,0:T(8,128)(2,1)S(1)}, bf16[96,3072]{1,0:T(8,128)(2,1)S(1)}, u32[]{:S(2)}, u32[]{:S(2)}) collective-permute-start(bf16[96,3072]{1,0:T(8,128)(2,1)S(1)} %collective-permute-done.6.refs_2_.refs_5_), channel_id=1, source_target_pairs={{0,1},{1,0},{2,3},{3,2},{4,5},{5,4},{6,7},{7,6},{8,9},{9,8},{10,11... | collective-permute-start | bytes 1769480 | tf_op jit(solution)/shard_map/ppermute | solution.py:563
  60.7 2.9 %collective-permute-start.17 = (bf16[64,3072]{1,0:T(8,128)(2,1)S(1)}, bf16[64,3072]{1,0:T(8,128)(2,1)S(1)}, u32[]{:S(2)}, u32[]{:S(2)}) collective-permute-start(bf16[64,3072]{1,0:T(8,128)(2,1)S(1)} %collective-permute-done.10.refs_6_), channel_id=1, source_target_pairs={{0,1},{1,0},{2,3},{3,2},{4,5},{5,4},{6,7},{7,6},{8,9},{9,8},{10,11... | collective-permute-start | bytes 1179656 | tf_op jit(solution)/shard_map/ppermute | solution.py:563
  61.2 2.9 %collective-permute-start.18 = (bf16[64,3072]{1,0:T(8,128)(2,1)S(1)}, bf16[64,3072]{1,0:T(8,128)(2,1)S(1)}, u32[]{:S(2)}, u32[]{:S(2)}) collective-permute-start(bf16[64,3072]{1,0:T(8,128)(2,1)S(1)} %collective-permute-done.11.refs_7_), channel_id=1, source_target_pairs={{0,1},{1,0},{2,3},{3,2},{4,5},{5,4},{6,7},{7,6},{8,9},{9,8},{10,11... | collective-permute-start | bytes 1179656 | tf_op jit(solution)/shard_map/ppermute | solution.py:563
  64.3 17.1 %collective-permute-start.19 = (bf16[64,5120]{1,0:T(8,128)(2,1)}, bf16[64,5120]{1,0:T(8,128)(2,1)S(1)}, u32[]{:S(2)}, u32[]{:S(2)}) collective-permute-start(bf16[64,5120]{1,0:T(8,128)(2,1)} %get-tuple-element.182.refs_3_), channel_id=1, source_target_pairs={{0,8},{8,0},{16,24},{24,16},{1,9},{9,1},{17,25},{25,17},{2,10},{10... | collective-permute-start | bytes 1966088 | tf_op jit(solution)/shard_map/ppermute | solution.py:563
  65.8 16.7 %collective-permute-start.20 = (bf16[64,5120]{1,0:T(8,128)(2,1)}, bf16[64,5120]{1,0:T(8,128)(2,1)S(1)}, u32[]{:S(2)}, u32[]{:S(2)}) collective-permute-start(bf16[64,5120]{1,0:T(8,128)(2,1)} %get-tuple-element.182.refs_3_), channel_id=1, source_target_pairs={{0,16},{8,24},{16,0},{24,8},{1,17},{9,25},{17,1},{25,9},{2,18},{10... | collective-permute-start | bytes 1966088 | tf_op jit(solution)/shard_map/ppermute | solution.py:563
  66.3 16.2 %collective-permute-start.22 = (bf16[64,5120]{1,0:T(8,128)(2,1)}, bf16[64,5120]{1,0:T(8,128)(2,1)}, u32[]{:S(2)}, u32[]{:S(2)}) collective-permute-start(bf16[64,5120]{1,0:T(8,128)(2,1)} %get-tuple-element.182.refs_3_), channel_id=1, source_target_pairs={{0,1},{1,0},{2,3},{3,2},{4,5},{5,4},{6,7},{7,6},{8,9},{9,8},{10,11... | collective-permute-start | bytes 1966088 | tf_op jit(solution)/shard_map/ppermute | solution.py:563
  66.3 15.1 %collective-permute-start.21 = (bf16[32,5120]{1,0:T(8,128)(2,1)}, bf16[32,5120]{1,0:T(8,128)(2,1)}, u32[]{:S(2)}, u32[]{:S(2)}) collective-permute-start(bf16[32,5120]{1,0:T(8,128)(2,1)} %get-tuple-element.181), channel_id=1, source_target_pairs={{0,6},{1,7},{2,4},{3,5},{4,2},{5,3},{6,0},{7,1},{8,14},{9,15},{10,... | collective-permute-start | bytes 983048 | tf_op jit(solution)/shard_map/ppermute | solution.py:563
  82.5 15.7 %collective-permute-start.25 = (bf16[128,1024]{1,0:T(8,128)(2,1)}, bf16[128,1024]{1,0:T(8,128)(2,1)S(1)}, u32[]{:S(2)}, u32[]{:S(2)}) collective-permute-start(bf16[128,1024]{1,0:T(8,128)(2,1)} %down_ref.1), channel_id=1, source_target_pairs={{0,4},{1,5},{2,6},{3,7},{4,0},{5,1},{6,2},{7,3},{8,12},{9,13},{10,... | collective-permute-start | bytes 786440 | tf_op jit(solution)/shard_map/ppermute | solution.py:563
  84.5 13.7 %collective-permute-start.26 = (bf16[128,1024]{1,0:T(8,128)(2,1)}, bf16[128,1024]{1,0:T(8,128)(2,1)S(1)}, u32[]{:S(2)}, u32[]{:S(2)}) collective-permute-start(bf16[128,1024]{1,0:T(8,128)(2,1)} %down_ref.1), channel_id=1, source_target_pairs={{0,2},{1,3},{2,0},{3,1},{4,6},{5,7},{6,4},{7,5},{8,10},{9,11},{10,... | collective-permute-start | bytes 786440 | tf_op jit(solution)/shard_map/ppermute | solution.py:563
  84.7 13.5 %collective-permute-start.27 = (bf16[32,4096]{1,0:T(8,128)(2,1)S(1)}, bf16[32,4096]{1,0:T(8,128)(2,1)S(1)}, u32[]{:S(2)}, u32[]{:S(2)}) collective-permute-start(bf16[32,4096]{1,0:T(8,128)(2,1)S(1)} %get-tuple-element.194), channel_id=1, source_target_pairs={{0,16},{8,24},{16,0},{24,8},{1,17},{9,25},{17,1},{25,9},{2,18},{10... | collective-permute-start | bytes 786440 | tf_op jit(solution)/shard_map/ppermute | solution.py:563
  86.2 12.0 %collective-permute-start.23 = (bf16[32,5120]{1,0:T(8,128)(2,1)}, bf16[32,5120]{1,0:T(8,128)(2,1)}, u32[]{:S(2)}, u32[]{:S(2)}) collective-permute-start(bf16[32,5120]{1,0:T(8,128)(2,1)} %collective-permute-done.21.refs_6_), channel_id=1, source_target_pairs={{0,8},{8,0},{16,24},{24,16},{1,9},{9,1},{17,25},{25,17},{2,10},{10... | collective-permute-start | bytes 983048 | tf_op jit(solution)/shard_map/ppermute | solution.py:563
  87.1 12.0 %collective-permute-start.24 = (bf16[32,5120]{1,0:T(8,128)(2,1)}, bf16[32,5120]{1,0:T(8,128)(2,1)S(1)}, u32[]{:S(2)}, u32[]{:S(2)}) collective-permute-start(bf16[32,5120]{1,0:T(8,128)(2,1)} %collective-permute-done.21.refs_6_), channel_id=1, source_target_pairs={{0,16},{8,24},{16,0},{24,8},{1,17},{9,25},{17,1},{25,9},{2,18},{10... | collective-permute-start | bytes 983048 | tf_op jit(solution)/shard_map/ppermute | solution.py:563
  100.1 15.2 %collective-permute-start.28 = (bf16[64,5120]{1,0:T(8,128)(2,1)}, bf16[64,5120]{1,0:T(8,128)(2,1)}, u32[]{:S(2)}, u32[]{:S(2)}) collective-permute-start(bf16[64,5120]{1,0:T(8,128)(2,1)} %get-tuple-element.212), channel_id=1, source_target_pairs={{0,16},{8,24},{16,0},{24,8},{1,17},{9,25},{17,1},{25,9},{2,18},{10... | collective-permute-start | bytes 1966088 | tf_op jit(solution)/shard_map/ppermute | solution.py:563
  100.8 14.5 %collective-permute-start.29 = (bf16[64,5120]{1,0:T(8,128)(2,1)S(1)}, bf16[64,5120]{1,0:T(8,128)(2,1)}, u32[]{:S(2)}, u32[]{:S(2)}) collective-permute-start(bf16[64,5120]{1,0:T(8,128)(2,1)S(1)} %get-tuple-element.213), channel_id=1, source_target_pairs={{0,8},{8,0},{16,24},{24,16},{1,9},{9,1},{17,25},{25,17},{2,10},{10... | collective-permute-start | bytes 1966088 | tf_op jit(solution)/shard_map/ppermute | solution.py:563
  102.1 13.2 %collective-permute-start.31 = (bf16[64,5120]{1,0:T(8,128)(2,1)S(1)}, bf16[64,5120]{1,0:T(8,128)(2,1)S(1)}, u32[]{:S(2)}, u32[]{:S(2)}) collective-permute-start(bf16[64,5120]{1,0:T(8,128)(2,1)S(1)} %collective-permute-done.19.refs_1_.refs_4_), channel_id=1, source_target_pairs={{0,1},{1,0},{2,3},{3,2},{4,5},{5,4},{6,7},{7,6},{8,9},{9,8},{10,11... | collective-permute-start | bytes 1966088 | tf_op jit(solution)/shard_map/ppermute | solution.py:563
  102.1 13.2 %collective-permute-start.32 = (bf16[64,5120]{1,0:T(8,128)(2,1)S(1)}, bf16[64,5120]{1,0:T(8,128)(2,1)}, u32[]{:S(2)}, u32[]{:S(2)}) collective-permute-start(bf16[64,5120]{1,0:T(8,128)(2,1)S(1)} %collective-permute-done.20.refs_2_.refs_5_), channel_id=1, source_target_pairs={{0,1},{1,0},{2,3},{3,2},{4,5},{5,4},{6,7},{7,6},{8,9},{9,8},{10,11... | collective-permute-start | bytes 1966088 | tf_op jit(solution)/shard_map/ppermute | solution.py:563
  102.6 12.3 %collective-permute-start.30 = (bf16[128,1024]{1,0:T(8,128)(2,1)}, bf16[128,1024]{1,0:T(8,128)(2,1)S(1)}, u32[]{:S(2)}, u32[]{:S(2)}) collective-permute-start(bf16[128,1024]{1,0:T(8,128)(2,1)} %down_ref.1), channel_id=1, source_target_pairs={{0,6},{1,7},{2,4},{3,5},{4,2},{5,3},{6,0},{7,1},{8,14},{9,15},{10,... | collective-permute-start | bytes 786440 | tf_op jit(solution)/shard_map/ppermute | solution.py:563
  115.3 4.7 %collective-permute-start.36 = (bf16[64,5120]{1,0:T(8,128)(2,1)}, bf16[64,5120]{1,0:T(8,128)(2,1)S(1)}, u32[]{:S(2)}, u32[]{:S(2)}) collective-permute-start(bf16[64,5120]{1,0:T(8,128)(2,1)} %collective-permute-done.28.refs_9_), channel_id=1, source_target_pairs={{0,1},{1,0},{2,3},{3,2},{4,5},{5,4},{6,7},{7,6},{8,9},{9,8},{10,11... | collective-permute-start | bytes 1966088 | tf_op jit(solution)/shard_map/ppermute | solution.py:563
  115.4 4.7 %collective-permute-start.37 = (bf16[64,5120]{1,0:T(8,128)(2,1)}, bf16[64,5120]{1,0:T(8,128)(2,1)S(1)}, u32[]{:S(2)}, u32[]{:S(2)}) collective-permute-start(bf16[64,5120]{1,0:T(8,128)(2,1)} %collective-permute-done.29.refs_10_), channel_id=1, source_target_pairs={{0,1},{1,0},{2,3},{3,2},{4,5},{5,4},{6,7},{7,6},{8,9},{9,8},{10,11... | collective-permute-start | bytes 1966088 | tf_op jit(solution)/shard_map/ppermute | solution.py:563
  115.9 3.7 %collective-permute-start.33 = (bf16[32,5120]{1,0:T(8,128)(2,1)}, bf16[32,5120]{1,0:T(8,128)(2,1)S(1)}, u32[]{:S(2)}, u32[]{:S(2)}) collective-permute-start(bf16[32,5120]{1,0:T(8,128)(2,1)} %collective-permute-done.21.refs_6_), channel_id=1, source_target_pairs={{0,1},{1,0},{2,3},{3,2},{4,5},{5,4},{6,7},{7,6},{8,9},{9,8},{10,11... | collective-permute-start | bytes 983048 | tf_op jit(solution)/shard_map/ppermute | solution.py:563
  116.0 4.1 %collective-permute-start.34 = (bf16[32,5120]{1,0:T(8,128)(2,1)}, bf16[32,5120]{1,0:T(8,128)(2,1)S(1)}, u32[]{:S(2)}, u32[]{:S(2)}) collective-permute-start(bf16[32,5120]{1,0:T(8,128)(2,1)} %collective-permute-done.23.refs_7_), channel_id=1, source_target_pairs={{0,1},{1,0},{2,3},{3,2},{4,5},{5,4},{6,7},{7,6},{8,9},{9,8},{10,11... | collective-permute-start | bytes 983048 | tf_op jit(solution)/shard_map/ppermute | solution.py:563
  116.4 3.6 %collective-permute-start.35 = (bf16[32,5120]{1,0:T(8,128)(2,1)S(1)}, bf16[32,5120]{1,0:T(8,128)(2,1)S(1)}, u32[]{:S(2)}, u32[]{:S(2)}) collective-permute-start(bf16[32,5120]{1,0:T(8,128)(2,1)S(1)} %collective-permute-done.24.refs_3_.refs_8_), channel_id=1, source_target_pairs={{0,1},{1,0},{2,3},{3,2},{4,5},{5,4},{6,7},{7,6},{8,9},{9,8},{10,11... | collective-permute-start | bytes 983048 | tf_op jit(solution)/shard_map/ppermute | solution.py:563
  120.1 33.6 %collective-permute-start.40 = (bf16[32,4096]{1,0:T(8,128)(2,1)}, bf16[32,4096]{1,0:T(8,128)(2,1)S(1)}, u32[]{:S(2)}, u32[]{:S(2)}) collective-permute-start(bf16[32,4096]{1,0:T(8,128)(2,1)} %copy-done.31), channel_id=1, source_target_pairs={{0,4},{1,5},{2,6},{3,7},{4,0},{5,1},{6,2},{7,3},{8,12},{9,13},{10,... | collective-permute-start | bytes 786440 | tf_op jit(solution)/shard_map/ppermute | solution.py:563
  124.0 29.7 %collective-permute-start.41 = (bf16[32,4096]{1,0:T(8,128)(2,1)}, bf16[32,4096]{1,0:T(8,128)(2,1)S(1)}, u32[]{:S(2)}, u32[]{:S(2)}) collective-permute-start(bf16[32,4096]{1,0:T(8,128)(2,1)} %copy-done.31), channel_id=1, source_target_pairs={{0,6},{1,7},{2,4},{3,5},{4,2},{5,3},{6,0},{7,1},{8,14},{9,15},{10,... | collective-permute-start | bytes 786440 | tf_op jit(solution)/shard_map/ppermute | solution.py:563
  125.5 28.2 %collective-permute-start.42 = (bf16[32,4096]{1,0:T(8,128)(2,1)}, bf16[32,4096]{1,0:T(8,128)(2,1)S(1)}, u32[]{:S(2)}, u32[]{:S(2)}) collective-permute-start(bf16[32,4096]{1,0:T(8,128)(2,1)} %copy-done.31), channel_id=1, source_target_pairs={{0,2},{1,3},{2,0},{3,1},{4,6},{5,7},{6,4},{7,5},{8,10},{9,11},{10,... | collective-permute-start | bytes 786440 | tf_op jit(solution)/shard_map/ppermute | solution.py:563
  125.6 28.2 %collective-permute-start.38 = (bf16[384,1024]{1,0:T(8,128)(2,1)S(1)}, bf16[384,1024]{1,0:T(8,128)(2,1)S(1)}, u32[]{:S(2)}, u32[]{:S(2)}) collective-permute-start(bf16[384,1024]{1,0:T(8,128)(2,1)S(1)} %glue.9.refs_25_), channel_id=1, source_target_pairs={{0,8},{8,0},{16,24},{24,16},{1,9},{9,1},{17,25},{25,17},{2,10},{10... | collective-permute-start | bytes 2359304 | tf_op jit(solution)/shard_map/ppermute | solution.py:563
  126.3 28.3 %collective-permute-start.39 = (bf16[384,1024]{1,0:T(8,128)(2,1)S(1)}, bf16[384,1024]{1,0:T(8,128)(2,1)S(1)}, u32[]{:S(2)}, u32[]{:S(2)}) collective-permute-start(bf16[384,1024]{1,0:T(8,128)(2,1)S(1)} %glue.9.refs_25_), channel_id=1, source_target_pairs={{0,16},{8,24},{16,0},{24,8},{1,17},{9,25},{17,1},{25,9},{2,18},{10... | collective-permute-start | bytes 2359304 | tf_op jit(solution)/shard_map/ppermute | solution.py:563
  154.6 6.3 %collective-permute-start.45 = (bf16[384,1024]{1,0:T(8,128)(2,1)S(1)}, bf16[384,1024]{1,0:T(8,128)(2,1)S(1)}, u32[]{:S(2)}, u32[]{:S(2)}) collective-permute-start(bf16[384,1024]{1,0:T(8,128)(2,1)S(1)} %collective-permute-done.39.refs_27_), channel_id=1, source_target_pairs={{0,1},{1,0},{2,3},{3,2},{4,5},{5,4},{6,7},{7,6},{8,9},{9,8},{10,11... | collective-permute-start | bytes 2359304 | tf_op jit(solution)/shard_map/ppermute | solution.py:563
  154.7 6.2 %collective-permute-start.43 = (bf16[384,1024]{1,0:T(8,128)(2,1)S(1)}, bf16[384,1024]{1,0:T(8,128)(2,1)S(1)}, u32[]{:S(2)}, u32[]{:S(2)}) collective-permute-start(bf16[384,1024]{1,0:T(8,128)(2,1)S(1)} %glue.9.refs_25_), channel_id=1, source_target_pairs={{0,1},{1,0},{2,3},{3,2},{4,5},{5,4},{6,7},{7,6},{8,9},{9,8},{10,11... | collective-permute-start | bytes 2359304 | tf_op jit(solution)/shard_map/ppermute | solution.py:563
  155.1 5.8 %collective-permute-start.44 = (bf16[384,1024]{1,0:T(8,128)(2,1)S(1)}, bf16[384,1024]{1,0:T(8,128)(2,1)S(1)}, u32[]{:S(2)}, u32[]{:S(2)}) collective-permute-start(bf16[384,1024]{1,0:T(8,128)(2,1)S(1)} %collective-permute-done.38.refs_26_), channel_id=1, source_target_pairs={{0,1},{1,0},{2,3},{3,2},{4,5},{5,4},{6,7},{7,6},{8,9},{9,8},{10,11... | collective-permute-start | bytes 2359304 | tf_op jit(solution)/shard_map/ppermute | solution.py:563
  155.2 2.6 %collective-permute-start.47 = (bf16[32,4096]{1,0:T(8,128)(2,1)}, bf16[32,4096]{1,0:T(8,128)(2,1)S(1)}, u32[]{:S(2)}, u32[]{:S(2)}) collective-permute-start(bf16[32,4096]{1,0:T(8,128)(2,1)} %copy-done.32), channel_id=1, source_target_pairs={{0,1},{1,0},{2,3},{3,2},{4,5},{5,4},{6,7},{7,6},{8,9},{9,8},{10,11... | collective-permute-start | bytes 786440 | tf_op jit(solution)/shard_map/ppermute | solution.py:563
  155.7 3.0 %collective-permute-start.48 = (bf16[32,4096]{1,0:T(8,128)(2,1)}, bf16[32,4096]{1,0:T(8,128)(2,1)S(1)}, u32[]{:S(2)}, u32[]{:S(2)}) collective-permute-start(bf16[32,4096]{1,0:T(8,128)(2,1)} %copy-done.33), channel_id=1, source_target_pairs={{0,1},{1,0},{2,3},{3,2},{4,5},{5,4},{6,7},{7,6},{8,9},{9,8},{10,11... | collective-permute-start | bytes 786440 | tf_op jit(solution)/shard_map/ppermute | solution.py:563
  (41 other events, 404.9 us)

commit v7 on v6

--- a/solution.py
+++ b/solution.py
@@ -696,14 +696,17 @@
                 (cols_feed, (0, 0, tall, at_feed), (1, 0, tall, 0)),
                 (cols_feed, (2, tall, tall, 0), (3, 0, tall, 0)),
             )
-            crossed, crossed_more, down_three, x_pair_core, y_pair_core = stage(
-                "yx3cc", (left, right, w_down, x_pair, y_pair), x_last, *attended
+            crossed, crossed_more, down_three, corner_one, x_pair_core = stage(
+                "yx31c", (left, right, w_down, cross_down, x_pair), x_last, *attended
             )
         attended = attend(scalars, qkv, width, seq, attended)
     context, powers, inverse = attended
     if special:
-        cores = stage(
-            "ccccc", (feed_three, x_last, y_last, crossed, crossed_more), context, down_three
+        y_pair_core, *cores = stage(
+            "cccccc",
+            (y_pair, feed_three, x_last, y_last, crossed, crossed_more),
+            context,
+            down_three,
         )
         feed_parts = both(
             [
@@ -723,9 +726,10 @@
             (down_one, down_two, down_three),
             (width, *((n, 0, w_down.shape[0], 0) for n in range(3))),
         )
-        x_far, y_far, *diagonal = stage(
-            "xy231", (far, far, cross_down, cross_down, cross_down), *cores
-        )
+        x_far, y_far, *diagonal, far_core = stage(
+            "xy23c", (far, far, cross_down, cross_down, far), *cores
+        )
+        diagonal.append(corner_one)
     normed, spread, gl, gp = join(
         scalars, seqs, tokens, context, feed_parts, vectors, bias_in[None]
     )
@@ -733,15 +737,18 @@
         x_far, cross_down, gl = after((x_far, cross_down, gl), y_far, *diagonal)
     if special:
         mine = [
-            (after(far, x_far), (0, rest, 0)),
             (x_far, (1, rest, 0)),
             (y_far, (2, rest, 0)),
             (cross_down, (3, (0,), 0)),
             *((block, (3, (k,), 0)) for block, k in zip(diagonal, (2, 3, 1))),
         ]
         down_parts = both(
-            [*((array, (chip, (0,), at_down)) for chip, array in enumerate(near)), *mine],
-            [*near_core, *(over_core(block) for block, _ in mine)],
+            [
+                *((array, (chip, (0,), at_down)) for chip, array in enumerate(near)),
+                (far, (0, rest, 0)),
+                *mine,
+            ],
+            [*near_core, far_core, *(over_core(after(block, gl)) for block, _ in mine)],
         )
     output, d_joined, d_context, sums, sum_in = turn(
         scalars, seqs, gl, gp, normed, spread, cotangent, feed_parts, down_parts, vectors

time: 252 us -> 250 us (level)
  no operation moved by 1% of the time
where the time goes in v7:
time: 250 us
  Pallas kernels  138 us (55%)
  waiting for transfers between devices  47.9 us (19%)
  starting transfers between devices  41.9 us (17%)
  blocking collectives  10.5 us (4%)
  local copies, waits for them, and re-layouts  6.56 us (3%)
  other arithmetic  3.31 us (1%)
    ppermute x50, waiting for transfers between devices, hop(): return lax.ppermute(block, axis, [(i, i ^ flip) for i in range(size)])  47.9 us
    pallas_call x1, Pallas kernels, turn(): pl.pallas_call(functools.partial(turn_body, seqs, tags_of(feeds), tags_of...  44.2 us
    ppermute x50, starting transfers between devices, hop(): return lax.ppermute(block, axis, [(i, i ^ flip) for i in range(size)])  41.9 us
    pallas_call x1, Pallas kernels, back(): pl.pallas_call(functools.partial(back_body, seqs, tags_of(sources)), out_...  31.4 us
    pallas_call x1, Pallas kernels, join(): pl.pallas_call(functools.partial(join_body, seqs, tags_of(sources)), out_...  25.9 us
    pallas_call x2, Pallas kernels, attend(): pl.pallas_call(functools.partial(attend_body, seq), out_shape=(shape_of((...  20.4 us
    pallas_call x1, Pallas kernels, project(): pl.pallas_call(functools.partial(project_body, seqs, tags_of(sources)), o...  12.4 us
    all_to_all x1, blocking collectives, on_device(): mine = jnp.sum(lax.all_to_all(rows, BOTH, 0, 0, tiled=True), axis=0)  10.5 us
  transfers between devices with their start and end apart: 50, of which 16 were waited for; matrix products, arithmetic and copies ran while one was open for 2% of the time, Pallas kernels for 24%

profile of v7, /device:TPU:0, one launch (start us, length us, event | category | flops | bytes accessed | tf_op | source)
XLA Modules:
  0.0 249.7 jit_solution(13387057098203580270)
XLA Ops:
  0.6 2.1 pack.1
  2.7 3.0 %collective-permute-start.3 = (bf16[32,12288]{1,0:T(8,128)(2,1)}, bf16[32,12288]{1,0:T(8,128)(2,1)S(1)}, u32[]{:S(2)}, u32[]{:S(2)}) collective-permute-start(bf16[32,12288]{1,0:T(8,128)(2,1)} %get-tuple-element.158.refs_0_.refs_22_), channel_id=1, source_target_pairs={{0,8},{8,0},{16,24},{24,16},{1,9},{9,1},{17,25},{25,17},{2,10},{10... | collective-permute-start | bytes 2359304 | tf_op jit(solution)/shard_map/ppermute | solution.py:563
  5.7 1.5 collective-permute-start.4
  7.3 2.6 %collective-permute-start = (bf16[32,3072]{1,0:T(8,128)(2,1)}, bf16[32,3072]{1,0:T(8,128)(2,1)S(1)}, u32[]{:S(2)}, u32[]{:S(2)}) collective-permute-start(bf16[32,3072]{1,0:T(8,128)(2,1)} %qkv_ref.1), channel_id=1, source_target_pairs={{0,4},{1,5},{2,6},{3,7},{4,0},{5,1},{6,2},{7,3},{8,12},{9,13},{10,... | collective-permute-start | bytes 589832 | tf_op jit(solution)/shard_map/ppermute | solution.py:563
  9.9 1.3 collective-permute-start.1
  11.4 1.4 stack.43.vec_ref
  12.9 1.2 pad_add_fusion.len_ref
  14.1 1.3 pad_maximum_fusion.1
  15.4 8.7 %collective-permute-done.refs_1_ = bf16[32,3072]{1,0:T(8,128)(2,1)S(1)} collective-permute-done((bf16[32,3072]{1,0:T(8,128)(2,1)}, bf16[32,3072]{1,0:T(8,128)(2,1)S(1)}, u32[]{:S(2)}, u32[]{:S(2)}) %collective-permute-start) | collective-permute-done | bytes 196640 | tf_op jit(solution)/shard_map/ppermute | solution.py:563
  24.3 0.8 collective-permute-done.4.refs_2_.refs_24_
  26.1 1.7 collective-permute-start.6
  27.8 3.7 %collective-permute-start.7 = (bf16[32,5120]{1,0:T(8,128)(2,1)}, bf16[32,5120]{1,0:T(8,128)(2,1)S(1)}, u32[]{:S(2)}, u32[]{:S(2)}) collective-permute-start(bf16[32,5120]{1,0:T(8,128)(2,1)} %get-tuple-element.188), channel_id=1, source_target_pairs={{0,4},{1,5},{2,6},{3,7},{4,0},{5,1},{6,2},{7,3},{8,12},{9,13},{10,... | collective-permute-start | bytes 983048 | tf_op jit(solution)/shard_map/ppermute | solution.py:563
  31.4 14.6 %collective-permute-done.7.refs_1_ = bf16[32,5120]{1,0:T(8,128)(2,1)S(1)} collective-permute-done((bf16[32,5120]{1,0:T(8,128)(2,1)}, bf16[32,5120]{1,0:T(8,128)(2,1)S(1)}, u32[]{:S(2)}, u32[]{:S(2)}) %collective-permute-start.7) | collective-permute-done | bytes 327712 | tf_op jit(solution)/shard_map/ppermute | solution.py:563
  46.1 0.9 copy-done.11
  47.6 1.5 collective-permute-start.10
  49.2 1.5 collective-permute-start.11
  50.7 9.3 %collective-permute-done.12.refs_0_ = bf16[32,5120]{1,0:T(8,128)(2,1)S(1)} collective-permute-done((bf16[32,5120]{1,0:T(8,128)(2,1)}, bf16[32,5120]{1,0:T(8,128)(2,1)S(1)}, u32[]{:S(2)}, u32[]{:S(2)}) %collective-permute-start.12) | collective-permute-done | bytes 327712 | tf_op jit(solution)/shard_map/ppermute | solution.py:563
  61.2 0.9 glue.7
  62.1 1.4 collective-permute-done.17.refs_14_
  64.3 1.5 collective-permute-start.19
  66.3 2.6 %collective-permute-start.21 = (bf16[32,5120]{1,0:T(8,128)(2,1)}, bf16[32,5120]{1,0:T(8,128)(2,1)}, u32[]{:S(2)}, u32[]{:S(2)}) collective-permute-start(bf16[32,5120]{1,0:T(8,128)(2,1)} %get-tuple-element.188), channel_id=1, source_target_pairs={{0,6},{1,7},{2,4},{3,5},{4,2},{5,3},{6,0},{7,1},{8,14},{9,15},{10,... | collective-permute-start | bytes 983048 | tf_op jit(solution)/shard_map/ppermute | solution.py:563
  68.9 12.4 %project.1.q_ref.k_ref.v_ref = bf16[1024,3072]{1,0:T(8,128)(2,1)} custom-call(s32[5]{0:T(128)} %pad_add_fusion.len_ref, bf16[1024,1024]{1,0:T(8,128)(2,1)} %x_ref.2, f32[1,3072]{1,0:T(1,128)} %bitcast.21, f32[1,3072]{1,0:T(1,128)} %constant.37.clone.1.scale_ref, bf16[32,12288]{1,0:T(8,128)(2,1)} %get-tuple-element.158.refs_0_.refs_22_, ...), custom_call_target="tpu_custom_call" | custom-call | flops 6442450944 | tf_op jit(solution)/shard_map/project/pallas_call | solution.py:147
  81.4 1.1 collective-permute-done.20.refs_2_.refs_5_
  82.5 2.0 collective-permute-start.25
  84.6 1.5 collective-permute-start.27
  86.2 0.9 collective-permute-start.23
  87.1 0.7 collective-permute-start.24
  87.9 10.2 %attend.2 = (bf16[1024,1024]{1,0:T(8,128)(2,1)}, bf16[32,512,512]{2,1,0:T(8,128)(2,1)}, f32[1024,1024]{1,0:T(8,128)}) custom-call(s32[5]{0:T(128)} %pad_add_fusion.len_ref, bf16[1024,3072]{1,0:T(8,128)(2,1)} %project.1.q_ref.k_ref.v_ref, bf16[1024,3072]{1,0:T(8,128)(2,1)} %project.1.q_ref.k_ref.v_ref, bf16[1024,3072]{1,0:T(8,128)(2,1)} %project.1.q_ref.k_ref.v_ref), custom_call_target="tpu_custom_call" | custom-call | flops 4294967296 | tf_op jit(solution)/shard_map/attend/pallas_call | solution.py:220
  98.1 1.0 collective-permute-done.24.refs_3_.refs_8_
  99.1 0.9 glue.8
  100.0 1.1 collective-permute-start.28
  101.1 1.1 collective-permute-start.29
  102.2 2.0 collective-permute-start.30
  104.2 0.8 collective-permute-start.31
  105.0 10.3 %attend.3 = (bf16[1024,1024]{1,0:T(8,128)(2,1)}, bf16[32,512,512]{2,1,0:T(8,128)(2,1)}, f32[1024,1024]{1,0:T(8,128)}) custom-call(s32[5]{0:T(128)} %pad_add_fusion.len_ref, bf16[1024,3072]{1,0:T(8,128)(2,1)} %project.1.q_ref.k_ref.v_ref, bf16[1024,3072]{1,0:T(8,128)(2,1)} %project.1.q_ref.k_ref.v_ref, ...), custom_call_target="tpu_custom_call", output_to_operand_aliasing={{0}: (4, {}), {1}: (5, {}), {2}: (6, {})} | custom-call | flops 4294967296 | tf_op jit(solution)/shard_map/attend/pallas_call | solution.py:220
  115.3 3.3 %collective-permute-done.31.refs_31_ = bf16[32,4096]{1,0:T(8,128)(2,1)} collective-permute-done((bf16[32,4096]{1,0:T(8,128)(2,1)}, bf16[32,4096]{1,0:T(8,128)(2,1)}, u32[]{:S(2)}, u32[]{:S(2)}) %collective-permute-start.31) | collective-permute-done | bytes 262176 | tf_op jit(solution)/shard_map/ppermute | solution.py:563
  120.5 0.7 copy-done.30
  121.4 2.8 %collective-permute-done.35.refs_18_ = bf16[32,5120]{1,0:T(8,128)(2,1)S(1)} collective-permute-done((bf16[32,5120]{1,0:T(8,128)(2,1)}, bf16[32,5120]{1,0:T(8,128)(2,1)S(1)}, u32[]{:S(2)}, u32[]{:S(2)}) %collective-permute-start.35) | collective-permute-done | bytes 327712 | tf_op jit(solution)/shard_map/ppermute | solution.py:563
  124.3 0.7 collective-permute-start.41
  125.1 1.9 collective-permute-start.42
  127.1 0.8 collective-permute-start.39
  127.9 1.0 collective-permute-start.40
  128.9 25.9 %join.1 = (f32[1024,1024]{1,0:T(8,128)}, f32[1024,128]{1,0:T(8,128)}, bf16[1024,4096]{1,0:T(8,128)(2,1)}, bf16[1024,4096]{1,0:T(8,128)(2,1)}) custom-call(s32[5]{0:T(128)} %pad_add_fusion.len_ref, bf16[1024,1024]{1,0:T(8,128)(2,1)} %x_ref.2, bf16[1024,1024]{1,0:T(8,128)(2,1)} %get-tuple-element.227.o_ref, f32[8,1024]{1,0:T(8,128)} %stack.43.vec_ref, ...), custom_call_target="tpu_custom_call" | custom-call | flops 10737418240 | tf_op jit(solution)/shard_map/join/pallas_call | solution.py:290
  156.5 1.8 collective-permute-done.47.refs_39_
  159.1 0.7 collective-permute-done.49.refs_41_
  161.4 44.2 %turn.1 = (bf16[1024,1024]{1,0:T(8,128)(2,1)}, f32[1024,1024]{1,0:T(8,128)}, bf16[1024,1024]{1,0:T(8,128)(2,1)}, f32[8,1024]{1,0:T(8,128)}, f32[1,4096]{1,0:T(1,128)}) custom-call(s32[5]{0:T(128)} %pad_add_fusion.len_ref, bf16[1024,4096]{1,0:T(8,128)(2,1)} %get-tuple-element.253.gl_ref, f32[1024,1024]{1,0:T(8,128)} %get-tuple-element.254.u_ref, ...), custom_call_target="tpu_custom_call" | custom-call | flops 27917287424 | tf_op jit(solution)/shard_map/turn/pallas_call | solution.py:407
  205.6 31.4 %back.1 = (bf16[1024,1024]{1,0:T(8,128)(2,1)}, f32[1,1024]{1,0:T(1,128)}) custom-call(s32[5]{0:T(128)} %pad_add_fusion.len_ref, bf16[1024,3072]{1,0:T(8,128)(2,1)} %project.1.q_ref.k_ref.v_ref, bf16[1024,3072]{1,0:T(8,128)(2,1)} %project.1.q_ref.k_ref.v_ref, bf16[1024,3072]{1,0:T(8,128)(2,1)} %project.1.q_ref.k_ref.v_ref, ...), custom_call_target="tpu_custom_call" | custom-call | flops 17179869184 | tf_op jit(solution)/shard_map/back/pallas_call | solution.py:524
  238.1 10.5 %all_to_all.9 = f32[32,1,320]{2,1,0:T(1,128)S(1)} all-to-all(f32[32,1,320]{2,1,0:T(1,128)S(1)} %copy.30), channel_id=1, replica_groups=mesh['dp'=4,'fsdp'=8] {'dp','fsdp'}, dimensions={0} | all-to-all | bytes 81920 | tf_op jit(solution)/shard_map/all_to_all | solution.py:760
  (155 shorter events, 12.9 us)
Async XLA Ops:
  2.7 21.5 %collective-permute-start.3 = (bf16[32,12288]{1,0:T(8,128)(2,1)}, bf16[32,12288]{1,0:T(8,128)(2,1)S(1)}, u32[]{:S(2)}, u32[]{:S(2)}) collective-permute-start(bf16[32,12288]{1,0:T(8,128)(2,1)} %get-tuple-element.158.refs_0_.refs_22_), channel_id=1, source_target_pairs={{0,8},{8,0},{16,24},{24,16},{1,9},{9,1},{17,25},{25,17},{2,10},{10... | collective-permute-start | bytes 2359304 | tf_op jit(solution)/shard_map/ppermute | solution.py:563
  5.7 19.3 %collective-permute-start.4 = (bf16[32,12288]{1,0:T(8,128)(2,1)}, bf16[32,12288]{1,0:T(8,128)(2,1)}, u32[]{:S(2)}, u32[]{:S(2)}) collective-permute-start(bf16[32,12288]{1,0:T(8,128)(2,1)} %get-tuple-element.158.refs_0_.refs_22_), channel_id=1, source_target_pairs={{0,16},{8,24},{16,0},{24,8},{1,17},{9,25},{17,1},{25,9},{2,18},{10... | collective-permute-start | bytes 2359304 | tf_op jit(solution)/shard_map/ppermute | solution.py:563
  7.3 16.8 %collective-permute-start = (bf16[32,3072]{1,0:T(8,128)(2,1)}, bf16[32,3072]{1,0:T(8,128)(2,1)S(1)}, u32[]{:S(2)}, u32[]{:S(2)}) collective-permute-start(bf16[32,3072]{1,0:T(8,128)(2,1)} %qkv_ref.1), channel_id=1, source_target_pairs={{0,4},{1,5},{2,6},{3,7},{4,0},{5,1},{6,2},{7,3},{8,12},{9,13},{10,... | collective-permute-start | bytes 589832 | tf_op jit(solution)/shard_map/ppermute | solution.py:563
  9.9 14.3 %collective-permute-start.1 = (bf16[32,3072]{1,0:T(8,128)(2,1)}, bf16[32,3072]{1,0:T(8,128)(2,1)S(1)}, u32[]{:S(2)}, u32[]{:S(2)}) collective-permute-start(bf16[32,3072]{1,0:T(8,128)(2,1)} %qkv_ref.1), channel_id=1, source_target_pairs={{0,6},{1,7},{2,4},{3,5},{4,2},{5,3},{6,0},{7,1},{8,14},{9,15},{10,... | collective-permute-start | bytes 589832 | tf_op jit(solution)/shard_map/ppermute | solution.py:563
  11.2 13.0 %collective-permute-start.2 = (bf16[32,3072]{1,0:T(8,128)(2,1)}, bf16[32,3072]{1,0:T(8,128)(2,1)S(1)}, u32[]{:S(2)}, u32[]{:S(2)}) collective-permute-start(bf16[32,3072]{1,0:T(8,128)(2,1)} %qkv_ref.1), channel_id=1, source_target_pairs={{0,2},{1,3},{2,0},{3,1},{4,6},{5,7},{6,4},{7,5},{8,10},{9,11},{10,... | collective-permute-start | bytes 589832 | tf_op jit(solution)/shard_map/ppermute | solution.py:563
  25.1 21.0 %collective-permute-start.8 = (bf16[32,12288]{1,0:T(8,128)(2,1)}, bf16[32,12288]{1,0:T(8,128)(2,1)S(1)}, u32[]{:S(2)}, u32[]{:S(2)}) collective-permute-start(bf16[32,12288]{1,0:T(8,128)(2,1)} %get-tuple-element.158.refs_0_.refs_22_), channel_id=1, source_target_pairs={{0,1},{1,0},{2,3},{3,2},{4,5},{5,4},{6,7},{7,6},{8,9},{9,8},{10,11... | collective-permute-start | bytes 2359304 | tf_op jit(solution)/shard_map/ppermute | solution.py:563
  25.2 21.8 %collective-permute-start.9 = (bf16[32,12288]{1,0:T(8,128)(2,1)S(1)}, bf16[32,12288]{1,0:T(8,128)(2,1)}, u32[]{:S(2)}, u32[]{:S(2)}) collective-permute-start(bf16[32,12288]{1,0:T(8,128)(2,1)S(1)} %collective-permute-done.3.refs_0_.refs_2_.refs_1_.refs_23_), channel_id=1, source_target_pairs={{0,1},{1,0},{2,3},{3,2},{4,5},{5,4},{6,7},{7,6},{8,9},{9,8},{10,11... | collective-permute-start | bytes 2359304 | tf_op jit(solution)/shard_map/ppermute | solution.py:563
  25.7 20.4 %collective-permute-start.5 = (bf16[96,3072]{1,0:T(8,128)(2,1)S(1)}, bf16[96,3072]{1,0:T(8,128)(2,1)S(1)}, u32[]{:S(2)}, u32[]{:S(2)}) collective-permute-start(bf16[96,3072]{1,0:T(8,128)(2,1)S(1)} %glue.5.refs_3_), channel_id=1, source_target_pairs={{0,8},{8,0},{16,24},{24,16},{1,9},{9,1},{17,25},{25,17},{2,10},{10... | collective-permute-start | bytes 1769480 | tf_op jit(solution)/shard_map/ppermute | solution.py:563
  26.1 20.0 %collective-permute-start.6 = (bf16[96,3072]{1,0:T(8,128)(2,1)S(1)}, bf16[96,3072]{1,0:T(8,128)(2,1)S(1)}, u32[]{:S(2)}, u32[]{:S(2)}) collective-permute-start(bf16[96,3072]{1,0:T(8,128)(2,1)S(1)} %glue.5.refs_3_), channel_id=1, source_target_pairs={{0,16},{8,24},{16,0},{24,8},{1,17},{9,25},{17,1},{25,9},{2,18},{10... | collective-permute-start | bytes 1769480 | tf_op jit(solution)/shard_map/ppermute | solution.py:563
  27.8 18.3 %collective-permute-start.7 = (bf16[32,5120]{1,0:T(8,128)(2,1)}, bf16[32,5120]{1,0:T(8,128)(2,1)S(1)}, u32[]{:S(2)}, u32[]{:S(2)}) collective-permute-start(bf16[32,5120]{1,0:T(8,128)(2,1)} %get-tuple-element.188), channel_id=1, source_target_pairs={{0,4},{1,5},{2,6},{3,7},{4,0},{5,1},{6,2},{7,3},{8,12},{9,13},{10,... | collective-permute-start | bytes 983048 | tf_op jit(solution)/shard_map/ppermute | solution.py:563
  47.1 13.0 %collective-permute-start.13 = (bf16[32,12288]{1,0:T(8,128)(2,1)}, bf16[32,12288]{1,0:T(8,128)(2,1)S(1)}, u32[]{:S(2)}, u32[]{:S(2)}) collective-permute-start(bf16[32,12288]{1,0:T(8,128)(2,1)} %collective-permute-done.4.refs_2_.refs_24_), channel_id=1, source_target_pairs={{0,1},{1,0},{2,3},{3,2},{4,5},{5,4},{6,7},{7,6},{8,9},{9,8},{10,11... | collective-permute-start | bytes 2359304 | tf_op jit(solution)/shard_map/ppermute | solution.py:563
  47.1 12.9 %collective-permute-start.14 = (bf16[96,3072]{1,0:T(8,128)(2,1)S(1)}, bf16[96,3072]{1,0:T(8,128)(2,1)S(1)}, u32[]{:S(2)}, u32[]{:S(2)}) collective-permute-start(bf16[96,3072]{1,0:T(8,128)(2,1)S(1)} %glue.5.refs_3_), channel_id=1, source_target_pairs={{0,1},{1,0},{2,3},{3,2},{4,5},{5,4},{6,7},{7,6},{8,9},{9,8},{10,11... | collective-permute-start | bytes 1769480 | tf_op jit(solution)/shard_map/ppermute | solution.py:563
  47.6 12.4 %collective-permute-start.10 = (bf16[64,3072]{1,0:T(8,128)(2,1)S(1)}, bf16[64,3072]{1,0:T(8,128)(2,1)S(1)}, u32[]{:S(2)}, u32[]{:S(2)}) collective-permute-start(bf16[64,3072]{1,0:T(8,128)(2,1)S(1)} %get-tuple-element.168), channel_id=1, source_target_pairs={{0,16},{8,24},{16,0},{24,8},{1,17},{9,25},{17,1},{25,9},{2,18},{10... | collective-permute-start | bytes 1179656 | tf_op jit(solution)/shard_map/ppermute | solution.py:563
  49.2 10.8 %collective-permute-start.11 = (bf16[64,3072]{1,0:T(8,128)(2,1)S(1)}, bf16[64,3072]{1,0:T(8,128)(2,1)S(1)}, u32[]{:S(2)}, u32[]{:S(2)}) collective-permute-start(bf16[64,3072]{1,0:T(8,128)(2,1)S(1)} %get-tuple-element.169), channel_id=1, source_target_pairs={{0,8},{8,0},{16,24},{24,16},{1,9},{9,1},{17,25},{25,17},{2,10},{10... | collective-permute-start | bytes 1179656 | tf_op jit(solution)/shard_map/ppermute | solution.py:563
  50.7 9.3 %collective-permute-start.12 = (bf16[32,5120]{1,0:T(8,128)(2,1)}, bf16[32,5120]{1,0:T(8,128)(2,1)S(1)}, u32[]{:S(2)}, u32[]{:S(2)}) collective-permute-start(bf16[32,5120]{1,0:T(8,128)(2,1)} %get-tuple-element.188), channel_id=1, source_target_pairs={{0,2},{1,3},{2,0},{3,1},{4,6},{5,7},{6,4},{7,5},{8,10},{9,11},{10,... | collective-permute-start | bytes 983048 | tf_op jit(solution)/shard_map/ppermute | solution.py:563
  60.1 4.0 %collective-permute-start.15 = (bf16[96,3072]{1,0:T(8,128)(2,1)S(1)}, bf16[96,3072]{1,0:T(8,128)(2,1)S(1)}, u32[]{:S(2)}, u32[]{:S(2)}) collective-permute-start(bf16[96,3072]{1,0:T(8,128)(2,1)S(1)} %collective-permute-done.5.refs_1_.refs_4_), channel_id=1, source_target_pairs={{0,1},{1,0},{2,3},{3,2},{4,5},{5,4},{6,7},{7,6},{8,9},{9,8},{10,11... | collective-permute-start | bytes 1769480 | tf_op jit(solution)/shard_map/ppermute | solution.py:563
  60.1 4.0 %collective-permute-start.16 = (bf16[96,3072]{1,0:T(8,128)(2,1)S(1)}, bf16[96,3072]{1,0:T(8,128)(2,1)S(1)}, u32[]{:S(2)}, u32[]{:S(2)}) collective-permute-start(bf16[96,3072]{1,0:T(8,128)(2,1)S(1)} %collective-permute-done.6.refs_2_.refs_5_), channel_id=1, source_target_pairs={{0,1},{1,0},{2,3},{3,2},{4,5},{5,4},{6,7},{7,6},{8,9},{9,8},{10,11... | collective-permute-start | bytes 1769480 | tf_op jit(solution)/shard_map/ppermute | solution.py:563
  60.6 2.9 %collective-permute-start.17 = (bf16[64,3072]{1,0:T(8,128)(2,1)S(1)}, bf16[64,3072]{1,0:T(8,128)(2,1)S(1)}, u32[]{:S(2)}, u32[]{:S(2)}) collective-permute-start(bf16[64,3072]{1,0:T(8,128)(2,1)S(1)} %collective-permute-done.10.refs_6_), channel_id=1, source_target_pairs={{0,1},{1,0},{2,3},{3,2},{4,5},{5,4},{6,7},{7,6},{8,9},{9,8},{10,11... | collective-permute-start | bytes 1179656 | tf_op jit(solution)/shard_map/ppermute | solution.py:563
  61.2 2.9 %collective-permute-start.18 = (bf16[64,3072]{1,0:T(8,128)(2,1)S(1)}, bf16[64,3072]{1,0:T(8,128)(2,1)S(1)}, u32[]{:S(2)}, u32[]{:S(2)}) collective-permute-start(bf16[64,3072]{1,0:T(8,128)(2,1)S(1)} %collective-permute-done.11.refs_7_), channel_id=1, source_target_pairs={{0,1},{1,0},{2,3},{3,2},{4,5},{5,4},{6,7},{7,6},{8,9},{9,8},{10,11... | collective-permute-start | bytes 1179656 | tf_op jit(solution)/shard_map/ppermute | solution.py:563
  64.3 17.1 %collective-permute-start.19 = (bf16[64,5120]{1,0:T(8,128)(2,1)}, bf16[64,5120]{1,0:T(8,128)(2,1)S(1)}, u32[]{:S(2)}, u32[]{:S(2)}) collective-permute-start(bf16[64,5120]{1,0:T(8,128)(2,1)} %get-tuple-element.189.refs_3_), channel_id=1, source_target_pairs={{0,8},{8,0},{16,24},{24,16},{1,9},{9,1},{17,25},{25,17},{2,10},{10... | collective-permute-start | bytes 1966088 | tf_op jit(solution)/shard_map/ppermute | solution.py:563
  65.8 16.7 %collective-permute-start.20 = (bf16[64,5120]{1,0:T(8,128)(2,1)}, bf16[64,5120]{1,0:T(8,128)(2,1)S(1)}, u32[]{:S(2)}, u32[]{:S(2)}) collective-permute-start(bf16[64,5120]{1,0:T(8,128)(2,1)} %get-tuple-element.189.refs_3_), channel_id=1, source_target_pairs={{0,16},{8,24},{16,0},{24,8},{1,17},{9,25},{17,1},{25,9},{2,18},{10... | collective-permute-start | bytes 1966088 | tf_op jit(solution)/shard_map/ppermute | solution.py:563
  66.3 16.2 %collective-permute-start.22 = (bf16[64,5120]{1,0:T(8,128)(2,1)}, bf16[64,5120]{1,0:T(8,128)(2,1)}, u32[]{:S(2)}, u32[]{:S(2)}) collective-permute-start(bf16[64,5120]{1,0:T(8,128)(2,1)} %get-tuple-element.189.refs_3_), channel_id=1, source_target_pairs={{0,1},{1,0},{2,3},{3,2},{4,5},{5,4},{6,7},{7,6},{8,9},{9,8},{10,11... | collective-permute-start | bytes 1966088 | tf_op jit(solution)/shard_map/ppermute | solution.py:563
  66.3 15.1 %collective-permute-start.21 = (bf16[32,5120]{1,0:T(8,128)(2,1)}, bf16[32,5120]{1,0:T(8,128)(2,1)}, u32[]{:S(2)}, u32[]{:S(2)}) collective-permute-start(bf16[32,5120]{1,0:T(8,128)(2,1)} %get-tuple-element.188), channel_id=1, source_target_pairs={{0,6},{1,7},{2,4},{3,5},{4,2},{5,3},{6,0},{7,1},{8,14},{9,15},{10,... | collective-permute-start | bytes 983048 | tf_op jit(solution)/shard_map/ppermute | solution.py:563
  82.5 15.6 %collective-permute-start.25 = (bf16[128,1024]{1,0:T(8,128)(2,1)}, bf16[128,1024]{1,0:T(8,128)(2,1)S(1)}, u32[]{:S(2)}, u32[]{:S(2)}) collective-permute-start(bf16[128,1024]{1,0:T(8,128)(2,1)} %down_ref.1), channel_id=1, source_target_pairs={{0,4},{1,5},{2,6},{3,7},{4,0},{5,1},{6,2},{7,3},{8,12},{9,13},{10,... | collective-permute-start | bytes 786440 | tf_op jit(solution)/shard_map/ppermute | solution.py:563
  84.5 13.6 %collective-permute-start.26 = (bf16[128,1024]{1,0:T(8,128)(2,1)}, bf16[128,1024]{1,0:T(8,128)(2,1)S(1)}, u32[]{:S(2)}, u32[]{:S(2)}) collective-permute-start(bf16[128,1024]{1,0:T(8,128)(2,1)} %down_ref.1), channel_id=1, source_target_pairs={{0,2},{1,3},{2,0},{3,1},{4,6},{5,7},{6,4},{7,5},{8,10},{9,11},{10,... | collective-permute-start | bytes 786440 | tf_op jit(solution)/shard_map/ppermute | solution.py:563
  84.6 13.4 %collective-permute-start.27 = (bf16[32,4096]{1,0:T(8,128)(2,1)S(1)}, bf16[32,4096]{1,0:T(8,128)(2,1)S(1)}, u32[]{:S(2)}, u32[]{:S(2)}) collective-permute-start(bf16[32,4096]{1,0:T(8,128)(2,1)S(1)} %get-tuple-element.201), channel_id=1, source_target_pairs={{0,16},{8,24},{16,0},{24,8},{1,17},{9,25},{17,1},{25,9},{2,18},{10... | collective-permute-start | bytes 786440 | tf_op jit(solution)/shard_map/ppermute | solution.py:563
  86.2 11.9 %collective-permute-start.23 = (bf16[32,5120]{1,0:T(8,128)(2,1)}, bf16[32,5120]{1,0:T(8,128)(2,1)S(1)}, u32[]{:S(2)}, u32[]{:S(2)}) collective-permute-start(bf16[32,5120]{1,0:T(8,128)(2,1)} %collective-permute-done.21.refs_6_), channel_id=1, source_target_pairs={{0,8},{8,0},{16,24},{24,16},{1,9},{9,1},{17,25},{25,17},{2,10},{10... | collective-permute-start | bytes 983048 | tf_op jit(solution)/shard_map/ppermute | solution.py:563
  87.1 12.0 %collective-permute-start.24 = (bf16[32,5120]{1,0:T(8,128)(2,1)}, bf16[32,5120]{1,0:T(8,128)(2,1)S(1)}, u32[]{:S(2)}, u32[]{:S(2)}) collective-permute-start(bf16[32,5120]{1,0:T(8,128)(2,1)} %collective-permute-done.21.refs_6_), channel_id=1, source_target_pairs={{0,16},{8,24},{16,0},{24,8},{1,17},{9,25},{17,1},{25,9},{2,18},{10... | collective-permute-start | bytes 983048 | tf_op jit(solution)/shard_map/ppermute | solution.py:563
  100.0 18.5 %collective-permute-start.28 = (bf16[64,5120]{1,0:T(8,128)(2,1)}, bf16[64,5120]{1,0:T(8,128)(2,1)}, u32[]{:S(2)}, u32[]{:S(2)}) collective-permute-start(bf16[64,5120]{1,0:T(8,128)(2,1)} %get-tuple-element.219), channel_id=1, source_target_pairs={{0,16},{8,24},{16,0},{24,8},{1,17},{9,25},{17,1},{25,9},{2,18},{10... | collective-permute-start | bytes 1966088 | tf_op jit(solution)/shard_map/ppermute | solution.py:563
  101.1 17.5 %collective-permute-start.29 = (bf16[64,5120]{1,0:T(8,128)(2,1)S(1)}, bf16[64,5120]{1,0:T(8,128)(2,1)}, u32[]{:S(2)}, u32[]{:S(2)}) collective-permute-start(bf16[64,5120]{1,0:T(8,128)(2,1)S(1)} %get-tuple-element.220), channel_id=1, source_target_pairs={{0,8},{8,0},{16,24},{24,16},{1,9},{9,1},{17,25},{25,17},{2,10},{10... | collective-permute-start | bytes 1966088 | tf_op jit(solution)/shard_map/ppermute | solution.py:563
  102.2 16.4 %collective-permute-start.32 = (bf16[64,5120]{1,0:T(8,128)(2,1)S(1)}, bf16[64,5120]{1,0:T(8,128)(2,1)S(1)}, u32[]{:S(2)}, u32[]{:S(2)}) collective-permute-start(bf16[64,5120]{1,0:T(8,128)(2,1)S(1)} %collective-permute-done.19.refs_1_.refs_4_), channel_id=1, source_target_pairs={{0,1},{1,0},{2,3},{3,2},{4,5},{5,4},{6,7},{7,6},{8,9},{9,8},{10,11... | collective-permute-start | bytes 1966088 | tf_op jit(solution)/shard_map/ppermute | solution.py:563
  102.2 13.1 %collective-permute-start.30 = (bf16[128,1024]{1,0:T(8,128)(2,1)}, bf16[128,1024]{1,0:T(8,128)(2,1)S(1)}, u32[]{:S(2)}, u32[]{:S(2)}) collective-permute-start(bf16[128,1024]{1,0:T(8,128)(2,1)} %down_ref.1), channel_id=1, source_target_pairs={{0,6},{1,7},{2,4},{3,5},{4,2},{5,3},{6,0},{7,1},{8,14},{9,15},{10,... | collective-permute-start | bytes 786440 | tf_op jit(solution)/shard_map/ppermute | solution.py:563
  104.2 14.4 %collective-permute-start.31 = (bf16[32,4096]{1,0:T(8,128)(2,1)}, bf16[32,4096]{1,0:T(8,128)(2,1)}, u32[]{:S(2)}, u32[]{:S(2)}) collective-permute-start(bf16[32,4096]{1,0:T(8,128)(2,1)} %copy-done.33), channel_id=1, source_target_pairs={{0,2},{1,3},{2,0},{3,1},{4,6},{5,7},{6,4},{7,5},{8,10},{9,11},{10,... | collective-permute-start | bytes 786440 | tf_op jit(solution)/shard_map/ppermute | solution.py:563
  118.7 5.6 %collective-permute-start.33 = (bf16[64,5120]{1,0:T(8,128)(2,1)S(1)}, bf16[64,5120]{1,0:T(8,128)(2,1)S(1)}, u32[]{:S(2)}, u32[]{:S(2)}) collective-permute-start(bf16[64,5120]{1,0:T(8,128)(2,1)S(1)} %collective-permute-done.20.refs_2_.refs_5_), channel_id=1, source_target_pairs={{0,1},{1,0},{2,3},{3,2},{4,5},{5,4},{6,7},{7,6},{8,9},{9,8},{10,11... | collective-permute-start | bytes 1966088 | tf_op jit(solution)/shard_map/ppermute | solution.py:563
  119.2 5.1 %collective-permute-start.37 = (bf16[64,5120]{1,0:T(8,128)(2,1)}, bf16[64,5120]{1,0:T(8,128)(2,1)S(1)}, u32[]{:S(2)}, u32[]{:S(2)}) collective-permute-start(bf16[64,5120]{1,0:T(8,128)(2,1)} %collective-permute-done.28.refs_9_), channel_id=1, source_target_pairs={{0,1},{1,0},{2,3},{3,2},{4,5},{5,4},{6,7},{7,6},{8,9},{9,8},{10,11... | collective-permute-start | bytes 1966088 | tf_op jit(solution)/shard_map/ppermute | solution.py:563
  119.2 5.0 %collective-permute-start.38 = (bf16[64,5120]{1,0:T(8,128)(2,1)}, bf16[64,5120]{1,0:T(8,128)(2,1)S(1)}, u32[]{:S(2)}, u32[]{:S(2)}) collective-permute-start(bf16[64,5120]{1,0:T(8,128)(2,1)} %collective-permute-done.29.refs_10_), channel_id=1, source_target_pairs={{0,1},{1,0},{2,3},{3,2},{4,5},{5,4},{6,7},{7,6},{8,9},{9,8},{10,11... | collective-permute-start | bytes 1966088 | tf_op jit(solution)/shard_map/ppermute | solution.py:563
  119.7 4.6 %collective-permute-start.35 = (bf16[32,5120]{1,0:T(8,128)(2,1)}, bf16[32,5120]{1,0:T(8,128)(2,1)S(1)}, u32[]{:S(2)}, u32[]{:S(2)}) collective-permute-start(bf16[32,5120]{1,0:T(8,128)(2,1)} %copy-done.29), channel_id=1, source_target_pairs={{0,1},{1,0},{2,3},{3,2},{4,5},{5,4},{6,7},{7,6},{8,9},{9,8},{10,11... | collective-permute-start | bytes 983048 | tf_op jit(solution)/shard_map/ppermute | solution.py:563
  121.2 3.0 %collective-permute-start.36 = (bf16[32,5120]{1,0:T(8,128)(2,1)S(1)}, bf16[32,5120]{1,0:T(8,128)(2,1)S(1)}, u32[]{:S(2)}, u32[]{:S(2)}) collective-permute-start(bf16[32,5120]{1,0:T(8,128)(2,1)S(1)} %collective-permute-done.24.refs_3_.refs_8_), channel_id=1, source_target_pairs={{0,1},{1,0},{2,3},{3,2},{4,5},{5,4},{6,7},{7,6},{8,9},{9,8},{10,11... | collective-permute-start | bytes 983048 | tf_op jit(solution)/shard_map/ppermute | solution.py:563
  124.3 30.5 %collective-permute-start.41 = (bf16[32,4096]{1,0:T(8,128)(2,1)}, bf16[32,4096]{1,0:T(8,128)(2,1)}, u32[]{:S(2)}, u32[]{:S(2)}) collective-permute-start(bf16[32,4096]{1,0:T(8,128)(2,1)} %copy-done.33), channel_id=1, source_target_pairs={{0,4},{1,5},{2,6},{3,7},{4,0},{5,1},{6,2},{7,3},{8,12},{9,13},{10,... | collective-permute-start | bytes 786440 | tf_op jit(solution)/shard_map/ppermute | solution.py:563
  125.1 29.7 %collective-permute-start.42 = (bf16[32,4096]{1,0:T(8,128)(2,1)}, bf16[32,4096]{1,0:T(8,128)(2,1)}, u32[]{:S(2)}, u32[]{:S(2)}) collective-permute-start(bf16[32,4096]{1,0:T(8,128)(2,1)} %copy-done.33), channel_id=1, source_target_pairs={{0,6},{1,7},{2,4},{3,5},{4,2},{5,3},{6,0},{7,1},{8,14},{9,15},{10,... | collective-permute-start | bytes 786440 | tf_op jit(solution)/shard_map/ppermute | solution.py:563
  127.1 27.8 %collective-permute-start.39 = (bf16[384,1024]{1,0:T(8,128)(2,1)S(1)}, bf16[384,1024]{1,0:T(8,128)(2,1)S(1)}, u32[]{:S(2)}, u32[]{:S(2)}) collective-permute-start(bf16[384,1024]{1,0:T(8,128)(2,1)S(1)} %glue.9.refs_25_), channel_id=1, source_target_pairs={{0,8},{8,0},{16,24},{24,16},{1,9},{9,1},{17,25},{25,17},{2,10},{10... | collective-permute-start | bytes 2359304 | tf_op jit(solution)/shard_map/ppermute | solution.py:563
  127.9 27.0 %collective-permute-start.40 = (bf16[384,1024]{1,0:T(8,128)(2,1)S(1)}, bf16[384,1024]{1,0:T(8,128)(2,1)S(1)}, u32[]{:S(2)}, u32[]{:S(2)}) collective-permute-start(bf16[384,1024]{1,0:T(8,128)(2,1)S(1)} %glue.9.refs_25_), channel_id=1, source_target_pairs={{0,16},{8,24},{16,0},{24,8},{1,17},{9,25},{17,1},{25,9},{2,18},{10... | collective-permute-start | bytes 2359304 | tf_op jit(solution)/shard_map/ppermute | solution.py:563
  128.9 26.0 %collective-permute-start.43 = (bf16[384,1024]{1,0:T(8,128)(2,1)S(1)}, bf16[384,1024]{1,0:T(8,128)(2,1)S(1)}, u32[]{:S(2)}, u32[]{:S(2)}) collective-permute-start(bf16[384,1024]{1,0:T(8,128)(2,1)S(1)} %glue.9.refs_25_), channel_id=1, source_target_pairs={{0,1},{1,0},{2,3},{3,2},{4,5},{5,4},{6,7},{7,6},{8,9},{9,8},{10,11... | collective-permute-start | bytes 2359304 | tf_op jit(solution)/shard_map/ppermute | solution.py:563
  154.9 5.3 %collective-permute-start.45 = (bf16[384,1024]{1,0:T(8,128)(2,1)S(1)}, bf16[384,1024]{1,0:T(8,128)(2,1)S(1)}, u32[]{:S(2)}, u32[]{:S(2)}) collective-permute-start(bf16[384,1024]{1,0:T(8,128)(2,1)S(1)} %collective-permute-done.40.refs_27_), channel_id=1, source_target_pairs={{0,1},{1,0},{2,3},{3,2},{4,5},{5,4},{6,7},{7,6},{8,9},{9,8},{10,11... | collective-permute-start | bytes 2359304 | tf_op jit(solution)/shard_map/ppermute | solution.py:563
  155.4 4.8 %collective-permute-start.44 = (bf16[384,1024]{1,0:T(8,128)(2,1)S(1)}, bf16[384,1024]{1,0:T(8,128)(2,1)S(1)}, u32[]{:S(2)}, u32[]{:S(2)}) collective-permute-start(bf16[384,1024]{1,0:T(8,128)(2,1)S(1)} %collective-permute-done.39.refs_26_), channel_id=1, source_target_pairs={{0,1},{1,0},{2,3},{3,2},{4,5},{5,4},{6,7},{7,6},{8,9},{9,8},{10,11... | collective-permute-start | bytes 2359304 | tf_op jit(solution)/shard_map/ppermute | solution.py:563
  155.5 2.8 %collective-permute-start.47 = (bf16[32,4096]{1,0:T(8,128)(2,1)}, bf16[32,4096]{1,0:T(8,128)(2,1)S(1)}, u32[]{:S(2)}, u32[]{:S(2)}) collective-permute-start(bf16[32,4096]{1,0:T(8,128)(2,1)} %collective-permute-done.41.refs_29_), channel_id=1, source_target_pairs={{0,1},{1,0},{2,3},{3,2},{4,5},{5,4},{6,7},{7,6},{8,9},{9,8},{10,11... | collective-permute-start | bytes 786440 | tf_op jit(solution)/shard_map/ppermute | solution.py:563
  155.9 3.1 %collective-permute-start.48 = (bf16[32,4096]{1,0:T(8,128)(2,1)}, bf16[32,4096]{1,0:T(8,128)(2,1)S(1)}, u32[]{:S(2)}, u32[]{:S(2)}) collective-permute-start(bf16[32,4096]{1,0:T(8,128)(2,1)} %collective-permute-done.42.refs_30_), channel_id=1, source_target_pairs={{0,1},{1,0},{2,3},{3,2},{4,5},{5,4},{6,7},{7,6},{8,9},{9,8},{10,11... | collective-permute-start | bytes 786440 | tf_op jit(solution)/shard_map/ppermute | solution.py:563
  156.0 3.8 %collective-permute-start.49 = (bf16[32,4096]{1,0:T(8,128)(2,1)}, bf16[32,4096]{1,0:T(8,128)(2,1)S(1)}, u32[]{:S(2)}, u32[]{:S(2)}) collective-permute-start(bf16[32,4096]{1,0:T(8,128)(2,1)} %collective-permute-done.31.refs_31_), channel_id=1, source_target_pairs={{0,1},{1,0},{2,3},{3,2},{4,5},{5,4},{6,7},{7,6},{8,9},{9,8},{10,11... | collective-permute-start | bytes 786440 | tf_op jit(solution)/shard_map/ppermute | solution.py:563
  (40 other events, 401.5 us)
